TPU v7x, 256 devices: a whole 4x4x8 slice. The times are simulated.
256 devices in a mesh: src: 32 (over z, y_lo, core), tgt: 8 (over y_hi, x).
Axes of the slice: x: 4, y: 4 (y_hi: 2, y_lo: 2; y = y_hi * 2 + y_lo), z: 8, core: 2. Of those that a mesh axis runs over, the one named last changes fastest.
Arguments:
- sources: bfloat16 [49152, 256], P('src'), may hold values from -6 to 6, as said below
- targets: bfloat16 [12288, 256], P('tgt'), may hold values from -6 to 6, as said below
- pairs: int32 [32, 8, 24, 2], P('src', 'tgt'), may hold values from 0 to 5, as said below
- counts: int32 [32, 8], P('src', 'tgt'), may hold values from 6 to 24, as said below
Outputs:
- forward_map: float32 [49152, 256], P(('src', 'tgt'))
- backward_map: float32 [12288, 256], P(('tgt', 'src'))
Inputs may be any that keep to these rules, and one draw needn't show every extreme that they name: `sources`: latent entries lie within this range. `targets`: latent entries lie within this range. On each device all 24 slots hold distinct pairs; the first 6 slots name each of its source clusters once and each of its target clusters once. `counts`: uneven over devices; in every draw some device keeps all 24 slots.
All inputs are finite; a program needn't handle non-finite values.
Results may differ from a plain program's by a relative error of at most 0.0003.
Values sent between devices are 32-bit elements; how exact they have to be, the bound alone decides.
No kernel may reach another device: no remote copies, remote signals or barrier semaphores. Data moves between devices by JAX's collectives and lax.ppermute only.
A program may use at most 192 MiB of HBM per device.

v0:
```python
import math

import jax
import jax.numpy as jnp
from jax import lax
from jax.sharding import PartitionSpec as P

BLK = 256
ITERS = 2


NEG_FILL = -1e30
turn_pairs = 8


def fold_block(running, scores, reduce_dim, block_ids, usable):
    local_max = jnp.max(scores, axis=reduce_dim)
    masked = jnp.where(usable[:, None], local_max, NEG_FILL)
    owners = (
        block_ids[:, None] == jnp.arange(running[0].shape[0], dtype=jnp.int32)[None, :]
    ) & usable[:, None]
    candidate = jnp.max(jnp.where(owners[:, :, None], masked[:, None, :], NEG_FILL), axis=0)
    highest = jnp.maximum(running[0], candidate)
    rescale_by = jnp.exp(running[0] - highest)
    lifted = jnp.where(usable[:, None], jnp.exp(local_max - highest[block_ids]), 0.0)
    weights = jnp.exp(scores - jnp.expand_dims(local_max, reduce_dim))
    owner_table = owners.astype(jnp.float32)
    summed = running[1] * rescale_by + jnp.einsum(
        "pb,pi->bi",
        owner_table,
        jnp.sum(weights, axis=reduce_dim) * lifted,
        precision=lax.Precision.HIGHEST,
    )
    return (highest, summed)


def row_log_sums(highest, summed):
    widest = lax.pmax(highest, "tgt")
    summed = lax.psum(summed * jnp.exp(highest - widest), "tgt")
    highest = widest
    return highest + jnp.log(summed)


def col_log_sums(highest, summed):
    widest = lax.pmax(highest, "src")
    summed = lax.psum(summed * jnp.exp(highest - widest), "src")
    highest = widest
    return highest + jnp.log(summed)


def per_device(sources, targets, pairs, counts):
    width = sources.shape[1]
    temper = math.sqrt(width) / 4.0
    blocks = sources.shape[0] // BLK
    src_blocks = sources.reshape(blocks, BLK, width)
    tgt_blocks = targets.reshape(blocks, BLK, width)
    src_half = 0.5 * jnp.sum(jnp.square(src_blocks.astype(jnp.float32)), axis=-1)
    tgt_half = 0.5 * jnp.sum(jnp.square(tgt_blocks.astype(jnp.float32)), axis=-1)
    pair_src = pairs[0, 0, :, 0]
    pair_tgt = pairs[0, 0, :, 1]
    slot_count = pairs.shape[2]
    kept = counts[0, 0]
    turns = (kept + turn_pairs - 1) // turn_pairs

    def sweep(visit, initial):

        def one_turn(turn_index, running):
            slots = turn_index * turn_pairs + jnp.arange(turn_pairs, dtype=jnp.int32)
            usable = slots < kept
            slots = jnp.minimum(slots, slot_count - 1)
            src_ids = pair_src[slots]
            tgt_ids = pair_tgt[slots]
            src_tile = src_blocks[src_ids]
            tgt_tile = tgt_blocks[tgt_ids]
            cross = jnp.einsum(
                "pid,pjd->pij", src_tile, tgt_tile, preferred_element_type=jnp.float32
            )
            pair_cost = src_half[src_ids][:, :, None] + tgt_half[tgt_ids][:, None, :] - cross
            return visit(running, pair_cost, src_tile, tgt_tile, src_ids, tgt_ids, usable)

        return lax.fori_loop(0, turns, one_turn, initial)

    empty_high = jnp.full((blocks, BLK), NEG_FILL, jnp.float32)
    empty_sum = jnp.zeros((blocks, BLK), jnp.float32)
    empty_image = jnp.zeros((blocks, BLK, width), jnp.float32)

    def log_sums(src_pot, tgt_pot):

        def visit(running, pair_cost, src_tile, tgt_tile, src_ids, tgt_ids, usable):
            row_scores = (tgt_pot[tgt_ids][:, None, :] - pair_cost) / temper
            col_scores = (src_pot[src_ids][:, :, None] - pair_cost) / temper
            rows = fold_block(running[0], row_scores, 2, src_ids, usable)
            cols = fold_block(running[1], col_scores, 1, tgt_ids, usable)
            return (rows, cols)

        rows, cols = sweep(visit, ((empty_high, empty_sum), (empty_high, empty_sum)))
        return (row_log_sums(rows[0], rows[1]), col_log_sums(cols[0], cols[1]))

    src_pot = jnp.zeros((blocks, BLK), jnp.float32)
    tgt_pot = jnp.zeros((blocks, BLK), jnp.float32)
    for sweep_index in range(ITERS):
        row_lse, col_lse = log_sums(src_pot, tgt_pot)
        src_pot, tgt_pot = (0.5 * (src_pot - temper * row_lse), 0.5 * (tgt_pot - temper * col_lse))
    row_lse, col_lse = log_sums(src_pot, tgt_pot)

    def visit_project(running, pair_cost, src_tile, tgt_tile, src_ids, tgt_ids, usable):
        row_weights = jnp.exp(
            (tgt_pot[tgt_ids][:, None, :] - pair_cost) / temper - row_lse[src_ids][:, :, None]
        )
        col_weights = jnp.exp(
            (src_pot[src_ids][:, :, None] - pair_cost) / temper - col_lse[tgt_ids][:, None, :]
        )
        row_weights = jnp.where(usable[:, None, None], row_weights, 0.0)
        col_weights = jnp.where(usable[:, None, None], col_weights, 0.0)
        src_owner = (
            (src_ids[:, None] == jnp.arange(blocks, dtype=jnp.int32)[None, :]) & usable[:, None]
        ).astype(jnp.float32)
        tgt_owner = (
            (tgt_ids[:, None] == jnp.arange(blocks, dtype=jnp.int32)[None, :]) & usable[:, None]
        ).astype(jnp.float32)
        forward_part = jnp.einsum(
            "pij,pjd->pid",
            row_weights,
            tgt_tile.astype(jnp.float32),
            precision=lax.Precision.HIGHEST,
        )
        backward_part = jnp.einsum(
            "pij,pid->pjd",
            col_weights,
            src_tile.astype(jnp.float32),
            precision=lax.Precision.HIGHEST,
        )
        forward = running[0] + jnp.einsum(
            "pb,pid->bid", src_owner, forward_part, precision=lax.Precision.HIGHEST
        )
        backward = running[1] + jnp.einsum(
            "pb,pid->bid", tgt_owner, backward_part, precision=lax.Precision.HIGHEST
        )
        return (forward, backward)

    forward, backward = sweep(visit_project, (empty_image, empty_image))
    forward_map = lax.psum_scatter(
        forward.reshape(-1, width), "tgt", scatter_dimension=0, tiled=True
    )
    backward_map = lax.psum_scatter(
        backward.reshape(-1, width), "src", scatter_dimension=0, tiled=True
    )
    return (forward_map, backward_map)


def solution(mesh):
    return jax.shard_map(
        per_device,
        mesh=mesh,
        in_specs=(P("src", None), P("tgt", None), P("src", "tgt", None, None), P("src", "tgt")),
        out_specs=(P(("src", "tgt"), None), P(("tgt", "src"), None)),
        check_vma=False,
    )
```

profile of v0, /device:TPU:8, one launch (start us, length us, event | category | flops | bytes accessed | tf_op | source)
XLA Modules:
  0.0 863.4 jit_solution(16594880988196243230)
XLA Ops:
  11.6 24.4 %while.60 = (s32[]{:T(128)}, f32[6,256]{1,0:T(8,128)S(1)}, f32[6,256]{1,0:T(8,128)S(1)}, f32[6,256]{1,0:T(8,128)S(1)}, f32[6,256]{1,0:T(8,128)S(1)}, /*index=5*/...) while((s32[]{:T(128)}, f32[6,256]{1,0:T(8,128)S(1)}, ...), condition=%wide.region_9.10_spmd, body=%wide.region_2.9_spmd.sunk | while | flops 278237696 | bytes 17231120 | solution.py:81
  17.5 2.4 fusion.193
  29.7 2.4 fusion.193
  36.0 35.9 %pmax.43 = f32[6,256]{1,0:T(8,128)S(1)} all-reduce(f32[6,256]{1,0:T(8,128)S(1)} %get-tuple-element.316), channel_id=1, replica_groups=mesh['src'=32,'tgt'=8] {'tgt'}, use_global_device_ids=true, to_apply=%region_12.13 | all-reduce | flops 1536 | bytes 12288 | tf_op jit(solution)/shard_map/pmax | solution.py:38
  71.9 19.2 %psum.43 = f32[6,256]{1,0:T(8,128)S(1)} all-reduce(f32[6,256]{1,0:T(8,128)S(1)} %exponential_multiply_fusion.4), channel_id=1, replica_groups=mesh['src'=32,'tgt'=8] {'tgt'}, use_global_device_ids=true, to_apply=%region_13.14 | all-reduce | flops 1536 | bytes 12288 | tf_op jit(solution)/shard_map/psum | solution.py:39
  91.1 50.2 %pmax.42 = f32[6,256]{1,0:T(8,128)S(1)} all-reduce(f32[6,256]{1,0:T(8,128)S(1)} %get-tuple-element.314), channel_id=1, replica_groups=mesh['src'=32,'tgt'=8] {'src'}, use_global_device_ids=true, to_apply=%region_10.11 | all-reduce | flops 1536 | bytes 12288 | tf_op jit(solution)/shard_map/pmax | solution.py:45
  141.3 54.4 %psum.42 = f32[6,256]{1,0:T(8,128)S(1)} all-reduce(f32[6,256]{1,0:T(8,128)S(1)} %exponential_multiply_fusion.5), channel_id=1, replica_groups=mesh['src'=32,'tgt'=8] {'src'}, use_global_device_ids=true, to_apply=%region_11.12 | all-reduce | flops 1536 | bytes 12288 | tf_op jit(solution)/shard_map/psum | solution.py:46
  195.8 24.4 %while.61 = (s32[]{:T(128)}, f32[6,256]{1,0:T(8,128)S(1)}, f32[6,256]{1,0:T(8,128)S(1)}, f32[6,256]{1,0:T(8,128)S(1)}, f32[6,256]{1,0:T(8,128)S(1)}, /*index=5*/...) while((s32[]{:T(128)}, f32[6,256]{1,0:T(8,128)S(1)}, ...), condition=%wide.region_21.22_spmd, body=%wide.region_14.21_spmd.sunk | while | flops 278237696 | bytes 17224980 | solution.py:81
  220.1 33.6 %pmax.45 = f32[6,256]{1,0:T(8,128)S(1)} all-reduce(f32[6,256]{1,0:T(8,128)S(1)} %get-tuple-element.320), channel_id=1, replica_groups=mesh['src'=32,'tgt'=8] {'tgt'}, use_global_device_ids=true, to_apply=%region_24.25 | all-reduce | flops 1536 | bytes 12288 | tf_op jit(solution)/shard_map/pmax | solution.py:38
  253.7 19.2 %psum.45 = f32[6,256]{1,0:T(8,128)S(1)} all-reduce(f32[6,256]{1,0:T(8,128)S(1)} %exponential_multiply_fusion.2), channel_id=1, replica_groups=mesh['src'=32,'tgt'=8] {'tgt'}, use_global_device_ids=true, to_apply=%region_25.26 | all-reduce | flops 1536 | bytes 12288 | tf_op jit(solution)/shard_map/psum | solution.py:39
  273.0 51.8 %pmax.44 = f32[6,256]{1,0:T(8,128)S(1)} all-reduce(f32[6,256]{1,0:T(8,128)S(1)} %get-tuple-element.318), channel_id=1, replica_groups=mesh['src'=32,'tgt'=8] {'src'}, use_global_device_ids=true, to_apply=%region_22.23 | all-reduce | flops 1536 | bytes 12288 | tf_op jit(solution)/shard_map/pmax | solution.py:45
  324.8 54.0 %psum.44 = f32[6,256]{1,0:T(8,128)S(1)} all-reduce(f32[6,256]{1,0:T(8,128)S(1)} %exponential_multiply_fusion.3), channel_id=1, replica_groups=mesh['src'=32,'tgt'=8] {'src'}, use_global_device_ids=true, to_apply=%region_23.24 | all-reduce | flops 1536 | bytes 12288 | tf_op jit(solution)/shard_map/psum | solution.py:46
  378.9 24.4 %while.62 = (s32[]{:T(128)}, f32[6,256]{1,0:T(8,128)S(1)}, f32[6,256]{1,0:T(8,128)S(1)}, f32[6,256]{1,0:T(8,128)S(1)}, f32[6,256]{1,0:T(8,128)S(1)}, /*index=5*/...) while((s32[]{:T(128)}, f32[6,256]{1,0:T(8,128)S(1)}, ...), condition=%wide.region_33.34_spmd, body=%wide.region_26.33_spmd.sunk | while | flops 278237696 | bytes 17224980 | solution.py:81
  403.3 65.6 %pmax.47 = f32[6,256]{1,0:T(8,128)S(1)} all-reduce(f32[6,256]{1,0:T(8,128)S(1)} %get-tuple-element.324), channel_id=1, replica_groups=mesh['src'=32,'tgt'=8] {'src'}, use_global_device_ids=true, to_apply=%region_36.37 | all-reduce | flops 1536 | bytes 12288 | tf_op jit(solution)/shard_map/pmax | solution.py:45
  468.9 54.0 %psum.47 = f32[6,256]{1,0:T(8,128)S(1)} all-reduce(f32[6,256]{1,0:T(8,128)S(1)} %exponential_multiply_fusion), channel_id=1, replica_groups=mesh['src'=32,'tgt'=8] {'src'}, use_global_device_ids=true, to_apply=%region_37.38 | all-reduce | flops 1536 | bytes 12288 | tf_op jit(solution)/shard_map/psum | solution.py:46
  523.0 23.2 %pmax.46 = f32[6,256]{1,0:T(8,128)S(1)} all-reduce(f32[6,256]{1,0:T(8,128)S(1)} %get-tuple-element.322), channel_id=1, replica_groups=mesh['src'=32,'tgt'=8] {'tgt'}, use_global_device_ids=true, to_apply=%region_34.35 | all-reduce | flops 1536 | bytes 12288 | tf_op jit(solution)/shard_map/pmax | solution.py:38
  546.2 19.2 %psum.46 = f32[6,256]{1,0:T(8,128)S(1)} all-reduce(f32[6,256]{1,0:T(8,128)S(1)} %exponential_multiply_fusion.1), channel_id=1, replica_groups=mesh['src'=32,'tgt'=8] {'tgt'}, use_global_device_ids=true, to_apply=%region_35.36 | all-reduce | flops 1536 | bytes 12288 | tf_op jit(solution)/shard_map/psum | solution.py:39
  568.3 57.2 %while.63 = (s32[]{:T(128)}, f32[6,256,256]{2,0,1:T(8,128)}, f32[6,256,256]{2,0,1:T(8,128)}, s32[]{:T(128)}, s32[24]{0:T(128)S(1)}, /*index=5*/s32[]{:T(128)}, s...) while((s32[]{:T(128)}, f32[6,256,256]{2,0,1:T(8,128)}, ...), condition=%wide.region_39.40_spmd, body=%wide.region_38.39_spmd.sunk | while | flops 3572239616 | bytes 29537244 | solution.py:81
  571.9 3.0 fusion.230
  577.9 4.3 fusion.233
  582.2 5.2 fusion.234
  588.5 3.3 fusion.231
  591.8 5.1 fusion.232
  600.5 3.0 fusion.230
  606.5 4.3 fusion.233
  610.8 5.2 fusion.234
  617.1 3.3 fusion.231
  620.4 5.1 fusion.232
  625.6 3.3 copy.13
  628.9 3.2 copy.14
  632.1 107.9 %reduce-scatter.3.cloned.1.call-done = f32[192,256]{1,0:T(8,128)} async-done(((f32[1536,256]{1,0:T(8,128)}), f32[192,256]{1,0:T(8,128)}) %reduce-scatter.3.cloned.1.call-update) | async-done | bytes 196624 | tf_op jit(solution)/shard_map/reduce_scatter | solution.py:142
  740.1 116.5 %reduce-scatter.5.cloned.1.call-done = f32[48,256]{1,0:T(8,128)} async-done(((f32[1536,256]{1,0:T(8,128)}), f32[48,256]{1,0:T(8,128)}) %reduce-scatter.5.cloned.1.call-update) | async-done | bytes 49168 | tf_op jit(solution)/shard_map/reduce_scatter | solution.py:145
  (267 shorter events, 89.4 us)
Async XLA Ops:
  7.2 732.9 %reduce-scatter.3.cloned.1.call-start = ((), (), s32[]{:S(2)}) async-start(), calls=%async_computation.2 | async-start | bytes 1769472 | tf_op jit(solution)/shard_map/reduce_scatter | solution.py:142
  11.6 3.7 copy-start
  11.6 4.3 copy-start.4
  23.8 3.7 copy-start
  23.8 4.3 copy-start.4
  195.8 3.6 copy-start.1
  195.8 4.3 copy-start.5
  208.0 3.6 copy-start.1
  208.0 4.3 copy-start.5
  378.9 3.6 copy-start.2
  378.9 4.3 copy-start.6
  391.1 3.6 copy-start.2
  391.1 4.3 copy-start.6
  565.4 2.9 copy-start.3
  565.4 2.9 copy-start.7
  628.8 227.8 %reduce-scatter.5.cloned.1.call-start = ((), (), s32[]{:S(2)}) async-start(), calls=%async_computation.3 | async-start | bytes 1622016 | tf_op jit(solution)/shard_map/reduce_scatter | solution.py:145
Sparse Core Ops, SparseCore 0:
  629.0 111.0 reduce-scatter.2
  743.1 113.3 reduce-scatter.4
where the time goes:
time: 869 us; the launch traced here: 863 us
  blocking collectives  480 us (55%)
  waiting for transfers between devices  224 us (26%)
  local copies, waits for them, and re-layouts  65.5 us (8%)
  matrix products  58.4 us (7%)
  other arithmetic  18.5 us (2%)
  between operations  15.1 us (2%)
    pmax x3, blocking collectives, col_log_sums(): widest = lax.pmax(highest, 'src')  168 us
    psum x3, blocking collectives, col_log_sums(): summed = lax.psum(summed * jnp.exp(highest - widest), 'src')  162 us
    reduce_scatter x1, waiting for transfers between devices, per_device(): lax.psum_scatter(backward.reshape(-1, width), 'src', scatter_dimension=0,...  117 us
    reduce_scatter x1, waiting for transfers between devices, per_device(): lax.psum_scatter(forward.reshape(-1, width), 'tgt', scatter_dimension=0,...  108 us
    pmax x3, blocking collectives, row_log_sums(): widest = lax.pmax(highest, 'tgt')  92.6 us
    psum x3, blocking collectives, row_log_sums(): summed = lax.psum(summed * jnp.exp(highest - widest), 'tgt')  57.7 us
    dot_general x8, matrix products, one_turn(): jnp.einsum('pid,pjd->pij', src_tile, tgt_tile, preferred_element_type=jnp...  20.4 us
  transfers between devices with their start and end apart: 2, of which 2 were waited for; matrix products, arithmetic and copies ran while one was open for 0% of the time, Pallas kernels for 0%

commit v1 on v0

v1 whole, which is shorter than its diff:
```python
import functools
import math

import jax
import jax.numpy as jnp
from jax import lax
from jax.experimental import pallas as pl
from jax.experimental.pallas import tpu as pltpu
from jax.sharding import PartitionSpec as P

BLK = 256
ITERS = 2
NEG = -1e30
VMEM_BYTES = 24 * 1024 * 1024


def log_sum(parts):
    high = functools.reduce(jnp.maximum, parts)
    total = functools.reduce(jnp.add, [jnp.exp2(part - high) for part in parts])
    return high + jnp.log2(total)


def down_rows(lanes, blocks, wide_ref):
    upright = jnp.transpose(lanes)
    for b in range(blocks):
        wide_ref[b] = jnp.broadcast_to(upright[:, b : b + 1], (BLK, 128))


def norms(z_ref, scale, blocks, wide_ref):
    lane = lax.broadcasted_iota(jnp.int32, (BLK, 128), 1)
    gathered = jnp.zeros((BLK, 128), jnp.float32)
    for b in range(blocks):
        z = z_ref[b].astype(jnp.float32)
        half = jnp.sum(z * z, axis=1, keepdims=True) * (-0.5 * scale)
        wide = jnp.broadcast_to(half, (BLK, 128))
        wide_ref[b] = wide
        gathered = jnp.where(lane == b, wide, gathered)
    return jnp.transpose(gathered)[:8]


def over_pairs(pairs_ref, kept, visit):
    def two(step, carry):
        p = 2 * step
        visit(pairs_ref[2 * p], pairs_ref[2 * p + 1])
        visit(pairs_ref[2 * p + 2], pairs_ref[2 * p + 3])
        return carry

    lax.fori_loop(0, kept // 2, two, 0)

    @pl.when(kept % 2 == 1)
    def _():
        p = kept - 1
        visit(pairs_ref[2 * p], pairs_ref[2 * p + 1])


def cross(a, b):
    return lax.dot_general(a, b, (((1,), (1,)), ((), ())), preferred_element_type=jnp.float32)


def fold(scores, wide, scale, high_ref, sum_ref, b):
    for h in range(2):
        at = slice(128 * h, 128 * h + 128)
        t = (scores[:, at] * scale + wide).reshape(BLK // 8, 8, 128)
        old = high_ref[b, :, at]
        high = jnp.maximum(old, jnp.max(t, axis=0))
        total = jnp.sum(jnp.exp2(t - high[None]), axis=0)
        sum_ref[b, :, at] = sum_ref[b, :, at] * jnp.exp2(old - high) + total
        high_ref[b, :, at] = high


def settle(high_ref, sum_ref, blocks):
    rows = []
    for b in range(blocks):
        high = high_ref[b]
        top = jnp.max(high, axis=0, keepdims=True)
        total = jnp.sum(sum_ref[b] * jnp.exp2(high - top), axis=0, keepdims=True)
        rows.append(top + jnp.log2(total))
    rows += [jnp.zeros((1, BLK), jnp.float32)] * (8 - blocks)
    return jnp.concatenate(rows, axis=0)


def start_potentials(x_ref, y_ref, rest, first, n_row, n_col, scale, blocks, f_wide, g_wide):
    if first:
        return norms(x_ref, scale, blocks, f_wide), norms(y_ref, scale, blocks, g_wide), rest
    f_old, g_old = rest[0][...], rest[1][...]
    rows = [part for r in rest[2 : 2 + n_row] for part in parts_of(r)]
    cols = [part for r in rest[2 + n_row : 2 + n_row + n_col] for part in parts_of(r)]
    f = 0.5 * (f_old - log_sum(rows))
    g = 0.5 * (g_old - log_sum(cols))
    down_rows(f, blocks, f_wide)
    down_rows(g, blocks, g_wide)
    return f, g, rest[2 + n_row + n_col :]


def parts_of(ref):
    if len(ref.shape) == 2:
        return [ref[...]]
    return [ref[k] for k in range(ref.shape[0])]


def pass_sums(pairs_ref, kept, x_ref, y_ref, scale, f_wide, g_wide, row_high, row_sum, col_high, col_sum):
    for ref in (row_high, col_high):
        ref[...] = jnp.full(ref.shape, NEG, jnp.float32)
    for ref in (row_sum, col_sum):
        ref[...] = jnp.zeros(ref.shape, jnp.float32)

    def visit(s, t):
        xs, yt = x_ref[s], y_ref[t]
        fold(cross(yt, xs), g_wide[t], scale, row_high, row_sum, s)
        fold(cross(xs, yt), f_wide[s], scale, col_high, col_sum, t)

    over_pairs(pairs_ref, kept, visit)


def sweep_kernel(first, n_row, n_col, scale, blocks, pairs_ref, count_ref, x_ref, y_ref, *rest):
    scratch = rest[-6:]
    f_wide, g_wide, row_high, row_sum, col_high, col_sum = scratch
    f, g, outs = start_potentials(
        x_ref, y_ref, rest[:-6], first, n_row, n_col, scale, blocks, f_wide, g_wide
    )
    f_out, g_out, row_out, col_out = outs
    f_out[...] = f
    g_out[...] = g
    pass_sums(pairs_ref, count_ref[0], x_ref, y_ref, scale, *scratch)
    row_out[...] = settle(row_high, row_sum, blocks)
    col_out[...] = settle(col_high, col_sum, blocks)


def split_two(w):
    high = w.astype(jnp.bfloat16)
    return high, (w - high.astype(jnp.float32)).astype(jnp.bfloat16)


def weigh(scores, scale, lanes, wide):
    halves = []
    for h in range(2):
        at = slice(128 * h, 128 * h + 128)
        t = (scores[:, at] * scale - wide).reshape(BLK // 8, 8, 128) + lanes[:, at][None]
        halves.append(jnp.exp2(t).reshape(BLK, 128))
    return jnp.concatenate(halves, axis=1)


def emit(image, log_sums, blocks, out_ref):
    n, rows = out_ref.shape[0], (blocks * BLK) // out_ref.shape[0]
    lane = lax.broadcasted_iota(jnp.int32, (1, BLK), 1)
    shifted = {}
    for b in range(n):
        done = 0
        while done < rows:
            at = b * rows + done
            k, off = at // BLK, at % BLK
            take = min(rows - done, BLK - off)
            out_ref[b, done : done + take, :] = image[k, off : off + take, :]
            done += take
        for part in range(0, rows, BLK):
            at = b * rows + part
            k, off = at // BLK, at % BLK
            if off not in shifted:
                shifted[off] = pltpu.roll(log_sums, BLK - off, 1) if off else log_sums
            turned = shifted[off]
            line = turned[k : k + 1]
            if off and k + 1 < blocks:
                line = jnp.where(lane < BLK - off, line, turned[k + 1 : k + 2])
            spot = rows + part // BLK
            out_ref[b, spot : spot + 1, :] = line


def project_kernel(n_row, n_col, scale, blocks, pairs_ref, count_ref, x_ref, y_ref, *rest):
    scratch = rest[-6:]
    f_wide, g_wide, row_high, row_sum, col_high, col_sum = scratch
    f_lanes, g_lanes, forward, backward = rest[-10:-6]
    f, g, outs = start_potentials(
        x_ref, y_ref, rest[:-10], False, n_row, n_col, scale, blocks, f_wide, g_wide
    )
    forward_out, backward_out = outs
    kept = count_ref[0]
    pass_sums(pairs_ref, kept, x_ref, y_ref, scale, *scratch)
    row = settle(row_high, row_sum, blocks)
    col = settle(col_high, col_sum, blocks)
    for b in range(blocks):
        f_lanes[b] = jnp.broadcast_to(f[b : b + 1], (8, BLK))
        g_lanes[b] = jnp.broadcast_to(g[b : b + 1], (8, BLK))
    down_rows(row, blocks, f_wide)
    down_rows(col, blocks, g_wide)
    forward[...] = jnp.zeros(forward.shape, jnp.float32)
    backward[...] = jnp.zeros(backward.shape, jnp.float32)

    def visit(s, t):
        xs, yt = x_ref[s], y_ref[t]
        high, low = split_two(weigh(cross(xs, yt), scale, g_lanes[t], f_wide[s]))
        forward[s] += jnp.dot(high, yt, preferred_element_type=jnp.float32) + jnp.dot(
            low, yt, preferred_element_type=jnp.float32
        )
        high, low = split_two(weigh(cross(yt, xs), scale, f_lanes[s], g_wide[t]))
        backward[t] += jnp.dot(high, xs, preferred_element_type=jnp.float32) + jnp.dot(
            low, xs, preferred_element_type=jnp.float32
        )

    over_pairs(pairs_ref, kept, visit)
    emit(forward, row, blocks, forward_out)
    emit(backward, col, blocks, backward_out)


def merge_kernel(rows, parts_ref, out_ref):
    n = parts_ref.shape[0]
    for part in range(0, rows, BLK):
        spot = rows + part // BLK
        size = min(BLK, rows - part)
        logs = jnp.concatenate([parts_ref[d, spot : spot + 1, :] for d in range(n)], axis=0)
        high = jnp.max(logs, axis=0, keepdims=True)
        lifted = jnp.exp2(logs - high)
        weights = lifted / jnp.sum(lifted, axis=0, keepdims=True)
        upright = jnp.transpose(weights)
        total = jnp.zeros((size, BLK), jnp.float32)
        for d in range(n):
            total += upright[:size, d : d + 1] * parts_ref[d, part : part + size, :]
        out_ref[part : part + size, :] = total


def in_vmem(n):
    return [pl.BlockSpec(memory_space=pltpu.VMEM)] * n


def shape(*dims):
    return jax.ShapeDtypeStruct(dims, jnp.float32)


def sums_scratch(blocks):
    return [pltpu.VMEM((blocks, BLK, 128), jnp.float32)] * 2 + [
        pltpu.VMEM((blocks, 8, BLK), jnp.float32)
    ] * 4


def gather_by_permutes(mine, axis, moves):
    return [mine] + [lax.ppermute(mine, axis, move) for move in moves]


def turns(groups):
    size = len(groups[0])
    return [
        [(g[k], g[(k + r) % size]) for g in groups for k in range(size)] for r in range(1, size)
    ]


def per_device(n_src, n_tgt, sources, targets, pairs, counts):
    width = sources.shape[1]
    scale = math.log2(math.e) / (math.sqrt(width) / 4.0)
    blocks = sources.shape[0] // BLK
    x = sources.reshape(blocks, BLK, width)
    y = targets.reshape(blocks, BLK, width)
    pair_list = pairs.reshape(-1)
    kept = counts.reshape(-1)
    head = [pl.BlockSpec(memory_space=pltpu.SMEM)] * 2 + in_vmem(2)
    params = pltpu.CompilerParams(vmem_limit_bytes=VMEM_BYTES)

    def sweep(first, extra, n_row, n_col):
        return pl.pallas_call(
            functools.partial(sweep_kernel, first, n_row, n_col, scale, blocks),
            out_shape=[shape(8, BLK)] * 4,
            in_specs=head + in_vmem(len(extra)),
            out_specs=in_vmem(4),
            scratch_shapes=sums_scratch(blocks),
            compiler_params=params,
        )(pair_list, kept, x, y, *extra)

    all_tgt = turns([list(range(n_tgt))])
    near = turns([list(range(k, k + 4)) for k in range(0, n_src, 4)])
    far = turns([list(range(k, n_src, 4)) for k in range(4)])

    f, g, row, col = sweep(True, [], 0, 0)
    rows = gather_by_permutes(row, "tgt", all_tgt)
    cols = [lax.all_gather(col, "src")]
    f, g, row, col = sweep(False, [f, g, *rows, *cols], len(rows), len(cols))

    rows = [lax.all_gather(row, "tgt")]
    col = log_sum(gather_by_permutes(col, "src", near))
    cols = gather_by_permutes(col, "src", far)
    extra = [f, g, *rows, *cols]
    f_rows, b_rows = blocks * BLK // n_tgt, blocks * BLK // n_src
    forward, backward = pl.pallas_call(
        functools.partial(project_kernel, len(rows), len(cols), scale, blocks),
        out_shape=[shape(n_tgt, f_rows + 8, width), shape(n_src, b_rows + 8, width)],
        in_specs=head + in_vmem(len(extra)),
        out_specs=in_vmem(2),
        scratch_shapes=[pltpu.VMEM((blocks, 8, BLK), jnp.float32)] * 2
        + [pltpu.VMEM((blocks, BLK, width), jnp.float32)] * 2
        + sums_scratch(blocks),
        compiler_params=params,
    )(pair_list, kept, x, y, *extra)

    def merge(parts, rows):
        return pl.pallas_call(
            functools.partial(merge_kernel, rows),
            out_shape=shape(rows, width),
            in_specs=in_vmem(1),
            out_specs=pl.BlockSpec(memory_space=pltpu.VMEM),
            compiler_params=params,
        )(parts)

    forward = lax.all_to_all(forward, "tgt", 0, 0, tiled=True)
    backward = lax.all_to_all(backward, "src", 0, 0, tiled=True)
    return (merge(forward, f_rows), merge(backward, b_rows))


def solution(mesh):
    return jax.shard_map(
        functools.partial(per_device, mesh.shape["src"], mesh.shape["tgt"]),
        mesh=mesh,
        in_specs=(P("src", None), P("tgt", None), P("src", "tgt", None, None), P("src", "tgt")),
        out_specs=(P(("src", "tgt"), None), P(("tgt", "src"), None)),
        check_vma=False,
    )
```

time: 869 us -> 211 us (0.24)
  blocking collectives: 480 us -> 91.2 us
  waiting for transfers between devices: 224 us -> 46.6 us
  local copies, waits for them, and re-layouts: 65.5 us -> 3.12 us
  matrix products: 58.4 us -> 0 us
  Pallas kernels: 0 us -> 33.7 us
  starting transfers between devices: 0.08 us -> 32.8 us
  other arithmetic: 18.5 us -> 0.03 us
  between operations: 15.1 us -> 1.39 us
    pmax x6 -> x0, blocking collectives: 260 us -> none  [the longest x3 168 us: col_log_sums(): widest = lax.pmax(highest, 'src')]
    reduce_scatter x2 -> x0, waiting for transfers between devices: 224 us -> none  [the longest x1 117 us: per_device(): lax.psum_scatter(backward.reshape(-1, width), 'src', scatter_dimension=0,...]
    psum x6 -> x0, blocking collectives: 220 us -> none  [the longest x3 162 us: col_log_sums(): summed = lax.psum(summed * jnp.exp(highest - widest), 'src')]
    all_gather x0 -> x2, blocking collectives: none -> 72.5 us  [the longest x1 37.2 us: per_device(): cols = [lax.all_gather(col, 'src')]]
    dot_general x28 -> x0, matrix products: 58.4 us -> none  [the longest x8 20.4 us: one_turn(): jnp.einsum('pid,pjd->pij', src_tile, tgt_tile, preferred_element_type=jnp...]
    gather x80 -> x0, local copies, waits for them, and re-layouts: 55.2 us -> none  [the longest x8 10.8 us: one_turn(): tgt_tile = tgt_blocks[tgt_ids]]
    all_to_all x0 -> x1, waiting for transfers between devices: none -> 43.5 us  [per_device(): backward = lax.all_to_all(backward, 'src', 0, 0, tiled=True)]
    pallas_call x0 -> x5, Pallas kernels: none -> 33.7 us  [the longest x1 17.7 us: per_device(): pl.pallas_call(functools.partial(project_kernel, len(rows), len(cols), sc...]
  transfers between devices with their start and end apart: 2 -> 18, of which waited for: 2 -> 3; matrix products, arithmetic and copies ran while one was open for 0% -> 0% of each run, Pallas kernels for 0% -> 1%
where the time goes in v1:
time: 211 us; the launch traced here: 209 us
  blocking collectives  91.2 us (43%)
  waiting for transfers between devices  46.6 us (22%)
  Pallas kernels  33.7 us (16%)
  starting transfers between devices  32.8 us (16%)
  local copies, waits for them, and re-layouts  3.12 us (1%)
    all_to_all x1, waiting for transfers between devices, per_device(): backward = lax.all_to_all(backward, 'src', 0, 0, tiled=True)  43.5 us
    all_gather x1, blocking collectives, per_device(): cols = [lax.all_gather(col, 'src')]  37.2 us
    all_gather x1, blocking collectives, per_device(): rows = [lax.all_gather(row, 'tgt')]  35.3 us
    ppermute x17, starting transfers between devices, gather_by_permutes(): return [mine] + [lax.ppermute(mine, axis, move) for move in moves]  23.9 us
    all_to_all x1, blocking collectives, per_device(): forward = lax.all_to_all(forward, 'tgt', 0, 0, tiled=True)  18.7 us
    pallas_call x1, Pallas kernels, per_device(): pl.pallas_call(functools.partial(project_kernel, len(rows), len(cols), sc...  17.7 us
    pallas_call x2, Pallas kernels, sweep(): pl.pallas_call(functools.partial(sweep_kernel, first, n_row, n_col, scale...  13.7 us
    all_to_all x1, starting transfers between devices, per_device(): backward = lax.all_to_all(backward, 'src', 0, 0, tiled=True)  8.86 us
  transfers between devices with their start and end apart: 18, of which 3 were waited for; matrix products, arithmetic and copies ran while one was open for 0% of the time, Pallas kernels for 1%

profile of v1, /device:TPU:8, one launch (start us, length us, event | category | flops | bytes accessed | tf_op | source)
XLA Modules:
  0.0 208.8 jit_solution(4567691555231217566)
XLA Ops:
  1.3 0.8 copy.7
  2.0 0.1 reshape.16.pairs_ref
  2.1 0.0 copy-start
  2.1 1.1 copy-done
  3.3 1.1 copy-done.1
  4.4 6.8 %shard_map.59 = (f32[8,256]{1,0:T(8,128)S(1)}, f32[8,256]{1,0:T(8,128)S(1)}, f32[8,256]{1,0:T(8,128)S(1)}, f32[8,256]{1,0:T(8,128)S(1)}) custom-call(s32[48]{0:T(128)S(1)} %reshape.16.pairs_ref, s32[1]{0:T(128)} %bitcast.7.count_ref, bf16[6,256,256]{2,1,0:T(8,128)(2,1)S(1)} %bitcast.10, bf16[6,256,256]{2,1,0:T(8,128)(2,1)S(1)} %bitcast.13), custom_call_target="tpu_custom_call" | custom-call | tf_op jit(solution)/shard_map/pallas_call | solution.py:257
  11.2 1.8 collective-permute-start.6
  13.0 2.6 %collective-permute-start.5 = (f32[8,256]{1,0:T(8,128)S(1)}, f32[8,256]{1,0:T(8,128)S(1)}, u32[]{:S(2)}, u32[]{:S(2)}) collective-permute-start(f32[8,256]{1,0:T(8,128)S(1)} %get-tuple-element.14.rest_2_), channel_id=1, source_target_pairs={{0,6},{1,7},{2,0},{3,1},{4,2},{5,3},{6,4},{7,5},{8,14},{9,15},{10,... | collective-permute-start | bytes 24584 | tf_op jit(solution)/shard_map/ppermute | solution.py:235
  15.6 0.0 collective-permute-start.4
  15.6 4.3 %collective-permute-start.3 = (f32[8,256]{1,0:T(8,128)S(1)}, f32[8,256]{1,0:T(8,128)S(1)}, u32[]{:S(2)}, u32[]{:S(2)}) collective-permute-start(f32[8,256]{1,0:T(8,128)S(1)} %get-tuple-element.14.rest_2_), channel_id=1, source_target_pairs={{0,4},{1,5},{2,6},{3,7},{4,0},{5,1},{6,2},{7,3},{8,12},{9,13},{10,... | collective-permute-start | bytes 24584 | tf_op jit(solution)/shard_map/ppermute | solution.py:235
  19.9 2.1 collective-permute-start.1
  22.0 0.0 collective-permute-done.5.rest_8_
  22.0 37.2 %all-gather = f32[256,256]{1,0:T(8,128)S(1)} all-gather(f32[8,256]{1,0:T(8,128)S(1)} %get-tuple-element.15), channel_id=2, replica_groups=mesh['src'=32,'tgt'=8] {'src'}, dimensions={0}, use_global_device_ids=true | all-gather | bytes 270336 | tf_op jit(solution)/shard_map/all_gather | solution.py:272
  59.2 7.0 %shard_map.60 = (f32[8,256]{1,0:T(8,128)S(1)}, f32[8,256]{1,0:T(8,128)S(1)}, f32[8,256]{1,0:T(8,128)S(1)}, f32[8,256]{1,0:T(8,128)S(1)}) custom-call(s32[48]{0:T(128)S(1)} %reshape.16.pairs_ref, s32[1]{0:T(128)} %bitcast.8.count_ref, bf16[6,256,256]{2,1,0:T(8,128)(2,1)S(1)} %bitcast.11, bf16[6,256,256]{2,1,0:T(8,128)(2,1)S(1)} %bitcast.14, ...), custom_call_target="tpu_custom_call" | custom-call | tf_op jit(solution)/shard_map/pallas_call | solution.py:257
  66.2 0.1 collective-permute-start.9
  66.3 1.6 collective-permute-start.8
  67.9 2.1 %collective-permute-done.8 = f32[8,256]{1,0:T(8,128)S(1)} collective-permute-done((f32[8,256]{1,0:T(8,128)S(1)}, f32[8,256]{1,0:T(8,128)S(1)}, u32[]{:S(2)}, u32[]{:S(2)}) %collective-permute-start.8) | collective-permute-done | bytes 8224 | tf_op jit(solution)/shard_map/ppermute | solution.py:235
  70.1 0.9 collective-permute-done.7
  71.0 0.7 collective-permute-start.16
  71.7 0.1 collective-permute-start.15
  71.8 3.2 %collective-permute-start.14 = (f32[8,256]{1,0:T(8,128)S(1)}, f32[8,256]{1,0:T(8,128)S(1)}, u32[]{:S(2)}, u32[]{:S(2)}) collective-permute-start(f32[8,256]{1,0:T(8,128)S(1)} %multiply_add_fusion.rest_3_), channel_id=1, source_target_pairs={{0,160},{32,192},{64,224},{96,0},{128,32},{160,64},{192,96},{224,1... | collective-permute-start | bytes 24584 | tf_op jit(solution)/shard_map/ppermute | solution.py:235
  75.1 2.7 %collective-permute-start.13 = (f32[8,256]{1,0:T(8,128)S(1)}, f32[8,256]{1,0:T(8,128)S(1)}, u32[]{:S(2)}, u32[]{:S(2)}) collective-permute-start(f32[8,256]{1,0:T(8,128)S(1)} %multiply_add_fusion.rest_3_), channel_id=1, source_target_pairs={{0,128},{32,160},{64,192},{96,224},{128,0},{160,32},{192,64},{224,... | collective-permute-start | bytes 24584 | tf_op jit(solution)/shard_map/ppermute | solution.py:235
  77.7 2.3 %collective-permute-start.12 = (f32[8,256]{1,0:T(8,128)S(1)}, f32[8,256]{1,0:T(8,128)S(1)}, u32[]{:S(2)}, u32[]{:S(2)}) collective-permute-start(f32[8,256]{1,0:T(8,128)S(1)} %multiply_add_fusion.rest_3_), channel_id=1, source_target_pairs={{0,96},{32,128},{64,160},{96,192},{128,224},{160,0},{192,32},{224,... | collective-permute-start | bytes 24584 | tf_op jit(solution)/shard_map/ppermute | solution.py:235
  80.0 2.1 %collective-permute-start.11 = (f32[8,256]{1,0:T(8,128)S(1)}, f32[8,256]{1,0:T(8,128)S(1)}, u32[]{:S(2)}, u32[]{:S(2)}) collective-permute-start(f32[8,256]{1,0:T(8,128)S(1)} %multiply_add_fusion.rest_3_), channel_id=1, source_target_pairs={{0,64},{32,96},{64,128},{96,160},{128,192},{160,224},{192,0},{224,... | collective-permute-start | bytes 24584 | tf_op jit(solution)/shard_map/ppermute | solution.py:235
  82.2 0.3 collective-permute-start.10
  82.4 35.3 %all-gather.1 = f32[64,256]{1,0:T(8,128)S(1)} all-gather(f32[8,256]{1,0:T(8,128)S(1)} %get-tuple-element.18), channel_id=3, replica_groups=mesh['src'=32,'tgt'=8] {'tgt'}, dimensions={0}, use_global_device_ids=true | all-gather | bytes 73728 | tf_op jit(solution)/shard_map/all_gather | solution.py:275
  117.7 17.7 %shard_map.61 = (f32[8,200,256]{2,1,0:T(8,128)S(1)}, f32[32,56,256]{2,1,0:T(8,128)S(1)}) custom-call(s32[48]{0:T(128)S(1)} %reshape.16.pairs_ref, s32[1]{0:T(128)} %bitcast.9.count_ref, bf16[6,256,256]{2,1,0:T(8,128)(2,1)S(1)} %bitcast.12, bf16[6,256,256]{2,1,0:T(8,128)(2,1)S(1)} %bitcast.15, f32[8,256]{1,0:T(8,128)S(1)} %get-tuple-element.16.rest_0_, ...), custom_call_target="tpu_custom_call" | custom-call | tf_op jit(solution)/shard_map/pallas_call | solution.py:280
  135.5 18.7 %all_to_all.10.parts_ref = f32[8,200,256]{2,1,0:T(8,128)S(1)} all-to-all(f32[8,200,256]{2,1,0:T(8,128)S(1)} %get-tuple-element.20), channel_id=1, replica_groups=mesh['src'=32,'tgt'=8] {'tgt'}, dimensions={0} | all-to-all | bytes 3276800 | tf_op jit(solution)/shard_map/all_to_all | solution.py:300
  154.1 8.9 %all-to-all-start.1 = ((f32[32,56,256]{2,1,0:T(8,128)}), f32[32,56,256]{2,1,0:T(8,128)S(1)}, u32[]{:S(2)}, u32[]{:S(2)}) async-start(f32[32,56,256]{2,1,0:T(8,128)} %copy-done.2), calls=%async_computation.1 | async-start | bytes 3670016 | tf_op jit(solution)/shard_map/all_to_all | solution.py:301
  163.0 1.2 shard_map.62
  164.2 43.5 %all-to-all-done.1.parts_ref = f32[32,56,256]{2,1,0:T(8,128)S(1)} async-done(((f32[32,56,256]{2,1,0:T(8,128)}), f32[32,56,256]{2,1,0:T(8,128)S(1)}, u32[]{:S(2)}, u32[]{:S(2)}) %all-to-all-start.1) | async-done | bytes 1835040 | tf_op jit(solution)/shard_map/all_to_all | solution.py:301
  207.7 1.1 shard_map.63
  (21 shorter events, 0.1 us)
Async XLA Ops:
  2.1 1.1 copy-start
  3.3 1.1 copy-start.1
  11.2 8.7 %collective-permute-start.6 = (f32[8,256]{1,0:T(8,128)S(1)}, f32[8,256]{1,0:T(8,128)S(1)}, u32[]{:S(2)}, u32[]{:S(2)}) collective-permute-start(f32[8,256]{1,0:T(8,128)S(1)} %get-tuple-element.14.rest_2_), channel_id=1, source_target_pairs={{0,7},{1,0},{2,1},{3,2},{4,3},{5,4},{6,5},{7,6},{8,15},{9,8},{10,9... | collective-permute-start | bytes 24584 | tf_op jit(solution)/shard_map/ppermute | solution.py:235
  13.0 9.0 %collective-permute-start.5 = (f32[8,256]{1,0:T(8,128)S(1)}, f32[8,256]{1,0:T(8,128)S(1)}, u32[]{:S(2)}, u32[]{:S(2)}) collective-permute-start(f32[8,256]{1,0:T(8,128)S(1)} %get-tuple-element.14.rest_2_), channel_id=1, source_target_pairs={{0,6},{1,7},{2,0},{3,1},{4,2},{5,3},{6,4},{7,5},{8,14},{9,15},{10,... | collective-permute-start | bytes 24584 | tf_op jit(solution)/shard_map/ppermute | solution.py:235
  15.6 43.6 %collective-permute-start.4 = (f32[8,256]{1,0:T(8,128)S(1)}, f32[8,256]{1,0:T(8,128)S(1)}, u32[]{:S(2)}, u32[]{:S(2)}) collective-permute-start(f32[8,256]{1,0:T(8,128)S(1)} %get-tuple-element.14.rest_2_), channel_id=1, source_target_pairs={{0,5},{1,6},{2,7},{3,0},{4,1},{5,2},{6,3},{7,4},{8,13},{9,14},{10,... | collective-permute-start | bytes 24584 | tf_op jit(solution)/shard_map/ppermute | solution.py:235
  15.6 43.6 %collective-permute-start.3 = (f32[8,256]{1,0:T(8,128)S(1)}, f32[8,256]{1,0:T(8,128)S(1)}, u32[]{:S(2)}, u32[]{:S(2)}) collective-permute-start(f32[8,256]{1,0:T(8,128)S(1)} %get-tuple-element.14.rest_2_), channel_id=1, source_target_pairs={{0,4},{1,5},{2,6},{3,7},{4,0},{5,1},{6,2},{7,3},{8,12},{9,13},{10,... | collective-permute-start | bytes 24584 | tf_op jit(solution)/shard_map/ppermute | solution.py:235
  19.9 39.3 %collective-permute-start.2 = (f32[8,256]{1,0:T(8,128)S(1)}, f32[8,256]{1,0:T(8,128)S(1)}, u32[]{:S(2)}, u32[]{:S(2)}) collective-permute-start(f32[8,256]{1,0:T(8,128)S(1)} %get-tuple-element.14.rest_2_), channel_id=1, source_target_pairs={{0,3},{1,4},{2,5},{3,6},{4,7},{5,0},{6,1},{7,2},{8,11},{9,12},{10,... | collective-permute-start | bytes 24584 | tf_op jit(solution)/shard_map/ppermute | solution.py:235
  19.9 39.3 %collective-permute-start.1 = (f32[8,256]{1,0:T(8,128)S(1)}, f32[8,256]{1,0:T(8,128)S(1)}, u32[]{:S(2)}, u32[]{:S(2)}) collective-permute-start(f32[8,256]{1,0:T(8,128)S(1)} %get-tuple-element.14.rest_2_), channel_id=1, source_target_pairs={{0,2},{1,3},{2,4},{3,5},{4,6},{5,7},{6,0},{7,1},{8,10},{9,11},{10,... | collective-permute-start | bytes 24584 | tf_op jit(solution)/shard_map/ppermute | solution.py:235
  22.0 37.3 %collective-permute-start = (f32[8,256]{1,0:T(8,128)S(1)}, f32[8,256]{1,0:T(8,128)S(1)}, u32[]{:S(2)}, u32[]{:S(2)}) collective-permute-start(f32[8,256]{1,0:T(8,128)S(1)} %get-tuple-element.14.rest_2_), channel_id=1, source_target_pairs={{0,1},{1,2},{2,3},{3,4},{4,5},{5,6},{6,7},{7,0},{8,9},{9,10},{10,1... | collective-permute-start | bytes 24584 | tf_op jit(solution)/shard_map/ppermute | solution.py:235
  66.2 1.7 collective-permute-start.9
  66.3 3.7 %collective-permute-start.8 = (f32[8,256]{1,0:T(8,128)S(1)}, f32[8,256]{1,0:T(8,128)S(1)}, u32[]{:S(2)}, u32[]{:S(2)}) collective-permute-start(f32[8,256]{1,0:T(8,128)S(1)} %get-tuple-element.19), channel_id=1, source_target_pairs={{0,16},{8,24},{16,0},{24,8},{32,48},{40,56},{48,32},{56,40},{64,80... | collective-permute-start | bytes 24584 | tf_op jit(solution)/shard_map/ppermute | solution.py:235
  67.9 3.1 %collective-permute-start.7 = (f32[8,256]{1,0:T(8,128)S(1)}, f32[8,256]{1,0:T(8,128)S(1)}, u32[]{:S(2)}, u32[]{:S(2)}) collective-permute-start(f32[8,256]{1,0:T(8,128)S(1)} %get-tuple-element.19), channel_id=1, source_target_pairs={{0,8},{8,16},{16,24},{24,0},{32,40},{40,48},{48,56},{56,32},{64,72... | collective-permute-start | bytes 24584 | tf_op jit(solution)/shard_map/ppermute | solution.py:235
  71.0 9.0 %collective-permute-start.16 = (f32[8,256]{1,0:T(8,128)S(1)}, f32[8,256]{1,0:T(8,128)S(1)}, u32[]{:S(2)}, u32[]{:S(2)}) collective-permute-start(f32[8,256]{1,0:T(8,128)S(1)} %multiply_add_fusion.rest_3_), channel_id=1, source_target_pairs={{0,224},{32,0},{64,32},{96,64},{128,96},{160,128},{192,160},{224,1... | collective-permute-start | bytes 24584 | tf_op jit(solution)/shard_map/ppermute | solution.py:235
  71.7 10.4 %collective-permute-start.15 = (f32[8,256]{1,0:T(8,128)S(1)}, f32[8,256]{1,0:T(8,128)S(1)}, u32[]{:S(2)}, u32[]{:S(2)}) collective-permute-start(f32[8,256]{1,0:T(8,128)S(1)} %multiply_add_fusion.rest_3_), channel_id=1, source_target_pairs={{0,192},{32,224},{64,0},{96,32},{128,64},{160,96},{192,128},{224,1... | collective-permute-start | bytes 24584 | tf_op jit(solution)/shard_map/ppermute | solution.py:235
  71.8 45.9 %collective-permute-start.14 = (f32[8,256]{1,0:T(8,128)S(1)}, f32[8,256]{1,0:T(8,128)S(1)}, u32[]{:S(2)}, u32[]{:S(2)}) collective-permute-start(f32[8,256]{1,0:T(8,128)S(1)} %multiply_add_fusion.rest_3_), channel_id=1, source_target_pairs={{0,160},{32,192},{64,224},{96,0},{128,32},{160,64},{192,96},{224,1... | collective-permute-start | bytes 24584 | tf_op jit(solution)/shard_map/ppermute | solution.py:235
  75.1 42.7 %collective-permute-start.13 = (f32[8,256]{1,0:T(8,128)S(1)}, f32[8,256]{1,0:T(8,128)S(1)}, u32[]{:S(2)}, u32[]{:S(2)}) collective-permute-start(f32[8,256]{1,0:T(8,128)S(1)} %multiply_add_fusion.rest_3_), channel_id=1, source_target_pairs={{0,128},{32,160},{64,192},{96,224},{128,0},{160,32},{192,64},{224,... | collective-permute-start | bytes 24584 | tf_op jit(solution)/shard_map/ppermute | solution.py:235
  77.7 40.0 %collective-permute-start.12 = (f32[8,256]{1,0:T(8,128)S(1)}, f32[8,256]{1,0:T(8,128)S(1)}, u32[]{:S(2)}, u32[]{:S(2)}) collective-permute-start(f32[8,256]{1,0:T(8,128)S(1)} %multiply_add_fusion.rest_3_), channel_id=1, source_target_pairs={{0,96},{32,128},{64,160},{96,192},{128,224},{160,0},{192,32},{224,... | collective-permute-start | bytes 24584 | tf_op jit(solution)/shard_map/ppermute | solution.py:235
  80.0 37.7 %collective-permute-start.11 = (f32[8,256]{1,0:T(8,128)S(1)}, f32[8,256]{1,0:T(8,128)S(1)}, u32[]{:S(2)}, u32[]{:S(2)}) collective-permute-start(f32[8,256]{1,0:T(8,128)S(1)} %multiply_add_fusion.rest_3_), channel_id=1, source_target_pairs={{0,64},{32,96},{64,128},{96,160},{128,192},{160,224},{192,0},{224,... | collective-permute-start | bytes 24584 | tf_op jit(solution)/shard_map/ppermute | solution.py:235
  82.2 35.6 %collective-permute-start.10 = (f32[8,256]{1,0:T(8,128)S(1)}, f32[8,256]{1,0:T(8,128)S(1)}, u32[]{:S(2)}, u32[]{:S(2)}) collective-permute-start(f32[8,256]{1,0:T(8,128)S(1)} %multiply_add_fusion.rest_3_), channel_id=1, source_target_pairs={{0,32},{32,64},{64,96},{96,128},{128,160},{160,192},{192,224},{224... | collective-permute-start | bytes 24584 | tf_op jit(solution)/shard_map/ppermute | solution.py:235
  135.4 18.7 %copy-start.2 = (f32[32,56,256]{2,1,0:T(8,128)}, f32[32,56,256]{2,1,0:T(8,128)S(1)}, u32[]{:S(2)}) copy-start(f32[32,56,256]{2,1,0:T(8,128)S(1)} %get-tuple-element.21) | copy-start | bytes 5505028
  154.1 53.5 %all-to-all-start.1 = ((f32[32,56,256]{2,1,0:T(8,128)}), f32[32,56,256]{2,1,0:T(8,128)S(1)}, u32[]{:S(2)}, u32[]{:S(2)}) async-start(f32[32,56,256]{2,1,0:T(8,128)} %copy-done.2), calls=%async_computation.1 | async-start | bytes 3670016 | tf_op jit(solution)/shard_map/all_to_all | solution.py:301

commit v2 on v1

--- a/solution.py
+++ b/solution.py
@@ -140,81 +140,107 @@
     return jnp.concatenate(halves, axis=1)
 
 
-def emit(image, log_sums, blocks, out_ref):
-    n, rows = out_ref.shape[0], (blocks * BLK) // out_ref.shape[0]
+def receivers_lines(log_sums, n, blocks):
+    rows = blocks * BLK // n
     lane = lax.broadcasted_iota(jnp.int32, (1, BLK), 1)
-    shifted = {}
+    shifted, lines = {}, []
     for b in range(n):
-        done = 0
-        while done < rows:
-            at = b * rows + done
-            k, off = at // BLK, at % BLK
-            take = min(rows - done, BLK - off)
-            out_ref[b, done : done + take, :] = image[k, off : off + take, :]
-            done += take
-        for part in range(0, rows, BLK):
-            at = b * rows + part
-            k, off = at // BLK, at % BLK
-            if off not in shifted:
-                shifted[off] = pltpu.roll(log_sums, BLK - off, 1) if off else log_sums
-            turned = shifted[off]
-            line = turned[k : k + 1]
-            if off and k + 1 < blocks:
-                line = jnp.where(lane < BLK - off, line, turned[k + 1 : k + 2])
-            spot = rows + part // BLK
-            out_ref[b, spot : spot + 1, :] = line
-
-
-def project_kernel(n_row, n_col, scale, blocks, pairs_ref, count_ref, x_ref, y_ref, *rest):
+        k, off = b * rows // BLK, b * rows % BLK
+        if off not in shifted:
+            shifted[off] = pltpu.roll(log_sums, BLK - off, 1) if off else log_sums
+        line = shifted[off][k : k + 1]
+        if off and k + 1 < blocks:
+            line = jnp.where(lane < BLK - off, line, shifted[off][k + 1 : k + 2])
+        lines.append(line)
+    return lines
+
+
+def images(pairs_ref, kept, a_ref, b_ref, scale, lanes, wide, image_ref, turned):
+    image_ref[...] = jnp.zeros(image_ref.shape, jnp.float32)
+
+    def visit(s, t):
+        a, b = (t, s) if turned else (s, t)
+        at, bt = a_ref[a], b_ref[b]
+        high, low = split_two(weigh(cross(at, bt), scale, lanes[b], wide[a]))
+        rows = pl.ds(pl.multiple_of(a * BLK, BLK), BLK)
+        image_ref[rows, :] += jnp.dot(high, bt, preferred_element_type=jnp.float32) + jnp.dot(
+            low, bt, preferred_element_type=jnp.float32
+        )
+
+    over_pairs(pairs_ref, kept, visit)
+
+
+def spread_lanes(values, blocks, lanes_ref):
+    for b in range(blocks):
+        lanes_ref[b] = jnp.broadcast_to(values[b : b + 1], (8, BLK))
+
+
+def backward_kernel(n_row, n_col, scale, blocks, core_ref, pairs_ref, count_ref, x_ref, y_ref, *rest):
     scratch = rest[-6:]
     f_wide, g_wide, row_high, row_sum, col_high, col_sum = scratch
-    f_lanes, g_lanes, forward, backward = rest[-10:-6]
+    lanes, backward = rest[-8:-6]
     f, g, outs = start_potentials(
-        x_ref, y_ref, rest[:-10], False, n_row, n_col, scale, blocks, f_wide, g_wide
+        x_ref, y_ref, rest[:-8], False, n_row, n_col, scale, blocks, f_wide, g_wide
     )
-    forward_out, backward_out = outs
+    g_out, row_out, keep_out, send_out = outs
     kept = count_ref[0]
     pass_sums(pairs_ref, kept, x_ref, y_ref, scale, *scratch)
-    row = settle(row_high, row_sum, blocks)
+    g_out[...] = g
+    row_out[...] = settle(row_high, row_sum, blocks)
     col = settle(col_high, col_sum, blocks)
-    for b in range(blocks):
-        f_lanes[b] = jnp.broadcast_to(f[b : b + 1], (8, BLK))
-        g_lanes[b] = jnp.broadcast_to(g[b : b + 1], (8, BLK))
-    down_rows(row, blocks, f_wide)
+    spread_lanes(f, blocks, lanes)
     down_rows(col, blocks, g_wide)
-    forward[...] = jnp.zeros(forward.shape, jnp.float32)
-    backward[...] = jnp.zeros(backward.shape, jnp.float32)
-
-    def visit(s, t):
-        xs, yt = x_ref[s], y_ref[t]
-        high, low = split_two(weigh(cross(xs, yt), scale, g_lanes[t], f_wide[s]))
-        forward[s] += jnp.dot(high, yt, preferred_element_type=jnp.float32) + jnp.dot(
-            low, yt, preferred_element_type=jnp.float32
+    images(pairs_ref, kept, y_ref, x_ref, scale, lanes, g_wide, backward, True)
+    half = keep_out.shape[0]
+    rows = blocks * BLK // (2 * half)
+    lines = receivers_lines(col, 2 * half, blocks)
+    core = core_ref[0]
+    for q in range(half):
+        for ref, side in ((keep_out, core), (send_out, 1 - core)):
+            first = pl.multiple_of((2 * q + side) * rows, 16)
+            ref[q, :rows, :] = backward[pl.ds(first, rows), :]
+            ref[q, rows : rows + 1, :] = jnp.where(side == 0, lines[2 * q], lines[2 * q + 1])
+
+
+def forward_kernel(scale, blocks, pairs_ref, count_ref, x_ref, y_ref, g_ref, row_ref, out, lanes, wide, forward):
+    row = row_ref[...]
+    spread_lanes(g_ref[...], blocks, lanes)
+    down_rows(row, blocks, wide)
+    images(pairs_ref, count_ref[0], x_ref, y_ref, scale, lanes, wide, forward, False)
+    n = out.shape[0]
+    rows = blocks * BLK // n
+    lines = receivers_lines(row, n, blocks)
+    for b in range(n):
+        out[b, :rows, :] = forward[b * rows : (b + 1) * rows, :]
+        out[b, rows : rows + 1, :] = lines[b]
+
+
+def pair_kernel(rows, a_ref, b_ref, out_ref):
+    n = a_ref.shape[0]
+    a = jnp.concatenate([a_ref[q, rows : rows + 1, :] for q in range(n)], axis=0)
+    b = jnp.concatenate([b_ref[q, rows : rows + 1, :] for q in range(n)], axis=0)
+    high = jnp.maximum(a, b)
+    both = jnp.exp2(a - high) + jnp.exp2(b - high)
+    merged = high + jnp.log2(both)
+    a_part = jnp.transpose(jnp.exp2(a - high) / both)
+    b_part = jnp.transpose(jnp.exp2(b - high) / both)
+    for q in range(n):
+        out_ref[q, :rows, :] = (
+            a_part[:rows, q : q + 1] * a_ref[q, :rows, :]
+            + b_part[:rows, q : q + 1] * b_ref[q, :rows, :]
         )
-        high, low = split_two(weigh(cross(yt, xs), scale, f_lanes[s], g_wide[t]))
-        backward[t] += jnp.dot(high, xs, preferred_element_type=jnp.float32) + jnp.dot(
-            low, xs, preferred_element_type=jnp.float32
-        )
-
-    over_pairs(pairs_ref, kept, visit)
-    emit(forward, row, blocks, forward_out)
-    emit(backward, col, blocks, backward_out)
+        out_ref[q, rows : rows + 1, :] = merged[q : q + 1]
 
 
 def merge_kernel(rows, parts_ref, out_ref):
     n = parts_ref.shape[0]
-    for part in range(0, rows, BLK):
-        spot = rows + part // BLK
-        size = min(BLK, rows - part)
-        logs = jnp.concatenate([parts_ref[d, spot : spot + 1, :] for d in range(n)], axis=0)
-        high = jnp.max(logs, axis=0, keepdims=True)
-        lifted = jnp.exp2(logs - high)
-        weights = lifted / jnp.sum(lifted, axis=0, keepdims=True)
-        upright = jnp.transpose(weights)
-        total = jnp.zeros((size, BLK), jnp.float32)
-        for d in range(n):
-            total += upright[:size, d : d + 1] * parts_ref[d, part : part + size, :]
-        out_ref[part : part + size, :] = total
+    logs = jnp.concatenate([parts_ref[d, rows : rows + 1, :] for d in range(n)], axis=0)
+    lifted = jnp.exp2(logs - jnp.max(logs, axis=0, keepdims=True))
+    upright = jnp.transpose(lifted / jnp.sum(lifted, axis=0, keepdims=True))
+    total = jnp.zeros((rows, BLK), jnp.float32)
+    for d in range(n):
+        total += upright[:rows, d : d + 1] * parts_ref[d, :rows, :]
+    out_ref[...] = total
 
 
 def in_vmem(n):
@@ -229,17 +255,6 @@
     return [pltpu.VMEM((blocks, BLK, 128), jnp.float32)] * 2 + [
         pltpu.VMEM((blocks, 8, BLK), jnp.float32)
     ] * 4
-
-
-def gather_by_permutes(mine, axis, moves):
-    return [mine] + [lax.ppermute(mine, axis, move) for move in moves]
-
-
-def turns(groups):
-    size = len(groups[0])
-    return [
-        [(g[k], g[(k + r) % size]) for g in groups for k in range(size)] for r in range(1, size)
-    ]
 
 
 def per_device(n_src, n_tgt, sources, targets, pairs, counts):
@@ -263,30 +278,58 @@
             compiler_params=params,
         )(pair_list, kept, x, y, *extra)
 
-    all_tgt = turns([list(range(n_tgt))])
-    near = turns([list(range(k, k + 4)) for k in range(0, n_src, 4)])
-    far = turns([list(range(k, n_src, 4)) for k in range(4)])
+    def spread(mine, axis, size, groups=None):
+        copies = jnp.broadcast_to(mine[None], (size, *mine.shape))
+        return lax.all_to_all(copies, axis, 0, 0, axis_index_groups=groups, tiled=True)
+
+    near = [list(range(k, k + 4)) for k in range(0, n_src, 4)]
+    far = [list(range(k, n_src, 4)) for k in range(4)]
 
     f, g, row, col = sweep(True, [], 0, 0)
-    rows = gather_by_permutes(row, "tgt", all_tgt)
-    cols = [lax.all_gather(col, "src")]
-    f, g, row, col = sweep(False, [f, g, *rows, *cols], len(rows), len(cols))
-
-    rows = [lax.all_gather(row, "tgt")]
-    col = log_sum(gather_by_permutes(col, "src", near))
-    cols = gather_by_permutes(col, "src", far)
-    extra = [f, g, *rows, *cols]
+    rows = spread(row, "tgt", n_tgt)
+    cols = spread(col, "src", n_src)
+    f, g, row, col = sweep(False, [f, g, rows, cols], 1, 1)
+
+    rows = spread(row, "tgt", n_tgt)
+    col = log_sum(list(spread(col, "src", 4, near)))
+    cols = spread(col, "src", n_src // 4, far)
+
     f_rows, b_rows = blocks * BLK // n_tgt, blocks * BLK // n_src
-    forward, backward = pl.pallas_call(
-        functools.partial(project_kernel, len(rows), len(cols), scale, blocks),
-        out_shape=[shape(n_tgt, f_rows + 8, width), shape(n_src, b_rows + 8, width)],
-        in_specs=head + in_vmem(len(extra)),
-        out_specs=in_vmem(2),
-        scratch_shapes=[pltpu.VMEM((blocks, 8, BLK), jnp.float32)] * 2
-        + [pltpu.VMEM((blocks, BLK, width), jnp.float32)] * 2
+    half = n_src // 2
+    core = lax.axis_index("src").astype(jnp.int32) % 2
+    g, row, keep, send = pl.pallas_call(
+        functools.partial(backward_kernel, 1, 1, scale, blocks),
+        out_shape=[shape(8, BLK)] * 2 + [shape(half, b_rows + 8, width)] * 2,
+        in_specs=[pl.BlockSpec(memory_space=pltpu.SMEM)] + head + in_vmem(4),
+        out_specs=in_vmem(4),
+        scratch_shapes=[
+            pltpu.VMEM((blocks, 8, BLK), jnp.float32),
+            pltpu.VMEM((blocks * BLK, width), jnp.float32),
+        ]
         + sums_scratch(blocks),
         compiler_params=params,
-    )(pair_list, kept, x, y, *extra)
+    )(core.reshape(1), pair_list, kept, x, y, f, g, rows, cols)
+    came = lax.ppermute(send, "src", [(k, k ^ 1) for k in range(n_src)])
+    forward = pl.pallas_call(
+        functools.partial(forward_kernel, scale, blocks),
+        out_shape=shape(n_tgt, f_rows + 8, width),
+        in_specs=head + in_vmem(2),
+        out_specs=pl.BlockSpec(memory_space=pltpu.VMEM),
+        scratch_shapes=[
+            pltpu.VMEM((blocks, 8, BLK), jnp.float32),
+            pltpu.VMEM((blocks, BLK, 128), jnp.float32),
+            pltpu.VMEM((blocks * BLK, width), jnp.float32),
+        ],
+        compiler_params=params,
+        cost_estimate=pl.CostEstimate(flops=3 * 10**9, bytes_accessed=4 * 10**6, transcendentals=0),
+    )(pair_list, kept, x, y, g, row)
+    backward = pl.pallas_call(
+        functools.partial(pair_kernel, b_rows),
+        out_shape=shape(half, b_rows + 8, width),
+        in_specs=in_vmem(2),
+        out_specs=pl.BlockSpec(memory_space=pltpu.VMEM),
+        compiler_params=params,
+    )(keep, came)
 
     def merge(parts, rows):
         return pl.pallas_call(
@@ -297,8 +340,9 @@
             compiler_params=params,
         )(parts)
 
+    same_core = [list(range(k, n_src, 2)) for k in range(2)]
+    backward = lax.all_to_all(backward, "src", 0, 0, axis_index_groups=same_core, tiled=True)
     forward = lax.all_to_all(forward, "tgt", 0, 0, tiled=True)
-    backward = lax.all_to_all(backward, "src", 0, 0, tiled=True)
     return (merge(forward, f_rows), merge(backward, b_rows))
 
 

time: 211 us -> 161 us (0.76)
  blocking collectives: 91.2 us -> 43.8 us
  waiting for transfers between devices: 46.6 us -> 61.9 us
  starting transfers between devices: 32.8 us -> 19.2 us
  Pallas kernels: 33.7 us -> 27.2 us
  local copies, waits for them, and re-layouts: 3.12 us -> 5.36 us
    all_gather x2 -> x0, blocking collectives: 72.5 us -> none  [the longest x1 37.2 us: per_device(): cols = [lax.all_gather(col, 'src')]]
    all_to_all x1 -> x3, blocking collectives: 18.7 us -> 43.8 us  [spread(): lax.all_to_all(copies, axis, 0, 0, axis_index_groups=groups, tiled=True)]
    ppermute x17 -> x1, starting transfers between devices: 23.9 us -> 0.37 us  [per_device(): came = lax.ppermute(send, 'src', [(k, k ^ 1) for k in range(n_src)])]
    all_to_all x1 -> x4, waiting for transfers between devices: 43.5 us -> 59.7 us  [the longest x1 23.2 us: per_device(): lax.all_to_all(backward, 'src', 0, 0, axis_index_groups=same_core, tiled=...]
    all_to_all x1 -> x4, starting transfers between devices: 8.86 us -> 18.9 us  [the longest x1 7.47 us: per_device(): lax.all_to_all(backward, 'src', 0, 0, axis_index_groups=same_core, tiled=...]
    pallas_call x2, Pallas kernels: 13.7 us -> 8.95 us  [sweep(): pl.pallas_call(functools.partial(sweep_kernel, first, n_row, n_col, scale...]
    pallas_call x1 -> x3, Pallas kernels: 17.7 us -> 16.1 us  [the longest x1 8.85 us: per_device(): pl.pallas_call(functools.partial(backward_kernel, 1, 1, scale, blocks), o...]
  transfers between devices with their start and end apart: 18 -> 5, of which waited for: 3 -> 5; matrix products, arithmetic and copies ran while one was open for 0% -> 0% of each run, Pallas kernels for 1% -> 2%
where the time goes in v2:
time: 161 us; the launch traced here: 159 us
  waiting for transfers between devices  61.9 us (38%)
  blocking collectives  43.8 us (27%)
  Pallas kernels  27.2 us (17%)
  starting transfers between devices  19.2 us (12%)
  local copies, waits for them, and re-layouts  5.36 us (3%)
    all_to_all x3, blocking collectives, spread(): lax.all_to_all(copies, axis, 0, 0, axis_index_groups=groups, tiled=True)  43.8 us
    all_to_all x1, waiting for transfers between devices, per_device(): lax.all_to_all(backward, 'src', 0, 0, axis_index_groups=same_core, tiled=...  23.2 us
    all_to_all x1, waiting for transfers between devices, per_device(): forward = lax.all_to_all(forward, 'tgt', 0, 0, tiled=True)  20.3 us
    all_to_all x2, waiting for transfers between devices, spread(): lax.all_to_all(copies, axis, 0, 0, axis_index_groups=groups, tiled=True)  16.2 us
    pallas_call x2, Pallas kernels, sweep(): pl.pallas_call(functools.partial(sweep_kernel, first, n_row, n_col, scale...  8.95 us
    pallas_call x1, Pallas kernels, per_device(): pl.pallas_call(functools.partial(backward_kernel, 1, 1, scale, blocks), o...  8.85 us
    all_to_all x1, starting transfers between devices, per_device(): lax.all_to_all(backward, 'src', 0, 0, axis_index_groups=same_core, tiled=...  7.47 us
    all_to_all x2, starting transfers between devices, spread(): lax.all_to_all(copies, axis, 0, 0, axis_index_groups=groups, tiled=True)  7.43 us
  transfers between devices with their start and end apart: 5, of which 5 were waited for; matrix products, arithmetic and copies ran while one was open for 0% of the time, Pallas kernels for 2%

profile of v2, /device:TPU:8, one launch (start us, length us, event | category | flops | bytes accessed | tf_op | source)
XLA Modules:
  0.0 158.8 jit_solution(17497519964514740684)
XLA Ops:
  1.3 0.8 copy.7
  2.0 0.1 reshape.23.pairs_ref
  2.1 0.0 copy-start
  2.1 1.1 copy-done
  3.3 1.1 copy-done.2
  4.4 4.4 %shard_map.59 = (f32[8,256]{1,0:T(8,128)S(1)}, f32[8,256]{1,0:T(8,128)S(1)}, f32[8,256]{1,0:T(8,128)S(1)}, f32[8,256]{1,0:T(8,128)S(1)}) custom-call(s32[48]{0:T(128)S(1)} %reshape.23.pairs_ref, s32[1]{0:T(128)} %bitcast.8.count_ref, bf16[6,256,256]{2,1,0:T(8,128)(2,1)S(1)} %bitcast.12, bf16[6,256,256]{2,1,0:T(8,128)(2,1)S(1)} %bitcast.16), custom_call_target="tpu_custom_call" | custom-call | tf_op jit(solution)/shard_map/pallas_call | solution.py:272
  8.8 13.5 %all_to_all.35.rest_2_ = f32[8,8,256]{2,1,0:T(8,128)S(1)} all-to-all(f32[8,8,256]{2,1,0:T(8,128)S(1)} %broadcast_in_dim.12), channel_id=1, replica_groups=mesh['src'=32,'tgt'=8] {'tgt'}, dimensions={0} | all-to-all | bytes 131072 | tf_op jit(solution)/shard_map/all_to_all | solution.py:283
  22.4 24.5 %all_to_all.36.rest_3_ = f32[32,8,256]{2,1,0:T(8,128)S(1)} all-to-all(f32[32,8,256]{2,1,0:T(8,128)S(1)} %broadcast_in_dim.13), channel_id=1, replica_groups=mesh['src'=32,'tgt'=8] {'src'}, dimensions={0} | all-to-all | bytes 524288 | tf_op jit(solution)/shard_map/all_to_all | solution.py:283
  46.8 4.6 %shard_map.60 = (f32[8,256]{1,0:T(8,128)S(1)}, f32[8,256]{1,0:T(8,128)S(1)}, f32[8,256]{1,0:T(8,128)S(1)}, f32[8,256]{1,0:T(8,128)S(1)}) custom-call(s32[48]{0:T(128)S(1)} %reshape.23.pairs_ref, s32[1]{0:T(128)} %bitcast.9.count_ref, bf16[6,256,256]{2,1,0:T(8,128)(2,1)S(1)} %bitcast.13, bf16[6,256,256]{2,1,0:T(8,128)(2,1)S(1)} %bitcast.17, ...), custom_call_target="tpu_custom_call" | custom-call | tf_op jit(solution)/shard_map/pallas_call | solution.py:272
  51.4 5.7 %all_to_all.37 = f32[4,8,256]{2,1,0:T(8,128)S(1)} all-to-all(f32[4,8,256]{2,1,0:T(8,128)S(1)} %broadcast_in_dim.15), channel_id=1, replica_groups={{0,8,16,24},{32,40,48,56},{64,72,80,88},{96,104,112,120},{128,136,144,1..., dimensions={0} | all-to-all | bytes 65536 | tf_op jit(solution)/shard_map/all_to_all | solution.py:283
  57.2 0.6 broadcast_in_dim.14
  57.8 3.4 %all-to-all-start.2 = ((f32[8,8,256]{2,1,0:T(8,128)}), f32[8,8,256]{2,1,0:T(8,128)S(1)}, u32[]{:S(2)}, u32[]{:S(2)}) async-start(f32[8,8,256]{2,1,0:T(8,128)} %broadcast_in_dim.14), calls=%async_computation.2 | async-start | bytes 131072 | tf_op jit(solution)/shard_map/all_to_all | solution.py:283
  61.3 7.8 %all-to-all-done.2.rest_2_ = f32[8,8,256]{2,1,0:T(8,128)S(1)} async-done(((f32[8,8,256]{2,1,0:T(8,128)}), f32[8,8,256]{2,1,0:T(8,128)S(1)}, u32[]{:S(2)}, u32[]{:S(2)}) %all-to-all-start.2) | async-done | bytes 65568 | tf_op jit(solution)/shard_map/all_to_all | solution.py:283
  69.1 0.6 broadcast_in_dim.17
  69.7 4.0 %all-to-all-start.4 = ((f32[8,8,256]{2,1,0:T(8,128)}), f32[8,8,256]{2,1,0:T(8,128)S(1)}, u32[]{:S(2)}, u32[]{:S(2)}) async-start(f32[8,8,256]{2,1,0:T(8,128)} %broadcast_in_dim.17), calls=%async_computation.4 | async-start | bytes 131072 | tf_op jit(solution)/shard_map/all_to_all | solution.py:283
  73.7 8.4 %all-to-all-done.4.rest_3_ = f32[8,8,256]{2,1,0:T(8,128)S(1)} async-done(((f32[8,8,256]{2,1,0:T(8,128)}), f32[8,8,256]{2,1,0:T(8,128)S(1)}, u32[]{:S(2)}, u32[]{:S(2)}) %all-to-all-start.4) | async-done | bytes 65568 | tf_op jit(solution)/shard_map/all_to_all | solution.py:283
  82.1 0.0 copy-done.1
  82.1 0.0 copy-done.3
  82.1 8.9 %shard_map.61 = (f32[8,256]{1,0:T(8,128)S(1)}, f32[8,256]{1,0:T(8,128)S(1)}, f32[16,56,256]{2,1,0:T(8,128)S(1)}, f32[16,56,256]{2,1,0:T(8,128)S(1)}) custom-call(s32[1]{0:T(128)} %bitcast.3.core_ref, s32[48]{0:T(128)S(1)} %reshape.23.pairs_ref, s32[1]{0:T(128)} %bitcast.10.count_ref, bf16[6,256,256]{2,1,0:T(8,128)(2,1)S(1)} %bitcast.14, ...), custom_call_target="tpu_custom_call" | custom-call | tf_op jit(solution)/shard_map/pallas_call | solution.py:300
  91.0 0.0 copy-start.4
  91.0 0.9 copy-done.4
  91.9 5.9 %shard_map.62 = f32[8,200,256]{2,1,0:T(8,128)} custom-call(s32[48]{0:T(128)S(1)} %reshape.23.pairs_ref, s32[1]{0:T(128)} %bitcast.11.count_ref, bf16[6,256,256]{2,1,0:T(8,128)(2,1)S(1)} %bitcast.15, bf16[6,256,256]{2,1,0:T(8,128)(2,1)S(1)} %bitcast.19, f32[8,256]{1,0:T(8,128)S(1)} %get-tuple-element.22.g_ref, f32[8,256]{1,0:T(8,128)S(1)} %get-tuple-element.23.row_ref), custom_call_target="tpu_custom_call" | custom-call | flops 3000000000 | bytes 4000000 | tf_op jit(solution)/shard_map/pallas_call | solution.py:313
  97.9 4.0 %all-to-all-start.5 = ((f32[8,200,256]{2,1,0:T(8,128)}), f32[8,200,256]{2,1,0:T(8,128)S(1)}, u32[]{:S(2)}, u32[]{:S(2)}) async-start(f32[8,200,256]{2,1,0:T(8,128)} %shard_map.62), calls=%async_computation.5 | async-start | bytes 3276800 | tf_op jit(solution)/shard_map/all_to_all | solution.py:345
  101.8 0.0 copy-done.5
  101.8 0.4 collective-permute-start
  102.2 2.2 %collective-permute-done.b_ref = f32[16,56,256]{2,1,0:T(8,128)S(1)} collective-permute-done((f32[16,56,256]{2,1,0:T(8,128)S(1)}, f32[16,56,256]{2,1,0:T(8,128)S(1)}, u32[]{:S(2)}, u32[]{:S(2)}) %collective-permute-start) | collective-permute-done | bytes 917536 | tf_op jit(solution)/shard_map/ppermute | solution.py:312
  104.4 1.3 shard_map.64
  105.7 20.3 %all-to-all-done.5.parts_ref = f32[8,200,256]{2,1,0:T(8,128)S(1)} async-done(((f32[8,200,256]{2,1,0:T(8,128)}), f32[8,200,256]{2,1,0:T(8,128)S(1)}, u32[]{:S(2)}, u32[]{:S(2)}) %all-to-all-start.5) | async-done | bytes 1638432 | tf_op jit(solution)/shard_map/all_to_all | solution.py:345
  126.1 7.5 %all-to-all-start.6 = ((f32[16,56,256]{2,1,0:T(8,128)}), f32[16,56,256]{2,1,0:T(8,128)S(1)}, u32[]{:S(2)}, u32[]{:S(2)}) async-start(f32[16,56,256]{2,1,0:T(8,128)} %shard_map.64), calls=%async_computation.6 | async-start | bytes 1835008 | tf_op jit(solution)/shard_map/all_to_all | solution.py:344
  133.6 1.2 shard_map.63
  134.7 23.2 %all-to-all-done.6.parts_ref = f32[16,56,256]{2,1,0:T(8,128)S(1)} async-done(((f32[16,56,256]{2,1,0:T(8,128)}), f32[16,56,256]{2,1,0:T(8,128)S(1)}, u32[]{:S(2)}, u32[]{:S(2)}) %all-to-all-start.6) | async-done | bytes 917536 | tf_op jit(solution)/shard_map/all_to_all | solution.py:344
  157.9 0.9 shard_map.65
  (8 shorter events, 0.1 us)
Async XLA Ops:
  2.1 1.1 copy-start
  3.3 1.1 copy-start.2
  22.3 59.8 %copy-start.1 = (bf16[1536,256]{1,0:T(8,128)(2,1)S(1)}, bf16[1536,256]{1,0:T(8,128)(2,1)}, u32[]{:S(2)}) copy-start(bf16[1536,256]{1,0:T(8,128)(2,1)} %param.4) | copy-start | bytes 2359300
  22.3 59.8 %copy-start.3 = (bf16[1536,256]{1,0:T(8,128)(2,1)S(1)}, bf16[1536,256]{1,0:T(8,128)(2,1)}, u32[]{:S(2)}) copy-start(bf16[1536,256]{1,0:T(8,128)(2,1)} %param.5) | copy-start | bytes 2359300
  57.8 11.3 %all-to-all-start.2 = ((f32[8,8,256]{2,1,0:T(8,128)}), f32[8,8,256]{2,1,0:T(8,128)S(1)}, u32[]{:S(2)}, u32[]{:S(2)}) async-start(f32[8,8,256]{2,1,0:T(8,128)} %broadcast_in_dim.14), calls=%async_computation.2 | async-start | bytes 131072 | tf_op jit(solution)/shard_map/all_to_all | solution.py:283
  69.7 12.4 %all-to-all-start.4 = ((f32[8,8,256]{2,1,0:T(8,128)}), f32[8,8,256]{2,1,0:T(8,128)S(1)}, u32[]{:S(2)}, u32[]{:S(2)}) async-start(f32[8,8,256]{2,1,0:T(8,128)} %broadcast_in_dim.17), calls=%async_computation.4 | async-start | bytes 131072 | tf_op jit(solution)/shard_map/all_to_all | solution.py:283
  91.0 0.9 copy-start.4
  97.9 4.0 %copy-start.5 = (f32[16,56,256]{2,1,0:T(8,128)S(1)}, f32[16,56,256]{2,1,0:T(8,128)}, u32[]{:S(2)}) copy-start(f32[16,56,256]{2,1,0:T(8,128)} %copy-done.4) | copy-start | bytes 2752516
  97.9 28.2 %all-to-all-start.5 = ((f32[8,200,256]{2,1,0:T(8,128)}), f32[8,200,256]{2,1,0:T(8,128)S(1)}, u32[]{:S(2)}, u32[]{:S(2)}) async-start(f32[8,200,256]{2,1,0:T(8,128)} %shard_map.62), calls=%async_computation.5 | async-start | bytes 3276800 | tf_op jit(solution)/shard_map/all_to_all | solution.py:345
  101.8 2.6 %collective-permute-start = (f32[16,56,256]{2,1,0:T(8,128)S(1)}, f32[16,56,256]{2,1,0:T(8,128)S(1)}, u32[]{:S(2)}, u32[]{:S(2)}) collective-permute-start(f32[16,56,256]{2,1,0:T(8,128)S(1)} %copy-done.5), channel_id=1, source_target_pairs={{0,8},{8,0},{16,24},{24,16},{32,40},{40,32},{48,56},{56,48},{64,72... | collective-permute-start | bytes 2752520 | tf_op jit(solution)/shard_map/ppermute | solution.py:312
  126.1 31.8 %all-to-all-start.6 = ((f32[16,56,256]{2,1,0:T(8,128)}), f32[16,56,256]{2,1,0:T(8,128)S(1)}, u32[]{:S(2)}, u32[]{:S(2)}) async-start(f32[16,56,256]{2,1,0:T(8,128)} %shard_map.64), calls=%async_computation.6 | async-start | bytes 1835008 | tf_op jit(solution)/shard_map/all_to_all | solution.py:344

commit v3 on v2

--- a/solution.py
+++ b/solution.py
@@ -41,8 +41,8 @@
 def over_pairs(pairs_ref, kept, visit):
     def two(step, carry):
         p = 2 * step
-        visit(pairs_ref[2 * p], pairs_ref[2 * p + 1])
-        visit(pairs_ref[2 * p + 2], pairs_ref[2 * p + 3])
+        visit(pairs_ref[0, p], pairs_ref[1, p])
+        visit(pairs_ref[0, p + 1], pairs_ref[1, p + 1])
         return carry
 
     lax.fori_loop(0, kept // 2, two, 0)
@@ -50,7 +50,7 @@
     @pl.when(kept % 2 == 1)
     def _():
         p = kept - 1
-        visit(pairs_ref[2 * p], pairs_ref[2 * p + 1])
+        visit(pairs_ref[0, p], pairs_ref[1, p])
 
 
 def cross(a, b):
@@ -202,17 +202,22 @@
             ref[q, rows : rows + 1, :] = jnp.where(side == 0, lines[2 * q], lines[2 * q + 1])
 
 
-def forward_kernel(scale, blocks, pairs_ref, count_ref, x_ref, y_ref, g_ref, row_ref, out, lanes, wide, forward):
+def forward_kernel(
+    scale, blocks, place_ref, pairs_ref, count_ref, x_ref, y_ref, g_ref, row_ref, *rest
+):
+    outs, (lanes, wide, forward, lines_ref) = rest[:-4], rest[-4:]
     row = row_ref[...]
     spread_lanes(g_ref[...], blocks, lanes)
     down_rows(row, blocks, wide)
     images(pairs_ref, count_ref[0], x_ref, y_ref, scale, lanes, wide, forward, False)
-    n = out.shape[0]
+    n = len(outs)
     rows = blocks * BLK // n
-    lines = receivers_lines(row, n, blocks)
-    for b in range(n):
-        out[b, :rows, :] = forward[b * rows : (b + 1) * rows, :]
-        out[b, rows : rows + 1, :] = lines[b]
+    for b, line in enumerate(receivers_lines(row, n, blocks)):
+        lines_ref[b] = line
+    for r, out in enumerate(outs):
+        to = place_ref[0] ^ r
+        out[:rows, :] = forward[pl.ds(pl.multiple_of(to * rows, 16), rows), :]
+        out[rows : rows + 1, :] = lines_ref[to]
 
 
 def pair_kernel(rows, a_ref, b_ref, out_ref):
@@ -232,14 +237,15 @@
         out_ref[q, rows : rows + 1, :] = merged[q : q + 1]
 
 
-def merge_kernel(rows, parts_ref, out_ref):
-    n = parts_ref.shape[0]
-    logs = jnp.concatenate([parts_ref[d, rows : rows + 1, :] for d in range(n)], axis=0)
+def merge_kernel(rows, *refs):
+    out_ref = refs[-1]
+    parts = [p for ref in refs[:-1] for p in ([ref] if len(ref.shape) == 2 else [ref.at[d] for d in range(ref.shape[0])])]
+    logs = jnp.concatenate([part[rows : rows + 1, :] for part in parts], axis=0)
     lifted = jnp.exp2(logs - jnp.max(logs, axis=0, keepdims=True))
     upright = jnp.transpose(lifted / jnp.sum(lifted, axis=0, keepdims=True))
     total = jnp.zeros((rows, BLK), jnp.float32)
-    for d in range(n):
-        total += upright[:rows, d : d + 1] * parts_ref[d, :rows, :]
+    for d, part in enumerate(parts):
+        total += upright[:rows, d : d + 1] * part[:rows, :]
     out_ref[...] = total
 
 
@@ -263,7 +269,7 @@
     blocks = sources.shape[0] // BLK
     x = sources.reshape(blocks, BLK, width)
     y = targets.reshape(blocks, BLK, width)
-    pair_list = pairs.reshape(-1)
+    pair_list = jnp.transpose(pairs[0, 0])
     kept = counts.reshape(-1)
     head = [pl.BlockSpec(memory_space=pltpu.SMEM)] * 2 + in_vmem(2)
     params = pltpu.CompilerParams(vmem_limit_bytes=VMEM_BYTES)
@@ -278,29 +284,38 @@
             compiler_params=params,
         )(pair_list, kept, x, y, *extra)
 
-    def spread(mine, axis, size, groups=None):
-        copies = jnp.broadcast_to(mine[None], (size, *mine.shape))
-        return lax.all_to_all(copies, axis, 0, 0, axis_index_groups=groups, tiled=True)
-
-    near = [list(range(k, k + 4)) for k in range(0, n_src, 4)]
-    far = [list(range(k, n_src, 4)) for k in range(4)]
+    def swap(value, axis, size, bit):
+        return lax.ppermute(value, axis, [(k, k ^ bit) for k in range(size)])
+
+    def butterfly(row, col):
+        bit = 1
+        while bit < max(n_src, n_tgt):
+            row_came = swap(row, "tgt", n_tgt, bit) if bit < n_tgt else None
+            col_came = swap(col, "src", n_src, bit) if bit < n_src else None
+            if 2 * bit < n_tgt:
+                row = log_sum([row, row_came])
+            elif 2 * bit == n_tgt:
+                rows = [row, row_came]
+            if 2 * bit < n_src:
+                col = log_sum([col, col_came])
+            elif 2 * bit == n_src:
+                cols = [col, col_came]
+            bit *= 2
+        return rows, cols
 
     f, g, row, col = sweep(True, [], 0, 0)
-    rows = spread(row, "tgt", n_tgt)
-    cols = spread(col, "src", n_src)
-    f, g, row, col = sweep(False, [f, g, rows, cols], 1, 1)
-
-    rows = spread(row, "tgt", n_tgt)
-    col = log_sum(list(spread(col, "src", 4, near)))
-    cols = spread(col, "src", n_src // 4, far)
+    rows, cols = butterfly(row, col)
+    f, g, row, col = sweep(False, [f, g, *rows, *cols], 2, 2)
+    rows, cols = butterfly(row, col)
 
     f_rows, b_rows = blocks * BLK // n_tgt, blocks * BLK // n_src
     half = n_src // 2
+    scalar = pl.BlockSpec(memory_space=pltpu.SMEM)
     core = lax.axis_index("src").astype(jnp.int32) % 2
     g, row, keep, send = pl.pallas_call(
-        functools.partial(backward_kernel, 1, 1, scale, blocks),
+        functools.partial(backward_kernel, 2, 2, scale, blocks),
         out_shape=[shape(8, BLK)] * 2 + [shape(half, b_rows + 8, width)] * 2,
-        in_specs=[pl.BlockSpec(memory_space=pltpu.SMEM)] + head + in_vmem(4),
+        in_specs=[scalar] + head + in_vmem(6),
         out_specs=in_vmem(4),
         scratch_shapes=[
             pltpu.VMEM((blocks, 8, BLK), jnp.float32),
@@ -308,21 +323,22 @@
         ]
         + sums_scratch(blocks),
         compiler_params=params,
-    )(core.reshape(1), pair_list, kept, x, y, f, g, rows, cols)
-    came = lax.ppermute(send, "src", [(k, k ^ 1) for k in range(n_src)])
+    )(core.reshape(1), pair_list, kept, x, y, f, g, *rows, *cols)
+    came = swap(send, "src", n_src, 1)
     forward = pl.pallas_call(
         functools.partial(forward_kernel, scale, blocks),
-        out_shape=shape(n_tgt, f_rows + 8, width),
-        in_specs=head + in_vmem(2),
-        out_specs=pl.BlockSpec(memory_space=pltpu.VMEM),
+        out_shape=[shape(f_rows + 8, width)] * n_tgt,
+        in_specs=[scalar] + head + in_vmem(2),
+        out_specs=in_vmem(n_tgt),
         scratch_shapes=[
             pltpu.VMEM((blocks, 8, BLK), jnp.float32),
             pltpu.VMEM((blocks, BLK, 128), jnp.float32),
             pltpu.VMEM((blocks * BLK, width), jnp.float32),
+            pltpu.VMEM((n_tgt, 1, BLK), jnp.float32),
         ],
         compiler_params=params,
-        cost_estimate=pl.CostEstimate(flops=3 * 10**9, bytes_accessed=4 * 10**6, transcendentals=0),
-    )(pair_list, kept, x, y, g, row)
+        cost_estimate=pl.CostEstimate(flops=6 * 10**9, bytes_accessed=4 * 10**6, transcendentals=0),
+    )(lax.axis_index("tgt").astype(jnp.int32).reshape(1), pair_list, kept, x, y, g, row)
     backward = pl.pallas_call(
         functools.partial(pair_kernel, b_rows),
         out_shape=shape(half, b_rows + 8, width),
@@ -330,20 +346,21 @@
         out_specs=pl.BlockSpec(memory_space=pltpu.VMEM),
         compiler_params=params,
     )(keep, came)
+    backward, forward = lax.optimization_barrier((backward, forward))
 
     def merge(parts, rows):
         return pl.pallas_call(
             functools.partial(merge_kernel, rows),
             out_shape=shape(rows, width),
-            in_specs=in_vmem(1),
+            in_specs=in_vmem(len(parts)),
             out_specs=pl.BlockSpec(memory_space=pltpu.VMEM),
             compiler_params=params,
-        )(parts)
+        )(*parts)
 
     same_core = [list(range(k, n_src, 2)) for k in range(2)]
     backward = lax.all_to_all(backward, "src", 0, 0, axis_index_groups=same_core, tiled=True)
-    forward = lax.all_to_all(forward, "tgt", 0, 0, tiled=True)
-    return (merge(forward, f_rows), merge(backward, b_rows))
+    forward = [forward[0]] + [swap(forward[r], "tgt", n_tgt, r) for r in range(1, n_tgt)]
+    return (merge(forward, f_rows), merge([backward], b_rows))
 
 
 def solution(mesh):

time: 161 us -> 130 us (0.81)
  starting transfers between devices: 19.2 us -> 72.8 us
  blocking collectives: 43.8 us -> 0 us
  waiting for transfers between devices: 61.9 us -> 34.3 us
  Pallas kernels: 27.2 us -> 17.5 us
  local copies, waits for them, and re-layouts: 5.36 us -> 3.01 us
    ppermute x1 -> x24, starting transfers between devices: 0.37 us -> 52 us  [swap(): return lax.ppermute(value, axis, [(k, k ^ bit) for k in range(size)])]
    all_to_all x3 -> x0, blocking collectives: 43.8 us -> none  [spread(): lax.all_to_all(copies, axis, 0, 0, axis_index_groups=groups, tiled=True)]
    all_to_all x3 -> x0, waiting for transfers between devices: 36.5 us -> none  [the longest x1 20.3 us: per_device(): forward = lax.all_to_all(forward, 'tgt', 0, 0, tiled=True)]
    ppermute x1 -> x24, waiting for transfers between devices: 2.19 us -> 34.2 us  [swap(): return lax.ppermute(value, axis, [(k, k ^ bit) for k in range(size)])]
    all_to_all x1, waiting for transfers between devices: 23.2 us -> 0.01 us  [per_device(): lax.all_to_all(backward, 'src', 0, 0, axis_index_groups=same_core, tiled=...]
    all_to_all x1, starting transfers between devices: 7.47 us -> 20.8 us  [per_device(): lax.all_to_all(backward, 'src', 0, 0, axis_index_groups=same_core, tiled=...]
    all_to_all x3 -> x0, starting transfers between devices: 11.4 us -> none  [the longest x2 7.43 us: spread(): lax.all_to_all(copies, axis, 0, 0, axis_index_groups=groups, tiled=True)]
    pallas_call x2, Pallas kernels: 8.95 us -> 5.34 us  [sweep(): pl.pallas_call(functools.partial(sweep_kernel, first, n_row, n_col, scale...]
  transfers between devices with their start and end apart: 5 -> 25, of which waited for: 5 -> 14; matrix products, arithmetic and copies ran while one was open for 0% -> 0% of each run, Pallas kernels for 2% -> 3%
where the time goes in v3:
time: 130 us; the launch traced here: 129 us
  starting transfers between devices  72.8 us (56%)
  waiting for transfers between devices  34.3 us (26%)
  Pallas kernels  17.5 us (13%)
  local copies, waits for them, and re-layouts  3.01 us (2%)
  between operations  1.58 us (1%)
    ppermute x24, starting transfers between devices, swap(): return lax.ppermute(value, axis, [(k, k ^ bit) for k in range(size)])  52 us
    ppermute x24, waiting for transfers between devices, swap(): return lax.ppermute(value, axis, [(k, k ^ bit) for k in range(size)])  34.2 us
    all_to_all x1, starting transfers between devices, per_device(): lax.all_to_all(backward, 'src', 0, 0, axis_index_groups=same_core, tiled=...  20.8 us
    pallas_call x1, Pallas kernels, per_device(): pl.pallas_call(functools.partial(backward_kernel, 2, 2, scale, blocks), o...  5.97 us
    pallas_call x2, Pallas kernels, sweep(): pl.pallas_call(functools.partial(sweep_kernel, first, n_row, n_col, scale...  5.34 us
    unnamed x42, local copies, waits for them, and re-layouts  3.01 us
    pallas_call x1, Pallas kernels, per_device(): pl.pallas_call(functools.partial(forward_kernel, scale, blocks), out_shap...  2.71 us
  transfers between devices with their start and end apart: 25, of which 14 were waited for; matrix products, arithmetic and copies ran while one was open for 0% of the time, Pallas kernels for 3%

profile of v3, /device:TPU:8, one launch (start us, length us, event | category | flops | bytes accessed | tf_op | source)
XLA Modules:
  0.0 129.4 jit_solution(10235628730477607877)
XLA Ops:
  2.0 1.1 copy-done
  3.1 1.1 copy-done.2
  4.2 2.6 %shard_map.59 = (f32[8,256]{1,0:T(8,128)S(1)}, f32[8,256]{1,0:T(8,128)S(1)}, f32[8,256]{1,0:T(8,128)S(1)}, f32[8,256]{1,0:T(8,128)S(1)}) custom-call(s32[2,24]{1,0:T(2,128)S(1)} %bitcast.20, s32[1]{0:T(128)} %bitcast.8.count_ref, bf16[6,256,256]{2,1,0:T(8,128)(2,1)S(1)} %bitcast.12, bf16[6,256,256]{2,1,0:T(8,128)(2,1)S(1)} %bitcast.16), custom_call_target="tpu_custom_call" | custom-call | tf_op jit(solution)/shard_map/pallas_call | solution.py:278
  6.9 1.2 collective-permute-done.3
  8.1 6.1 %collective-permute-start.4 = (f32[8,256]{1,0:T(8,128)S(1)}, f32[8,256]{1,0:T(8,128)S(1)}, u32[]{:S(2)}, u32[]{:S(2)}) collective-permute-start(f32[8,256]{1,0:T(8,128)S(1)} %multiply_add_fusion.9), channel_id=1, source_target_pairs={{0,16},{8,24},{16,0},{24,8},{32,48},{40,56},{48,32},{56,40},{64,80... | collective-permute-start | bytes 24584 | tf_op jit(solution)/shard_map/ppermute | solution.py:288
  14.2 1.6 %collective-permute-done.4 = f32[8,256]{1,0:T(8,128)S(1)} collective-permute-done((f32[8,256]{1,0:T(8,128)S(1)}, f32[8,256]{1,0:T(8,128)S(1)}, u32[]{:S(2)}, u32[]{:S(2)}) %collective-permute-start.4) | collective-permute-done | bytes 8224 | tf_op jit(solution)/shard_map/ppermute | solution.py:288
  16.0 1.9 %collective-permute-done = f32[8,256]{1,0:T(8,128)S(1)} collective-permute-done((f32[8,256]{1,0:T(8,128)S(1)}, f32[8,256]{1,0:T(8,128)S(1)}, u32[]{:S(2)}, u32[]{:S(2)}) %collective-permute-start) | collective-permute-done | bytes 8224 | tf_op jit(solution)/shard_map/ppermute | solution.py:288
  19.6 3.1 %collective-permute-start.6 = (f32[8,256]{1,0:T(8,128)S(1)}, f32[8,256]{1,0:T(8,128)S(1)}, u32[]{:S(2)}, u32[]{:S(2)}) collective-permute-start(f32[8,256]{1,0:T(8,128)S(1)} %multiply_add_fusion.7), channel_id=1, source_target_pairs={{0,64},{8,72},{16,80},{24,88},{32,96},{40,104},{48,112},{56,120},{... | collective-permute-start | bytes 24584 | tf_op jit(solution)/shard_map/ppermute | solution.py:288
  23.1 3.8 %collective-permute-start.2 = (f32[8,256]{1,0:T(8,128)S(1)}, f32[8,256]{1,0:T(8,128)S(1)}, u32[]{:S(2)}, u32[]{:S(2)}) collective-permute-start(f32[8,256]{1,0:T(8,128)S(1)} %multiply_add_fusion.10.rest_2_), channel_id=1, source_target_pairs={{0,4},{1,5},{2,6},{3,7},{4,0},{5,1},{6,2},{7,3},{8,12},{9,13},{10,... | collective-permute-start | bytes 24584 | tf_op jit(solution)/shard_map/ppermute | solution.py:288
  27.0 4.7 %collective-permute-start.7 = (f32[8,256]{1,0:T(8,128)S(1)}, f32[8,256]{1,0:T(8,128)S(1)}, u32[]{:S(2)}, u32[]{:S(2)}) collective-permute-start(f32[8,256]{1,0:T(8,128)S(1)} %multiply_add_fusion.6.rest_4_), channel_id=1, source_target_pairs={{0,128},{8,136},{16,144},{24,152},{32,160},{40,168},{48,176},{56,1... | collective-permute-start | bytes 24584 | tf_op jit(solution)/shard_map/ppermute | solution.py:288
  31.7 2.9 %collective-permute-done.7.rest_5_ = f32[8,256]{1,0:T(8,128)S(1)} collective-permute-done((f32[8,256]{1,0:T(8,128)S(1)}, f32[8,256]{1,0:T(8,128)S(1)}, u32[]{:S(2)}, u32[]{:S(2)}) %collective-permute-start.7) | collective-permute-done | bytes 8224 | tf_op jit(solution)/shard_map/ppermute | solution.py:288
  34.7 2.8 %shard_map.60 = (f32[8,256]{1,0:T(8,128)S(1)}, f32[8,256]{1,0:T(8,128)S(1)}, f32[8,256]{1,0:T(8,128)S(1)}, f32[8,256]{1,0:T(8,128)S(1)}) custom-call(s32[2,24]{1,0:T(2,128)S(1)} %bitcast.21, s32[1]{0:T(128)} %bitcast.9.count_ref, bf16[6,256,256]{2,1,0:T(8,128)(2,1)S(1)} %bitcast.13, bf16[6,256,256]{2,1,0:T(8,128)(2,1)S(1)} %bitcast.17, ...), custom_call_target="tpu_custom_call" | custom-call | tf_op jit(solution)/shard_map/pallas_call | solution.py:278
  37.5 1.2 collective-permute-done.11
  38.7 4.5 %collective-permute-start.12 = (f32[8,256]{1,0:T(8,128)S(1)}, f32[8,256]{1,0:T(8,128)S(1)}, u32[]{:S(2)}, u32[]{:S(2)}) collective-permute-start(f32[8,256]{1,0:T(8,128)S(1)} %multiply_add_fusion.3), channel_id=1, source_target_pairs={{0,16},{8,24},{16,0},{24,8},{32,48},{40,56},{48,32},{56,40},{64,80... | collective-permute-start | bytes 24584 | tf_op jit(solution)/shard_map/ppermute | solution.py:288
  43.4 1.5 %collective-permute-done.12 = f32[8,256]{1,0:T(8,128)S(1)} collective-permute-done((f32[8,256]{1,0:T(8,128)S(1)}, f32[8,256]{1,0:T(8,128)S(1)}, u32[]{:S(2)}, u32[]{:S(2)}) %collective-permute-start.12) | collective-permute-done | bytes 8224 | tf_op jit(solution)/shard_map/ppermute | solution.py:288
  45.3 1.6 %collective-permute-done.8 = f32[8,256]{1,0:T(8,128)S(1)} collective-permute-done((f32[8,256]{1,0:T(8,128)S(1)}, f32[8,256]{1,0:T(8,128)S(1)}, u32[]{:S(2)}, u32[]{:S(2)}) %collective-permute-start.8) | collective-permute-done | bytes 8224 | tf_op jit(solution)/shard_map/ppermute | solution.py:288
  46.9 1.2 collective-permute-start.9
  48.6 2.4 %collective-permute-start.14 = (f32[8,256]{1,0:T(8,128)S(1)}, f32[8,256]{1,0:T(8,128)S(1)}, u32[]{:S(2)}, u32[]{:S(2)}) collective-permute-start(f32[8,256]{1,0:T(8,128)S(1)} %multiply_add_fusion.1), channel_id=1, source_target_pairs={{0,64},{8,72},{16,80},{24,88},{32,96},{40,104},{48,112},{56,120},{... | collective-permute-start | bytes 24584 | tf_op jit(solution)/shard_map/ppermute | solution.py:288
  51.1 1.1 collective-permute-done.9
  52.2 2.9 %collective-permute-start.10 = (f32[8,256]{1,0:T(8,128)S(1)}, f32[8,256]{1,0:T(8,128)S(1)}, u32[]{:S(2)}, u32[]{:S(2)}) collective-permute-start(f32[8,256]{1,0:T(8,128)S(1)} %multiply_add_fusion.4.rest_2_), channel_id=1, source_target_pairs={{0,4},{1,5},{2,6},{3,7},{4,0},{5,1},{6,2},{7,3},{8,12},{9,13},{10,... | collective-permute-start | bytes 24584 | tf_op jit(solution)/shard_map/ppermute | solution.py:288
  55.1 4.9 %collective-permute-start.15 = (f32[8,256]{1,0:T(8,128)S(1)}, f32[8,256]{1,0:T(8,128)S(1)}, u32[]{:S(2)}, u32[]{:S(2)}) collective-permute-start(f32[8,256]{1,0:T(8,128)S(1)} %multiply_add_fusion.rest_4_), channel_id=1, source_target_pairs={{0,128},{8,136},{16,144},{24,152},{32,160},{40,168},{48,176},{56,1... | collective-permute-start | bytes 24584 | tf_op jit(solution)/shard_map/ppermute | solution.py:288
  60.0 2.9 %collective-permute-done.15.rest_5_ = f32[8,256]{1,0:T(8,128)S(1)} collective-permute-done((f32[8,256]{1,0:T(8,128)S(1)}, f32[8,256]{1,0:T(8,128)S(1)}, u32[]{:S(2)}, u32[]{:S(2)}) %collective-permute-start.15) | collective-permute-done | bytes 8224 | tf_op jit(solution)/shard_map/ppermute | solution.py:288
  62.9 6.0 %shard_map.61 = (f32[8,256]{1,0:T(8,128)S(1)}, f32[8,256]{1,0:T(8,128)S(1)}, f32[16,56,256]{2,1,0:T(8,128)S(1)}, f32[16,56,256]{2,1,0:T(8,128)}) custom-call(s32[1]{0:T(128)} %bitcast.core_ref, s32[2,24]{1,0:T(2,128)S(1)} %bitcast.22, s32[1]{0:T(128)} %bitcast.10.count_ref, bf16[6,256,256]{2,1,0:T(8,128)(2,1)S(1)} %bitcast.14, ...), custom_call_target="tpu_custom_call" | custom-call | tf_op jit(solution)/shard_map/pallas_call | solution.py:315
  68.9 2.7 %shard_map.63 = (f32[200,256]{1,0:T(8,128)S(1)}, f32[200,256]{1,0:T(8,128)S(1)}, f32[200,256]{1,0:T(8,128)S(1)}, f32[200,256]{1,0:T(8,128)S(1)}, f32[200,256]{1,...) custom-call(s32[1]{0:T(128)} %bitcast.7.place_ref, s32[2,24]{1,0:T(2,128)S(1)} %bitcast.23, ...), custom_call_target="tpu_custom_call" | custom-call | flops 6000000000 | bytes 4000000 | tf_op jit(solution)/shard_map/pallas_call | solution.py:328
  71.7 1.4 %shard_map.62 = f32[16,56,256]{2,1,0:T(8,128)} custom-call(f32[16,56,256]{2,1,0:T(8,128)S(1)} %get-tuple-element.39.a_ref, f32[16,56,256]{2,1,0:T(8,128)S(1)} %collective-permute-done.16.b_ref), custom_call_target="tpu_custom_call" | custom-call | tf_op jit(solution)/shard_map/pallas_call | solution.py:342
  73.2 20.8 %all-to-all-start = ((f32[16,56,256]{2,1,0:T(8,128)}), f32[16,56,256]{2,1,0:T(8,128)S(1)}, u32[]{:S(2)}, u32[]{:S(2)}) async-start(f32[16,56,256]{2,1,0:T(8,128)} %shard_map.62), calls=%async_computation | async-start | bytes 1835008 | tf_op jit(solution)/shard_map/all_to_all | solution.py:361
  94.1 3.7 %collective-permute-start.18 = (f32[200,256]{1,0:T(8,128)S(1)}, f32[200,256]{1,0:T(8,128)S(1)}, u32[]{:S(2)}, u32[]{:S(2)}) collective-permute-start(f32[200,256]{1,0:T(8,128)S(1)} %copy-done.18), channel_id=1, source_target_pairs={{0,2},{1,3},{2,0},{3,1},{4,6},{5,7},{6,4},{7,5},{8,10},{9,11},{10,... | collective-permute-start | bytes 614408 | tf_op jit(solution)/shard_map/ppermute | solution.py:288
  98.8 2.8 %collective-permute-start.20 = (f32[200,256]{1,0:T(8,128)S(1)}, f32[200,256]{1,0:T(8,128)S(1)}, u32[]{:S(2)}, u32[]{:S(2)}) collective-permute-start(f32[200,256]{1,0:T(8,128)S(1)} %copy-done.14), channel_id=1, source_target_pairs={{0,4},{1,5},{2,6},{3,7},{4,0},{5,1},{6,2},{7,3},{8,12},{9,13},{10,... | collective-permute-start | bytes 614408 | tf_op jit(solution)/shard_map/ppermute | solution.py:288
  101.8 5.8 %collective-permute-start.22 = (f32[200,256]{1,0:T(8,128)S(1)}, f32[200,256]{1,0:T(8,128)S(1)}, u32[]{:S(2)}, u32[]{:S(2)}) collective-permute-start(f32[200,256]{1,0:T(8,128)S(1)} %copy-done.10), channel_id=1, source_target_pairs={{0,6},{1,7},{2,4},{3,5},{4,2},{5,3},{6,0},{7,1},{8,14},{9,15},{10,... | collective-permute-start | bytes 614408 | tf_op jit(solution)/shard_map/ppermute | solution.py:288
  108.2 2.8 %collective-permute-start.23 = (f32[200,256]{1,0:T(8,128)S(1)}, f32[200,256]{1,0:T(8,128)S(1)}, u32[]{:S(2)}, u32[]{:S(2)}) collective-permute-start(f32[200,256]{1,0:T(8,128)S(1)} %copy-done.8), channel_id=1, source_target_pairs={{0,7},{1,6},{2,5},{3,4},{4,3},{5,2},{6,1},{7,0},{8,15},{9,14},{10,... | collective-permute-start | bytes 614408 | tf_op jit(solution)/shard_map/ppermute | solution.py:288
  110.9 16.3 %collective-permute-done.20.refs_4_ = f32[200,256]{1,0:T(8,128)S(1)} collective-permute-done((f32[200,256]{1,0:T(8,128)S(1)}, f32[200,256]{1,0:T(8,128)S(1)}, u32[]{:S(2)}, u32[]{:S(2)}) %collective-permute-start.20) | collective-permute-done | bytes 204832 | tf_op jit(solution)/shard_map/ppermute | solution.py:288
  127.3 1.2 shard_map.64
  (79 shorter events, 7.2 us)
Async XLA Ops:
  6.8 1.3 collective-permute-start.3
  8.1 7.7 %collective-permute-start.4 = (f32[8,256]{1,0:T(8,128)S(1)}, f32[8,256]{1,0:T(8,128)S(1)}, u32[]{:S(2)}, u32[]{:S(2)}) collective-permute-start(f32[8,256]{1,0:T(8,128)S(1)} %multiply_add_fusion.9), channel_id=1, source_target_pairs={{0,16},{8,24},{16,0},{24,8},{32,48},{40,56},{48,32},{56,40},{64,80... | collective-permute-start | bytes 24584 | tf_op jit(solution)/shard_map/ppermute | solution.py:288
  14.2 3.7 %collective-permute-start = (f32[8,256]{1,0:T(8,128)S(1)}, f32[8,256]{1,0:T(8,128)S(1)}, u32[]{:S(2)}, u32[]{:S(2)}) collective-permute-start(f32[8,256]{1,0:T(8,128)S(1)} %get-tuple-element.33), channel_id=1, source_target_pairs={{0,1},{1,0},{2,3},{3,2},{4,5},{5,4},{6,7},{7,6},{8,9},{9,8},{10,11... | collective-permute-start | bytes 24584 | tf_op jit(solution)/shard_map/ppermute | solution.py:288
  15.9 3.7 %collective-permute-start.5 = (f32[8,256]{1,0:T(8,128)S(1)}, f32[8,256]{1,0:T(8,128)S(1)}, u32[]{:S(2)}, u32[]{:S(2)}) collective-permute-start(f32[8,256]{1,0:T(8,128)S(1)} %multiply_add_fusion.8), channel_id=1, source_target_pairs={{0,32},{8,40},{16,48},{24,56},{32,0},{40,8},{48,16},{56,24},{64,96... | collective-permute-start | bytes 24584 | tf_op jit(solution)/shard_map/ppermute | solution.py:288
  17.9 5.2 %collective-permute-start.1 = (f32[8,256]{1,0:T(8,128)S(1)}, f32[8,256]{1,0:T(8,128)S(1)}, u32[]{:S(2)}, u32[]{:S(2)}) collective-permute-start(f32[8,256]{1,0:T(8,128)S(1)} %multiply_add_fusion.11), channel_id=1, source_target_pairs={{0,2},{1,3},{2,0},{3,1},{4,6},{5,7},{6,4},{7,5},{8,10},{9,11},{10,... | collective-permute-start | bytes 24584 | tf_op jit(solution)/shard_map/ppermute | solution.py:288
  19.6 7.4 %collective-permute-start.6 = (f32[8,256]{1,0:T(8,128)S(1)}, f32[8,256]{1,0:T(8,128)S(1)}, u32[]{:S(2)}, u32[]{:S(2)}) collective-permute-start(f32[8,256]{1,0:T(8,128)S(1)} %multiply_add_fusion.7), channel_id=1, source_target_pairs={{0,64},{8,72},{16,80},{24,88},{32,96},{40,104},{48,112},{56,120},{... | collective-permute-start | bytes 24584 | tf_op jit(solution)/shard_map/ppermute | solution.py:288
  23.1 8.6 %collective-permute-start.2 = (f32[8,256]{1,0:T(8,128)S(1)}, f32[8,256]{1,0:T(8,128)S(1)}, u32[]{:S(2)}, u32[]{:S(2)}) collective-permute-start(f32[8,256]{1,0:T(8,128)S(1)} %multiply_add_fusion.10.rest_2_), channel_id=1, source_target_pairs={{0,4},{1,5},{2,6},{3,7},{4,0},{5,1},{6,2},{7,3},{8,12},{9,13},{10,... | collective-permute-start | bytes 24584 | tf_op jit(solution)/shard_map/ppermute | solution.py:288
  27.0 7.6 %collective-permute-start.7 = (f32[8,256]{1,0:T(8,128)S(1)}, f32[8,256]{1,0:T(8,128)S(1)}, u32[]{:S(2)}, u32[]{:S(2)}) collective-permute-start(f32[8,256]{1,0:T(8,128)S(1)} %multiply_add_fusion.6.rest_4_), channel_id=1, source_target_pairs={{0,128},{8,136},{16,144},{24,152},{32,160},{40,168},{48,176},{56,1... | collective-permute-start | bytes 24584 | tf_op jit(solution)/shard_map/ppermute | solution.py:288
  34.6 28.2 %copy-start.1 = (bf16[1536,256]{1,0:T(8,128)(2,1)S(1)}, bf16[1536,256]{1,0:T(8,128)(2,1)}, u32[]{:S(2)}) copy-start(bf16[1536,256]{1,0:T(8,128)(2,1)} %param.4) | copy-start | bytes 2359300
  34.6 28.2 %copy-start.3 = (bf16[1536,256]{1,0:T(8,128)(2,1)S(1)}, bf16[1536,256]{1,0:T(8,128)(2,1)}, u32[]{:S(2)}) copy-start(bf16[1536,256]{1,0:T(8,128)(2,1)} %param.5) | copy-start | bytes 2359300
  37.4 1.3 collective-permute-start.11
  38.7 6.2 %collective-permute-start.12 = (f32[8,256]{1,0:T(8,128)S(1)}, f32[8,256]{1,0:T(8,128)S(1)}, u32[]{:S(2)}, u32[]{:S(2)}) collective-permute-start(f32[8,256]{1,0:T(8,128)S(1)} %multiply_add_fusion.3), channel_id=1, source_target_pairs={{0,16},{8,24},{16,0},{24,8},{32,48},{40,56},{48,32},{56,40},{64,80... | collective-permute-start | bytes 24584 | tf_op jit(solution)/shard_map/ppermute | solution.py:288
  43.2 3.7 %collective-permute-start.8 = (f32[8,256]{1,0:T(8,128)S(1)}, f32[8,256]{1,0:T(8,128)S(1)}, u32[]{:S(2)}, u32[]{:S(2)}) collective-permute-start(f32[8,256]{1,0:T(8,128)S(1)} %get-tuple-element.37), channel_id=1, source_target_pairs={{0,1},{1,0},{2,3},{3,2},{4,5},{5,4},{6,7},{7,6},{8,9},{9,8},{10,11... | collective-permute-start | bytes 24584 | tf_op jit(solution)/shard_map/ppermute | solution.py:288
  44.9 3.7 %collective-permute-start.13 = (f32[8,256]{1,0:T(8,128)S(1)}, f32[8,256]{1,0:T(8,128)S(1)}, u32[]{:S(2)}, u32[]{:S(2)}) collective-permute-start(f32[8,256]{1,0:T(8,128)S(1)} %multiply_add_fusion.2), channel_id=1, source_target_pairs={{0,32},{8,40},{16,48},{24,56},{32,0},{40,8},{48,16},{56,24},{64,96... | collective-permute-start | bytes 24584 | tf_op jit(solution)/shard_map/ppermute | solution.py:288
  46.9 5.2 %collective-permute-start.9 = (f32[8,256]{1,0:T(8,128)S(1)}, f32[8,256]{1,0:T(8,128)S(1)}, u32[]{:S(2)}, u32[]{:S(2)}) collective-permute-start(f32[8,256]{1,0:T(8,128)S(1)} %multiply_add_fusion.5), channel_id=1, source_target_pairs={{0,2},{1,3},{2,0},{3,1},{4,6},{5,7},{6,4},{7,5},{8,10},{9,11},{10,... | collective-permute-start | bytes 24584 | tf_op jit(solution)/shard_map/ppermute | solution.py:288
  48.6 6.4 %collective-permute-start.14 = (f32[8,256]{1,0:T(8,128)S(1)}, f32[8,256]{1,0:T(8,128)S(1)}, u32[]{:S(2)}, u32[]{:S(2)}) collective-permute-start(f32[8,256]{1,0:T(8,128)S(1)} %multiply_add_fusion.1), channel_id=1, source_target_pairs={{0,64},{8,72},{16,80},{24,88},{32,96},{40,104},{48,112},{56,120},{... | collective-permute-start | bytes 24584 | tf_op jit(solution)/shard_map/ppermute | solution.py:288
  52.2 7.8 %collective-permute-start.10 = (f32[8,256]{1,0:T(8,128)S(1)}, f32[8,256]{1,0:T(8,128)S(1)}, u32[]{:S(2)}, u32[]{:S(2)}) collective-permute-start(f32[8,256]{1,0:T(8,128)S(1)} %multiply_add_fusion.4.rest_2_), channel_id=1, source_target_pairs={{0,4},{1,5},{2,6},{3,7},{4,0},{5,1},{6,2},{7,3},{8,12},{9,13},{10,... | collective-permute-start | bytes 24584 | tf_op jit(solution)/shard_map/ppermute | solution.py:288
  55.1 7.8 %collective-permute-start.15 = (f32[8,256]{1,0:T(8,128)S(1)}, f32[8,256]{1,0:T(8,128)S(1)}, u32[]{:S(2)}, u32[]{:S(2)}) collective-permute-start(f32[8,256]{1,0:T(8,128)S(1)} %multiply_add_fusion.rest_4_), channel_id=1, source_target_pairs={{0,128},{8,136},{16,144},{24,152},{32,160},{40,168},{48,176},{56,1... | collective-permute-start | bytes 24584 | tf_op jit(solution)/shard_map/ppermute | solution.py:288
  68.9 2.8 %collective-permute-start.16 = (f32[16,56,256]{2,1,0:T(8,128)}, f32[16,56,256]{2,1,0:T(8,128)S(1)}, u32[]{:S(2)}, u32[]{:S(2)}) collective-permute-start(f32[16,56,256]{2,1,0:T(8,128)} %get-tuple-element.40), channel_id=1, source_target_pairs={{0,8},{8,0},{16,24},{24,16},{32,40},{40,32},{48,56},{56,48},{64,72... | collective-permute-start | bytes 2752520 | tf_op jit(solution)/shard_map/ppermute | solution.py:288
  73.1 25.7 %copy-start.14 = (f32[200,256]{1,0:T(8,128)S(1)}, f32[200,256]{1,0:T(8,128)}, u32[]{:S(2)}) copy-start(f32[200,256]{1,0:T(8,128)} %copy-done.13) | copy-start | bytes 614404
  73.1 28.5 %copy-start.12 = (f32[200,256]{1,0:T(8,128)S(1)}, f32[200,256]{1,0:T(8,128)}, u32[]{:S(2)}) copy-start(f32[200,256]{1,0:T(8,128)} %copy-done.11) | copy-start | bytes 614404
  73.1 28.7 %copy-start.10 = (f32[200,256]{1,0:T(8,128)S(1)}, f32[200,256]{1,0:T(8,128)}, u32[]{:S(2)}) copy-start(f32[200,256]{1,0:T(8,128)} %copy-done.9) | copy-start | bytes 614404
  73.2 35.0 %copy-start.8 = (f32[200,256]{1,0:T(8,128)S(1)}, f32[200,256]{1,0:T(8,128)}, u32[]{:S(2)}) copy-start(f32[200,256]{1,0:T(8,128)} %copy-done.7) | copy-start | bytes 614404
  73.2 54.1 %copy-start.5 = (f32[200,256]{1,0:T(8,128)S(1)}, f32[200,256]{1,0:T(8,128)}, u32[]{:S(2)}) copy-start(f32[200,256]{1,0:T(8,128)} %copy-done.4) | copy-start | bytes 614404
  73.2 55.3 %all-to-all-start = ((f32[16,56,256]{2,1,0:T(8,128)}), f32[16,56,256]{2,1,0:T(8,128)S(1)}, u32[]{:S(2)}, u32[]{:S(2)}) async-start(f32[16,56,256]{2,1,0:T(8,128)} %shard_map.62), calls=%async_computation | async-start | bytes 1835008 | tf_op jit(solution)/shard_map/all_to_all | solution.py:361
  94.0 7.9 %collective-permute-start.17 = (f32[200,256]{1,0:T(8,128)S(1)}, f32[200,256]{1,0:T(8,128)S(1)}, u32[]{:S(2)}, u32[]{:S(2)}) collective-permute-start(f32[200,256]{1,0:T(8,128)S(1)} %copy-done.20), channel_id=1, source_target_pairs={{0,1},{1,0},{2,3},{3,2},{4,5},{5,4},{6,7},{7,6},{8,9},{9,8},{10,11... | collective-permute-start | bytes 614408 | tf_op jit(solution)/shard_map/ppermute | solution.py:288
  94.1 14.1 %collective-permute-start.18 = (f32[200,256]{1,0:T(8,128)S(1)}, f32[200,256]{1,0:T(8,128)S(1)}, u32[]{:S(2)}, u32[]{:S(2)}) collective-permute-start(f32[200,256]{1,0:T(8,128)S(1)} %copy-done.18), channel_id=1, source_target_pairs={{0,2},{1,3},{2,0},{3,1},{4,6},{5,7},{6,4},{7,5},{8,10},{9,11},{10,... | collective-permute-start | bytes 614408 | tf_op jit(solution)/shard_map/ppermute | solution.py:288
  97.8 13.1 %collective-permute-start.19 = (f32[200,256]{1,0:T(8,128)S(1)}, f32[200,256]{1,0:T(8,128)S(1)}, u32[]{:S(2)}, u32[]{:S(2)}) collective-permute-start(f32[200,256]{1,0:T(8,128)S(1)} %copy-done.16), channel_id=1, source_target_pairs={{0,3},{1,2},{2,1},{3,0},{4,7},{5,6},{6,5},{7,4},{8,11},{9,10},{10,... | collective-permute-start | bytes 614408 | tf_op jit(solution)/shard_map/ppermute | solution.py:288
  98.8 28.5 %collective-permute-start.20 = (f32[200,256]{1,0:T(8,128)S(1)}, f32[200,256]{1,0:T(8,128)S(1)}, u32[]{:S(2)}, u32[]{:S(2)}) collective-permute-start(f32[200,256]{1,0:T(8,128)S(1)} %copy-done.14), channel_id=1, source_target_pairs={{0,4},{1,5},{2,6},{3,7},{4,0},{5,1},{6,2},{7,3},{8,12},{9,13},{10,... | collective-permute-start | bytes 614408 | tf_op jit(solution)/shard_map/ppermute | solution.py:288
  101.6 25.6 %collective-permute-start.21 = (f32[200,256]{1,0:T(8,128)S(1)}, f32[200,256]{1,0:T(8,128)S(1)}, u32[]{:S(2)}, u32[]{:S(2)}) collective-permute-start(f32[200,256]{1,0:T(8,128)S(1)} %copy-done.12), channel_id=1, source_target_pairs={{0,5},{1,4},{2,7},{3,6},{4,1},{5,0},{6,3},{7,2},{8,13},{9,12},{10,... | collective-permute-start | bytes 614408 | tf_op jit(solution)/shard_map/ppermute | solution.py:288
  101.8 25.4 %collective-permute-start.22 = (f32[200,256]{1,0:T(8,128)S(1)}, f32[200,256]{1,0:T(8,128)S(1)}, u32[]{:S(2)}, u32[]{:S(2)}) collective-permute-start(f32[200,256]{1,0:T(8,128)S(1)} %copy-done.10), channel_id=1, source_target_pairs={{0,6},{1,7},{2,4},{3,5},{4,2},{5,3},{6,0},{7,1},{8,14},{9,15},{10,... | collective-permute-start | bytes 614408 | tf_op jit(solution)/shard_map/ppermute | solution.py:288
  108.2 19.1 %collective-permute-start.23 = (f32[200,256]{1,0:T(8,128)S(1)}, f32[200,256]{1,0:T(8,128)S(1)}, u32[]{:S(2)}, u32[]{:S(2)}) collective-permute-start(f32[200,256]{1,0:T(8,128)S(1)} %copy-done.8), channel_id=1, source_target_pairs={{0,7},{1,6},{2,5},{3,4},{4,3},{5,2},{6,1},{7,0},{8,15},{9,14},{10,... | collective-permute-start | bytes 614408 | tf_op jit(solution)/shard_map/ppermute | solution.py:288
  (14 other events, 81.0 us)

commit v4 on v3

--- a/solution.py
+++ b/solution.py
@@ -11,6 +11,7 @@
 BLK = 256
 ITERS = 2
 NEG = -1e30
+RING = 4
 VMEM_BYTES = 24 * 1024 * 1024
 
 
@@ -205,19 +206,31 @@
 def forward_kernel(
     scale, blocks, place_ref, pairs_ref, count_ref, x_ref, y_ref, g_ref, row_ref, *rest
 ):
-    outs, (lanes, wide, forward, lines_ref) = rest[:-4], rest[-4:]
+    own, up, down, up_next, down_next = rest[:-4]
+    lanes, wide, forward, lines_ref = rest[-4:]
     row = row_ref[...]
     spread_lanes(g_ref[...], blocks, lanes)
     down_rows(row, blocks, wide)
     images(pairs_ref, count_ref[0], x_ref, y_ref, scale, lanes, wide, forward, False)
-    n = len(outs)
+    n = lines_ref.shape[0]
     rows = blocks * BLK // n
     for b, line in enumerate(receivers_lines(row, n, blocks)):
         lines_ref[b] = line
-    for r, out in enumerate(outs):
-        to = place_ref[0] ^ r
+    me = place_ref[0]
+
+    def put(out, r, high):
+        to = ((me + r) % RING) + RING * high
         out[:rows, :] = forward[pl.ds(pl.multiple_of(to * rows, 16), rows), :]
         out[rows : rows + 1, :] = lines_ref[to]
+
+    put(up.at[0], 2, 0)
+    put(up.at[1], 1, 1)
+    put(down.at[0], 2, 1)
+    put(down.at[1], 3, 0)
+    put(own.at[0], 0, 0)
+    put(own.at[1], 0, 1)
+    put(up_next, 1, 0)
+    put(down_next, 3, 1)
 
 
 def pair_kernel(rows, a_ref, b_ref, out_ref):
@@ -237,16 +250,52 @@
         out_ref[q, rows : rows + 1, :] = merged[q : q + 1]
 
 
-def merge_kernel(rows, *refs):
-    out_ref = refs[-1]
-    parts = [p for ref in refs[:-1] for p in ([ref] if len(ref.shape) == 2 else [ref.at[d] for d in range(ref.shape[0])])]
+def blend(parts, rows):
     logs = jnp.concatenate([part[rows : rows + 1, :] for part in parts], axis=0)
-    lifted = jnp.exp2(logs - jnp.max(logs, axis=0, keepdims=True))
-    upright = jnp.transpose(lifted / jnp.sum(lifted, axis=0, keepdims=True))
+    high = jnp.max(logs, axis=0, keepdims=True)
+    lifted = jnp.exp2(logs - high)
+    whole = jnp.sum(lifted, axis=0, keepdims=True)
+    upright = jnp.transpose(lifted / whole)
     total = jnp.zeros((rows, BLK), jnp.float32)
     for d, part in enumerate(parts):
         total += upright[:rows, d : d + 1] * part[:rows, :]
-    out_ref[...] = total
+    return total, high + jnp.log2(whole)
+
+
+def put_blend(out, blended, rows):
+    out[:rows, :] = blended[0]
+    if out.shape[0] > rows:
+        out[rows : rows + 1, :] = blended[1]
+
+
+def z_kernel(rows, place_ref, parts_ref, keep_ref, send_ref):
+    for out, low in ((keep_ref, place_ref[0]), (send_ref, 1 - place_ref[0])):
+        parts = [parts_ref.at[d, low] for d in range(parts_ref.shape[0])]
+        put_blend(out, blend(parts, rows), rows)
+
+
+def relay_kernel(rows, up_next, up_came, down_next, down_came, up_out, down_out):
+    put_blend(up_out, blend([up_next, up_came.at[0]], rows), rows)
+    put_blend(down_out, blend([down_next, down_came.at[0]], rows), rows)
+
+
+def x_kernel(rows, place_ref, own, up_came, down_came, up_second, down_second, keep_ref, send_ref):
+    low = blend([own.at[0], up_second, down_came.at[1]], rows)
+    high = blend([own.at[1], down_second, up_came.at[1]], rows)
+
+    @pl.when(place_ref[0] == 0)
+    def _():
+        put_blend(keep_ref, low, rows)
+        put_blend(send_ref, high, rows)
+
+    @pl.when(place_ref[0] == 1)
+    def _():
+        put_blend(keep_ref, high, rows)
+        put_blend(send_ref, low, rows)
+
+
+def last_kernel(rows, a_ref, b_ref, out_ref):
+    put_blend(out_ref, blend([a_ref, b_ref], rows), rows)
 
 
 def in_vmem(n):
@@ -287,35 +336,42 @@
     def swap(value, axis, size, bit):
         return lax.ppermute(value, axis, [(k, k ^ bit) for k in range(size)])
 
-    def butterfly(row, col):
-        bit = 1
-        while bit < max(n_src, n_tgt):
-            row_came = swap(row, "tgt", n_tgt, bit) if bit < n_tgt else None
-            col_came = swap(col, "src", n_src, bit) if bit < n_src else None
-            if 2 * bit < n_tgt:
-                row = log_sum([row, row_came])
-            elif 2 * bit == n_tgt:
-                rows = [row, row_came]
-            if 2 * bit < n_src:
-                col = log_sum([col, col_came])
-            elif 2 * bit == n_src:
-                cols = [col, col_came]
-            bit *= 2
-        return rows, cols
+    n_z = n_src // 4
+    along_z = [list(range(k, n_src, 4)) for k in range(4)]
+
+    def exchange(row, col):
+        col = log_sum([col, swap(col, "src", n_src, 1)])
+        row = log_sum([row, swap(row, "tgt", n_tgt, 1)])
+        col = log_sum([col, swap(col, "src", n_src, 2)])
+        row = log_sum([row, swap(row, "tgt", n_tgt, 2)])
+        copies = jnp.broadcast_to(col[None], (n_z, *col.shape))
+        cols = lax.all_to_all(copies, "src", 0, 0, axis_index_groups=along_z, tiled=True)
+        return [row, swap(row, "tgt", n_tgt, 4)], [cols]
 
     f, g, row, col = sweep(True, [], 0, 0)
-    rows, cols = butterfly(row, col)
-    f, g, row, col = sweep(False, [f, g, *rows, *cols], 2, 2)
-    rows, cols = butterfly(row, col)
+    rows, cols = exchange(row, col)
+    f, g, row, col = sweep(False, [f, g, *rows, *cols], 2, 1)
+    rows, cols = exchange(row, col)
 
     f_rows, b_rows = blocks * BLK // n_tgt, blocks * BLK // n_src
     half = n_src // 2
     scalar = pl.BlockSpec(memory_space=pltpu.SMEM)
-    core = lax.axis_index("src").astype(jnp.int32) % 2
+    s_at = lax.axis_index("src").astype(jnp.int32).reshape(1)
+    t_at = lax.axis_index("tgt").astype(jnp.int32).reshape(1)
+
+    def call(kernel, operands, outs, places=()):
+        return pl.pallas_call(
+            kernel,
+            out_shape=outs,
+            in_specs=[scalar] * len(places) + in_vmem(len(operands)),
+            out_specs=in_vmem(len(outs)),
+            compiler_params=params,
+        )(*places, *operands)
+
     g, row, keep, send = pl.pallas_call(
-        functools.partial(backward_kernel, 2, 2, scale, blocks),
+        functools.partial(backward_kernel, 2, 1, scale, blocks),
         out_shape=[shape(8, BLK)] * 2 + [shape(half, b_rows + 8, width)] * 2,
-        in_specs=[scalar] + head + in_vmem(6),
+        in_specs=[scalar] + head + in_vmem(5),
         out_specs=in_vmem(4),
         scratch_shapes=[
             pltpu.VMEM((blocks, 8, BLK), jnp.float32),
@@ -323,13 +379,15 @@
         ]
         + sums_scratch(blocks),
         compiler_params=params,
-    )(core.reshape(1), pair_list, kept, x, y, f, g, *rows, *cols)
+    )(s_at % 2, pair_list, kept, x, y, f, g, *rows, *cols)
     came = swap(send, "src", n_src, 1)
+    block = shape(f_rows + 8, width)
+    two = shape(2, f_rows + 8, width)
     forward = pl.pallas_call(
         functools.partial(forward_kernel, scale, blocks),
-        out_shape=[shape(f_rows + 8, width)] * n_tgt,
+        out_shape=[two, two, two, block, block],
         in_specs=[scalar] + head + in_vmem(2),
-        out_specs=in_vmem(n_tgt),
+        out_specs=in_vmem(5),
         scratch_shapes=[
             pltpu.VMEM((blocks, 8, BLK), jnp.float32),
             pltpu.VMEM((blocks, BLK, 128), jnp.float32),
@@ -338,29 +396,48 @@
         ],
         compiler_params=params,
         cost_estimate=pl.CostEstimate(flops=6 * 10**9, bytes_accessed=4 * 10**6, transcendentals=0),
-    )(lax.axis_index("tgt").astype(jnp.int32).reshape(1), pair_list, kept, x, y, g, row)
-    backward = pl.pallas_call(
-        functools.partial(pair_kernel, b_rows),
-        out_shape=shape(half, b_rows + 8, width),
-        in_specs=in_vmem(2),
-        out_specs=pl.BlockSpec(memory_space=pltpu.VMEM),
-        compiler_params=params,
-    )(keep, came)
-    backward, forward = lax.optimization_barrier((backward, forward))
-
-    def merge(parts, rows):
-        return pl.pallas_call(
-            functools.partial(merge_kernel, rows),
-            out_shape=shape(rows, width),
-            in_specs=in_vmem(len(parts)),
-            out_specs=pl.BlockSpec(memory_space=pltpu.VMEM),
-            compiler_params=params,
-        )(*parts)
-
-    same_core = [list(range(k, n_src, 2)) for k in range(2)]
-    backward = lax.all_to_all(backward, "src", 0, 0, axis_index_groups=same_core, tiled=True)
-    forward = [forward[0]] + [swap(forward[r], "tgt", n_tgt, r) for r in range(1, n_tgt)]
-    return (merge(forward, f_rows), merge([backward], b_rows))
+    )(t_at % RING, pair_list, kept, x, y, g, row)
+    came, forward = lax.optimization_barrier((came, forward))
+
+    (backward,) = call(
+        functools.partial(pair_kernel, b_rows), [keep, came], [shape(half, b_rows + 8, width)]
+    )
+    backward = lax.all_to_all(
+        backward.reshape(n_z, 2, b_rows + 8, width),
+        "src",
+        0,
+        0,
+        axis_index_groups=along_z,
+        tiled=True,
+    )
+    small = shape(b_rows + 8, width)
+    keep, send = call(
+        functools.partial(z_kernel, b_rows), [backward], [small, small], [s_at // 2 % 2]
+    )
+    came = swap(send, "src", n_src, 2)
+    (backward,) = call(functools.partial(last_kernel, b_rows), [keep, came], [shape(b_rows, width)])
+
+    ups = [(k, k // RING * RING + (k + 1) % RING) for k in range(n_tgt)]
+    downs = [(b, a) for a, b in ups]
+    own, up, down, up_next, down_next = forward
+    up_came = lax.ppermute(up, "tgt", ups)
+    down_came = lax.ppermute(down, "tgt", downs)
+    up, down = call(
+        functools.partial(relay_kernel, f_rows),
+        [up_next, up_came, down_next, down_came],
+        [block, block],
+    )
+    up_second = lax.ppermute(up, "tgt", ups)
+    down_second = lax.ppermute(down, "tgt", downs)
+    keep, send = call(
+        functools.partial(x_kernel, f_rows),
+        [own, up_came, down_came, up_second, down_second],
+        [block, block],
+        [t_at // RING],
+    )
+    came = swap(send, "tgt", n_tgt, RING)
+    (forward,) = call(functools.partial(last_kernel, f_rows), [keep, came], [shape(f_rows, width)])
+    return (forward, backward)
 
 
 def solution(mesh):

time: 130 us -> 122 us (0.938); the launches traced: 129 us -> 123 us
  starting transfers between devices: 72.8 us -> 55.1 us
  Pallas kernels: 17.5 us -> 28 us
  local copies, waits for them, and re-layouts: 3.01 us -> 6.54 us
  waiting for transfers between devices: 34.3 us -> 31.5 us
    ppermute x24 -> x13, starting transfers between devices: 52 us -> 23 us  [swap(): return lax.ppermute(value, axis, [(k, k ^ bit) for k in range(size)])]
    ppermute x24 -> x13, waiting for transfers between devices: 34.2 us -> 11.2 us  [swap(): return lax.ppermute(value, axis, [(k, k ^ bit) for k in range(size)])]
    ppermute x0 -> x4, waiting for transfers between devices: none -> 10.7 us  [the longest x1 6.98 us: per_device(): up_came = lax.ppermute(up, 'tgt', ups)]
    all_to_all x1 -> x3, waiting for transfers between devices: 0.01 us -> 9.57 us  [the longest x2 6.21 us: exchange(): lax.all_to_all(copies, 'src', 0, 0, axis_index_groups=along_z, tiled=True)]
    ppermute x0 -> x4, starting transfers between devices: none -> 6.61 us  [the longest x1 3.22 us: per_device(): down_second = lax.ppermute(down, 'tgt', downs)]
    all_to_all x1 -> x3, starting transfers between devices: 20.8 us -> 25.5 us  [the longest x2 13.5 us: exchange(): lax.all_to_all(copies, 'src', 0, 0, axis_index_groups=along_z, tiled=True)]
    pallas_call x4 -> x7, Pallas kernels: 9.46 us -> 14.1 us  [the longest x1 9.82 us: per_device(): pl.pallas_call(functools.partial(backward_kernel, 2, 1, scale, blocks), o...]
    pallas_call x2, Pallas kernels: 5.34 us -> 8.96 us  [sweep(): pl.pallas_call(functools.partial(sweep_kernel, first, n_row, n_col, scale...]
  transfers between devices with their start and end apart: 25 -> 20, of which waited for: 14 -> 10; matrix products, arithmetic and copies ran while one was open for 0% -> 1% of each run, Pallas kernels for 3% -> 6%
where the time goes in v4:
time: 122 us; the launch traced here: 123 us
  starting transfers between devices  55.1 us (45%)
  waiting for transfers between devices  31.5 us (26%)
  Pallas kernels  28 us (23%)
  local copies, waits for them, and re-layouts  6.54 us (5%)
  between operations  1.46 us (1%)
    ppermute x13, starting transfers between devices, swap(): return lax.ppermute(value, axis, [(k, k ^ bit) for k in range(size)])  23 us
    all_to_all x2, starting transfers between devices, exchange(): lax.all_to_all(copies, 'src', 0, 0, axis_index_groups=along_z, tiled=True)  13.5 us
    all_to_all x1, starting transfers between devices, per_device(): lax.all_to_all(backward.reshape(n_z, 2, b_rows + 8, width), 'src', 0, 0,...  12 us
    ppermute x13, waiting for transfers between devices, swap(): return lax.ppermute(value, axis, [(k, k ^ bit) for k in range(size)])  11.2 us
    pallas_call x1, Pallas kernels, per_device(): pl.pallas_call(functools.partial(backward_kernel, 2, 1, scale, blocks), o...  9.82 us
    pallas_call x2, Pallas kernels, sweep(): pl.pallas_call(functools.partial(sweep_kernel, first, n_row, n_col, scale...  8.96 us
    ppermute x1, waiting for transfers between devices, per_device(): up_came = lax.ppermute(up, 'tgt', ups)  6.98 us
    all_to_all x2, waiting for transfers between devices, exchange(): lax.all_to_all(copies, 'src', 0, 0, axis_index_groups=along_z, tiled=True)  6.21 us
  transfers between devices with their start and end apart: 20, of which 10 were waited for; matrix products, arithmetic and copies ran while one was open for 1% of the time, Pallas kernels for 6%

profile of v4, /device:TPU:8, one launch (start us, length us, event | category | flops | bytes accessed | tf_op | source)
XLA Modules:
  0.0 122.8 jit_solution(13806562038051906369)
XLA Ops:
  2.0 1.1 copy-done
  3.1 1.1 copy-done.2
  4.2 4.4 %shard_map.59 = (f32[8,256]{1,0:T(8,128)S(1)}, f32[8,256]{1,0:T(8,128)S(1)}, f32[8,256]{1,0:T(8,128)S(1)}, f32[8,256]{1,0:T(8,128)S(1)}) custom-call(s32[2,24]{1,0:T(2,128)S(1)} %bitcast.21, s32[1]{0:T(128)} %bitcast.9.count_ref, bf16[6,256,256]{2,1,0:T(8,128)(2,1)S(1)} %bitcast.13, bf16[6,256,256]{2,1,0:T(8,128)(2,1)S(1)} %bitcast.17), custom_call_target="tpu_custom_call" | custom-call | tf_op jit(solution)/shard_map/pallas_call | solution.py:327
  8.7 2.2 %collective-permute-start = (f32[8,256]{1,0:T(8,128)S(1)}, f32[8,256]{1,0:T(8,128)S(1)}, u32[]{:S(2)}, u32[]{:S(2)}) collective-permute-start(f32[8,256]{1,0:T(8,128)S(1)} %get-tuple-element.33), channel_id=1, source_target_pairs={{0,1},{1,0},{2,3},{3,2},{4,5},{5,4},{6,7},{7,6},{8,9},{9,8},{10,11... | collective-permute-start | bytes 24584 | tf_op jit(solution)/shard_map/ppermute | solution.py:337
  10.9 1.2 %collective-permute-start.4 = (f32[8,256]{1,0:T(8,128)S(1)}, f32[8,256]{1,0:T(8,128)S(1)}, u32[]{:S(2)}, u32[]{:S(2)}) collective-permute-start(f32[8,256]{1,0:T(8,128)S(1)} %multiply_add_fusion.5), channel_id=1, source_target_pairs={{0,16},{8,24},{16,0},{24,8},{32,48},{40,56},{48,32},{56,40},{64,80... | collective-permute-start | bytes 24584 | tf_op jit(solution)/shard_map/ppermute | solution.py:337
  12.6 4.0 %collective-permute-start.1 = (f32[8,256]{1,0:T(8,128)S(1)}, f32[8,256]{1,0:T(8,128)S(1)}, u32[]{:S(2)}, u32[]{:S(2)}) collective-permute-start(f32[8,256]{1,0:T(8,128)S(1)} %multiply_add_fusion.7), channel_id=1, source_target_pairs={{0,2},{1,3},{2,0},{3,1},{4,6},{5,7},{6,4},{7,5},{8,10},{9,11},{10,... | collective-permute-start | bytes 24584 | tf_op jit(solution)/shard_map/ppermute | solution.py:337
  17.2 8.9 %all-to-all-start = ((f32[8,8,256]{2,1,0:T(8,128)}), f32[8,8,256]{2,1,0:T(8,128)S(1)}, u32[]{:S(2)}, u32[]{:S(2)}) async-start(f32[8,8,256]{2,1,0:T(8,128)} %broadcast_in_dim.4), calls=%async_computation | async-start | bytes 131072 | tf_op jit(solution)/shard_map/all_to_all | solution.py:348
  26.2 2.3 %collective-permute-start.2 = (f32[8,256]{1,0:T(8,128)S(1)}, f32[8,256]{1,0:T(8,128)S(1)}, u32[]{:S(2)}, u32[]{:S(2)}) collective-permute-start(f32[8,256]{1,0:T(8,128)S(1)} %multiply_add_fusion.6.rest_2_), channel_id=1, source_target_pairs={{0,4},{1,5},{2,6},{3,7},{4,0},{5,1},{6,2},{7,3},{8,12},{9,13},{10,... | collective-permute-start | bytes 24584 | tf_op jit(solution)/shard_map/ppermute | solution.py:337
  28.5 2.9 %collective-permute-done.2.rest_3_ = f32[8,256]{1,0:T(8,128)S(1)} collective-permute-done((f32[8,256]{1,0:T(8,128)S(1)}, f32[8,256]{1,0:T(8,128)S(1)}, u32[]{:S(2)}, u32[]{:S(2)}) %collective-permute-start.2) | collective-permute-done | bytes 8224 | tf_op jit(solution)/shard_map/ppermute | solution.py:337
  31.4 3.1 %all-to-all-done.rest_4_ = f32[8,8,256]{2,1,0:T(8,128)S(1)} async-done(((f32[8,8,256]{2,1,0:T(8,128)}), f32[8,8,256]{2,1,0:T(8,128)S(1)}, u32[]{:S(2)}, u32[]{:S(2)}) %all-to-all-start) | async-done | bytes 65568 | tf_op jit(solution)/shard_map/all_to_all | solution.py:348
  34.5 4.6 %shard_map.60 = (f32[8,256]{1,0:T(8,128)S(1)}, f32[8,256]{1,0:T(8,128)S(1)}, f32[8,256]{1,0:T(8,128)S(1)}, f32[8,256]{1,0:T(8,128)S(1)}) custom-call(s32[2,24]{1,0:T(2,128)S(1)} %bitcast.22, s32[1]{0:T(128)} %bitcast.10.count_ref, bf16[6,256,256]{2,1,0:T(8,128)(2,1)S(1)} %bitcast.14, bf16[6,256,256]{2,1,0:T(8,128)(2,1)S(1)} %bitcast.18, ...), custom_call_target="tpu_custom_call" | custom-call | tf_op jit(solution)/shard_map/pallas_call | solution.py:327
  39.2 2.1 %collective-permute-start.5 = (f32[8,256]{1,0:T(8,128)S(1)}, f32[8,256]{1,0:T(8,128)S(1)}, u32[]{:S(2)}, u32[]{:S(2)}) collective-permute-start(f32[8,256]{1,0:T(8,128)S(1)} %get-tuple-element.37), channel_id=1, source_target_pairs={{0,1},{1,0},{2,3},{3,2},{4,5},{5,4},{6,7},{7,6},{8,9},{9,8},{10,11... | collective-permute-start | bytes 24584 | tf_op jit(solution)/shard_map/ppermute | solution.py:337
  41.7 1.2 collective-permute-done.5
  43.0 3.1 %collective-permute-start.6 = (f32[8,256]{1,0:T(8,128)S(1)}, f32[8,256]{1,0:T(8,128)S(1)}, u32[]{:S(2)}, u32[]{:S(2)}) collective-permute-start(f32[8,256]{1,0:T(8,128)S(1)} %multiply_add_fusion.3), channel_id=1, source_target_pairs={{0,2},{1,3},{2,0},{3,1},{4,6},{5,7},{6,4},{7,5},{8,10},{9,11},{10,... | collective-permute-start | bytes 24584 | tf_op jit(solution)/shard_map/ppermute | solution.py:337
  46.7 4.6 %all-to-all-start.1 = ((f32[8,8,256]{2,1,0:T(8,128)}), f32[8,8,256]{2,1,0:T(8,128)S(1)}, u32[]{:S(2)}, u32[]{:S(2)}) async-start(f32[8,8,256]{2,1,0:T(8,128)} %broadcast_in_dim.5), calls=%async_computation.1 | async-start | bytes 131072 | tf_op jit(solution)/shard_map/all_to_all | solution.py:348
  51.3 2.3 %collective-permute-start.7 = (f32[8,256]{1,0:T(8,128)S(1)}, f32[8,256]{1,0:T(8,128)S(1)}, u32[]{:S(2)}, u32[]{:S(2)}) collective-permute-start(f32[8,256]{1,0:T(8,128)S(1)} %multiply_add_fusion.2.rest_2_), channel_id=1, source_target_pairs={{0,4},{1,5},{2,6},{3,7},{4,0},{5,1},{6,2},{7,3},{8,12},{9,13},{10,... | collective-permute-start | bytes 24584 | tf_op jit(solution)/shard_map/ppermute | solution.py:337
  53.6 3.0 %collective-permute-done.7.rest_3_ = f32[8,256]{1,0:T(8,128)S(1)} collective-permute-done((f32[8,256]{1,0:T(8,128)S(1)}, f32[8,256]{1,0:T(8,128)S(1)}, u32[]{:S(2)}, u32[]{:S(2)}) %collective-permute-start.7) | collective-permute-done | bytes 8224 | tf_op jit(solution)/shard_map/ppermute | solution.py:337
  56.6 3.1 %all-to-all-done.1.rest_4_ = f32[8,8,256]{2,1,0:T(8,128)S(1)} async-done(((f32[8,8,256]{2,1,0:T(8,128)}), f32[8,8,256]{2,1,0:T(8,128)S(1)}, u32[]{:S(2)}, u32[]{:S(2)}) %all-to-all-start.1) | async-done | bytes 65568 | tf_op jit(solution)/shard_map/all_to_all | solution.py:348
  59.7 9.8 %shard_map.61 = (f32[8,256]{1,0:T(8,128)S(1)}, f32[8,256]{1,0:T(8,128)S(1)}, f32[16,56,256]{2,1,0:T(8,128)S(1)}, f32[16,56,256]{2,1,0:T(8,128)}) custom-call(s32[1]{0:T(128)S(6)} %select_n.24.core_ref, s32[2,24]{1,0:T(2,128)S(1)} %bitcast.23, s32[1]{0:T(128)} %bitcast.11.count_ref, bf16[6,256,256]{2,1,0:T(8,128)(2,1)S(1)} %bitcast.15, ...), custom_call_target="tpu_custom_call" | custom-call | tf_op jit(solution)/shard_map/pallas_call | solution.py:371
  69.5 5.0 %shard_map.62 = (f32[2,200,256]{2,1,0:T(8,128)S(1)}, f32[2,200,256]{2,1,0:T(8,128)S(1)}, f32[2,200,256]{2,1,0:T(8,128)S(1)}, f32[200,256]{1,0:T(8,128)S(1)}, f32[200,256]{1,0:T(8,128)S(1)}) custom-call(s32[1]{0:T(128)S(6)} %select_n.25.place_ref, s32[2,24]{1,0:T(2,128)S(1)} %bitcast.24, s32[1]{0:T(128)} %bitcast.12.count_ref, ...), custom_call_target="tpu_custom_call" | custom-call | flops 6000000000 | bytes 4000000 | tf_op jit(solution)/shard_map/pallas_call | solution.py:386
  76.8 1.3 %shard_map.66 = f32[16,56,256]{2,1,0:T(8,128)} custom-call(f32[16,56,256]{2,1,0:T(8,128)S(1)} %get-tuple-element.56.a_ref, f32[16,56,256]{2,1,0:T(8,128)S(1)} %collective-permute-done.10.b_ref), custom_call_target="tpu_custom_call" | custom-call | tf_op jit(solution)/shard_map/pallas_call | solution.py:363
  78.1 12.0 %all-to-all-start.2 = ((f32[8,2,56,256]{3,2,1,0:T(8,128)}), f32[8,2,56,256]{3,2,1,0:T(8,128)S(1)}, u32[]{:S(2)}, u32[]{:S(2)}) async-start(f32[8,2,56,256]{3,2,1,0:T(8,128)} %bitcast.8), calls=%async_computation.2 | async-start | bytes 1835008 | tf_op jit(solution)/shard_map/all_to_all | solution.py:405
  90.2 3.2 %collective-permute-start.12 = (f32[2,200,256]{2,1,0:T(8,128)S(1)}, f32[2,200,256]{2,1,0:T(8,128)S(1)}, u32[]{:S(2)}, u32[]{:S(2)}) collective-permute-start(f32[2,200,256]{2,1,0:T(8,128)S(1)} %copy-done.12), channel_id=1, source_target_pairs={{1,0},{2,1},{3,2},{0,3},{5,4},{6,5},{7,6},{4,7},{9,8},{10,9},{11,1... | collective-permute-start | bytes 1228808 | tf_op jit(solution)/shard_map/ppermute | solution.py:424
  93.5 7.0 %collective-permute-done.11.up_came = f32[2,200,256]{2,1,0:T(8,128)S(1)} collective-permute-done((f32[2,200,256]{2,1,0:T(8,128)S(1)}, f32[2,200,256]{2,1,0:T(8,128)S(1)}, u32[]{:S(2)}, u32[]{:S(2)}) %collective-permute-start.11) | collective-permute-done | bytes 409632 | tf_op jit(solution)/shard_map/ppermute | solution.py:423
  100.9 3.2 %collective-permute-start.14 = (f32[200,256]{1,0:T(8,128)S(1)}, f32[200,256]{1,0:T(8,128)S(1)}, u32[]{:S(2)}, u32[]{:S(2)}) collective-permute-start(f32[200,256]{1,0:T(8,128)S(1)} %get-tuple-element.53), channel_id=1, source_target_pairs={{1,0},{2,1},{3,2},{0,3},{5,4},{6,5},{7,6},{4,7},{9,8},{10,9},{11,1... | collective-permute-start | bytes 614408 | tf_op jit(solution)/shard_map/ppermute | solution.py:431
  104.2 3.7 %collective-permute-done.13.up_second = f32[200,256]{1,0:T(8,128)S(1)} collective-permute-done((f32[200,256]{1,0:T(8,128)S(1)}, f32[200,256]{1,0:T(8,128)S(1)}, u32[]{:S(2)}, u32[]{:S(2)}) %collective-permute-start.13) | collective-permute-done | bytes 204832 | tf_op jit(solution)/shard_map/ppermute | solution.py:430
  108.4 2.5 %collective-permute-start.15 = (f32[200,256]{1,0:T(8,128)S(1)}, f32[200,256]{1,0:T(8,128)S(1)}, u32[]{:S(2)}, u32[]{:S(2)}) collective-permute-start(f32[200,256]{1,0:T(8,128)S(1)} %get-tuple-element.55), channel_id=1, source_target_pairs={{0,4},{1,5},{2,6},{3,7},{4,0},{5,1},{6,2},{7,3},{8,12},{9,13},{10,... | collective-permute-start | bytes 614408 | tf_op jit(solution)/shard_map/ppermute | solution.py:337
  110.8 3.4 %all-to-all-done.2.parts_ref = f32[8,2,56,256]{3,2,1,0:T(8,128)S(1)} async-done(((f32[8,2,56,256]{3,2,1,0:T(8,128)}), f32[8,2,56,256]{3,2,1,0:T(8,128)S(1)}, u32[]{:S(2)}, u32[]{:S(2)}) %all-to-all-start.2) | async-done | bytes 917536 | tf_op jit(solution)/shard_map/all_to_all | solution.py:405
  114.5 2.7 %collective-permute-start.16 = (f32[56,256]{1,0:T(8,128)S(1)}, f32[56,256]{1,0:T(8,128)S(1)}, u32[]{:S(2)}, u32[]{:S(2)}) collective-permute-start(f32[56,256]{1,0:T(8,128)S(1)} %get-tuple-element.59), channel_id=1, source_target_pairs={{0,16},{8,24},{16,0},{24,8},{32,48},{40,56},{48,32},{56,40},{64,80... | collective-permute-start | bytes 172040 | tf_op jit(solution)/shard_map/ppermute | solution.py:337
  117.2 1.0 shard_map.65
  118.2 3.8 %collective-permute-done.16.b_ref = f32[56,256]{1,0:T(8,128)S(1)} collective-permute-done((f32[56,256]{1,0:T(8,128)S(1)}, f32[56,256]{1,0:T(8,128)S(1)}, u32[]{:S(2)}, u32[]{:S(2)}) %collective-permute-start.16) | collective-permute-done | bytes 57376 | tf_op jit(solution)/shard_map/ppermute | solution.py:337
  121.9 0.8 shard_map.68
  (58 shorter events, 6.7 us)
Async XLA Ops:
  2.0 1.1 copy-start
  3.1 1.1 copy-start.2
  4.2 30.3 %copy-start.1 = (bf16[1536,256]{1,0:T(8,128)(2,1)S(1)}, bf16[1536,256]{1,0:T(8,128)(2,1)}, u32[]{:S(2)}) copy-start(bf16[1536,256]{1,0:T(8,128)(2,1)} %param.4) | copy-start | bytes 2359300
  4.2 30.3 %copy-start.3 = (bf16[1536,256]{1,0:T(8,128)(2,1)S(1)}, bf16[1536,256]{1,0:T(8,128)(2,1)}, u32[]{:S(2)}) copy-start(bf16[1536,256]{1,0:T(8,128)(2,1)} %param.5) | copy-start | bytes 2359300
  8.6 2.3 %collective-permute-start.3 = (f32[8,256]{1,0:T(8,128)S(1)}, f32[8,256]{1,0:T(8,128)S(1)}, u32[]{:S(2)}, u32[]{:S(2)}) collective-permute-start(f32[8,256]{1,0:T(8,128)S(1)} %get-tuple-element.34), channel_id=1, source_target_pairs={{0,8},{8,0},{16,24},{24,16},{32,40},{40,32},{48,56},{56,48},{64,72... | collective-permute-start | bytes 24584 | tf_op jit(solution)/shard_map/ppermute | solution.py:337
  8.7 3.8 %collective-permute-start = (f32[8,256]{1,0:T(8,128)S(1)}, f32[8,256]{1,0:T(8,128)S(1)}, u32[]{:S(2)}, u32[]{:S(2)}) collective-permute-start(f32[8,256]{1,0:T(8,128)S(1)} %get-tuple-element.33), channel_id=1, source_target_pairs={{0,1},{1,0},{2,3},{3,2},{4,5},{5,4},{6,7},{7,6},{8,9},{9,8},{10,11... | collective-permute-start | bytes 24584 | tf_op jit(solution)/shard_map/ppermute | solution.py:337
  10.9 5.6 %collective-permute-start.4 = (f32[8,256]{1,0:T(8,128)S(1)}, f32[8,256]{1,0:T(8,128)S(1)}, u32[]{:S(2)}, u32[]{:S(2)}) collective-permute-start(f32[8,256]{1,0:T(8,128)S(1)} %multiply_add_fusion.5), channel_id=1, source_target_pairs={{0,16},{8,24},{16,0},{24,8},{32,48},{40,56},{48,32},{56,40},{64,80... | collective-permute-start | bytes 24584 | tf_op jit(solution)/shard_map/ppermute | solution.py:337
  12.6 13.6 %collective-permute-start.1 = (f32[8,256]{1,0:T(8,128)S(1)}, f32[8,256]{1,0:T(8,128)S(1)}, u32[]{:S(2)}, u32[]{:S(2)}) collective-permute-start(f32[8,256]{1,0:T(8,128)S(1)} %multiply_add_fusion.7), channel_id=1, source_target_pairs={{0,2},{1,3},{2,0},{3,1},{4,6},{5,7},{6,4},{7,5},{8,10},{9,11},{10,... | collective-permute-start | bytes 24584 | tf_op jit(solution)/shard_map/ppermute | solution.py:337
  17.2 17.3 %all-to-all-start = ((f32[8,8,256]{2,1,0:T(8,128)}), f32[8,8,256]{2,1,0:T(8,128)S(1)}, u32[]{:S(2)}, u32[]{:S(2)}) async-start(f32[8,8,256]{2,1,0:T(8,128)} %broadcast_in_dim.4), calls=%async_computation | async-start | bytes 131072 | tf_op jit(solution)/shard_map/all_to_all | solution.py:348
  26.2 5.2 %collective-permute-start.2 = (f32[8,256]{1,0:T(8,128)S(1)}, f32[8,256]{1,0:T(8,128)S(1)}, u32[]{:S(2)}, u32[]{:S(2)}) collective-permute-start(f32[8,256]{1,0:T(8,128)S(1)} %multiply_add_fusion.6.rest_2_), channel_id=1, source_target_pairs={{0,4},{1,5},{2,6},{3,7},{4,0},{5,1},{6,2},{7,3},{8,12},{9,13},{10,... | collective-permute-start | bytes 24584 | tf_op jit(solution)/shard_map/ppermute | solution.py:337
  39.1 2.2 %collective-permute-start.8 = (f32[8,256]{1,0:T(8,128)S(1)}, f32[8,256]{1,0:T(8,128)S(1)}, u32[]{:S(2)}, u32[]{:S(2)}) collective-permute-start(f32[8,256]{1,0:T(8,128)S(1)} %get-tuple-element.38), channel_id=1, source_target_pairs={{0,8},{8,0},{16,24},{24,16},{32,40},{40,32},{48,56},{56,48},{64,72... | collective-permute-start | bytes 24584 | tf_op jit(solution)/shard_map/ppermute | solution.py:337
  39.2 3.7 %collective-permute-start.5 = (f32[8,256]{1,0:T(8,128)S(1)}, f32[8,256]{1,0:T(8,128)S(1)}, u32[]{:S(2)}, u32[]{:S(2)}) collective-permute-start(f32[8,256]{1,0:T(8,128)S(1)} %get-tuple-element.37), channel_id=1, source_target_pairs={{0,1},{1,0},{2,3},{3,2},{4,5},{5,4},{6,7},{7,6},{8,9},{9,8},{10,11... | collective-permute-start | bytes 24584 | tf_op jit(solution)/shard_map/ppermute | solution.py:337
  41.3 4.7 %collective-permute-start.9 = (f32[8,256]{1,0:T(8,128)S(1)}, f32[8,256]{1,0:T(8,128)S(1)}, u32[]{:S(2)}, u32[]{:S(2)}) collective-permute-start(f32[8,256]{1,0:T(8,128)S(1)} %multiply_add_fusion.1), channel_id=1, source_target_pairs={{0,16},{8,24},{16,0},{24,8},{32,48},{40,56},{48,32},{56,40},{64,80... | collective-permute-start | bytes 24584 | tf_op jit(solution)/shard_map/ppermute | solution.py:337
  43.0 8.3 %collective-permute-start.6 = (f32[8,256]{1,0:T(8,128)S(1)}, f32[8,256]{1,0:T(8,128)S(1)}, u32[]{:S(2)}, u32[]{:S(2)}) collective-permute-start(f32[8,256]{1,0:T(8,128)S(1)} %multiply_add_fusion.3), channel_id=1, source_target_pairs={{0,2},{1,3},{2,0},{3,1},{4,6},{5,7},{6,4},{7,5},{8,10},{9,11},{10,... | collective-permute-start | bytes 24584 | tf_op jit(solution)/shard_map/ppermute | solution.py:337
  46.7 13.0 %all-to-all-start.1 = ((f32[8,8,256]{2,1,0:T(8,128)}), f32[8,8,256]{2,1,0:T(8,128)S(1)}, u32[]{:S(2)}, u32[]{:S(2)}) async-start(f32[8,8,256]{2,1,0:T(8,128)} %broadcast_in_dim.5), calls=%async_computation.1 | async-start | bytes 131072 | tf_op jit(solution)/shard_map/all_to_all | solution.py:348
  51.3 5.2 %collective-permute-start.7 = (f32[8,256]{1,0:T(8,128)S(1)}, f32[8,256]{1,0:T(8,128)S(1)}, u32[]{:S(2)}, u32[]{:S(2)}) collective-permute-start(f32[8,256]{1,0:T(8,128)S(1)} %multiply_add_fusion.2.rest_2_), channel_id=1, source_target_pairs={{0,4},{1,5},{2,6},{3,7},{4,0},{5,1},{6,2},{7,3},{8,12},{9,13},{10,... | collective-permute-start | bytes 24584 | tf_op jit(solution)/shard_map/ppermute | solution.py:337
  69.5 7.3 %collective-permute-start.10 = (f32[16,56,256]{2,1,0:T(8,128)}, f32[16,56,256]{2,1,0:T(8,128)S(1)}, u32[]{:S(2)}, u32[]{:S(2)}) collective-permute-start(f32[16,56,256]{2,1,0:T(8,128)} %get-tuple-element.39), channel_id=1, source_target_pairs={{0,8},{8,0},{16,24},{24,16},{32,40},{40,32},{48,56},{56,48},{64,72... | collective-permute-start | bytes 2752520 | tf_op jit(solution)/shard_map/ppermute | solution.py:337
  75.2 0.8 copy-start.11
  76.7 1.4 %copy-start.6 = (f32[200,256]{1,0:T(8,128)}, f32[200,256]{1,0:T(8,128)S(1)}, u32[]{:S(2)}) copy-start(f32[200,256]{1,0:T(8,128)S(1)} %get-tuple-element.50.up_next) | copy-start | bytes 614404
  76.7 1.4 %copy-start.8 = (f32[200,256]{1,0:T(8,128)}, f32[200,256]{1,0:T(8,128)S(1)}, u32[]{:S(2)}) copy-start(f32[200,256]{1,0:T(8,128)S(1)} %get-tuple-element.51.down_next) | copy-start | bytes 614404
  78.1 12.0 %copy-start.14 = (f32[2,200,256]{2,1,0:T(8,128)S(1)}, f32[2,200,256]{2,1,0:T(8,128)}, u32[]{:S(2)}) copy-start(f32[2,200,256]{2,1,0:T(8,128)} %copy-done.13) | copy-start | bytes 1228804
  78.1 12.1 %copy-start.12 = (f32[2,200,256]{2,1,0:T(8,128)S(1)}, f32[2,200,256]{2,1,0:T(8,128)}, u32[]{:S(2)}) copy-start(f32[2,200,256]{2,1,0:T(8,128)} %copy-done.11) | copy-start | bytes 1228804
  78.1 22.3 %copy-start.7 = (f32[200,256]{1,0:T(8,128)S(1)}, f32[200,256]{1,0:T(8,128)}, u32[]{:S(2)}) copy-start(f32[200,256]{1,0:T(8,128)} %copy-done.6) | copy-start | bytes 614404
  78.1 22.3 %copy-start.9 = (f32[200,256]{1,0:T(8,128)S(1)}, f32[200,256]{1,0:T(8,128)}, u32[]{:S(2)}) copy-start(f32[200,256]{1,0:T(8,128)} %copy-done.8) | copy-start | bytes 614404
  78.1 36.1 %all-to-all-start.2 = ((f32[8,2,56,256]{3,2,1,0:T(8,128)}), f32[8,2,56,256]{3,2,1,0:T(8,128)S(1)}, u32[]{:S(2)}, u32[]{:S(2)}) async-start(f32[8,2,56,256]{3,2,1,0:T(8,128)} %bitcast.8), calls=%async_computation.2 | async-start | bytes 1835008 | tf_op jit(solution)/shard_map/all_to_all | solution.py:405
  90.1 17.8 %copy-start.5 = (f32[2,200,256]{2,1,0:T(8,128)S(1)}, f32[2,200,256]{2,1,0:T(8,128)}, u32[]{:S(2)}) copy-start(f32[2,200,256]{2,1,0:T(8,128)} %copy-done.4) | copy-start | bytes 1228804
  90.1 10.3 %collective-permute-start.11 = (f32[2,200,256]{2,1,0:T(8,128)S(1)}, f32[2,200,256]{2,1,0:T(8,128)S(1)}, u32[]{:S(2)}, u32[]{:S(2)}) collective-permute-start(f32[2,200,256]{2,1,0:T(8,128)S(1)} %copy-done.14), channel_id=1, source_target_pairs={{0,1},{1,2},{2,3},{3,0},{4,5},{5,6},{6,7},{7,4},{8,9},{9,10},{10,1... | collective-permute-start | bytes 1228808 | tf_op jit(solution)/shard_map/ppermute | solution.py:423
  90.2 10.2 %collective-permute-start.12 = (f32[2,200,256]{2,1,0:T(8,128)S(1)}, f32[2,200,256]{2,1,0:T(8,128)S(1)}, u32[]{:S(2)}, u32[]{:S(2)}) collective-permute-start(f32[2,200,256]{2,1,0:T(8,128)S(1)} %copy-done.12), channel_id=1, source_target_pairs={{1,0},{2,1},{3,2},{0,3},{5,4},{6,5},{7,6},{4,7},{9,8},{10,9},{11,1... | collective-permute-start | bytes 1228808 | tf_op jit(solution)/shard_map/ppermute | solution.py:424
  100.8 7.0 %collective-permute-start.13 = (f32[200,256]{1,0:T(8,128)S(1)}, f32[200,256]{1,0:T(8,128)S(1)}, u32[]{:S(2)}, u32[]{:S(2)}) collective-permute-start(f32[200,256]{1,0:T(8,128)S(1)} %get-tuple-element.52), channel_id=1, source_target_pairs={{0,1},{1,2},{2,3},{3,0},{4,5},{5,6},{6,7},{7,4},{8,9},{9,10},{10,1... | collective-permute-start | bytes 614408 | tf_op jit(solution)/shard_map/ppermute | solution.py:430
  100.9 7.0 %collective-permute-start.14 = (f32[200,256]{1,0:T(8,128)S(1)}, f32[200,256]{1,0:T(8,128)S(1)}, u32[]{:S(2)}, u32[]{:S(2)}) collective-permute-start(f32[200,256]{1,0:T(8,128)S(1)} %get-tuple-element.53), channel_id=1, source_target_pairs={{1,0},{2,1},{3,2},{0,3},{5,4},{6,5},{7,6},{4,7},{9,8},{10,9},{11,1... | collective-permute-start | bytes 614408 | tf_op jit(solution)/shard_map/ppermute | solution.py:431
  108.4 8.8 %collective-permute-start.15 = (f32[200,256]{1,0:T(8,128)S(1)}, f32[200,256]{1,0:T(8,128)S(1)}, u32[]{:S(2)}, u32[]{:S(2)}) collective-permute-start(f32[200,256]{1,0:T(8,128)S(1)} %get-tuple-element.55), channel_id=1, source_target_pairs={{0,4},{1,5},{2,6},{3,7},{4,0},{5,1},{6,2},{7,3},{8,12},{9,13},{10,... | collective-permute-start | bytes 614408 | tf_op jit(solution)/shard_map/ppermute | solution.py:337
  114.5 7.5 %collective-permute-start.16 = (f32[56,256]{1,0:T(8,128)S(1)}, f32[56,256]{1,0:T(8,128)S(1)}, u32[]{:S(2)}, u32[]{:S(2)}) collective-permute-start(f32[56,256]{1,0:T(8,128)S(1)} %get-tuple-element.59), channel_id=1, source_target_pairs={{0,16},{8,24},{16,0},{24,8},{32,48},{40,56},{48,32},{56,40},{64,80... | collective-permute-start | bytes 172040 | tf_op jit(solution)/shard_map/ppermute | solution.py:337
  (3 other events, 2.2 us)

commit v5 on v4

--- a/solution.py
+++ b/solution.py
@@ -12,7 +12,6 @@
 ITERS = 2
 NEG = -1e30
 RING = 4
-VMEM_BYTES = 24 * 1024 * 1024
 
 
 def log_sum(parts):
@@ -27,15 +26,16 @@
         wide_ref[b] = jnp.broadcast_to(upright[:, b : b + 1], (BLK, 128))
 
 
-def norms(z_ref, scale, blocks, wide_ref):
+def norm(z, scale):
+    z = z.astype(jnp.float32)
+    return jnp.sum(z * z, axis=1, keepdims=True) * (-0.5 * scale)
+
+
+def across(columns):
     lane = lax.broadcasted_iota(jnp.int32, (BLK, 128), 1)
     gathered = jnp.zeros((BLK, 128), jnp.float32)
-    for b in range(blocks):
-        z = z_ref[b].astype(jnp.float32)
-        half = jnp.sum(z * z, axis=1, keepdims=True) * (-0.5 * scale)
-        wide = jnp.broadcast_to(half, (BLK, 128))
-        wide_ref[b] = wide
-        gathered = jnp.where(lane == b, wide, gathered)
+    for b, column in enumerate(columns):
+        gathered = jnp.where(lane == b, jnp.broadcast_to(column, (BLK, 128)), gathered)
     return jnp.transpose(gathered)[:8]
 
 
@@ -80,30 +80,46 @@
     return jnp.concatenate(rows, axis=0)
 
 
-def start_potentials(x_ref, y_ref, rest, first, n_row, n_col, scale, blocks, f_wide, g_wide):
-    if first:
-        return norms(x_ref, scale, blocks, f_wide), norms(y_ref, scale, blocks, g_wide), rest
-    f_old, g_old = rest[0][...], rest[1][...]
-    rows = [part for r in rest[2 : 2 + n_row] for part in parts_of(r)]
-    cols = [part for r in rest[2 + n_row : 2 + n_row + n_col] for part in parts_of(r)]
-    f = 0.5 * (f_old - log_sum(rows))
-    g = 0.5 * (g_old - log_sum(cols))
-    down_rows(f, blocks, f_wide)
-    down_rows(g, blocks, g_wide)
-    return f, g, rest[2 + n_row + n_col :]
-
-
-def parts_of(ref):
-    if len(ref.shape) == 2:
-        return [ref[...]]
-    return [ref[k] for k in range(ref.shape[0])]
+def new_potential(old_ref, refs):
+    parts = [part for r in refs for part in ([r[...]] if len(r.shape) == 2 else [r[k] for k in range(r.shape[0])])]
+    return 0.5 * (old_ref[...] - log_sum(parts))
+
+
+def exponentials(scores, scale, wide, lanes):
+    halves = []
+    for h in range(2):
+        at = slice(128 * h, 128 * h + 128)
+        t = (scores[:, at] * scale + wide).reshape(BLK // 8, 8, 128) + lanes[:, at][None]
+        halves.append(jnp.exp2(t))
+    return halves
+
+
+def add_sums(halves, row_acc, col_acc, s, t):
+    for h, e in enumerate(halves):
+        col_acc[t, :, 128 * h : 128 * h + 128] += jnp.sum(e, axis=0)
+    row_acc[s] += (halves[0] + halves[1]).reshape(BLK, 128)
+
+
+def totals(row_acc, col_acc, blocks):
+    columns = [jnp.sum(row_acc[b], axis=1, keepdims=True) for b in range(blocks)]
+    below = lax.broadcasted_iota(jnp.int32, (8, BLK), 0) >= blocks
+    row = jnp.where(below, 1.0, across(columns))
+    col = [jnp.sum(col_acc[b], axis=0, keepdims=True) for b in range(blocks)]
+    col = jnp.concatenate(col + [jnp.ones((8 - blocks, BLK), jnp.float32)], axis=0)
+    low = jnp.minimum(jnp.min(row), jnp.min(col))
+    high = jnp.maximum(jnp.max(row), jnp.max(col))
+    return columns, row, col, (low >= 2.0**-60) & (high <= 2.0**100)
+
+
+def clear(*refs):
+    for ref in refs:
+        ref[...] = jnp.zeros(ref.shape, jnp.float32)
 
 
 def pass_sums(pairs_ref, kept, x_ref, y_ref, scale, f_wide, g_wide, row_high, row_sum, col_high, col_sum):
     for ref in (row_high, col_high):
         ref[...] = jnp.full(ref.shape, NEG, jnp.float32)
-    for ref in (row_sum, col_sum):
-        ref[...] = jnp.zeros(ref.shape, jnp.float32)
+    clear(row_sum, col_sum)
 
     def visit(s, t):
         xs, yt = x_ref[s], y_ref[t]
@@ -113,18 +129,64 @@
     over_pairs(pairs_ref, kept, visit)
 
 
-def sweep_kernel(first, n_row, n_col, scale, blocks, pairs_ref, count_ref, x_ref, y_ref, *rest):
-    scratch = rest[-6:]
-    f_wide, g_wide, row_high, row_sum, col_high, col_sum = scratch
-    f, g, outs = start_potentials(
-        x_ref, y_ref, rest[:-6], first, n_row, n_col, scale, blocks, f_wide, g_wide
-    )
-    f_out, g_out, row_out, col_out = outs
+def sweep(pairs_ref, kept, x_ref, y_ref, f, g, shift, scale, blocks, outs, scratch):
+    row_out, col_out = outs
+    f_wide, g_wide, row_high, row_sum, col_high, col_sum, lanes, row_acc, col_acc = scratch
+    spread_lanes(g + shift, blocks, lanes)
+    clear(row_acc, col_acc)
+
+    def visit(s, t):
+        halves = exponentials(cross(x_ref[s], y_ref[t]), scale, f_wide[s], lanes[t])
+        add_sums(halves, row_acc, col_acc, s, t)
+
+    over_pairs(pairs_ref, kept, visit)
+    _, row, col, good = totals(row_acc, col_acc, blocks)
+    row_out[...] = jnp.log2(row) - (f + shift)
+    col_out[...] = jnp.log2(col) - (g + shift)
+
+    @pl.when(jnp.logical_not(good))
+    def _():
+        down_rows(g, blocks, g_wide)
+        pass_sums(pairs_ref, kept, x_ref, y_ref, scale, *scratch[:6])
+        row_out[...] = settle(row_high, row_sum, blocks)
+        col_out[...] = settle(col_high, col_sum, blocks)
+
+
+def first_kernel(scale, blocks, pairs_ref, count_ref, x_hbm, y_hbm, *rest):
+    f_out, g_out, row_out, col_out = rest[:4]
+    scratch, (x_ref, y_ref, arrived) = rest[4:-3], rest[-3:]
+    f_wide, g_wide = scratch[:2]
+    copies = [
+        pltpu.make_async_copy(far.at[b], near.at[b], arrived.at[k, b])
+        for b in range(blocks)
+        for k, (far, near) in enumerate(((x_hbm, x_ref), (y_hbm, y_ref)))
+    ]
+    for copy in copies:
+        copy.start()
+    f_columns, g_columns = [], []
+    for b in range(blocks):
+        copies[2 * b].wait()
+        f_columns.append(norm(x_ref[b], scale))
+        f_wide[b] = jnp.broadcast_to(f_columns[b], (BLK, 128))
+        copies[2 * b + 1].wait()
+        g_columns.append(norm(y_ref[b], scale))
+    f, g = across(f_columns), across(g_columns)
     f_out[...] = f
     g_out[...] = g
-    pass_sums(pairs_ref, count_ref[0], x_ref, y_ref, scale, *scratch)
-    row_out[...] = settle(row_high, row_sum, blocks)
-    col_out[...] = settle(col_high, col_sum, blocks)
+    shift = -(jnp.sum(f) + jnp.sum(g)) / (blocks * BLK)
+    sweep(pairs_ref, count_ref[0], x_ref, y_ref, f, g, shift, scale, blocks, (row_out, col_out), scratch)
+
+
+def second_kernel(n_row, scale, blocks, pairs_ref, count_ref, x_ref, y_ref, f_old, g_old, *rest):
+    parts, rest = rest[: n_row + 1], rest[n_row + 1 :]
+    f_out, g_out, row_out, col_out = rest[:4]
+    scratch = rest[4:]
+    f = new_potential(f_old, parts[:n_row])
+    g = new_potential(g_old, parts[n_row:])
+    f_out[...] = f
+    g_out[...] = g
+    down_rows(f, blocks, scratch[0])
+    sweep(pairs_ref, count_ref[0], x_ref, y_ref, f, g, 0.0, scale, blocks, (row_out, col_out), scratch)
 
 
 def split_two(w):
@@ -176,47 +238,73 @@
         lanes_ref[b] = jnp.broadcast_to(values[b : b + 1], (8, BLK))
 
 
-def backward_kernel(n_row, n_col, scale, blocks, core_ref, pairs_ref, count_ref, x_ref, y_ref, *rest):
-    scratch = rest[-6:]
-    f_wide, g_wide, row_high, row_sum, col_high, col_sum = scratch
-    lanes, backward = rest[-8:-6]
-    f, g, outs = start_potentials(
-        x_ref, y_ref, rest[:-8], False, n_row, n_col, scale, blocks, f_wide, g_wide
-    )
-    g_out, row_out, keep_out, send_out = outs
+def maps_kernel(n_row, scale, blocks, place_ref, pairs_ref, count_ref, x_ref, y_ref, f_old, g_old, *rest):
+    parts, rest = rest[: n_row + 1], rest[n_row + 1 :]
+    keep_out, send_out, own, up, down, up_next, down_next = rest[:7]
+    scratch = rest[7:16]
+    f_wide, g_wide, row_high, row_sum, col_high, col_sum, lanes, row_acc, col_acc = scratch
+    x_turned, forward, backward, turned, logs, lines_ref = rest[16:]
     kept = count_ref[0]
-    pass_sums(pairs_ref, kept, x_ref, y_ref, scale, *scratch)
-    g_out[...] = g
-    row_out[...] = settle(row_high, row_sum, blocks)
-    col = settle(col_high, col_sum, blocks)
-    spread_lanes(f, blocks, lanes)
-    down_rows(col, blocks, g_wide)
-    images(pairs_ref, kept, y_ref, x_ref, scale, lanes, g_wide, backward, True)
-    half = keep_out.shape[0]
-    rows = blocks * BLK // (2 * half)
-    lines = receivers_lines(col, 2 * half, blocks)
-    core = core_ref[0]
-    for q in range(half):
-        for ref, side in ((keep_out, core), (send_out, 1 - core)):
-            first = pl.multiple_of((2 * q + side) * rows, 16)
-            ref[q, :rows, :] = backward[pl.ds(first, rows), :]
-            ref[q, rows : rows + 1, :] = jnp.where(side == 0, lines[2 * q], lines[2 * q + 1])
-
-
-def forward_kernel(
-    scale, blocks, place_ref, pairs_ref, count_ref, x_ref, y_ref, g_ref, row_ref, *rest
-):
-    own, up, down, up_next, down_next = rest[:-4]
-    lanes, wide, forward, lines_ref = rest[-4:]
-    row = row_ref[...]
-    spread_lanes(g_ref[...], blocks, lanes)
-    down_rows(row, blocks, wide)
-    images(pairs_ref, count_ref[0], x_ref, y_ref, scale, lanes, wide, forward, False)
+    f = new_potential(f_old, parts[:n_row])
+    g = new_potential(g_old, parts[n_row:])
+    down_rows(f, blocks, f_wide)
+    spread_lanes(g, blocks, lanes)
+    clear(row_acc, col_acc, forward, turned)
+    diagonal = lax.broadcasted_iota(jnp.int32, (BLK, BLK), 0) == lax.broadcasted_iota(jnp.int32, (BLK, BLK), 1)
+    unit = jnp.where(diagonal, 1.0, 0.0).astype(jnp.bfloat16)
+    for b in range(blocks):
+        x_turned[b] = cross(unit, x_ref[b]).astype(jnp.bfloat16)
+
+    def visit(s, t):
+        xs, yt, xt = x_ref[s], y_ref[t], x_turned[s]
+        halves = exponentials(cross(xs, yt), scale, f_wide[s], lanes[t])
+        add_sums(halves, row_acc, col_acc, s, t)
+        e = jnp.concatenate([half.reshape(BLK, 128) for half in halves], axis=1)
+        high, low = split_two(e)
+        rows = pl.ds(pl.multiple_of(s * BLK, BLK), BLK)
+        forward[rows, :] += jnp.dot(
+            jnp.concatenate([high, low], axis=1),
+            jnp.concatenate([yt, yt], axis=0),
+            preferred_element_type=jnp.float32,
+        )
+        turned[t] += jnp.dot(
+            jnp.concatenate([xt, xt], axis=1),
+            jnp.concatenate([high, low], axis=0),
+            preferred_element_type=jnp.float32,
+        )
+
+    over_pairs(pairs_ref, kept, visit)
+    columns, row, col, good = totals(row_acc, col_acc, blocks)
+
+    @pl.when(good)
+    def _():
+        logs[0] = jnp.log2(row) - f
+        logs[1] = jnp.log2(col) - g
+        inverse = 1.0 / col
+        for b in range(blocks):
+            rows = slice(b * BLK, b * BLK + BLK)
+            forward[rows, :] = forward[rows, :] * (1.0 / columns[b])
+            backward[rows, :] = jnp.transpose(turned[b] * inverse[b : b + 1])
+
+    @pl.when(jnp.logical_not(good))
+    def _():
+        down_rows(g, blocks, g_wide)
+        pass_sums(pairs_ref, kept, x_ref, y_ref, scale, *scratch[:6])
+        row_log = settle(row_high, row_sum, blocks)
+        col_log = settle(col_high, col_sum, blocks)
+        logs[0] = row_log
+        logs[1] = col_log
+        down_rows(row_log, blocks, f_wide)
+        images(pairs_ref, kept, x_ref, y_ref, scale, lanes, f_wide, forward, False)
+        spread_lanes(f, blocks, lanes)
+        down_rows(col_log, blocks, g_wide)
+        images(pairs_ref, kept, y_ref, x_ref, scale, lanes, g_wide, backward, True)
+
     n = lines_ref.shape[0]
     rows = blocks * BLK // n
-    for b, line in enumerate(receivers_lines(row, n, blocks)):
+    for b, line in enumerate(receivers_lines(logs[0], n, blocks)):
         lines_ref[b] = line
-    me = place_ref[0]
+    me = place_ref[1]
 
     def put(out, r, high):
         to = ((me + r) % RING) + RING * high
@@ -231,6 +319,16 @@
     put(own.at[1], 0, 1)
     put(up_next, 1, 0)
     put(down_next, 3, 1)
+
+    half = keep_out.shape[0]
+    small = blocks * BLK // (2 * half)
+    lines = receivers_lines(logs[1], 2 * half, blocks)
+    core = place_ref[0]
+    for q in range(half):
+        for ref, side in ((keep_out, core), (send_out, 1 - core)):
+            first = pl.multiple_of((2 * q + side) * small, 16)
+            ref[q, :small, :] = backward[pl.ds(first, small), :]
+            ref[q, small : small + 1, :] = jnp.where(side == 0, lines[2 * q], lines[2 * q + 1])
 
 
 def pair_kernel(rows, a_ref, b_ref, out_ref):
@@ -307,9 +405,9 @@
 
 
 def sums_scratch(blocks):
-    return [pltpu.VMEM((blocks, BLK, 128), jnp.float32)] * 2 + [
-        pltpu.VMEM((blocks, 8, BLK), jnp.float32)
-    ] * 4
+    wide = pltpu.VMEM((blocks, BLK, 128), jnp.float32)
+    deep = pltpu.VMEM((blocks, 8, BLK), jnp.float32)
+    return [wide] * 2 + [deep] * 5 + [wide, deep]
 
 
 def per_device(n_src, n_tgt, sources, targets, pairs, counts):
@@ -320,18 +418,10 @@
     y = targets.reshape(blocks, BLK, width)
     pair_list = jnp.transpose(pairs[0, 0])
     kept = counts.reshape(-1)
-    head = [pl.BlockSpec(memory_space=pltpu.SMEM)] * 2 + in_vmem(2)
-    params = pltpu.CompilerParams(vmem_limit_bytes=VMEM_BYTES)
-
-    def sweep(first, extra, n_row, n_col):
-        return pl.pallas_call(
-            functools.partial(sweep_kernel, first, n_row, n_col, scale, blocks),
-            out_shape=[shape(8, BLK)] * 4,
-            in_specs=head + in_vmem(len(extra)),
-            out_specs=in_vmem(4),
-            scratch_shapes=sums_scratch(blocks),
-            compiler_params=params,
-        )(pair_list, kept, x, y, *extra)
+    smem = pl.BlockSpec(memory_space=pltpu.SMEM)
+    hbm = pl.BlockSpec(memory_space=pltpu.HBM)
+    large = pltpu.CompilerParams(vmem_limit_bytes=24 * 1024 * 1024)
+    little = pltpu.CompilerParams(vmem_limit_bytes=8 * 1024 * 1024)
 
     def swap(value, axis, size, bit):
         return lax.ppermute(value, axis, [(k, k ^ bit) for k in range(size)])
@@ -341,69 +431,74 @@
 
     def exchange(row, col):
         col = log_sum([col, swap(col, "src", n_src, 1)])
-        row = log_sum([row, swap(row, "tgt", n_tgt, 1)])
+        row = log_sum([row, swap(row, "tgt", n_tgt, RING)])
         col = log_sum([col, swap(col, "src", n_src, 2)])
         row = log_sum([row, swap(row, "tgt", n_tgt, 2)])
         copies = jnp.broadcast_to(col[None], (n_z, *col.shape))
         cols = lax.all_to_all(copies, "src", 0, 0, axis_index_groups=along_z, tiled=True)
-        return [row, swap(row, "tgt", n_tgt, 4)], [cols]
-
-    f, g, row, col = sweep(True, [], 0, 0)
-    rows, cols = exchange(row, col)
-    f, g, row, col = sweep(False, [f, g, *rows, *cols], 2, 1)
-    rows, cols = exchange(row, col)
+        return [row, swap(row, "tgt", n_tgt, 1), cols]
+
+    latents = pltpu.VMEM((blocks, BLK, width), jnp.bfloat16)
+    f, g, row, col = pl.pallas_call(
+        functools.partial(first_kernel, scale, blocks),
+        out_shape=[shape(8, BLK)] * 4,
+        in_specs=[smem] * 2 + [hbm] * 2,
+        out_specs=in_vmem(4),
+        scratch_shapes=sums_scratch(blocks)
+        + [latents] * 2
+        + [pltpu.SemaphoreType.DMA((2, blocks))],
+        compiler_params=pltpu.CompilerParams(vmem_limit_bytes=60 * 1024 * 1024),
+    )(pair_list, kept, x, y)
+    parts = exchange(row, col)
+    f, g, row, col = pl.pallas_call(
+        functools.partial(second_kernel, 2, scale, blocks),
+        out_shape=[shape(8, BLK)] * 4,
+        in_specs=[smem] * 2 + in_vmem(7),
+        out_specs=in_vmem(4),
+        scratch_shapes=sums_scratch(blocks),
+        compiler_params=large,
+    )(pair_list, kept, x, y, f, g, *parts)
+    parts = exchange(row, col)
 
     f_rows, b_rows = blocks * BLK // n_tgt, blocks * BLK // n_src
     half = n_src // 2
-    scalar = pl.BlockSpec(memory_space=pltpu.SMEM)
-    s_at = lax.axis_index("src").astype(jnp.int32).reshape(1)
-    t_at = lax.axis_index("tgt").astype(jnp.int32).reshape(1)
+    s_at = lax.axis_index("src").astype(jnp.int32)
+    t_at = lax.axis_index("tgt").astype(jnp.int32)
 
     def call(kernel, operands, outs, places=()):
         return pl.pallas_call(
             kernel,
             out_shape=outs,
-            in_specs=[scalar] * len(places) + in_vmem(len(operands)),
+            in_specs=[smem] * len(places) + in_vmem(len(operands)),
             out_specs=in_vmem(len(outs)),
-            compiler_params=params,
+            compiler_params=little,
         )(*places, *operands)
 
-    g, row, keep, send = pl.pallas_call(
-        functools.partial(backward_kernel, 2, 1, scale, blocks),
-        out_shape=[shape(8, BLK)] * 2 + [shape(half, b_rows + 8, width)] * 2,
-        in_specs=[scalar] + head + in_vmem(5),
-        out_specs=in_vmem(4),
-        scratch_shapes=[
-            pltpu.VMEM((blocks, 8, BLK), jnp.float32),
-            pltpu.VMEM((blocks * BLK, width), jnp.float32),
-        ]
-        + sums_scratch(blocks),
-        compiler_params=params,
-    )(s_at % 2, pair_list, kept, x, y, f, g, *rows, *cols)
-    came = swap(send, "src", n_src, 1)
     block = shape(f_rows + 8, width)
     two = shape(2, f_rows + 8, width)
-    forward = pl.pallas_call(
-        functools.partial(forward_kernel, scale, blocks),
-        out_shape=[two, two, two, block, block],
-        in_specs=[scalar] + head + in_vmem(2),
-        out_specs=in_vmem(5),
-        scratch_shapes=[
-            pltpu.VMEM((blocks, 8, BLK), jnp.float32),
-            pltpu.VMEM((blocks, BLK, 128), jnp.float32),
+    keep, send, own, up, down, up_next, down_next = pl.pallas_call(
+        functools.partial(maps_kernel, 2, scale, blocks),
+        out_shape=[shape(half, b_rows + 8, width)] * 2 + [two, two, two, block, block],
+        in_specs=[smem] * 3 + in_vmem(7),
+        out_specs=in_vmem(7),
+        scratch_shapes=sums_scratch(blocks)
+        + [
+            pltpu.VMEM((blocks, width, BLK), jnp.bfloat16),
             pltpu.VMEM((blocks * BLK, width), jnp.float32),
+            pltpu.VMEM((blocks * BLK, width), jnp.float32),
+            pltpu.VMEM((blocks, width, BLK), jnp.float32),
+            pltpu.VMEM((2, 8, BLK), jnp.float32),
             pltpu.VMEM((n_tgt, 1, BLK), jnp.float32),
         ],
-        compiler_params=params,
-        cost_estimate=pl.CostEstimate(flops=6 * 10**9, bytes_accessed=4 * 10**6, transcendentals=0),
-    )(t_at % RING, pair_list, kept, x, y, g, row)
-    came, forward = lax.optimization_barrier((came, forward))
-
-    (backward,) = call(
+        compiler_params=large,
+    )(jnp.stack([s_at % 2, t_at % RING]), pair_list, kept, x, y, f, g, *parts)
+    came = swap(send, "src", n_src, 1)
+
+    (paired,) = call(
         functools.partial(pair_kernel, b_rows), [keep, came], [shape(half, b_rows + 8, width)]
     )
     backward = lax.all_to_all(
-        backward.reshape(n_z, 2, b_rows + 8, width),
+        paired.reshape(n_z, 2, b_rows + 8, width),
         "src",
         0,
         0,
@@ -412,16 +507,16 @@
     )
     small = shape(b_rows + 8, width)
     keep, send = call(
-        functools.partial(z_kernel, b_rows), [backward], [small, small], [s_at // 2 % 2]
+        functools.partial(z_kernel, b_rows), [backward], [small, small], [(s_at // 2 % 2).reshape(1)]
     )
     came = swap(send, "src", n_src, 2)
     (backward,) = call(functools.partial(last_kernel, b_rows), [keep, came], [shape(b_rows, width)])
 
     ups = [(k, k // RING * RING + (k + 1) % RING) for k in range(n_tgt)]
     downs = [(b, a) for a, b in ups]
-    own, up, down, up_next, down_next = forward
     up_came = lax.ppermute(up, "tgt", ups)
     down_came = lax.ppermute(down, "tgt", downs)
+    up_came, down_came, _ = lax.optimization_barrier((up_came, down_came, paired))
     up, down = call(
         functools.partial(relay_kernel, f_rows),
         [up_next, up_came, down_next, down_came],
@@ -433,7 +528,7 @@
         functools.partial(x_kernel, f_rows),
         [own, up_came, down_came, up_second, down_second],
         [block, block],
-        [t_at // RING],
+        [(t_at // RING).reshape(1)],
     )
     came = swap(send, "tgt", n_tgt, RING)
     (forward,) = call(functools.partial(last_kernel, f_rows), [keep, came], [shape(f_rows, width)])

time: 122 us -> 143 us (1.17); the launches traced: 123 us -> 141 us
  Pallas kernels: 28 us -> 41.4 us
  waiting for transfers between devices: 31.5 us -> 37.9 us
  local copies, waits for them, and re-layouts: 6.54 us -> 1.97 us
  starting transfers between devices: 55.1 us -> 57.3 us
    pallas_call x10 -> x9, Pallas kernels: 28 us -> 41.4 us  [the longest x1 19.3 us: per_device(): pl.pallas_call(functools.partial(maps_kernel, 2, scale, blocks), out_shap...]
    unnamed x30 -> x12, local copies, waits for them, and re-layouts: 5.26 us -> 0.68 us
    all_to_all x2, waiting for transfers between devices: 6.21 us -> 9.11 us  [exchange(): lax.all_to_all(copies, 'src', 0, 0, axis_index_groups=along_z, tiled=True)]
    ppermute x1, waiting for transfers between devices: 6.98 us -> 9.2 us  [per_device(): up_came = lax.ppermute(up, 'tgt', ups)]
    all_to_all x1, starting transfers between devices: 12 us -> 13.9 us  [per_device(): lax.all_to_all(paired.reshape(n_z, 2, b_rows + 8, width), 'src', 0, 0, ax...]
    ppermute x13, starting transfers between devices: 23 us -> 24.8 us  [swap(): return lax.ppermute(value, axis, [(k, k ^ bit) for k in range(size)])]
    ppermute x1, starting transfers between devices: 0.08 us -> 1.82 us  [per_device(): up_second = lax.ppermute(up, 'tgt', ups)]
    ppermute x1, starting transfers between devices: 3.22 us -> 1.49 us  [per_device(): down_second = lax.ppermute(down, 'tgt', downs)]
  transfers between devices with their start and end apart: 20 -> 20, of which waited for: 10 -> 12; matrix products, arithmetic and copies ran while one was open for 1% -> 2% of each run, Pallas kernels for 6% -> 1%
where the time goes in v5:
time: 143 us; the launch traced here: 141 us
  starting transfers between devices  57.3 us (40%)
  Pallas kernels  41.4 us (29%)
  waiting for transfers between devices  37.9 us (27%)
  local copies, waits for them, and re-layouts  1.97 us (1%)
  between operations  1.49 us (1%)
    ppermute x13, starting transfers between devices, swap(): return lax.ppermute(value, axis, [(k, k ^ bit) for k in range(size)])  24.8 us
    pallas_call x1, Pallas kernels, per_device(): pl.pallas_call(functools.partial(maps_kernel, 2, scale, blocks), out_shap...  19.3 us
    all_to_all x1, starting transfers between devices, per_device(): lax.all_to_all(paired.reshape(n_z, 2, b_rows + 8, width), 'src', 0, 0, ax...  13.9 us
    ppermute x13, waiting for transfers between devices, swap(): return lax.ppermute(value, axis, [(k, k ^ bit) for k in range(size)])  12.3 us
    all_to_all x2, starting transfers between devices, exchange(): lax.all_to_all(copies, 'src', 0, 0, axis_index_groups=along_z, tiled=True)  12 us
    pallas_call x1, Pallas kernels, per_device(): pl.pallas_call(functools.partial(first_kernel, scale, blocks), out_shape=...  10.4 us
    ppermute x1, waiting for transfers between devices, per_device(): up_came = lax.ppermute(up, 'tgt', ups)  9.2 us
    all_to_all x2, waiting for transfers between devices, exchange(): lax.all_to_all(copies, 'src', 0, 0, axis_index_groups=along_z, tiled=True)  9.11 us
  transfers between devices with their start and end apart: 20, of which 12 were waited for; matrix products, arithmetic and copies ran while one was open for 2% of the time, Pallas kernels for 1%

profile of v5, /device:TPU:8, one launch (start us, length us, event | category | flops | bytes accessed | tf_op | source)
XLA Modules:
  0.0 140.9 jit_solution(1995327176317433920)
XLA Ops:
  1.3 10.4 %shard_map.59 = (f32[8,256]{1,0:T(8,128)}, f32[8,256]{1,0:T(8,128)}, f32[8,256]{1,0:T(8,128)}, f32[8,256]{1,0:T(8,128)}) custom-call(s32[2,24]{1,0:T(2,128)} %bitcast.20, s32[1]{0:T(128)} %bitcast.11.count_ref, bf16[6,256,256]{2,1,0:T(8,128)(2,1)} %bitcast.14, bf16[6,256,256]{2,1,0:T(8,128)(2,1)} %bitcast.17), custom_call_target="tpu_custom_call" | custom-call | tf_op jit(solution)/shard_map/pallas_call | solution.py:442
  11.8 3.4 %collective-permute-start = (f32[8,256]{1,0:T(8,128)}, f32[8,256]{1,0:T(8,128)S(1)}, u32[]{:S(2)}, u32[]{:S(2)}) collective-permute-start(f32[8,256]{1,0:T(8,128)} %get-tuple-element.27), channel_id=1, source_target_pairs={{0,4},{1,5},{2,6},{3,7},{4,0},{5,1},{6,2},{7,3},{8,12},{9,13},{10,... | collective-permute-start | bytes 24584 | tf_op jit(solution)/shard_map/ppermute | solution.py:427
  15.2 0.7 multiply_add_fusion.5
  15.9 2.0 %collective-permute-start.4 = (f32[8,256]{1,0:T(8,128)S(1)}, f32[8,256]{1,0:T(8,128)S(1)}, u32[]{:S(2)}, u32[]{:S(2)}) collective-permute-start(f32[8,256]{1,0:T(8,128)S(1)} %multiply_add_fusion.5), channel_id=1, source_target_pairs={{0,16},{8,24},{16,0},{24,8},{32,48},{40,56},{48,32},{56,40},{64,80... | collective-permute-start | bytes 24584 | tf_op jit(solution)/shard_map/ppermute | solution.py:427
  18.0 6.4 %collective-permute-start.1 = (f32[8,256]{1,0:T(8,128)S(1)}, f32[8,256]{1,0:T(8,128)S(1)}, u32[]{:S(2)}, u32[]{:S(2)}) collective-permute-start(f32[8,256]{1,0:T(8,128)S(1)} %multiply_add_fusion.7), channel_id=1, source_target_pairs={{0,2},{1,3},{2,0},{3,1},{4,6},{5,7},{6,4},{7,5},{8,10},{9,11},{10,... | collective-permute-start | bytes 24584 | tf_op jit(solution)/shard_map/ppermute | solution.py:427
  25.0 8.7 %all-to-all-start = ((f32[8,8,256]{2,1,0:T(8,128)}), f32[8,8,256]{2,1,0:T(8,128)S(1)}, u32[]{:S(2)}, u32[]{:S(2)}) async-start(f32[8,8,256]{2,1,0:T(8,128)} %broadcast_in_dim.4), calls=%async_computation | async-start | bytes 131072 | tf_op jit(solution)/shard_map/all_to_all | solution.py:438
  33.9 3.6 %collective-permute-done.2.rest_1_ = f32[8,256]{1,0:T(8,128)S(1)} collective-permute-done((f32[8,256]{1,0:T(8,128)S(1)}, f32[8,256]{1,0:T(8,128)S(1)}, u32[]{:S(2)}, u32[]{:S(2)}) %collective-permute-start.2) | collective-permute-done | bytes 8224 | tf_op jit(solution)/shard_map/ppermute | solution.py:427
  37.5 4.6 %all-to-all-done.rest_2_ = f32[8,8,256]{2,1,0:T(8,128)S(1)} async-done(((f32[8,8,256]{2,1,0:T(8,128)}), f32[8,8,256]{2,1,0:T(8,128)S(1)}, u32[]{:S(2)}, u32[]{:S(2)}) %all-to-all-start) | async-done | bytes 65568 | tf_op jit(solution)/shard_map/all_to_all | solution.py:438
  42.1 0.7 copy-done.2
  42.8 7.4 %shard_map.60 = (f32[8,256]{1,0:T(8,128)S(1)}, f32[8,256]{1,0:T(8,128)S(1)}, f32[8,256]{1,0:T(8,128)S(1)}, f32[8,256]{1,0:T(8,128)S(1)}) custom-call(s32[2,24]{1,0:T(2,128)S(1)} %bitcast.21, s32[1]{0:T(128)} %bitcast.12.count_ref, bf16[6,256,256]{2,1,0:T(8,128)(2,1)S(1)} %bitcast.15, bf16[6,256,256]{2,1,0:T(8,128)(2,1)S(1)} %bitcast.18, ...), custom_call_target="tpu_custom_call" | custom-call | tf_op jit(solution)/shard_map/pallas_call | solution.py:453
  50.3 1.8 %collective-permute-start.5 = (f32[8,256]{1,0:T(8,128)S(1)}, f32[8,256]{1,0:T(8,128)S(1)}, u32[]{:S(2)}, u32[]{:S(2)}) collective-permute-start(f32[8,256]{1,0:T(8,128)S(1)} %get-tuple-element.31), channel_id=1, source_target_pairs={{0,4},{1,5},{2,6},{3,7},{4,0},{5,1},{6,2},{7,3},{8,12},{9,13},{10,... | collective-permute-start | bytes 24584 | tf_op jit(solution)/shard_map/ppermute | solution.py:427
  52.0 3.1 %collective-permute-start.9 = (f32[8,256]{1,0:T(8,128)S(1)}, f32[8,256]{1,0:T(8,128)S(1)}, u32[]{:S(2)}, u32[]{:S(2)}) collective-permute-start(f32[8,256]{1,0:T(8,128)S(1)} %multiply_add_fusion.1), channel_id=1, source_target_pairs={{0,16},{8,24},{16,0},{24,8},{32,48},{40,56},{48,32},{56,40},{64,80... | collective-permute-start | bytes 24584 | tf_op jit(solution)/shard_map/ppermute | solution.py:427
  55.5 4.3 %collective-permute-start.6 = (f32[8,256]{1,0:T(8,128)S(1)}, f32[8,256]{1,0:T(8,128)S(1)}, u32[]{:S(2)}, u32[]{:S(2)}) collective-permute-start(f32[8,256]{1,0:T(8,128)S(1)} %multiply_add_fusion.3), channel_id=1, source_target_pairs={{0,2},{1,3},{2,0},{3,1},{4,6},{5,7},{6,4},{7,5},{8,10},{9,11},{10,... | collective-permute-start | bytes 24584 | tf_op jit(solution)/shard_map/ppermute | solution.py:427
  60.5 3.4 %all-to-all-start.1 = ((f32[8,8,256]{2,1,0:T(8,128)}), f32[8,8,256]{2,1,0:T(8,128)S(1)}, u32[]{:S(2)}, u32[]{:S(2)}) async-start(f32[8,8,256]{2,1,0:T(8,128)} %broadcast_in_dim.5), calls=%async_computation.1 | async-start | bytes 131072 | tf_op jit(solution)/shard_map/all_to_all | solution.py:438
  63.9 1.0 collective-permute-start.7
  65.0 2.6 %collective-permute-done.7.rest_1_ = f32[8,256]{1,0:T(8,128)S(1)} collective-permute-done((f32[8,256]{1,0:T(8,128)S(1)}, f32[8,256]{1,0:T(8,128)S(1)}, u32[]{:S(2)}, u32[]{:S(2)}) %collective-permute-start.7) | collective-permute-done | bytes 8224 | tf_op jit(solution)/shard_map/ppermute | solution.py:427
  67.6 4.5 %all-to-all-done.1.rest_2_ = f32[8,8,256]{2,1,0:T(8,128)S(1)} async-done(((f32[8,8,256]{2,1,0:T(8,128)}), f32[8,8,256]{2,1,0:T(8,128)S(1)}, u32[]{:S(2)}, u32[]{:S(2)}) %all-to-all-start.1) | async-done | bytes 65568 | tf_op jit(solution)/shard_map/all_to_all | solution.py:438
  72.2 19.3 %shard_map.61 = (f32[16,56,256]{2,1,0:T(8,128)S(1)}, f32[16,56,256]{2,1,0:T(8,128)S(1)}, f32[2,200,256]{2,1,0:T(8,128)S(1)}, f32[2,200,256]{2,1,0:T(8,128)S(1)},...) custom-call(s32[2]{0:T(128)S(1)} %pad_add_fusion.place_ref, s32[2,24]{1,0:T(2,128)S(1)} %bitcast.22, ...), custom_call_target="tpu_custom_call" | custom-call | tf_op jit(solution)/shard_map/pallas_call | solution.py:479
  91.6 2.5 %collective-permute-done.12.b_ref = f32[16,56,256]{2,1,0:T(8,128)S(1)} collective-permute-done((f32[16,56,256]{2,1,0:T(8,128)S(1)}, f32[16,56,256]{2,1,0:T(8,128)S(1)}, u32[]{:S(2)}, u32[]{:S(2)}) %collective-permute-start.12) | collective-permute-done | bytes 917536 | tf_op jit(solution)/shard_map/ppermute | solution.py:427
  94.1 1.4 shard_map.62
  95.4 13.9 %all-to-all-start.2 = ((f32[8,2,56,256]{3,2,1,0:T(8,128)}), f32[8,2,56,256]{3,2,1,0:T(8,128)S(1)}, u32[]{:S(2)}, u32[]{:S(2)}) async-start(f32[8,2,56,256]{3,2,1,0:T(8,128)} %bitcast.10), calls=%async_computation.2 | async-start | bytes 1835008 | tf_op jit(solution)/shard_map/all_to_all | solution.py:500
  109.8 2.7 %collective-permute-start.11 = (f32[2,200,256]{2,1,0:T(8,128)S(1)}, f32[2,200,256]{2,1,0:T(8,128)S(1)}, u32[]{:S(2)}, u32[]{:S(2)}) collective-permute-start(f32[2,200,256]{2,1,0:T(8,128)S(1)} %get-tuple-element.35), channel_id=1, source_target_pairs={{1,0},{2,1},{3,2},{0,3},{5,4},{6,5},{7,6},{4,7},{9,8},{10,9},{11,1... | collective-permute-start | bytes 1228808 | tf_op jit(solution)/shard_map/ppermute | solution.py:518
  112.5 9.2 %collective-permute-done.10.up_came = f32[2,200,256]{2,1,0:T(8,128)S(1)} collective-permute-done((f32[2,200,256]{2,1,0:T(8,128)S(1)}, f32[2,200,256]{2,1,0:T(8,128)S(1)}, u32[]{:S(2)}, u32[]{:S(2)}) %collective-permute-start.10) | collective-permute-done | bytes 409632 | tf_op jit(solution)/shard_map/ppermute | solution.py:517
  122.4 1.8 %collective-permute-start.13 = (f32[200,256]{1,0:T(8,128)S(1)}, f32[200,256]{1,0:T(8,128)S(1)}, u32[]{:S(2)}, u32[]{:S(2)}) collective-permute-start(f32[200,256]{1,0:T(8,128)S(1)} %get-tuple-element.42), channel_id=1, source_target_pairs={{0,1},{1,2},{2,3},{3,0},{4,5},{5,6},{6,7},{7,4},{8,9},{9,10},{10,1... | collective-permute-start | bytes 614408 | tf_op jit(solution)/shard_map/ppermute | solution.py:525
  124.2 1.5 %collective-permute-start.14 = (f32[200,256]{1,0:T(8,128)S(1)}, f32[200,256]{1,0:T(8,128)S(1)}, u32[]{:S(2)}, u32[]{:S(2)}) collective-permute-start(f32[200,256]{1,0:T(8,128)S(1)} %get-tuple-element.43), channel_id=1, source_target_pairs={{1,0},{2,1},{3,2},{0,3},{5,4},{6,5},{7,6},{4,7},{9,8},{10,9},{11,1... | collective-permute-start | bytes 614408 | tf_op jit(solution)/shard_map/ppermute | solution.py:526
  125.7 4.3 %collective-permute-done.13.up_second = f32[200,256]{1,0:T(8,128)S(1)} collective-permute-done((f32[200,256]{1,0:T(8,128)S(1)}, f32[200,256]{1,0:T(8,128)S(1)}, u32[]{:S(2)}, u32[]{:S(2)}) %collective-permute-start.13) | collective-permute-done | bytes 204832 | tf_op jit(solution)/shard_map/ppermute | solution.py:525
  130.5 2.3 %collective-permute-start.15 = (f32[200,256]{1,0:T(8,128)S(1)}, f32[200,256]{1,0:T(8,128)S(1)}, u32[]{:S(2)}, u32[]{:S(2)}) collective-permute-start(f32[200,256]{1,0:T(8,128)S(1)} %get-tuple-element.45), channel_id=1, source_target_pairs={{0,4},{1,5},{2,6},{3,7},{4,0},{5,1},{6,2},{7,3},{8,12},{9,13},{10,... | collective-permute-start | bytes 614408 | tf_op jit(solution)/shard_map/ppermute | solution.py:427
  132.8 2.7 %all-to-all-done.2.parts_ref = f32[8,2,56,256]{3,2,1,0:T(8,128)S(1)} async-done(((f32[8,2,56,256]{3,2,1,0:T(8,128)}), f32[8,2,56,256]{3,2,1,0:T(8,128)S(1)}, u32[]{:S(2)}, u32[]{:S(2)}) %all-to-all-start.2) | async-done | bytes 917536 | tf_op jit(solution)/shard_map/all_to_all | solution.py:500
  136.0 1.8 %collective-permute-done.15.b_ref = f32[200,256]{1,0:T(8,128)S(1)} collective-permute-done((f32[200,256]{1,0:T(8,128)S(1)}, f32[200,256]{1,0:T(8,128)S(1)}, u32[]{:S(2)}, u32[]{:S(2)}) %collective-permute-start.15) | collective-permute-done | bytes 204832 | tf_op jit(solution)/shard_map/ppermute | solution.py:427
  137.8 1.0 shard_map.65
  138.8 1.3 collective-permute-done.16.b_ref
  140.1 0.8 shard_map.67
  (40 shorter events, 4.4 us)
Async XLA Ops:
  1.3 40.8 %copy-start = (bf16[1536,256]{1,0:T(8,128)(2,1)S(1)}, bf16[1536,256]{1,0:T(8,128)(2,1)}, u32[]{:S(2)}) copy-start(bf16[1536,256]{1,0:T(8,128)(2,1)} %param.4) | copy-start | bytes 2359300
  1.3 40.8 %copy-start.1 = (bf16[1536,256]{1,0:T(8,128)(2,1)S(1)}, bf16[1536,256]{1,0:T(8,128)(2,1)}, u32[]{:S(2)}) copy-start(bf16[1536,256]{1,0:T(8,128)(2,1)} %param.5) | copy-start | bytes 2359300
  11.7 3.5 %collective-permute-start.3 = (f32[8,256]{1,0:T(8,128)}, f32[8,256]{1,0:T(8,128)S(1)}, u32[]{:S(2)}, u32[]{:S(2)}) collective-permute-start(f32[8,256]{1,0:T(8,128)} %get-tuple-element.28), channel_id=1, source_target_pairs={{0,8},{8,0},{16,24},{24,16},{32,40},{40,32},{48,56},{56,48},{64,72... | collective-permute-start | bytes 24584 | tf_op jit(solution)/shard_map/ppermute | solution.py:427
  11.8 6.1 %copy-start.5 = (f32[8,256]{1,0:T(8,128)S(1)}, f32[8,256]{1,0:T(8,128)}, u32[]{:S(2)}) copy-start(f32[8,256]{1,0:T(8,128)} %get-tuple-element.27) | copy-start | bytes 24580
  11.8 6.1 %collective-permute-start = (f32[8,256]{1,0:T(8,128)}, f32[8,256]{1,0:T(8,128)S(1)}, u32[]{:S(2)}, u32[]{:S(2)}) collective-permute-start(f32[8,256]{1,0:T(8,128)} %get-tuple-element.27), channel_id=1, source_target_pairs={{0,4},{1,5},{2,6},{3,7},{4,0},{5,1},{6,2},{7,3},{8,12},{9,13},{10,... | collective-permute-start | bytes 24584 | tf_op jit(solution)/shard_map/ppermute | solution.py:427
  15.9 8.5 %collective-permute-start.4 = (f32[8,256]{1,0:T(8,128)S(1)}, f32[8,256]{1,0:T(8,128)S(1)}, u32[]{:S(2)}, u32[]{:S(2)}) collective-permute-start(f32[8,256]{1,0:T(8,128)S(1)} %multiply_add_fusion.5), channel_id=1, source_target_pairs={{0,16},{8,24},{16,0},{24,8},{32,48},{40,56},{48,32},{56,40},{64,80... | collective-permute-start | bytes 24584 | tf_op jit(solution)/shard_map/ppermute | solution.py:427
  18.0 15.8 %collective-permute-start.1 = (f32[8,256]{1,0:T(8,128)S(1)}, f32[8,256]{1,0:T(8,128)S(1)}, u32[]{:S(2)}, u32[]{:S(2)}) collective-permute-start(f32[8,256]{1,0:T(8,128)S(1)} %multiply_add_fusion.7), channel_id=1, source_target_pairs={{0,2},{1,3},{2,0},{3,1},{4,6},{5,7},{6,4},{7,5},{8,10},{9,11},{10,... | collective-permute-start | bytes 24584 | tf_op jit(solution)/shard_map/ppermute | solution.py:427
  25.0 17.1 %all-to-all-start = ((f32[8,8,256]{2,1,0:T(8,128)}), f32[8,8,256]{2,1,0:T(8,128)S(1)}, u32[]{:S(2)}, u32[]{:S(2)}) async-start(f32[8,8,256]{2,1,0:T(8,128)} %broadcast_in_dim.4), calls=%async_computation | async-start | bytes 131072 | tf_op jit(solution)/shard_map/all_to_all | solution.py:438
  33.7 8.4 %copy-start.3 = (f32[8,256]{1,0:T(8,128)S(1)}, f32[8,256]{1,0:T(8,128)}, u32[]{:S(2)}) copy-start(f32[8,256]{1,0:T(8,128)} %get-tuple-element.25.f_old) | copy-start | bytes 24580
  33.7 8.4 %copy-start.4 = (f32[8,256]{1,0:T(8,128)S(1)}, f32[8,256]{1,0:T(8,128)}, u32[]{:S(2)}) copy-start(f32[8,256]{1,0:T(8,128)} %get-tuple-element.26.g_old) | copy-start | bytes 24580
  33.8 3.7 %collective-permute-start.2 = (f32[8,256]{1,0:T(8,128)S(1)}, f32[8,256]{1,0:T(8,128)S(1)}, u32[]{:S(2)}, u32[]{:S(2)}) collective-permute-start(f32[8,256]{1,0:T(8,128)S(1)} %multiply_add_fusion.6.rest_0_), channel_id=1, source_target_pairs={{0,1},{1,0},{2,3},{3,2},{4,5},{5,4},{6,7},{7,6},{8,9},{9,8},{10,11... | collective-permute-start | bytes 24584 | tf_op jit(solution)/shard_map/ppermute | solution.py:427
  42.1 0.7 copy-start.2
  50.1 1.9 %collective-permute-start.8 = (f32[8,256]{1,0:T(8,128)S(1)}, f32[8,256]{1,0:T(8,128)S(1)}, u32[]{:S(2)}, u32[]{:S(2)}) collective-permute-start(f32[8,256]{1,0:T(8,128)S(1)} %get-tuple-element.32), channel_id=1, source_target_pairs={{0,8},{8,0},{16,24},{24,16},{32,40},{40,32},{48,56},{56,48},{64,72... | collective-permute-start | bytes 24584 | tf_op jit(solution)/shard_map/ppermute | solution.py:427
  50.3 5.3 %collective-permute-start.5 = (f32[8,256]{1,0:T(8,128)S(1)}, f32[8,256]{1,0:T(8,128)S(1)}, u32[]{:S(2)}, u32[]{:S(2)}) collective-permute-start(f32[8,256]{1,0:T(8,128)S(1)} %get-tuple-element.31), channel_id=1, source_target_pairs={{0,4},{1,5},{2,6},{3,7},{4,0},{5,1},{6,2},{7,3},{8,12},{9,13},{10,... | collective-permute-start | bytes 24584 | tf_op jit(solution)/shard_map/ppermute | solution.py:427
  52.0 7.8 %collective-permute-start.9 = (f32[8,256]{1,0:T(8,128)S(1)}, f32[8,256]{1,0:T(8,128)S(1)}, u32[]{:S(2)}, u32[]{:S(2)}) collective-permute-start(f32[8,256]{1,0:T(8,128)S(1)} %multiply_add_fusion.1), channel_id=1, source_target_pairs={{0,16},{8,24},{16,0},{24,8},{32,48},{40,56},{48,32},{56,40},{64,80... | collective-permute-start | bytes 24584 | tf_op jit(solution)/shard_map/ppermute | solution.py:427
  55.5 8.3 %collective-permute-start.6 = (f32[8,256]{1,0:T(8,128)S(1)}, f32[8,256]{1,0:T(8,128)S(1)}, u32[]{:S(2)}, u32[]{:S(2)}) collective-permute-start(f32[8,256]{1,0:T(8,128)S(1)} %multiply_add_fusion.3), channel_id=1, source_target_pairs={{0,2},{1,3},{2,0},{3,1},{4,6},{5,7},{6,4},{7,5},{8,10},{9,11},{10,... | collective-permute-start | bytes 24584 | tf_op jit(solution)/shard_map/ppermute | solution.py:427
  60.5 11.7 %all-to-all-start.1 = ((f32[8,8,256]{2,1,0:T(8,128)}), f32[8,8,256]{2,1,0:T(8,128)S(1)}, u32[]{:S(2)}, u32[]{:S(2)}) async-start(f32[8,8,256]{2,1,0:T(8,128)} %broadcast_in_dim.5), calls=%async_computation.1 | async-start | bytes 131072 | tf_op jit(solution)/shard_map/all_to_all | solution.py:438
  63.9 3.7 %collective-permute-start.7 = (f32[8,256]{1,0:T(8,128)S(1)}, f32[8,256]{1,0:T(8,128)S(1)}, u32[]{:S(2)}, u32[]{:S(2)}) collective-permute-start(f32[8,256]{1,0:T(8,128)S(1)} %multiply_add_fusion.2.rest_0_), channel_id=1, source_target_pairs={{0,1},{1,0},{2,3},{3,2},{4,5},{5,4},{6,7},{7,6},{8,9},{9,8},{10,11... | collective-permute-start | bytes 24584 | tf_op jit(solution)/shard_map/ppermute | solution.py:427
  91.5 2.6 %collective-permute-start.12 = (f32[16,56,256]{2,1,0:T(8,128)S(1)}, f32[16,56,256]{2,1,0:T(8,128)S(1)}, u32[]{:S(2)}, u32[]{:S(2)}) collective-permute-start(f32[16,56,256]{2,1,0:T(8,128)S(1)} %get-tuple-element.37), channel_id=1, source_target_pairs={{0,8},{8,0},{16,24},{24,16},{32,40},{40,32},{48,56},{56,48},{64,72... | collective-permute-start | bytes 2752520 | tf_op jit(solution)/shard_map/ppermute | solution.py:427
  95.4 40.1 %all-to-all-start.2 = ((f32[8,2,56,256]{3,2,1,0:T(8,128)}), f32[8,2,56,256]{3,2,1,0:T(8,128)S(1)}, u32[]{:S(2)}, u32[]{:S(2)}) async-start(f32[8,2,56,256]{3,2,1,0:T(8,128)} %bitcast.10), calls=%async_computation.2 | async-start | bytes 1835008 | tf_op jit(solution)/shard_map/all_to_all | solution.py:500
  109.3 12.4 %collective-permute-start.10 = (f32[2,200,256]{2,1,0:T(8,128)S(1)}, f32[2,200,256]{2,1,0:T(8,128)S(1)}, u32[]{:S(2)}, u32[]{:S(2)}) collective-permute-start(f32[2,200,256]{2,1,0:T(8,128)S(1)} %get-tuple-element.34), channel_id=1, source_target_pairs={{0,1},{1,2},{2,3},{3,0},{4,5},{5,6},{6,7},{7,4},{8,9},{9,10},{10,1... | collective-permute-start | bytes 1228808 | tf_op jit(solution)/shard_map/ppermute | solution.py:517
  109.8 12.2 %collective-permute-start.11 = (f32[2,200,256]{2,1,0:T(8,128)S(1)}, f32[2,200,256]{2,1,0:T(8,128)S(1)}, u32[]{:S(2)}, u32[]{:S(2)}) collective-permute-start(f32[2,200,256]{2,1,0:T(8,128)S(1)} %get-tuple-element.35), channel_id=1, source_target_pairs={{1,0},{2,1},{3,2},{0,3},{5,4},{6,5},{7,6},{4,7},{9,8},{10,9},{11,1... | collective-permute-start | bytes 1228808 | tf_op jit(solution)/shard_map/ppermute | solution.py:518
  122.4 7.6 %collective-permute-start.13 = (f32[200,256]{1,0:T(8,128)S(1)}, f32[200,256]{1,0:T(8,128)S(1)}, u32[]{:S(2)}, u32[]{:S(2)}) collective-permute-start(f32[200,256]{1,0:T(8,128)S(1)} %get-tuple-element.42), channel_id=1, source_target_pairs={{0,1},{1,2},{2,3},{3,0},{4,5},{5,6},{6,7},{7,4},{8,9},{9,10},{10,1... | collective-permute-start | bytes 614408 | tf_op jit(solution)/shard_map/ppermute | solution.py:525
  124.2 5.8 %collective-permute-start.14 = (f32[200,256]{1,0:T(8,128)S(1)}, f32[200,256]{1,0:T(8,128)S(1)}, u32[]{:S(2)}, u32[]{:S(2)}) collective-permute-start(f32[200,256]{1,0:T(8,128)S(1)} %get-tuple-element.43), channel_id=1, source_target_pairs={{1,0},{2,1},{3,2},{0,3},{5,4},{6,5},{7,6},{4,7},{9,8},{10,9},{11,1... | collective-permute-start | bytes 614408 | tf_op jit(solution)/shard_map/ppermute | solution.py:526
  130.5 7.3 %collective-permute-start.15 = (f32[200,256]{1,0:T(8,128)S(1)}, f32[200,256]{1,0:T(8,128)S(1)}, u32[]{:S(2)}, u32[]{:S(2)}) collective-permute-start(f32[200,256]{1,0:T(8,128)S(1)} %get-tuple-element.45), channel_id=1, source_target_pairs={{0,4},{1,5},{2,6},{3,7},{4,0},{5,1},{6,2},{7,3},{8,12},{9,13},{10,... | collective-permute-start | bytes 614408 | tf_op jit(solution)/shard_map/ppermute | solution.py:427
  135.8 4.3 %collective-permute-start.16 = (f32[56,256]{1,0:T(8,128)S(1)}, f32[56,256]{1,0:T(8,128)S(1)}, u32[]{:S(2)}, u32[]{:S(2)}) collective-permute-start(f32[56,256]{1,0:T(8,128)S(1)} %get-tuple-element.47), channel_id=1, source_target_pairs={{0,16},{8,24},{16,0},{24,8},{32,48},{40,56},{48,32},{56,40},{64,80... | collective-permute-start | bytes 172040 | tf_op jit(solution)/shard_map/ppermute | solution.py:427

commit v6 on v5

--- a/solution.py
+++ b/solution.py
@@ -85,11 +85,11 @@
     return 0.5 * (old_ref[...] - log_sum(parts))
 
 
-def exponentials(scores, scale, wide, lanes):
+def exponentials(scores_ref, wide, lanes):
     halves = []
     for h in range(2):
         at = slice(128 * h, 128 * h + 128)
-        t = (scores[:, at] * scale + wide).reshape(BLK // 8, 8, 128) + lanes[:, at][None]
+        t = (scores_ref[:, at] + wide).reshape(BLK // 8, 8, 128) + lanes[:, at][None]
         halves.append(jnp.exp2(t))
     return halves
 
@@ -129,14 +129,14 @@
     over_pairs(pairs_ref, kept, visit)
 
 
-def sweep(pairs_ref, kept, x_ref, y_ref, f, g, shift, scale, blocks, outs, scratch):
+def sweep(pairs_ref, kept, x_ref, y_ref, scores_ref, f, g, shift, scale, blocks, outs, scratch):
     row_out, col_out = outs
     f_wide, g_wide, row_high, row_sum, col_high, col_sum, lanes, row_acc, col_acc = scratch
     spread_lanes(g + shift, blocks, lanes)
     clear(row_acc, col_acc)
 
     def visit(s, t):
-        halves = exponentials(cross(x_ref[s], y_ref[t]), scale, f_wide[s], lanes[t])
+        halves = exponentials(scores_ref.at[t, s], f_wide[s], lanes[t])
         add_sums(halves, row_acc, col_acc, s, t)
 
     over_pairs(pairs_ref, kept, visit)
@@ -152,32 +152,28 @@
         col_out[...] = settle(col_high, col_sum, blocks)
 
 
-def first_kernel(scale, blocks, pairs_ref, count_ref, x_hbm, y_hbm, *rest):
-    f_out, g_out, row_out, col_out = rest[:4]
-    scratch, (x_ref, y_ref, arrived) = rest[4:-3], rest[-3:]
+def first_kernel(scale, blocks, pairs_ref, count_ref, x_ref, y_ref, *rest):
+    scores_ref, f_out, g_out, row_out, col_out = rest[:5]
+    scratch = rest[5:]
     f_wide, g_wide = scratch[:2]
-    copies = [
-        pltpu.make_async_copy(far.at[b], near.at[b], arrived.at[k, b])
-        for b in range(blocks)
-        for k, (far, near) in enumerate(((x_hbm, x_ref), (y_hbm, y_ref)))
-    ]
-    for copy in copies:
-        copy.start()
     f_columns, g_columns = [], []
     for b in range(blocks):
-        copies[2 * b].wait()
         f_columns.append(norm(x_ref[b], scale))
         f_wide[b] = jnp.broadcast_to(f_columns[b], (BLK, 128))
-        copies[2 * b + 1].wait()
+    everything = x_ref[...].reshape(blocks * BLK, BLK)
+    for b in range(blocks):
+        scores = cross(everything, y_ref[b]) * scale
+        scores_ref[b] = scores.reshape(blocks, BLK, BLK)
         g_columns.append(norm(y_ref[b], scale))
     f, g = across(f_columns), across(g_columns)
     f_out[...] = f
     g_out[...] = g
     shift = -(jnp.sum(f) + jnp.sum(g)) / (blocks * BLK)
-    sweep(pairs_ref, count_ref[0], x_ref, y_ref, f, g, shift, scale, blocks, (row_out, col_out), scratch)
-
-
-def second_kernel(n_row, scale, blocks, pairs_ref, count_ref, x_ref, y_ref, f_old, g_old, *rest):
+    outs = (row_out, col_out)
+    sweep(pairs_ref, count_ref[0], x_ref, y_ref, scores_ref, f, g, shift, scale, blocks, outs, scratch)
+
+
+def second_kernel(n_row, scale, blocks, pairs_ref, count_ref, x_ref, y_ref, scores_ref, f_old, g_old, *rest):
     parts, rest = rest[: n_row + 1], rest[n_row + 1 :]
     f_out, g_out, row_out, col_out = rest[:4]
     scratch = rest[4:]
@@ -186,7 +182,8 @@
     f_out[...] = f
     g_out[...] = g
     down_rows(f, blocks, scratch[0])
-    sweep(pairs_ref, count_ref[0], x_ref, y_ref, f, g, 0.0, scale, blocks, (row_out, col_out), scratch)
+    outs = (row_out, col_out)
+    sweep(pairs_ref, count_ref[0], x_ref, y_ref, scores_ref, f, g, 0.0, scale, blocks, outs, scratch)
 
 
 def split_two(w):
@@ -238,12 +235,12 @@
         lanes_ref[b] = jnp.broadcast_to(values[b : b + 1], (8, BLK))
 
 
-def maps_kernel(n_row, scale, blocks, place_ref, pairs_ref, count_ref, x_ref, y_ref, f_old, g_old, *rest):
+def maps_kernel(n_row, scale, blocks, place_ref, pairs_ref, count_ref, x_ref, y_ref, scores_ref, f_old, g_old, *rest):
     parts, rest = rest[: n_row + 1], rest[n_row + 1 :]
     keep_out, send_out, own, up, down, up_next, down_next = rest[:7]
     scratch = rest[7:16]
     f_wide, g_wide, row_high, row_sum, col_high, col_sum, lanes, row_acc, col_acc = scratch
-    x_turned, forward, backward, turned, logs, lines_ref = rest[16:]
+    x_turned, forward, backward, turned, logs, lines_ref, *weights = rest[16:]
     kept = count_ref[0]
     f = new_potential(f_old, parts[:n_row])
     g = new_potential(g_old, parts[n_row:])
@@ -255,12 +252,23 @@
     for b in range(blocks):
         x_turned[b] = cross(unit, x_ref[b]).astype(jnp.bfloat16)
 
-    def visit(s, t):
-        xs, yt, xt = x_ref[s], y_ref[t], x_turned[s]
-        halves = exponentials(cross(xs, yt), scale, f_wide[s], lanes[t])
-        add_sums(halves, row_acc, col_acc, s, t)
-        e = jnp.concatenate([half.reshape(BLK, 128) for half in halves], axis=1)
-        high, low = split_two(e)
+    def weigh_pair(p, buffer):
+        at = jnp.minimum(p, kept - 1)
+        s, t = pairs_ref[0, at], pairs_ref[1, at]
+        halves = exponentials(scores_ref.at[t, s], f_wide[s], lanes[t])
+        counted = jnp.where(p < kept, 1.0, 0.0)
+        for h, e in enumerate(halves):
+            cols = slice(128 * h, 128 * h + 128)
+            col_acc[t, :, cols] += jnp.sum(e, axis=0) * counted
+            high, low = split_two(e.reshape(BLK, 128))
+            buffer[0, :, cols] = high
+            buffer[1, :, cols] = low
+        row_acc[s] += (halves[0] + halves[1]).reshape(BLK, 128) * counted
+
+    def add_pair(p, buffer):
+        s, t = pairs_ref[0, p], pairs_ref[1, p]
+        yt, xt = y_ref[t], x_turned[s]
+        high, low = buffer[0], buffer[1]
         rows = pl.ds(pl.multiple_of(s * BLK, BLK), BLK)
         forward[rows, :] += jnp.dot(
             jnp.concatenate([high, low], axis=1),
@@ -273,7 +281,22 @@
             preferred_element_type=jnp.float32,
         )
 
-    over_pairs(pairs_ref, kept, visit)
+    weigh_pair(0, weights[0])
+
+    def two(step, carry):
+        p = 2 * step
+        weigh_pair(p + 1, weights[1])
+        add_pair(p, weights[0])
+        weigh_pair(p + 2, weights[0])
+        add_pair(p + 1, weights[1])
+        return carry
+
+    lax.fori_loop(0, kept // 2, two, 0)
+
+    @pl.when(kept % 2 == 1)
+    def _():
+        add_pair(kept - 1, weights[0])
+
     columns, row, col, good = totals(row_acc, col_acc, blocks)
 
     @pl.when(good)
@@ -419,7 +442,6 @@
     pair_list = jnp.transpose(pairs[0, 0])
     kept = counts.reshape(-1)
     smem = pl.BlockSpec(memory_space=pltpu.SMEM)
-    hbm = pl.BlockSpec(memory_space=pltpu.HBM)
     large = pltpu.CompilerParams(vmem_limit_bytes=24 * 1024 * 1024)
     little = pltpu.CompilerParams(vmem_limit_bytes=8 * 1024 * 1024)
 
@@ -438,26 +460,23 @@
         cols = lax.all_to_all(copies, "src", 0, 0, axis_index_groups=along_z, tiled=True)
         return [row, swap(row, "tgt", n_tgt, 1), cols]
 
-    latents = pltpu.VMEM((blocks, BLK, width), jnp.bfloat16)
-    f, g, row, col = pl.pallas_call(
+    scores, f, g, row, col = pl.pallas_call(
         functools.partial(first_kernel, scale, blocks),
-        out_shape=[shape(8, BLK)] * 4,
-        in_specs=[smem] * 2 + [hbm] * 2,
-        out_specs=in_vmem(4),
-        scratch_shapes=sums_scratch(blocks)
-        + [latents] * 2
-        + [pltpu.SemaphoreType.DMA((2, blocks))],
-        compiler_params=pltpu.CompilerParams(vmem_limit_bytes=60 * 1024 * 1024),
+        out_shape=[shape(blocks, blocks, BLK, BLK)] + [shape(8, BLK)] * 4,
+        in_specs=[smem] * 2 + in_vmem(2),
+        out_specs=in_vmem(5),
+        scratch_shapes=sums_scratch(blocks),
+        compiler_params=large,
     )(pair_list, kept, x, y)
     parts = exchange(row, col)
     f, g, row, col = pl.pallas_call(
         functools.partial(second_kernel, 2, scale, blocks),
         out_shape=[shape(8, BLK)] * 4,
-        in_specs=[smem] * 2 + in_vmem(7),
+        in_specs=[smem] * 2 + in_vmem(8),
         out_specs=in_vmem(4),
         scratch_shapes=sums_scratch(blocks),
         compiler_params=large,
-    )(pair_list, kept, x, y, f, g, *parts)
+    )(pair_list, kept, x, y, scores, f, g, *parts)
     parts = exchange(row, col)
 
     f_rows, b_rows = blocks * BLK // n_tgt, blocks * BLK // n_src
@@ -465,13 +484,14 @@
     s_at = lax.axis_index("src").astype(jnp.int32)
     t_at = lax.axis_index("tgt").astype(jnp.int32)
 
-    def call(kernel, operands, outs, places=()):
+    def call(kernel, operands, outs, places=(), cost=None):
         return pl.pallas_call(
             kernel,
             out_shape=outs,
             in_specs=[smem] * len(places) + in_vmem(len(operands)),
             out_specs=in_vmem(len(outs)),
             compiler_params=little,
+            cost_estimate=cost,
         )(*places, *operands)
 
     block = shape(f_rows + 8, width)
@@ -479,7 +499,7 @@
     keep, send, own, up, down, up_next, down_next = pl.pallas_call(
         functools.partial(maps_kernel, 2, scale, blocks),
         out_shape=[shape(half, b_rows + 8, width)] * 2 + [two, two, two, block, block],
-        in_specs=[smem] * 3 + in_vmem(7),
+        in_specs=[smem] * 3 + in_vmem(8),
         out_specs=in_vmem(7),
         scratch_shapes=sums_scratch(blocks)
         + [
@@ -489,13 +509,18 @@
             pltpu.VMEM((blocks, width, BLK), jnp.float32),
             pltpu.VMEM((2, 8, BLK), jnp.float32),
             pltpu.VMEM((n_tgt, 1, BLK), jnp.float32),
+            pltpu.VMEM((2, BLK, BLK), jnp.bfloat16),
+            pltpu.VMEM((2, BLK, BLK), jnp.bfloat16),
         ],
         compiler_params=large,
-    )(jnp.stack([s_at % 2, t_at % RING]), pair_list, kept, x, y, f, g, *parts)
+    )(jnp.stack([s_at % 2, t_at % RING]), pair_list, kept, x, y, scores, f, g, *parts)
     came = swap(send, "src", n_src, 1)
 
     (paired,) = call(
-        functools.partial(pair_kernel, b_rows), [keep, came], [shape(half, b_rows + 8, width)]
+        functools.partial(pair_kernel, b_rows),
+        [keep, came],
+        [shape(half, b_rows + 8, width)],
+        cost=pl.CostEstimate(flops=10**10, bytes_accessed=3 * 10**7, transcendentals=0),
     )
     backward = lax.all_to_all(
         paired.reshape(n_z, 2, b_rows + 8, width),

time: 143 us -> 149 us (1.042)
  starting transfers between devices: 57.3 us -> 29.5 us
  local copies, waits for them, and re-layouts: 1.97 us -> 18.2 us
  Pallas kernels: 41.4 us -> 52.1 us
  waiting for transfers between devices: 37.9 us -> 46.8 us
    ppermute x13, starting transfers between devices: 24.8 us -> 5.77 us  [swap(): return lax.ppermute(value, axis, [(k, k ^ bit) for k in range(size)])]
    unnamed x12 -> x24, local copies, waits for them, and re-layouts: 0.68 us -> 16.9 us
    all_to_all x1, starting transfers between devices: 13.9 us -> 3.55 us  [per_device(): lax.all_to_all(paired.reshape(n_z, 2, b_rows + 8, width), 'src', 0, 0, ax...]
    pallas_call x1, Pallas kernels: 19.3 us -> 28.5 us  [per_device(): pl.pallas_call(functools.partial(maps_kernel, 2, scale, blocks), out_shap...]
    ppermute x13, waiting for transfers between devices: 12.3 us -> 20 us  [swap(): return lax.ppermute(value, axis, [(k, k ^ bit) for k in range(size)])]
    all_to_all x1, waiting for transfers between devices: 2.73 us -> 5.05 us  [per_device(): lax.all_to_all(paired.reshape(n_z, 2, b_rows + 8, width), 'src', 0, 0, ax...]
    pallas_call x1, Pallas kernels: 7.36 us -> 9.18 us  [per_device(): pl.pallas_call(functools.partial(second_kernel, 2, scale, blocks), out_sh...]
    ppermute x1, starting transfers between devices: 1.82 us -> 0.08 us  [per_device(): up_second = lax.ppermute(up, 'tgt', ups)]
  transfers between devices with their start and end apart: 20 -> 20, of which waited for: 12 -> 13; matrix products, arithmetic and copies ran while one was open for 2% -> 1% of each run, Pallas kernels for 1% -> 1%
where the time goes in v6:
time: 149 us; the launch traced here: 148 us
  Pallas kernels  52.1 us (35%)
  waiting for transfers between devices  46.8 us (31%)
  starting transfers between devices  29.5 us (20%)
  local copies, waits for them, and re-layouts  18.2 us (12%)
  between operations  1.57 us (1%)
    pallas_call x1, Pallas kernels, per_device(): pl.pallas_call(functools.partial(maps_kernel, 2, scale, blocks), out_shap...  28.5 us
    ppermute x13, waiting for transfers between devices, swap(): return lax.ppermute(value, axis, [(k, k ^ bit) for k in range(size)])  20 us
    unnamed x24, local copies, waits for them, and re-layouts  16.9 us
    all_to_all x2, starting transfers between devices, exchange(): lax.all_to_all(copies, 'src', 0, 0, axis_index_groups=along_z, tiled=True)  13.6 us
    pallas_call x1, Pallas kernels, per_device(): pl.pallas_call(functools.partial(first_kernel, scale, blocks), out_shape=...  10.2 us
    ppermute x1, waiting for transfers between devices, per_device(): up_came = lax.ppermute(up, 'tgt', ups)  9.48 us
    pallas_call x1, Pallas kernels, per_device(): pl.pallas_call(functools.partial(second_kernel, 2, scale, blocks), out_sh...  9.18 us
    all_to_all x2, waiting for transfers between devices, exchange(): lax.all_to_all(copies, 'src', 0, 0, axis_index_groups=along_z, tiled=True)  8.04 us
  transfers between devices with their start and end apart: 20, of which 13 were waited for; matrix products, arithmetic and copies ran while one was open for 1% of the time, Pallas kernels for 1%

profile of v6, /device:TPU:8, one launch (start us, length us, event | category | flops | bytes accessed | tf_op | source)
XLA Modules:
  0.0 148.4 jit_solution(2483753045055067060)
XLA Ops:
  1.3 1.1 copy-done.3
  2.4 1.1 copy-done.6
  4.3 10.2 %shard_map.59 = (f32[6,6,256,256]{3,2,1,0:T(8,128)S(1)}, f32[8,256]{1,0:T(8,128)S(1)}, f32[8,256]{1,0:T(8,128)S(1)}, f32[8,256]{1,0:T(8,128)S(1)}, f32[8,256]{1,0:T(8,128)S(1)}) custom-call(s32[2,24]{1,0:T(2,128)S(1)} %bitcast.20, s32[1]{0:T(128)} %bitcast.11.count_ref, bf16[6,256,256]{2,1,0:T(8,128)(2,1)S(1)} %bitcast.14, bf16[6,256,256]{2,1,0:T(8,128)(2,1)S(1)} %bitcast.17), custom_call_target="tpu_custom_call" | custom-call | tf_op jit(solution)/shard_map/pallas_call | solution.py:463
  14.5 3.6 %copy-done = f32[6,6,256,256]{3,2,1,0:T(8,128)} copy-done((f32[6,6,256,256]{3,2,1,0:T(8,128)}, f32[6,6,256,256]{3,2,1,0:T(8,128)S(1)}, u32[]{:S(2)}) %copy-start) | copy-done | bytes 9437208
  18.1 1.7 %collective-permute-start = (f32[8,256]{1,0:T(8,128)S(1)}, f32[8,256]{1,0:T(8,128)S(1)}, u32[]{:S(2)}, u32[]{:S(2)}) collective-permute-start(f32[8,256]{1,0:T(8,128)S(1)} %get-tuple-element.29), channel_id=1, source_target_pairs={{0,4},{1,5},{2,6},{3,7},{4,0},{5,1},{6,2},{7,3},{8,12},{9,13},{10,... | collective-permute-start | bytes 24584 | tf_op jit(solution)/shard_map/ppermute | solution.py:449
  19.8 1.1 collective-permute-start.4
  20.9 2.3 %collective-permute-done = f32[8,256]{1,0:T(8,128)S(1)} collective-permute-done((f32[8,256]{1,0:T(8,128)S(1)}, f32[8,256]{1,0:T(8,128)S(1)}, u32[]{:S(2)}, u32[]{:S(2)}) %collective-permute-start) | collective-permute-done | bytes 8224 | tf_op jit(solution)/shard_map/ppermute | solution.py:449
  24.7 10.2 %all-to-all-start = ((f32[8,8,256]{2,1,0:T(8,128)}), f32[8,8,256]{2,1,0:T(8,128)S(1)}, u32[]{:S(2)}, u32[]{:S(2)}) async-start(f32[8,8,256]{2,1,0:T(8,128)} %broadcast_in_dim.4), calls=%async_computation | async-start | bytes 131072 | tf_op jit(solution)/shard_map/all_to_all | solution.py:460
  35.1 3.6 %collective-permute-done.2.rest_1_ = f32[8,256]{1,0:T(8,128)S(1)} collective-permute-done((f32[8,256]{1,0:T(8,128)S(1)}, f32[8,256]{1,0:T(8,128)S(1)}, u32[]{:S(2)}, u32[]{:S(2)}) %collective-permute-start.2) | collective-permute-done | bytes 8224 | tf_op jit(solution)/shard_map/ppermute | solution.py:449
  38.7 4.6 %all-to-all-done.rest_2_ = f32[8,8,256]{2,1,0:T(8,128)S(1)} async-done(((f32[8,8,256]{2,1,0:T(8,128)}), f32[8,8,256]{2,1,0:T(8,128)S(1)}, u32[]{:S(2)}, u32[]{:S(2)}) %all-to-all-start) | async-done | bytes 65568 | tf_op jit(solution)/shard_map/all_to_all | solution.py:460
  43.3 3.7 %copy-done.1 = f32[6,6,256,256]{3,2,1,0:T(8,128)S(1)} copy-done((f32[6,6,256,256]{3,2,1,0:T(8,128)S(1)}, f32[6,6,256,256]{3,2,1,0:T(8,128)}, u32[]{:S(2)}) %copy-start.1) | copy-done | bytes 9437208
  47.0 1.1 copy-done.4
  48.1 1.1 copy-done.7
  49.9 9.2 %shard_map.60 = (f32[8,256]{1,0:T(8,128)S(1)}, f32[8,256]{1,0:T(8,128)S(1)}, f32[8,256]{1,0:T(8,128)S(1)}, f32[8,256]{1,0:T(8,128)S(1)}) custom-call(s32[2,24]{1,0:T(2,128)S(1)} %bitcast.21, s32[1]{0:T(128)} %bitcast.12.count_ref, bf16[6,256,256]{2,1,0:T(8,128)(2,1)S(1)} %bitcast.15, bf16[6,256,256]{2,1,0:T(8,128)(2,1)S(1)} %bitcast.18, ...), custom_call_target="tpu_custom_call" | custom-call | tf_op jit(solution)/shard_map/pallas_call | solution.py:472
  59.2 1.5 collective-permute-start.5
  60.8 3.7 %collective-permute-done.5 = f32[8,256]{1,0:T(8,128)S(1)} collective-permute-done((f32[8,256]{1,0:T(8,128)S(1)}, f32[8,256]{1,0:T(8,128)S(1)}, u32[]{:S(2)}, u32[]{:S(2)}) %collective-permute-start.5) | collective-permute-done | bytes 8224 | tf_op jit(solution)/shard_map/ppermute | solution.py:449
  65.3 3.4 %all-to-all-start.1 = ((f32[8,8,256]{2,1,0:T(8,128)}), f32[8,8,256]{2,1,0:T(8,128)S(1)}, u32[]{:S(2)}, u32[]{:S(2)}) async-start(f32[8,8,256]{2,1,0:T(8,128)} %broadcast_in_dim.5), calls=%async_computation.1 | async-start | bytes 131072 | tf_op jit(solution)/shard_map/all_to_all | solution.py:460
  68.7 1.1 collective-permute-done.6
  70.0 3.6 %collective-permute-done.7.rest_1_ = f32[8,256]{1,0:T(8,128)S(1)} collective-permute-done((f32[8,256]{1,0:T(8,128)S(1)}, f32[8,256]{1,0:T(8,128)S(1)}, u32[]{:S(2)}, u32[]{:S(2)}) %collective-permute-start.7) | collective-permute-done | bytes 8224 | tf_op jit(solution)/shard_map/ppermute | solution.py:449
  73.5 3.4 %all-to-all-done.1.rest_2_ = f32[8,8,256]{2,1,0:T(8,128)S(1)} async-done(((f32[8,8,256]{2,1,0:T(8,128)}), f32[8,8,256]{2,1,0:T(8,128)S(1)}, u32[]{:S(2)}, u32[]{:S(2)}) %all-to-all-start.1) | async-done | bytes 65568 | tf_op jit(solution)/shard_map/all_to_all | solution.py:460
  77.0 3.7 %copy-done.2 = f32[6,6,256,256]{3,2,1,0:T(8,128)S(1)} copy-done((f32[6,6,256,256]{3,2,1,0:T(8,128)S(1)}, f32[6,6,256,256]{3,2,1,0:T(8,128)}, u32[]{:S(2)}) %copy-start.2) | copy-done | bytes 9437208
  80.6 28.5 %shard_map.61 = (f32[16,56,256]{2,1,0:T(8,128)S(1)}, f32[16,56,256]{2,1,0:T(8,128)S(1)}, f32[2,200,256]{2,1,0:T(8,128)S(1)}, f32[2,200,256]{2,1,0:T(8,128)S(1)},...) custom-call(s32[2]{0:T(128)S(1)} %pad_add_fusion.place_ref, s32[2,24]{1,0:T(2,128)S(1)} %bitcast.22, ...), custom_call_target="tpu_custom_call" | custom-call | tf_op jit(solution)/shard_map/pallas_call | solution.py:499
  109.2 2.5 %collective-permute-done.12.b_ref = f32[16,56,256]{2,1,0:T(8,128)S(1)} collective-permute-done((f32[16,56,256]{2,1,0:T(8,128)S(1)}, f32[16,56,256]{2,1,0:T(8,128)S(1)}, u32[]{:S(2)}, u32[]{:S(2)}) %collective-permute-start.12) | collective-permute-done | bytes 917536 | tf_op jit(solution)/shard_map/ppermute | solution.py:449
  111.7 1.4 shard_map.62
  113.0 3.6 %all-to-all-start.2 = ((f32[8,2,56,256]{3,2,1,0:T(8,128)}), f32[8,2,56,256]{3,2,1,0:T(8,128)S(1)}, u32[]{:S(2)}, u32[]{:S(2)}) async-start(f32[8,2,56,256]{3,2,1,0:T(8,128)} %bitcast.10), calls=%async_computation.2 | async-start | bytes 1835008 | tf_op jit(solution)/shard_map/all_to_all | solution.py:525
  116.7 3.2 %collective-permute-start.11 = (f32[2,200,256]{2,1,0:T(8,128)S(1)}, f32[2,200,256]{2,1,0:T(8,128)S(1)}, u32[]{:S(2)}, u32[]{:S(2)}) collective-permute-start(f32[2,200,256]{2,1,0:T(8,128)S(1)} %get-tuple-element.37), channel_id=1, source_target_pairs={{1,0},{2,1},{3,2},{0,3},{5,4},{6,5},{7,6},{4,7},{9,8},{10,9},{11,1... | collective-permute-start | bytes 1228808 | tf_op jit(solution)/shard_map/ppermute | solution.py:543
  119.9 9.5 %collective-permute-done.10.up_came = f32[2,200,256]{2,1,0:T(8,128)S(1)} collective-permute-done((f32[2,200,256]{2,1,0:T(8,128)S(1)}, f32[2,200,256]{2,1,0:T(8,128)S(1)}, u32[]{:S(2)}, u32[]{:S(2)}) %collective-permute-start.10) | collective-permute-done | bytes 409632 | tf_op jit(solution)/shard_map/ppermute | solution.py:542
  129.9 3.2 %collective-permute-start.14 = (f32[200,256]{1,0:T(8,128)S(1)}, f32[200,256]{1,0:T(8,128)S(1)}, u32[]{:S(2)}, u32[]{:S(2)}) collective-permute-start(f32[200,256]{1,0:T(8,128)S(1)} %get-tuple-element.45), channel_id=1, source_target_pairs={{1,0},{2,1},{3,2},{0,3},{5,4},{6,5},{7,6},{4,7},{9,8},{10,9},{11,1... | collective-permute-start | bytes 614408 | tf_op jit(solution)/shard_map/ppermute | solution.py:551
  133.1 4.3 %collective-permute-done.13.up_second = f32[200,256]{1,0:T(8,128)S(1)} collective-permute-done((f32[200,256]{1,0:T(8,128)S(1)}, f32[200,256]{1,0:T(8,128)S(1)}, u32[]{:S(2)}, u32[]{:S(2)}) %collective-permute-start.13) | collective-permute-done | bytes 204832 | tf_op jit(solution)/shard_map/ppermute | solution.py:550
  137.9 5.1 %all-to-all-done.2.parts_ref = f32[8,2,56,256]{3,2,1,0:T(8,128)S(1)} async-done(((f32[8,2,56,256]{3,2,1,0:T(8,128)}), f32[8,2,56,256]{3,2,1,0:T(8,128)S(1)}, u32[]{:S(2)}, u32[]{:S(2)}) %all-to-all-start.2) | async-done | bytes 917536 | tf_op jit(solution)/shard_map/all_to_all | solution.py:525
  143.4 2.0 %collective-permute-done.15.b_ref = f32[200,256]{1,0:T(8,128)S(1)} collective-permute-done((f32[200,256]{1,0:T(8,128)S(1)}, f32[200,256]{1,0:T(8,128)S(1)}, u32[]{:S(2)}, u32[]{:S(2)}) %collective-permute-start.15) | collective-permute-done | bytes 204832 | tf_op jit(solution)/shard_map/ppermute | solution.py:449
  146.4 1.2 collective-permute-done.16.b_ref
  (52 shorter events, 7.5 us)
Async XLA Ops:
  0.6 76.3 %copy-start.11 = (s32[1,1,24,2]{2,3,1,0:T(2,128)S(1)}, s32[1,1,24,2]{2,3,1,0:T(2,128)}, u32[]{:S(2)}) copy-start(s32[1,1,24,2]{2,3,1,0:T(2,128)} %param.6) | copy-start | bytes 580
  1.3 1.1 copy-start.3
  2.4 1.1 copy-start.6
  3.6 0.7 copy-start.9
  4.2 72.7 %copy-start.5 = (bf16[1536,256]{1,0:T(8,128)(2,1)S(1)}, bf16[1536,256]{1,0:T(8,128)(2,1)}, u32[]{:S(2)}) copy-start(bf16[1536,256]{1,0:T(8,128)(2,1)} %param.4) | copy-start | bytes 2359300
  4.3 72.7 %copy-start.8 = (bf16[1536,256]{1,0:T(8,128)(2,1)S(1)}, bf16[1536,256]{1,0:T(8,128)(2,1)}, u32[]{:S(2)}) copy-start(bf16[1536,256]{1,0:T(8,128)(2,1)} %param.5) | copy-start | bytes 2359300
  14.5 3.6 %copy-start = (f32[6,6,256,256]{3,2,1,0:T(8,128)}, f32[6,6,256,256]{3,2,1,0:T(8,128)S(1)}, u32[]{:S(2)}) copy-start(f32[6,6,256,256]{3,2,1,0:T(8,128)S(1)} %get-tuple-element.26.scores_ref) | copy-start | bytes 28311556
  18.1 1.7 %collective-permute-start.3 = (f32[8,256]{1,0:T(8,128)S(1)}, f32[8,256]{1,0:T(8,128)S(1)}, u32[]{:S(2)}, u32[]{:S(2)}) collective-permute-start(f32[8,256]{1,0:T(8,128)S(1)} %get-tuple-element.30), channel_id=1, source_target_pairs={{0,8},{8,0},{16,24},{24,16},{32,40},{40,32},{48,56},{56,48},{64,72... | collective-permute-start | bytes 24584 | tf_op jit(solution)/shard_map/ppermute | solution.py:449
  18.1 5.2 %collective-permute-start = (f32[8,256]{1,0:T(8,128)S(1)}, f32[8,256]{1,0:T(8,128)S(1)}, u32[]{:S(2)}, u32[]{:S(2)}) collective-permute-start(f32[8,256]{1,0:T(8,128)S(1)} %get-tuple-element.29), channel_id=1, source_target_pairs={{0,4},{1,5},{2,6},{3,7},{4,0},{5,1},{6,2},{7,3},{8,12},{9,13},{10,... | collective-permute-start | bytes 24584 | tf_op jit(solution)/shard_map/ppermute | solution.py:449
  19.8 4.2 %collective-permute-start.4 = (f32[8,256]{1,0:T(8,128)S(1)}, f32[8,256]{1,0:T(8,128)S(1)}, u32[]{:S(2)}, u32[]{:S(2)}) collective-permute-start(f32[8,256]{1,0:T(8,128)S(1)} %multiply_add_fusion.5), channel_id=1, source_target_pairs={{0,16},{8,24},{16,0},{24,8},{32,48},{40,56},{48,32},{56,40},{64,80... | collective-permute-start | bytes 24584 | tf_op jit(solution)/shard_map/ppermute | solution.py:449
  23.3 11.6 %collective-permute-start.1 = (f32[8,256]{1,0:T(8,128)S(1)}, f32[8,256]{1,0:T(8,128)S(1)}, u32[]{:S(2)}, u32[]{:S(2)}) collective-permute-start(f32[8,256]{1,0:T(8,128)S(1)} %multiply_add_fusion.7), channel_id=1, source_target_pairs={{0,2},{1,3},{2,0},{3,1},{4,6},{5,7},{6,4},{7,5},{8,10},{9,11},{10,... | collective-permute-start | bytes 24584 | tf_op jit(solution)/shard_map/ppermute | solution.py:449
  24.7 18.6 %all-to-all-start = ((f32[8,8,256]{2,1,0:T(8,128)}), f32[8,8,256]{2,1,0:T(8,128)S(1)}, u32[]{:S(2)}, u32[]{:S(2)}) async-start(f32[8,8,256]{2,1,0:T(8,128)} %broadcast_in_dim.4), calls=%async_computation | async-start | bytes 131072 | tf_op jit(solution)/shard_map/all_to_all | solution.py:460
  35.0 3.7 %collective-permute-start.2 = (f32[8,256]{1,0:T(8,128)S(1)}, f32[8,256]{1,0:T(8,128)S(1)}, u32[]{:S(2)}, u32[]{:S(2)}) collective-permute-start(f32[8,256]{1,0:T(8,128)S(1)} %multiply_add_fusion.6.rest_0_), channel_id=1, source_target_pairs={{0,1},{1,0},{2,3},{3,2},{4,5},{5,4},{6,7},{7,6},{8,9},{9,8},{10,11... | collective-permute-start | bytes 24584 | tf_op jit(solution)/shard_map/ppermute | solution.py:449
  43.3 3.7 %copy-start.1 = (f32[6,6,256,256]{3,2,1,0:T(8,128)S(1)}, f32[6,6,256,256]{3,2,1,0:T(8,128)}, u32[]{:S(2)}) copy-start(f32[6,6,256,256]{3,2,1,0:T(8,128)} %copy-done) | copy-start | bytes 28311556
  47.0 1.1 copy-start.4
  48.1 1.1 copy-start.7
  49.2 0.7 copy-start.10
  59.1 1.6 %collective-permute-start.8 = (f32[8,256]{1,0:T(8,128)S(1)}, f32[8,256]{1,0:T(8,128)S(1)}, u32[]{:S(2)}, u32[]{:S(2)}) collective-permute-start(f32[8,256]{1,0:T(8,128)S(1)} %get-tuple-element.34), channel_id=1, source_target_pairs={{0,8},{8,0},{16,24},{24,16},{32,40},{40,32},{48,56},{56,48},{64,72... | collective-permute-start | bytes 24584 | tf_op jit(solution)/shard_map/ppermute | solution.py:449
  59.2 5.3 %collective-permute-start.5 = (f32[8,256]{1,0:T(8,128)S(1)}, f32[8,256]{1,0:T(8,128)S(1)}, u32[]{:S(2)}, u32[]{:S(2)}) collective-permute-start(f32[8,256]{1,0:T(8,128)S(1)} %get-tuple-element.33), channel_id=1, source_target_pairs={{0,4},{1,5},{2,6},{3,7},{4,0},{5,1},{6,2},{7,3},{8,12},{9,13},{10,... | collective-permute-start | bytes 24584 | tf_op jit(solution)/shard_map/ppermute | solution.py:449
  60.7 3.9 %collective-permute-start.9 = (f32[8,256]{1,0:T(8,128)S(1)}, f32[8,256]{1,0:T(8,128)S(1)}, u32[]{:S(2)}, u32[]{:S(2)}) collective-permute-start(f32[8,256]{1,0:T(8,128)S(1)} %multiply_add_fusion.1), channel_id=1, source_target_pairs={{0,16},{8,24},{16,0},{24,8},{32,48},{40,56},{48,32},{56,40},{64,80... | collective-permute-start | bytes 24584 | tf_op jit(solution)/shard_map/ppermute | solution.py:449
  64.5 5.2 %collective-permute-start.6 = (f32[8,256]{1,0:T(8,128)S(1)}, f32[8,256]{1,0:T(8,128)S(1)}, u32[]{:S(2)}, u32[]{:S(2)}) collective-permute-start(f32[8,256]{1,0:T(8,128)S(1)} %multiply_add_fusion.3), channel_id=1, source_target_pairs={{0,2},{1,3},{2,0},{3,1},{4,6},{5,7},{6,4},{7,5},{8,10},{9,11},{10,... | collective-permute-start | bytes 24584 | tf_op jit(solution)/shard_map/ppermute | solution.py:449
  65.3 11.7 %all-to-all-start.1 = ((f32[8,8,256]{2,1,0:T(8,128)}), f32[8,8,256]{2,1,0:T(8,128)S(1)}, u32[]{:S(2)}, u32[]{:S(2)}) async-start(f32[8,8,256]{2,1,0:T(8,128)} %broadcast_in_dim.5), calls=%async_computation.1 | async-start | bytes 131072 | tf_op jit(solution)/shard_map/all_to_all | solution.py:460
  69.8 3.7 %collective-permute-start.7 = (f32[8,256]{1,0:T(8,128)S(1)}, f32[8,256]{1,0:T(8,128)S(1)}, u32[]{:S(2)}, u32[]{:S(2)}) collective-permute-start(f32[8,256]{1,0:T(8,128)S(1)} %multiply_add_fusion.2.rest_0_), channel_id=1, source_target_pairs={{0,1},{1,0},{2,3},{3,2},{4,5},{5,4},{6,7},{7,6},{8,9},{9,8},{10,11... | collective-permute-start | bytes 24584 | tf_op jit(solution)/shard_map/ppermute | solution.py:449
  77.0 3.7 %copy-start.2 = (f32[6,6,256,256]{3,2,1,0:T(8,128)S(1)}, f32[6,6,256,256]{3,2,1,0:T(8,128)}, u32[]{:S(2)}) copy-start(f32[6,6,256,256]{3,2,1,0:T(8,128)} %copy-done) | copy-start | bytes 28311556
  109.1 2.6 %collective-permute-start.12 = (f32[16,56,256]{2,1,0:T(8,128)S(1)}, f32[16,56,256]{2,1,0:T(8,128)S(1)}, u32[]{:S(2)}, u32[]{:S(2)}) collective-permute-start(f32[16,56,256]{2,1,0:T(8,128)S(1)} %get-tuple-element.39), channel_id=1, source_target_pairs={{0,8},{8,0},{16,24},{24,16},{32,40},{40,32},{48,56},{56,48},{64,72... | collective-permute-start | bytes 2752520 | tf_op jit(solution)/shard_map/ppermute | solution.py:449
  113.0 30.0 %all-to-all-start.2 = ((f32[8,2,56,256]{3,2,1,0:T(8,128)}), f32[8,2,56,256]{3,2,1,0:T(8,128)S(1)}, u32[]{:S(2)}, u32[]{:S(2)}) async-start(f32[8,2,56,256]{3,2,1,0:T(8,128)} %bitcast.10), calls=%async_computation.2 | async-start | bytes 1835008 | tf_op jit(solution)/shard_map/all_to_all | solution.py:525
  116.6 12.8 %collective-permute-start.10 = (f32[2,200,256]{2,1,0:T(8,128)S(1)}, f32[2,200,256]{2,1,0:T(8,128)S(1)}, u32[]{:S(2)}, u32[]{:S(2)}) collective-permute-start(f32[2,200,256]{2,1,0:T(8,128)S(1)} %get-tuple-element.36), channel_id=1, source_target_pairs={{0,1},{1,2},{2,3},{3,0},{4,5},{5,6},{6,7},{7,4},{8,9},{9,10},{10,1... | collective-permute-start | bytes 1228808 | tf_op jit(solution)/shard_map/ppermute | solution.py:542
  116.7 12.7 %collective-permute-start.11 = (f32[2,200,256]{2,1,0:T(8,128)S(1)}, f32[2,200,256]{2,1,0:T(8,128)S(1)}, u32[]{:S(2)}, u32[]{:S(2)}) collective-permute-start(f32[2,200,256]{2,1,0:T(8,128)S(1)} %get-tuple-element.37), channel_id=1, source_target_pairs={{1,0},{2,1},{3,2},{0,3},{5,4},{6,5},{7,6},{4,7},{9,8},{10,9},{11,1... | collective-permute-start | bytes 1228808 | tf_op jit(solution)/shard_map/ppermute | solution.py:543
  129.8 7.6 %collective-permute-start.13 = (f32[200,256]{1,0:T(8,128)S(1)}, f32[200,256]{1,0:T(8,128)S(1)}, u32[]{:S(2)}, u32[]{:S(2)}) collective-permute-start(f32[200,256]{1,0:T(8,128)S(1)} %get-tuple-element.44), channel_id=1, source_target_pairs={{0,1},{1,2},{2,3},{3,0},{4,5},{5,6},{6,7},{7,4},{8,9},{9,10},{10,1... | collective-permute-start | bytes 614408 | tf_op jit(solution)/shard_map/ppermute | solution.py:550
  129.9 7.5 %collective-permute-start.14 = (f32[200,256]{1,0:T(8,128)S(1)}, f32[200,256]{1,0:T(8,128)S(1)}, u32[]{:S(2)}, u32[]{:S(2)}) collective-permute-start(f32[200,256]{1,0:T(8,128)S(1)} %get-tuple-element.45), channel_id=1, source_target_pairs={{1,0},{2,1},{3,2},{0,3},{5,4},{6,5},{7,6},{4,7},{9,8},{10,9},{11,1... | collective-permute-start | bytes 614408 | tf_op jit(solution)/shard_map/ppermute | solution.py:551
  137.8 7.6 %collective-permute-start.15 = (f32[200,256]{1,0:T(8,128)S(1)}, f32[200,256]{1,0:T(8,128)S(1)}, u32[]{:S(2)}, u32[]{:S(2)}) collective-permute-start(f32[200,256]{1,0:T(8,128)S(1)} %get-tuple-element.47), channel_id=1, source_target_pairs={{0,4},{1,5},{2,6},{3,7},{4,0},{5,1},{6,2},{7,3},{8,12},{9,13},{10,... | collective-permute-start | bytes 614408 | tf_op jit(solution)/shard_map/ppermute | solution.py:449
  143.3 4.3 %collective-permute-start.16 = (f32[56,256]{1,0:T(8,128)S(1)}, f32[56,256]{1,0:T(8,128)S(1)}, u32[]{:S(2)}, u32[]{:S(2)}) collective-permute-start(f32[56,256]{1,0:T(8,128)S(1)} %get-tuple-element.49), channel_id=1, source_target_pairs={{0,16},{8,24},{16,0},{24,8},{32,48},{40,56},{48,32},{56,40},{64,80... | collective-permute-start | bytes 172040 | tf_op jit(solution)/shard_map/ppermute | solution.py:449

commit v7 on v6

--- a/solution.py
+++ b/solution.py
@@ -152,18 +152,21 @@
         col_out[...] = settle(col_high, col_sum, blocks)
 
 
+def all_scores(x_ref, y_ref, scale, blocks, scores_ref):
+    everything = x_ref[...].reshape(blocks * BLK, BLK)
+    for t in range(blocks):
+        scores_ref[t] = (cross(everything, y_ref[t]) * scale).reshape(blocks, BLK, BLK)
+
+
 def first_kernel(scale, blocks, pairs_ref, count_ref, x_ref, y_ref, *rest):
-    scores_ref, f_out, g_out, row_out, col_out = rest[:5]
-    scratch = rest[5:]
+    f_out, g_out, row_out, col_out = rest[:4]
+    scratch, scores_ref = rest[4:-1], rest[-1]
+    all_scores(x_ref, y_ref, scale, blocks, scores_ref)
     f_wide, g_wide = scratch[:2]
     f_columns, g_columns = [], []
     for b in range(blocks):
         f_columns.append(norm(x_ref[b], scale))
         f_wide[b] = jnp.broadcast_to(f_columns[b], (BLK, 128))
-    everything = x_ref[...].reshape(blocks * BLK, BLK)
-    for b in range(blocks):
-        scores = cross(everything, y_ref[b]) * scale
-        scores_ref[b] = scores.reshape(blocks, BLK, BLK)
         g_columns.append(norm(y_ref[b], scale))
     f, g = across(f_columns), across(g_columns)
     f_out[...] = f
@@ -173,10 +176,11 @@
     sweep(pairs_ref, count_ref[0], x_ref, y_ref, scores_ref, f, g, shift, scale, blocks, outs, scratch)
 
 
-def second_kernel(n_row, scale, blocks, pairs_ref, count_ref, x_ref, y_ref, scores_ref, f_old, g_old, *rest):
+def second_kernel(n_row, scale, blocks, pairs_ref, count_ref, x_ref, y_ref, f_old, g_old, *rest):
     parts, rest = rest[: n_row + 1], rest[n_row + 1 :]
     f_out, g_out, row_out, col_out = rest[:4]
-    scratch = rest[4:]
+    scratch, scores_ref = rest[4:-1], rest[-1]
+    all_scores(x_ref, y_ref, scale, blocks, scores_ref)
     f = new_potential(f_old, parts[:n_row])
     g = new_potential(g_old, parts[n_row:])
     f_out[...] = f
@@ -235,12 +239,13 @@
         lanes_ref[b] = jnp.broadcast_to(values[b : b + 1], (8, BLK))
 
 
-def maps_kernel(n_row, scale, blocks, place_ref, pairs_ref, count_ref, x_ref, y_ref, scores_ref, f_old, g_old, *rest):
+def maps_kernel(n_row, scale, blocks, place_ref, pairs_ref, count_ref, x_ref, y_ref, f_old, g_old, *rest):
     parts, rest = rest[: n_row + 1], rest[n_row + 1 :]
-    keep_out, send_out, own, up, down, up_next, down_next = rest[:7]
+    keep_out, send_out, own, up_first, down_first, up_own, down_own = rest[:7]
     scratch = rest[7:16]
     f_wide, g_wide, row_high, row_sum, col_high, col_sum, lanes, row_acc, col_acc = scratch
-    x_turned, forward, backward, turned, logs, lines_ref, *weights = rest[16:]
+    scores_ref, x_turned, forward, backward, turned, logs, lines_ref, *weights = rest[16:]
+    all_scores(x_ref, y_ref, scale, blocks, scores_ref)
     kept = count_ref[0]
     f = new_potential(f_old, parts[:n_row])
     g = new_potential(g_old, parts[n_row:])
@@ -334,14 +339,14 @@
         out[:rows, :] = forward[pl.ds(pl.multiple_of(to * rows, 16), rows), :]
         out[rows : rows + 1, :] = lines_ref[to]
 
-    put(up.at[0], 2, 0)
-    put(up.at[1], 1, 1)
-    put(down.at[0], 2, 1)
-    put(down.at[1], 3, 0)
+    put(up_first, 2, 0)
+    put(down_first, 2, 1)
     put(own.at[0], 0, 0)
     put(own.at[1], 0, 1)
-    put(up_next, 1, 0)
-    put(down_next, 3, 1)
+    put(up_own.at[0], 1, 0)
+    put(up_own.at[1], 1, 1)
+    put(down_own.at[0], 3, 1)
+    put(down_own.at[1], 3, 0)
 
     half = keep_out.shape[0]
     small = blocks * BLK // (2 * half)
@@ -395,14 +400,18 @@
         put_blend(out, blend(parts, rows), rows)
 
 
-def relay_kernel(rows, up_next, up_came, down_next, down_came, up_out, down_out):
-    put_blend(up_out, blend([up_next, up_came.at[0]], rows), rows)
-    put_blend(down_out, blend([down_next, down_came.at[0]], rows), rows)
-
-
-def x_kernel(rows, place_ref, own, up_came, down_came, up_second, down_second, keep_ref, send_ref):
-    low = blend([own.at[0], up_second, down_came.at[1]], rows)
-    high = blend([own.at[1], down_second, up_came.at[1]], rows)
+def relay_kernel(
+    f_rows, b_rows, keep, came, up_own, up_came, down_own, down_came, paired, up_out, down_out
+):
+    pair_kernel(b_rows, keep, came, paired)
+    for own, relayed, out in ((up_own, up_came, up_out), (down_own, down_came, down_out)):
+        put_blend(out.at[0], blend([own.at[0], relayed], f_rows), f_rows)
+        out[1] = own[1]
+
+
+def x_kernel(rows, place_ref, own, up_came, down_came, keep_ref, send_ref):
+    low = blend([own.at[0], up_came.at[0], down_came.at[1]], rows)
+    high = blend([own.at[1], down_came.at[0], up_came.at[1]], rows)
 
     @pl.when(place_ref[0] == 0)
     def _():
@@ -430,7 +439,7 @@
 def sums_scratch(blocks):
     wide = pltpu.VMEM((blocks, BLK, 128), jnp.float32)
     deep = pltpu.VMEM((blocks, 8, BLK), jnp.float32)
-    return [wide] * 2 + [deep] * 5 + [wide, deep]
+    return [wide] * 2 + [deep] * 5 + [wide, deep, pltpu.VMEM((blocks, blocks, BLK, BLK), jnp.float32)]
 
 
 def per_device(n_src, n_tgt, sources, targets, pairs, counts):
@@ -442,7 +451,7 @@
     pair_list = jnp.transpose(pairs[0, 0])
     kept = counts.reshape(-1)
     smem = pl.BlockSpec(memory_space=pltpu.SMEM)
-    large = pltpu.CompilerParams(vmem_limit_bytes=24 * 1024 * 1024)
+    large = pltpu.CompilerParams(vmem_limit_bytes=36 * 1024 * 1024)
     little = pltpu.CompilerParams(vmem_limit_bytes=8 * 1024 * 1024)
 
     def swap(value, axis, size, bit):
@@ -452,19 +461,18 @@
     along_z = [list(range(k, n_src, 4)) for k in range(4)]
 
     def exchange(row, col):
-        col = log_sum([col, swap(col, "src", n_src, 1)])
         row = log_sum([row, swap(row, "tgt", n_tgt, RING)])
-        col = log_sum([col, swap(col, "src", n_src, 2)])
+        col = log_sum([col] + [swap(col, "src", n_src, bits) for bits in (1, 2, 3)])
         row = log_sum([row, swap(row, "tgt", n_tgt, 2)])
         copies = jnp.broadcast_to(col[None], (n_z, *col.shape))
         cols = lax.all_to_all(copies, "src", 0, 0, axis_index_groups=along_z, tiled=True)
         return [row, swap(row, "tgt", n_tgt, 1), cols]
 
-    scores, f, g, row, col = pl.pallas_call(
+    f, g, row, col = pl.pallas_call(
         functools.partial(first_kernel, scale, blocks),
-        out_shape=[shape(blocks, blocks, BLK, BLK)] + [shape(8, BLK)] * 4,
+        out_shape=[shape(8, BLK)] * 4,
         in_specs=[smem] * 2 + in_vmem(2),
-        out_specs=in_vmem(5),
+        out_specs=in_vmem(4),
         scratch_shapes=sums_scratch(blocks),
         compiler_params=large,
     )(pair_list, kept, x, y)
@@ -472,11 +480,11 @@
     f, g, row, col = pl.pallas_call(
         functools.partial(second_kernel, 2, scale, blocks),
         out_shape=[shape(8, BLK)] * 4,
-        in_specs=[smem] * 2 + in_vmem(8),
+        in_specs=[smem] * 2 + in_vmem(7),
         out_specs=in_vmem(4),
         scratch_shapes=sums_scratch(blocks),
         compiler_params=large,
-    )(pair_list, kept, x, y, scores, f, g, *parts)
+    )(pair_list, kept, x, y, f, g, *parts)
     parts = exchange(row, col)
 
     f_rows, b_rows = blocks * BLK // n_tgt, blocks * BLK // n_src
@@ -484,22 +492,21 @@
     s_at = lax.axis_index("src").astype(jnp.int32)
     t_at = lax.axis_index("tgt").astype(jnp.int32)
 
-    def call(kernel, operands, outs, places=(), cost=None):
+    def call(kernel, operands, outs, places=()):
         return pl.pallas_call(
             kernel,
             out_shape=outs,
             in_specs=[smem] * len(places) + in_vmem(len(operands)),
             out_specs=in_vmem(len(outs)),
             compiler_params=little,
-            cost_estimate=cost,
         )(*places, *operands)
 
     block = shape(f_rows + 8, width)
     two = shape(2, f_rows + 8, width)
-    keep, send, own, up, down, up_next, down_next = pl.pallas_call(
+    keep, send, own, up_first, down_first, up_own, down_own = pl.pallas_call(
         functools.partial(maps_kernel, 2, scale, blocks),
-        out_shape=[shape(half, b_rows + 8, width)] * 2 + [two, two, two, block, block],
-        in_specs=[smem] * 3 + in_vmem(8),
+        out_shape=[shape(half, b_rows + 8, width)] * 2 + [two, block, block, two, two],
+        in_specs=[smem] * 3 + in_vmem(7),
         out_specs=in_vmem(7),
         scratch_shapes=sums_scratch(blocks)
         + [
@@ -513,14 +520,17 @@
             pltpu.VMEM((2, BLK, BLK), jnp.bfloat16),
         ],
         compiler_params=large,
-    )(jnp.stack([s_at % 2, t_at % RING]), pair_list, kept, x, y, scores, f, g, *parts)
+    )(jnp.stack([s_at % 2, t_at % RING]), pair_list, kept, x, y, f, g, *parts)
     came = swap(send, "src", n_src, 1)
 
-    (paired,) = call(
-        functools.partial(pair_kernel, b_rows),
-        [keep, came],
-        [shape(half, b_rows + 8, width)],
-        cost=pl.CostEstimate(flops=10**10, bytes_accessed=3 * 10**7, transcendentals=0),
+    ups = [(k, k // RING * RING + (k + 1) % RING) for k in range(n_tgt)]
+    downs = [(b, a) for a, b in ups]
+    up_came = lax.ppermute(up_first, "tgt", ups)
+    down_came = lax.ppermute(down_first, "tgt", downs)
+    paired, up, down = call(
+        functools.partial(relay_kernel, f_rows, b_rows),
+        [keep, came, up_own, up_came, down_own, down_came],
+        [shape(half, b_rows + 8, width), two, two],
     )
     backward = lax.all_to_all(
         paired.reshape(n_z, 2, b_rows + 8, width),
@@ -537,21 +547,11 @@
     came = swap(send, "src", n_src, 2)
     (backward,) = call(functools.partial(last_kernel, b_rows), [keep, came], [shape(b_rows, width)])
 
-    ups = [(k, k // RING * RING + (k + 1) % RING) for k in range(n_tgt)]
-    downs = [(b, a) for a, b in ups]
     up_came = lax.ppermute(up, "tgt", ups)
     down_came = lax.ppermute(down, "tgt", downs)
-    up_came, down_came, _ = lax.optimization_barrier((up_came, down_came, paired))
-    up, down = call(
-        functools.partial(relay_kernel, f_rows),
-        [up_next, up_came, down_next, down_came],
-        [block, block],
-    )
-    up_second = lax.ppermute(up, "tgt", ups)
-    down_second = lax.ppermute(down, "tgt", downs)
     keep, send = call(
         functools.partial(x_kernel, f_rows),
-        [own, up_came, down_came, up_second, down_second],
+        [own, up_came, down_came],
         [block, block],
         [(t_at // RING).reshape(1)],
     )

time: 149 us -> 141 us (0.946)
  starting transfers between devices: 29.5 us -> 61.3 us
  Pallas kernels: 52.1 us -> 26.7 us
  local copies, waits for them, and re-layouts: 18.2 us -> 4.22 us
    ppermute x13 -> x15, starting transfers between devices: 5.77 us -> 25.9 us  [swap(): return lax.ppermute(value, axis, [(k, k ^ bit) for k in range(size)])]
    pallas_call x1, Pallas kernels: 28.5 us -> 12.4 us  [per_device(): pl.pallas_call(functools.partial(maps_kernel, 2, scale, blocks), out_shap...]
    unnamed x24 -> x10, local copies, waits for them, and re-layouts: 16.9 us -> 2.94 us
    ppermute x2, starting transfers between devices: 3.31 us -> 15.3 us  [the longest x1 15.3 us: per_device(): up_came = lax.ppermute(up_first, 'tgt', ups)]
    ppermute x13 -> x15, waiting for transfers between devices: 20 us -> 8.15 us  [swap(): return lax.ppermute(value, axis, [(k, k ^ bit) for k in range(size)])]
    all_to_all x1, waiting for transfers between devices: 5.05 us -> 12.7 us  [per_device(): lax.all_to_all(paired.reshape(n_z, 2, b_rows + 8, width), 'src', 0, 0, ax...]
    pallas_call x1, Pallas kernels: 10.2 us -> 5.21 us  [per_device(): pl.pallas_call(functools.partial(first_kernel, scale, blocks), out_shape=...]
    pallas_call x1, Pallas kernels: 9.18 us -> 5.14 us  [per_device(): pl.pallas_call(functools.partial(second_kernel, 2, scale, blocks), out_sh...]
  transfers between devices with their start and end apart: 20 -> 22, of which waited for: 13 -> 9; matrix products, arithmetic and copies ran while one was open for 1% -> 1% of each run, Pallas kernels for 1% -> 1%
where the time goes in v7:
time: 141 us; the launch traced here: 140 us
  starting transfers between devices  61.3 us (43%)
  waiting for transfers between devices  45.9 us (33%)
  Pallas kernels  26.7 us (19%)
  local copies, waits for them, and re-layouts  4.22 us (3%)
    ppermute x15, starting transfers between devices, swap(): return lax.ppermute(value, axis, [(k, k ^ bit) for k in range(size)])  25.9 us
    ppermute x1, starting transfers between devices, per_device(): up_came = lax.ppermute(up_first, 'tgt', ups)  15.3 us
    all_to_all x2, starting transfers between devices, exchange(): lax.all_to_all(copies, 'src', 0, 0, axis_index_groups=along_z, tiled=True)  13.2 us
    all_to_all x1, waiting for transfers between devices, per_device(): lax.all_to_all(paired.reshape(n_z, 2, b_rows + 8, width), 'src', 0, 0, ax...  12.7 us
    pallas_call x1, Pallas kernels, per_device(): pl.pallas_call(functools.partial(maps_kernel, 2, scale, blocks), out_shap...  12.4 us
    all_to_all x2, waiting for transfers between devices, exchange(): lax.all_to_all(copies, 'src', 0, 0, axis_index_groups=along_z, tiled=True)  9.22 us
    ppermute x1, waiting for transfers between devices, per_device(): up_came = lax.ppermute(up, 'tgt', ups)  8.67 us
    ppermute x15, waiting for transfers between devices, swap(): return lax.ppermute(value, axis, [(k, k ^ bit) for k in range(size)])  8.15 us
  transfers between devices with their start and end apart: 22, of which 9 were waited for; matrix products, arithmetic and copies ran while one was open for 1% of the time, Pallas kernels for 1%

profile of v7, /device:TPU:8, one launch (start us, length us, event | category | flops | bytes accessed | tf_op | source)
XLA Modules:
  0.0 139.6 jit_solution(9208946419269706379)
XLA Ops:
  1.3 0.7 copy-done.4
  2.0 1.1 copy-done
  3.1 1.1 copy-done.2
  4.2 5.2 %shard_map.59 = (f32[8,256]{1,0:T(8,128)S(1)}, f32[8,256]{1,0:T(8,128)S(1)}, f32[8,256]{1,0:T(8,128)S(1)}, f32[8,256]{1,0:T(8,128)S(1)}) custom-call(s32[2,24]{1,0:T(2,128)S(1)} %bitcast.20, s32[1]{0:T(128)} %bitcast.11.count_ref, bf16[6,256,256]{2,1,0:T(8,128)(2,1)S(1)} %bitcast.14, bf16[6,256,256]{2,1,0:T(8,128)(2,1)S(1)} %bitcast.17), custom_call_target="tpu_custom_call" | custom-call | tf_op jit(solution)/shard_map/pallas_call | solution.py:471
  9.4 5.5 %collective-permute-start = (f32[8,256]{1,0:T(8,128)S(1)}, f32[8,256]{1,0:T(8,128)S(1)}, u32[]{:S(2)}, u32[]{:S(2)}) collective-permute-start(f32[8,256]{1,0:T(8,128)S(1)} %get-tuple-element.26), channel_id=1, source_target_pairs={{0,4},{1,5},{2,6},{3,7},{4,0},{5,1},{6,2},{7,3},{8,12},{9,13},{10,... | collective-permute-start | bytes 24584 | tf_op jit(solution)/shard_map/ppermute | solution.py:458
  14.9 1.9 %collective-permute-start.3 = (f32[8,256]{1,0:T(8,128)S(1)}, f32[8,256]{1,0:T(8,128)S(1)}, u32[]{:S(2)}, u32[]{:S(2)}) collective-permute-start(f32[8,256]{1,0:T(8,128)S(1)} %get-tuple-element.27), channel_id=1, source_target_pairs={{0,8},{8,0},{16,24},{24,16},{32,40},{40,32},{48,56},{56,48},{64,72... | collective-permute-start | bytes 24584 | tf_op jit(solution)/shard_map/ppermute | solution.py:458
  16.8 4.5 %collective-permute-start.1 = (f32[8,256]{1,0:T(8,128)S(1)}, f32[8,256]{1,0:T(8,128)S(1)}, u32[]{:S(2)}, u32[]{:S(2)}) collective-permute-start(f32[8,256]{1,0:T(8,128)S(1)} %multiply_add_fusion.5), channel_id=1, source_target_pairs={{0,2},{1,3},{2,0},{3,1},{4,6},{5,7},{6,4},{7,5},{8,10},{9,11},{10,... | collective-permute-start | bytes 24584 | tf_op jit(solution)/shard_map/ppermute | solution.py:458
  21.4 0.6 broadcast_in_dim.4
  22.0 9.1 %all-to-all-start = ((f32[8,8,256]{2,1,0:T(8,128)}), f32[8,8,256]{2,1,0:T(8,128)S(1)}, u32[]{:S(2)}, u32[]{:S(2)}) async-start(f32[8,8,256]{2,1,0:T(8,128)} %broadcast_in_dim.4), calls=%async_computation | async-start | bytes 131072 | tf_op jit(solution)/shard_map/all_to_all | solution.py:468
  31.2 3.6 %collective-permute-done.2.rest_1_ = f32[8,256]{1,0:T(8,128)S(1)} collective-permute-done((f32[8,256]{1,0:T(8,128)S(1)}, f32[8,256]{1,0:T(8,128)S(1)}, u32[]{:S(2)}, u32[]{:S(2)}) %collective-permute-start.2) | collective-permute-done | bytes 8224 | tf_op jit(solution)/shard_map/ppermute | solution.py:458
  34.9 4.6 %all-to-all-done.rest_2_ = f32[8,8,256]{2,1,0:T(8,128)S(1)} async-done(((f32[8,8,256]{2,1,0:T(8,128)}), f32[8,8,256]{2,1,0:T(8,128)S(1)}, u32[]{:S(2)}, u32[]{:S(2)}) %all-to-all-start) | async-done | bytes 65568 | tf_op jit(solution)/shard_map/all_to_all | solution.py:468
  39.5 5.1 %shard_map.60 = (f32[8,256]{1,0:T(8,128)S(1)}, f32[8,256]{1,0:T(8,128)S(1)}, f32[8,256]{1,0:T(8,128)S(1)}, f32[8,256]{1,0:T(8,128)S(1)}) custom-call(s32[2,24]{1,0:T(2,128)S(1)} %bitcast.21, s32[1]{0:T(128)} %bitcast.12.count_ref, bf16[6,256,256]{2,1,0:T(8,128)(2,1)S(1)} %bitcast.15, bf16[6,256,256]{2,1,0:T(8,128)(2,1)S(1)} %bitcast.18, ...), custom_call_target="tpu_custom_call" | custom-call | tf_op jit(solution)/shard_map/pallas_call | solution.py:480
  44.6 5.5 %collective-permute-start.6 = (f32[8,256]{1,0:T(8,128)S(1)}, f32[8,256]{1,0:T(8,128)S(1)}, u32[]{:S(2)}, u32[]{:S(2)}) collective-permute-start(f32[8,256]{1,0:T(8,128)S(1)} %get-tuple-element.30), channel_id=1, source_target_pairs={{0,4},{1,5},{2,6},{3,7},{4,0},{5,1},{6,2},{7,3},{8,12},{9,13},{10,... | collective-permute-start | bytes 24584 | tf_op jit(solution)/shard_map/ppermute | solution.py:458
  50.1 1.9 %collective-permute-start.9 = (f32[8,256]{1,0:T(8,128)S(1)}, f32[8,256]{1,0:T(8,128)S(1)}, u32[]{:S(2)}, u32[]{:S(2)}) collective-permute-start(f32[8,256]{1,0:T(8,128)S(1)} %get-tuple-element.31), channel_id=1, source_target_pairs={{0,8},{8,0},{16,24},{24,16},{32,40},{40,32},{48,56},{56,48},{64,72... | collective-permute-start | bytes 24584 | tf_op jit(solution)/shard_map/ppermute | solution.py:458
  52.0 2.7 %collective-permute-start.7 = (f32[8,256]{1,0:T(8,128)S(1)}, f32[8,256]{1,0:T(8,128)S(1)}, u32[]{:S(2)}, u32[]{:S(2)}) collective-permute-start(f32[8,256]{1,0:T(8,128)S(1)} %multiply_add_fusion.2), channel_id=1, source_target_pairs={{0,2},{1,3},{2,0},{3,1},{4,6},{5,7},{6,4},{7,5},{8,10},{9,11},{10,... | collective-permute-start | bytes 24584 | tf_op jit(solution)/shard_map/ppermute | solution.py:458
  55.4 4.1 %all-to-all-start.1 = ((f32[8,8,256]{2,1,0:T(8,128)}), f32[8,8,256]{2,1,0:T(8,128)S(1)}, u32[]{:S(2)}, u32[]{:S(2)}) async-start(f32[8,8,256]{2,1,0:T(8,128)} %broadcast_in_dim.5), calls=%async_computation.1 | async-start | bytes 131072 | tf_op jit(solution)/shard_map/all_to_all | solution.py:468
  59.9 3.3 %collective-permute-done.8.rest_1_ = f32[8,256]{1,0:T(8,128)S(1)} collective-permute-done((f32[8,256]{1,0:T(8,128)S(1)}, f32[8,256]{1,0:T(8,128)S(1)}, u32[]{:S(2)}, u32[]{:S(2)}) %collective-permute-start.8) | collective-permute-done | bytes 8224 | tf_op jit(solution)/shard_map/ppermute | solution.py:458
  63.2 4.6 %all-to-all-done.1.rest_2_ = f32[8,8,256]{2,1,0:T(8,128)S(1)} async-done(((f32[8,8,256]{2,1,0:T(8,128)}), f32[8,8,256]{2,1,0:T(8,128)S(1)}, u32[]{:S(2)}, u32[]{:S(2)}) %all-to-all-start.1) | async-done | bytes 65568 | tf_op jit(solution)/shard_map/all_to_all | solution.py:468
  67.9 12.4 %shard_map.61 = (f32[16,56,256]{2,1,0:T(8,128)S(1)}, f32[16,56,256]{2,1,0:T(8,128)S(1)}, f32[2,200,256]{2,1,0:T(8,128)S(1)}, f32[200,256]{1,0:T(8,128)S(1)}, f32...) custom-call(s32[2]{0:T(128)S(1)} %pad_add_fusion.place_ref, s32[2,24]{1,0:T(2,128)S(1)} %bitcast.22, ...), custom_call_target="tpu_custom_call" | custom-call | tf_op jit(solution)/shard_map/pallas_call | solution.py:506
  80.2 0.8 collective-permute-start.12
  81.0 15.3 %collective-permute-start.13 = (f32[200,256]{1,0:T(8,128)S(1)}, f32[200,256]{1,0:T(8,128)S(1)}, u32[]{:S(2)}, u32[]{:S(2)}) collective-permute-start(f32[200,256]{1,0:T(8,128)S(1)} %get-tuple-element.36), channel_id=1, source_target_pairs={{0,1},{1,2},{2,3},{3,0},{4,5},{5,6},{6,7},{7,4},{8,9},{9,10},{10,1... | collective-permute-start | bytes 614408 | tf_op jit(solution)/shard_map/ppermute | solution.py:528
  96.3 4.9 %collective-permute-done.13.up_came = f32[200,256]{1,0:T(8,128)S(1)} collective-permute-done((f32[200,256]{1,0:T(8,128)S(1)}, f32[200,256]{1,0:T(8,128)S(1)}, u32[]{:S(2)}, u32[]{:S(2)}) %collective-permute-start.13) | collective-permute-done | bytes 204832 | tf_op jit(solution)/shard_map/ppermute | solution.py:528
  101.3 2.2 %collective-permute-done.14.down_came = f32[200,256]{1,0:T(8,128)S(1)} collective-permute-done((f32[200,256]{1,0:T(8,128)S(1)}, f32[200,256]{1,0:T(8,128)S(1)}, u32[]{:S(2)}, u32[]{:S(2)}) %collective-permute-start.14) | collective-permute-done | bytes 204832 | tf_op jit(solution)/shard_map/ppermute | solution.py:529
  103.5 1.4 %shard_map.62 = (f32[16,56,256]{2,1,0:T(8,128)}, f32[2,200,256]{2,1,0:T(8,128)S(1)}, f32[2,200,256]{2,1,0:T(8,128)S(1)}) custom-call(f32[16,56,256]{2,1,0:T(8,128)S(1)} %get-tuple-element.33.keep, f32[16,56,256]{2,1,0:T(8,128)S(1)} %collective-permute-done.12.came, f32[2,200,256]{2,1,0:T(8,128)S(1)} %get-tuple-element.35.up_own, ...), custom_call_target="tpu_custom_call" | custom-call | tf_op jit(solution)/shard_map/pallas_call | solution.py:496
  104.9 3.6 %all-to-all-start.2 = ((f32[8,2,56,256]{3,2,1,0:T(8,128)}), f32[8,2,56,256]{3,2,1,0:T(8,128)S(1)}, u32[]{:S(2)}, u32[]{:S(2)}) async-start(f32[8,2,56,256]{3,2,1,0:T(8,128)} %bitcast.10), calls=%async_computation.2 | async-start | bytes 1835008 | tf_op jit(solution)/shard_map/all_to_all | solution.py:535
  108.8 3.0 %collective-permute-start.16 = (f32[2,200,256]{2,1,0:T(8,128)S(1)}, f32[2,200,256]{2,1,0:T(8,128)S(1)}, u32[]{:S(2)}, u32[]{:S(2)}) collective-permute-start(f32[2,200,256]{2,1,0:T(8,128)S(1)} %get-tuple-element.40), channel_id=1, source_target_pairs={{1,0},{2,1},{3,2},{0,3},{5,4},{6,5},{7,6},{4,7},{9,8},{10,9},{11,1... | collective-permute-start | bytes 1228808 | tf_op jit(solution)/shard_map/ppermute | solution.py:551
  111.8 8.7 %collective-permute-done.15.up_came = f32[2,200,256]{2,1,0:T(8,128)S(1)} collective-permute-done((f32[2,200,256]{2,1,0:T(8,128)S(1)}, f32[2,200,256]{2,1,0:T(8,128)S(1)}, u32[]{:S(2)}, u32[]{:S(2)}) %collective-permute-start.15) | collective-permute-done | bytes 409632 | tf_op jit(solution)/shard_map/ppermute | solution.py:550
  121.4 12.7 %all-to-all-done.2.parts_ref = f32[8,2,56,256]{3,2,1,0:T(8,128)S(1)} async-done(((f32[8,2,56,256]{3,2,1,0:T(8,128)}), f32[8,2,56,256]{3,2,1,0:T(8,128)S(1)}, u32[]{:S(2)}, u32[]{:S(2)}) %all-to-all-start.2) | async-done | bytes 917536 | tf_op jit(solution)/shard_map/all_to_all | solution.py:535
  134.4 2.3 %collective-permute-start.18 = (f32[56,256]{1,0:T(8,128)S(1)}, f32[56,256]{1,0:T(8,128)S(1)}, u32[]{:S(2)}, u32[]{:S(2)}) collective-permute-start(f32[56,256]{1,0:T(8,128)S(1)} %get-tuple-element.45), channel_id=1, source_target_pairs={{0,16},{8,24},{16,0},{24,8},{32,48},{40,56},{48,32},{56,40},{64,80... | collective-permute-start | bytes 172040 | tf_op jit(solution)/shard_map/ppermute | solution.py:458
  136.6 1.0 shard_map.64
  137.6 1.2 collective-permute-done.18.b_ref
  138.8 0.8 shard_map.66
  (39 shorter events, 2.9 us)
Async XLA Ops:
  1.3 0.7 copy-start.4
  2.0 1.1 copy-start
  3.1 1.1 copy-start.2
  4.2 35.2 %copy-start.1 = (bf16[1536,256]{1,0:T(8,128)(2,1)S(1)}, bf16[1536,256]{1,0:T(8,128)(2,1)}, u32[]{:S(2)}) copy-start(bf16[1536,256]{1,0:T(8,128)(2,1)} %param.4) | copy-start | bytes 2359300
  4.2 35.2 %copy-start.3 = (bf16[1536,256]{1,0:T(8,128)(2,1)S(1)}, bf16[1536,256]{1,0:T(8,128)(2,1)}, u32[]{:S(2)}) copy-start(bf16[1536,256]{1,0:T(8,128)(2,1)} %param.5) | copy-start | bytes 2359300
  9.4 7.3 %collective-permute-start = (f32[8,256]{1,0:T(8,128)S(1)}, f32[8,256]{1,0:T(8,128)S(1)}, u32[]{:S(2)}, u32[]{:S(2)}) collective-permute-start(f32[8,256]{1,0:T(8,128)S(1)} %get-tuple-element.26), channel_id=1, source_target_pairs={{0,4},{1,5},{2,6},{3,7},{4,0},{5,1},{6,2},{7,3},{8,12},{9,13},{10,... | collective-permute-start | bytes 24584 | tf_op jit(solution)/shard_map/ppermute | solution.py:458
  14.9 6.4 %collective-permute-start.5 = (f32[8,256]{1,0:T(8,128)S(1)}, f32[8,256]{1,0:T(8,128)S(1)}, u32[]{:S(2)}, u32[]{:S(2)}) collective-permute-start(f32[8,256]{1,0:T(8,128)S(1)} %get-tuple-element.27), channel_id=1, source_target_pairs={{0,24},{8,16},{16,8},{24,0},{32,56},{40,48},{48,40},{56,32},{64,88... | collective-permute-start | bytes 24584 | tf_op jit(solution)/shard_map/ppermute | solution.py:458
  14.9 6.4 %collective-permute-start.4 = (f32[8,256]{1,0:T(8,128)S(1)}, f32[8,256]{1,0:T(8,128)S(1)}, u32[]{:S(2)}, u32[]{:S(2)}) collective-permute-start(f32[8,256]{1,0:T(8,128)S(1)} %get-tuple-element.27), channel_id=1, source_target_pairs={{0,16},{8,24},{16,0},{24,8},{32,48},{40,56},{48,32},{56,40},{64,80... | collective-permute-start | bytes 24584 | tf_op jit(solution)/shard_map/ppermute | solution.py:458
  14.9 6.4 %collective-permute-start.3 = (f32[8,256]{1,0:T(8,128)S(1)}, f32[8,256]{1,0:T(8,128)S(1)}, u32[]{:S(2)}, u32[]{:S(2)}) collective-permute-start(f32[8,256]{1,0:T(8,128)S(1)} %get-tuple-element.27), channel_id=1, source_target_pairs={{0,8},{8,0},{16,24},{24,16},{32,40},{40,32},{48,56},{56,48},{64,72... | collective-permute-start | bytes 24584 | tf_op jit(solution)/shard_map/ppermute | solution.py:458
  16.8 14.3 %collective-permute-start.1 = (f32[8,256]{1,0:T(8,128)S(1)}, f32[8,256]{1,0:T(8,128)S(1)}, u32[]{:S(2)}, u32[]{:S(2)}) collective-permute-start(f32[8,256]{1,0:T(8,128)S(1)} %multiply_add_fusion.5), channel_id=1, source_target_pairs={{0,2},{1,3},{2,0},{3,1},{4,6},{5,7},{6,4},{7,5},{8,10},{9,11},{10,... | collective-permute-start | bytes 24584 | tf_op jit(solution)/shard_map/ppermute | solution.py:458
  22.0 17.5 %all-to-all-start = ((f32[8,8,256]{2,1,0:T(8,128)}), f32[8,8,256]{2,1,0:T(8,128)S(1)}, u32[]{:S(2)}, u32[]{:S(2)}) async-start(f32[8,8,256]{2,1,0:T(8,128)} %broadcast_in_dim.4), calls=%async_computation | async-start | bytes 131072 | tf_op jit(solution)/shard_map/all_to_all | solution.py:468
  31.1 3.7 %collective-permute-start.2 = (f32[8,256]{1,0:T(8,128)S(1)}, f32[8,256]{1,0:T(8,128)S(1)}, u32[]{:S(2)}, u32[]{:S(2)}) collective-permute-start(f32[8,256]{1,0:T(8,128)S(1)} %multiply_add_fusion.4.rest_0_), channel_id=1, source_target_pairs={{0,1},{1,0},{2,3},{3,2},{4,5},{5,4},{6,7},{7,6},{8,9},{9,8},{10,11... | collective-permute-start | bytes 24584 | tf_op jit(solution)/shard_map/ppermute | solution.py:458
  44.6 7.3 %collective-permute-start.6 = (f32[8,256]{1,0:T(8,128)S(1)}, f32[8,256]{1,0:T(8,128)S(1)}, u32[]{:S(2)}, u32[]{:S(2)}) collective-permute-start(f32[8,256]{1,0:T(8,128)S(1)} %get-tuple-element.30), channel_id=1, source_target_pairs={{0,4},{1,5},{2,6},{3,7},{4,0},{5,1},{6,2},{7,3},{8,12},{9,13},{10,... | collective-permute-start | bytes 24584 | tf_op jit(solution)/shard_map/ppermute | solution.py:458
  50.1 4.6 %collective-permute-start.11 = (f32[8,256]{1,0:T(8,128)S(1)}, f32[8,256]{1,0:T(8,128)S(1)}, u32[]{:S(2)}, u32[]{:S(2)}) collective-permute-start(f32[8,256]{1,0:T(8,128)S(1)} %get-tuple-element.31), channel_id=1, source_target_pairs={{0,24},{8,16},{16,8},{24,0},{32,56},{40,48},{48,40},{56,32},{64,88... | collective-permute-start | bytes 24584 | tf_op jit(solution)/shard_map/ppermute | solution.py:458
  50.1 4.6 %collective-permute-start.10 = (f32[8,256]{1,0:T(8,128)S(1)}, f32[8,256]{1,0:T(8,128)S(1)}, u32[]{:S(2)}, u32[]{:S(2)}) collective-permute-start(f32[8,256]{1,0:T(8,128)S(1)} %get-tuple-element.31), channel_id=1, source_target_pairs={{0,16},{8,24},{16,0},{24,8},{32,48},{40,56},{48,32},{56,40},{64,80... | collective-permute-start | bytes 24584 | tf_op jit(solution)/shard_map/ppermute | solution.py:458
  50.1 4.6 %collective-permute-start.9 = (f32[8,256]{1,0:T(8,128)S(1)}, f32[8,256]{1,0:T(8,128)S(1)}, u32[]{:S(2)}, u32[]{:S(2)}) collective-permute-start(f32[8,256]{1,0:T(8,128)S(1)} %get-tuple-element.31), channel_id=1, source_target_pairs={{0,8},{8,0},{16,24},{24,16},{32,40},{40,32},{48,56},{56,48},{64,72... | collective-permute-start | bytes 24584 | tf_op jit(solution)/shard_map/ppermute | solution.py:458
  52.0 7.5 %collective-permute-start.7 = (f32[8,256]{1,0:T(8,128)S(1)}, f32[8,256]{1,0:T(8,128)S(1)}, u32[]{:S(2)}, u32[]{:S(2)}) collective-permute-start(f32[8,256]{1,0:T(8,128)S(1)} %multiply_add_fusion.2), channel_id=1, source_target_pairs={{0,2},{1,3},{2,0},{3,1},{4,6},{5,7},{6,4},{7,5},{8,10},{9,11},{10,... | collective-permute-start | bytes 24584 | tf_op jit(solution)/shard_map/ppermute | solution.py:458
  55.4 12.5 %all-to-all-start.1 = ((f32[8,8,256]{2,1,0:T(8,128)}), f32[8,8,256]{2,1,0:T(8,128)S(1)}, u32[]{:S(2)}, u32[]{:S(2)}) async-start(f32[8,8,256]{2,1,0:T(8,128)} %broadcast_in_dim.5), calls=%async_computation.1 | async-start | bytes 131072 | tf_op jit(solution)/shard_map/all_to_all | solution.py:468
  59.5 3.7 %collective-permute-start.8 = (f32[8,256]{1,0:T(8,128)S(1)}, f32[8,256]{1,0:T(8,128)S(1)}, u32[]{:S(2)}, u32[]{:S(2)}) collective-permute-start(f32[8,256]{1,0:T(8,128)S(1)} %multiply_add_fusion.1.rest_0_), channel_id=1, source_target_pairs={{0,1},{1,0},{2,3},{3,2},{4,5},{5,4},{6,7},{7,6},{8,9},{9,8},{10,11... | collective-permute-start | bytes 24584 | tf_op jit(solution)/shard_map/ppermute | solution.py:458
  80.2 23.2 %collective-permute-start.12 = (f32[16,56,256]{2,1,0:T(8,128)S(1)}, f32[16,56,256]{2,1,0:T(8,128)S(1)}, u32[]{:S(2)}, u32[]{:S(2)}) collective-permute-start(f32[16,56,256]{2,1,0:T(8,128)S(1)} %get-tuple-element.34), channel_id=1, source_target_pairs={{0,8},{8,0},{16,24},{24,16},{32,40},{40,32},{48,56},{56,48},{64,72... | collective-permute-start | bytes 2752520 | tf_op jit(solution)/shard_map/ppermute | solution.py:458
  81.0 20.2 %collective-permute-start.13 = (f32[200,256]{1,0:T(8,128)S(1)}, f32[200,256]{1,0:T(8,128)S(1)}, u32[]{:S(2)}, u32[]{:S(2)}) collective-permute-start(f32[200,256]{1,0:T(8,128)S(1)} %get-tuple-element.36), channel_id=1, source_target_pairs={{0,1},{1,2},{2,3},{3,0},{4,5},{5,6},{6,7},{7,4},{8,9},{9,10},{10,1... | collective-permute-start | bytes 614408 | tf_op jit(solution)/shard_map/ppermute | solution.py:528
  96.3 7.1 %collective-permute-start.14 = (f32[200,256]{1,0:T(8,128)S(1)}, f32[200,256]{1,0:T(8,128)S(1)}, u32[]{:S(2)}, u32[]{:S(2)}) collective-permute-start(f32[200,256]{1,0:T(8,128)S(1)} %get-tuple-element.38), channel_id=1, source_target_pairs={{1,0},{2,1},{3,2},{0,3},{5,4},{6,5},{7,6},{4,7},{9,8},{10,9},{11,1... | collective-permute-start | bytes 614408 | tf_op jit(solution)/shard_map/ppermute | solution.py:529
  104.9 29.2 %all-to-all-start.2 = ((f32[8,2,56,256]{3,2,1,0:T(8,128)}), f32[8,2,56,256]{3,2,1,0:T(8,128)S(1)}, u32[]{:S(2)}, u32[]{:S(2)}) async-start(f32[8,2,56,256]{3,2,1,0:T(8,128)} %bitcast.10), calls=%async_computation.2 | async-start | bytes 1835008 | tf_op jit(solution)/shard_map/all_to_all | solution.py:535
  108.5 12.0 %collective-permute-start.15 = (f32[2,200,256]{2,1,0:T(8,128)S(1)}, f32[2,200,256]{2,1,0:T(8,128)S(1)}, u32[]{:S(2)}, u32[]{:S(2)}) collective-permute-start(f32[2,200,256]{2,1,0:T(8,128)S(1)} %get-tuple-element.39), channel_id=1, source_target_pairs={{0,1},{1,2},{2,3},{3,0},{4,5},{5,6},{6,7},{7,4},{8,9},{9,10},{10,1... | collective-permute-start | bytes 1228808 | tf_op jit(solution)/shard_map/ppermute | solution.py:550
  108.8 11.6 %collective-permute-start.16 = (f32[2,200,256]{2,1,0:T(8,128)S(1)}, f32[2,200,256]{2,1,0:T(8,128)S(1)}, u32[]{:S(2)}, u32[]{:S(2)}) collective-permute-start(f32[2,200,256]{2,1,0:T(8,128)S(1)} %get-tuple-element.40), channel_id=1, source_target_pairs={{1,0},{2,1},{3,2},{0,3},{5,4},{6,5},{7,6},{4,7},{9,8},{10,9},{11,1... | collective-permute-start | bytes 1228808 | tf_op jit(solution)/shard_map/ppermute | solution.py:551
  120.9 15.8 %collective-permute-start.17 = (f32[200,256]{1,0:T(8,128)S(1)}, f32[200,256]{1,0:T(8,128)S(1)}, u32[]{:S(2)}, u32[]{:S(2)}) collective-permute-start(f32[200,256]{1,0:T(8,128)S(1)} %get-tuple-element.42), channel_id=1, source_target_pairs={{0,4},{1,5},{2,6},{3,7},{4,0},{5,1},{6,2},{7,3},{8,12},{9,13},{10,... | collective-permute-start | bytes 614408 | tf_op jit(solution)/shard_map/ppermute | solution.py:458
  134.4 4.4 %collective-permute-start.18 = (f32[56,256]{1,0:T(8,128)S(1)}, f32[56,256]{1,0:T(8,128)S(1)}, u32[]{:S(2)}, u32[]{:S(2)}) collective-permute-start(f32[56,256]{1,0:T(8,128)S(1)} %get-tuple-element.45), channel_id=1, source_target_pairs={{0,16},{8,24},{16,0},{24,8},{32,48},{40,56},{48,32},{56,40},{64,80... | collective-permute-start | bytes 172040 | tf_op jit(solution)/shard_map/ppermute | solution.py:458

commit v8 on v7

--- a/solution.py
+++ b/solution.py
@@ -394,19 +394,40 @@
         out[rows : rows + 1, :] = blended[1]
 
 
-def z_kernel(rows, place_ref, parts_ref, keep_ref, send_ref):
-    for out, low in ((keep_ref, place_ref[0]), (send_ref, 1 - place_ref[0])):
-        parts = [parts_ref.at[d, low] for d in range(parts_ref.shape[0])]
+def z_kernel(rows, place_ref, paired, up_came, down_came, keep_ref, send_ref):
+    here = 2 * place_ref[0]
+    for out, low in ((keep_ref, place_ref[1]), (send_ref, 1 - place_ref[1])):
+        parts = [paired.at[here + low], up_came.at[low], down_came.at[low]]
         put_blend(out, blend(parts, rows), rows)
 
 
-def relay_kernel(
-    f_rows, b_rows, keep, came, up_own, up_came, down_own, down_came, paired, up_out, down_out
-):
-    pair_kernel(b_rows, keep, came, paired)
+def relay_kernel(rows, up_own, up_came, down_own, down_came, up_out, down_out):
     for own, relayed, out in ((up_own, up_came, up_out), (down_own, down_came, down_out)):
-        put_blend(out.at[0], blend([own.at[0], relayed], f_rows), f_rows)
+        put_blend(out.at[0], blend([own.at[0], relayed], rows), rows)
         out[1] = own[1]
+
+
+def core_kernel(rows, place_ref, keep, came, paired, up_out, down_out):
+    pair_kernel(rows, keep, came, paired)
+    n = paired.shape[0] // 2
+    far = 2 * ((place_ref[0] + n // 2) % n)
+    up_out[...] = paired[far]
+    down_out[...] = paired[far + 1]
+
+
+def ring_kernel(rows, away, place_ref, paired, up_came, down_came, up_out, down_out):
+    n = paired.shape[0] // 2
+    up_at = 2 * ((place_ref[0] + away) % n)
+    down_at = 2 * ((place_ref[0] + n - away) % n)
+    for low in range(2):
+        for at, came, out, whole in ((up_at, up_came, up_out, 0), (down_at, down_came, down_out, 1)):
+            own = paired.at[at + low]
+            if len(came.shape) == 3:
+                put_blend(out.at[low], blend([own, came.at[low]], rows), rows)
+            elif low == whole:
+                put_blend(out.at[low], blend([own, came], rows), rows)
+            else:
+                out[low] = own[...]
 
 
 def x_kernel(rows, place_ref, own, up_came, down_came, keep_ref, send_ref):
@@ -527,26 +548,41 @@
     downs = [(b, a) for a, b in ups]
     up_came = lax.ppermute(up_first, "tgt", ups)
     down_came = lax.ppermute(down_first, "tgt", downs)
-    paired, up, down = call(
-        functools.partial(relay_kernel, f_rows, b_rows),
-        [keep, came, up_own, up_came, down_own, down_came],
-        [shape(half, b_rows + 8, width), two, two],
+    small = shape(b_rows + 8, width)
+    small_two = shape(2, b_rows + 8, width)
+    z_at = (s_at // 4).reshape(1)
+    paired, z_up, z_down = call(
+        functools.partial(core_kernel, b_rows),
+        [keep, came],
+        [shape(half, b_rows + 8, width), small, small],
+        [z_at],
     )
-    backward = lax.all_to_all(
-        paired.reshape(n_z, 2, b_rows + 8, width),
-        "src",
-        0,
-        0,
-        axis_index_groups=along_z,
-        tiled=True,
-    )
-    small = shape(b_rows + 8, width)
+    z_ups = [(k, (k + 4) % n_src) for k in range(n_src)]
+    z_downs = [(b, a) for a, b in z_ups]
+    for away in range(n_z // 2 - 1, -1, -1):
+        z_up = lax.ppermute(z_up, "src", z_ups)
+        z_down = lax.ppermute(z_down, "src", z_downs)
+        if away:
+            z_up, z_down = call(
+                functools.partial(ring_kernel, b_rows, away),
+                [paired, z_up, z_down],
+                [small_two, small_two],
+                [z_at],
+            )
     keep, send = call(
-        functools.partial(z_kernel, b_rows), [backward], [small, small], [(s_at // 2 % 2).reshape(1)]
+        functools.partial(z_kernel, b_rows),
+        [paired, z_up, z_down],
+        [small, small],
+        [jnp.stack([s_at // 4, s_at // 2 % 2])],
     )
     came = swap(send, "src", n_src, 2)
     (backward,) = call(functools.partial(last_kernel, b_rows), [keep, came], [shape(b_rows, width)])
 
+    up, down = call(
+        functools.partial(relay_kernel, f_rows),
+        [up_own, up_came, down_own, down_came],
+        [two, two],
+    )
     up_came = lax.ppermute(up, "tgt", ups)
     down_came = lax.ppermute(down, "tgt", downs)
     keep, send = call(

time: 141 us -> 142 us (level)
  Pallas kernels: 26.7 us -> 47 us
  starting transfers between devices: 61.3 us -> 51.9 us
  waiting for transfers between devices: 45.9 us -> 36.6 us
    ppermute x0 -> x8, starting transfers between devices: none -> 14.2 us  [the longest x4 12.5 us: per_device(): z_down = lax.ppermute(z_down, 'src', z_downs)]
    all_to_all x1 -> x0, waiting for transfers between devices: 12.7 us -> none  [per_device(): lax.all_to_all(paired.reshape(n_z, 2, b_rows + 8, width), 'src', 0, 0, ax...]
    ppermute x15, starting transfers between devices: 25.9 us -> 13.9 us  [swap(): return lax.ppermute(value, axis, [(k, k ^ bit) for k in range(size)])]
    pallas_call x1, Pallas kernels: 12.4 us -> 24 us  [per_device(): pl.pallas_call(functools.partial(maps_kernel, 2, scale, blocks), out_shap...]
    ppermute x1, waiting for transfers between devices: 8.67 us -> 0.01 us  [per_device(): up_came = lax.ppermute(up, 'tgt', ups)]
    ppermute x0 -> x8, waiting for transfers between devices: none -> 8.39 us  [the longest x4 8.38 us: per_device(): z_up = lax.ppermute(z_up, 'src', z_ups)]
    ppermute x1, starting transfers between devices: 15.3 us -> 7.78 us  [per_device(): up_came = lax.ppermute(up_first, 'tgt', ups)]
    ppermute x15, waiting for transfers between devices: 8.15 us -> 11.8 us  [swap(): return lax.ppermute(value, axis, [(k, k ^ bit) for k in range(size)])]
  transfers between devices with their start and end apart: 22 -> 29, of which waited for: 9 -> 13; matrix products, arithmetic and copies ran while one was open for 1% -> 1% of each run, Pallas kernels for 1% -> 4%
where the time goes in v8:
time: 142 us; the launch traced here: 141 us
  starting transfers between devices  51.9 us (37%)
  Pallas kernels  47 us (33%)
  waiting for transfers between devices  36.6 us (26%)
  local copies, waits for them, and re-layouts  4.23 us (3%)
  between operations  1.44 us (1%)
    pallas_call x1, Pallas kernels, per_device(): pl.pallas_call(functools.partial(maps_kernel, 2, scale, blocks), out_shap...  24 us
    ppermute x15, starting transfers between devices, swap(): return lax.ppermute(value, axis, [(k, k ^ bit) for k in range(size)])  13.9 us
    all_to_all x2, starting transfers between devices, exchange(): lax.all_to_all(copies, 'src', 0, 0, axis_index_groups=along_z, tiled=True)  12.9 us
    ppermute x4, starting transfers between devices, per_device(): z_down = lax.ppermute(z_down, 'src', z_downs)  12.5 us
    ppermute x15, waiting for transfers between devices, swap(): return lax.ppermute(value, axis, [(k, k ^ bit) for k in range(size)])  11.8 us
    all_to_all x2, waiting for transfers between devices, exchange(): lax.all_to_all(copies, 'src', 0, 0, axis_index_groups=along_z, tiled=True)  9.22 us
    ppermute x4, waiting for transfers between devices, per_device(): z_up = lax.ppermute(z_up, 'src', z_ups)  8.38 us
    pallas_call x1, Pallas kernels, per_device(): pl.pallas_call(functools.partial(first_kernel, scale, blocks), out_shape=...  8.31 us
  transfers between devices with their start and end apart: 29, of which 13 were waited for; matrix products, arithmetic and copies ran while one was open for 1% of the time, Pallas kernels for 4%

profile of v8, /device:TPU:8, one launch (start us, length us, event | category | flops | bytes accessed | tf_op | source)
XLA Modules:
  0.0 141.4 jit_solution(16119157689965129490)
XLA Ops:
  4.2 8.3 %shard_map.59 = (f32[8,256]{1,0:T(8,128)S(1)}, f32[8,256]{1,0:T(8,128)S(1)}, f32[8,256]{1,0:T(8,128)S(1)}, f32[8,256]{1,0:T(8,128)S(1)}) custom-call(s32[2,24]{1,0:T(2,128)S(1)} %bitcast.20, s32[1]{0:T(128)} %bitcast.11.count_ref, bf16[6,256,256]{2,1,0:T(8,128)(2,1)S(1)} %bitcast.14, bf16[6,256,256]{2,1,0:T(8,128)(2,1)S(1)} %bitcast.17), custom_call_target="tpu_custom_call" | custom-call | tf_op jit(solution)/shard_map/pallas_call | solution.py:492
  13.6 1.7 %collective-permute-start.5 = (f32[8,256]{1,0:T(8,128)S(1)}, f32[8,256]{1,0:T(8,128)S(1)}, u32[]{:S(2)}, u32[]{:S(2)}) collective-permute-start(f32[8,256]{1,0:T(8,128)S(1)} %get-tuple-element.35), channel_id=1, source_target_pairs={{0,24},{8,16},{16,8},{24,0},{32,56},{40,48},{48,40},{56,32},{64,88... | collective-permute-start | bytes 24584 | tf_op jit(solution)/shard_map/ppermute | solution.py:479
  15.5 2.3 %collective-permute-done = f32[8,256]{1,0:T(8,128)S(1)} collective-permute-done((f32[8,256]{1,0:T(8,128)S(1)}, f32[8,256]{1,0:T(8,128)S(1)}, u32[]{:S(2)}, u32[]{:S(2)}) %collective-permute-start) | collective-permute-done | bytes 8224 | tf_op jit(solution)/shard_map/ppermute | solution.py:479
  17.8 3.1 %collective-permute-start.1 = (f32[8,256]{1,0:T(8,128)S(1)}, f32[8,256]{1,0:T(8,128)S(1)}, u32[]{:S(2)}, u32[]{:S(2)}) collective-permute-start(f32[8,256]{1,0:T(8,128)S(1)} %multiply_add_fusion.5), channel_id=1, source_target_pairs={{0,2},{1,3},{2,0},{3,1},{4,6},{5,7},{6,4},{7,5},{8,10},{9,11},{10,... | collective-permute-start | bytes 24584 | tf_op jit(solution)/shard_map/ppermute | solution.py:479
  21.5 8.6 %all-to-all-start = ((f32[8,8,256]{2,1,0:T(8,128)}), f32[8,8,256]{2,1,0:T(8,128)S(1)}, u32[]{:S(2)}, u32[]{:S(2)}) async-start(f32[8,8,256]{2,1,0:T(8,128)} %broadcast_in_dim.4), calls=%async_computation | async-start | bytes 131072 | tf_op jit(solution)/shard_map/all_to_all | solution.py:489
  31.2 2.7 %collective-permute-done.2.rest_1_ = f32[8,256]{1,0:T(8,128)S(1)} collective-permute-done((f32[8,256]{1,0:T(8,128)S(1)}, f32[8,256]{1,0:T(8,128)S(1)}, u32[]{:S(2)}, u32[]{:S(2)}) %collective-permute-start.2) | collective-permute-done | bytes 8224 | tf_op jit(solution)/shard_map/ppermute | solution.py:479
  33.9 4.6 %all-to-all-done.rest_2_ = f32[8,8,256]{2,1,0:T(8,128)S(1)} async-done(((f32[8,8,256]{2,1,0:T(8,128)}), f32[8,8,256]{2,1,0:T(8,128)S(1)}, u32[]{:S(2)}, u32[]{:S(2)}) %all-to-all-start) | async-done | bytes 65568 | tf_op jit(solution)/shard_map/all_to_all | solution.py:489
  38.6 8.2 %shard_map.60 = (f32[8,256]{1,0:T(8,128)S(1)}, f32[8,256]{1,0:T(8,128)S(1)}, f32[8,256]{1,0:T(8,128)S(1)}, f32[8,256]{1,0:T(8,128)S(1)}) custom-call(s32[2,24]{1,0:T(2,128)S(1)} %bitcast.21, s32[1]{0:T(128)} %bitcast.12.count_ref, bf16[6,256,256]{2,1,0:T(8,128)(2,1)S(1)} %bitcast.15, bf16[6,256,256]{2,1,0:T(8,128)(2,1)S(1)} %bitcast.18, ...), custom_call_target="tpu_custom_call" | custom-call | tf_op jit(solution)/shard_map/pallas_call | solution.py:501
  46.8 1.4 collective-permute-start.6
  48.2 1.9 %collective-permute-start.9 = (f32[8,256]{1,0:T(8,128)S(1)}, f32[8,256]{1,0:T(8,128)S(1)}, u32[]{:S(2)}, u32[]{:S(2)}) collective-permute-start(f32[8,256]{1,0:T(8,128)S(1)} %get-tuple-element.39), channel_id=1, source_target_pairs={{0,8},{8,0},{16,24},{24,16},{32,40},{40,32},{48,56},{56,48},{64,72... | collective-permute-start | bytes 24584 | tf_op jit(solution)/shard_map/ppermute | solution.py:479
  50.0 2.0 %collective-permute-done.6 = f32[8,256]{1,0:T(8,128)S(1)} collective-permute-done((f32[8,256]{1,0:T(8,128)S(1)}, f32[8,256]{1,0:T(8,128)S(1)}, u32[]{:S(2)}, u32[]{:S(2)}) %collective-permute-start.6) | collective-permute-done | bytes 8224 | tf_op jit(solution)/shard_map/ppermute | solution.py:479
  52.1 1.3 collective-permute-start.7
  54.0 4.2 %all-to-all-start.1 = ((f32[8,8,256]{2,1,0:T(8,128)}), f32[8,8,256]{2,1,0:T(8,128)S(1)}, u32[]{:S(2)}, u32[]{:S(2)}) async-start(f32[8,8,256]{2,1,0:T(8,128)} %broadcast_in_dim.5), calls=%async_computation.1 | async-start | bytes 131072 | tf_op jit(solution)/shard_map/all_to_all | solution.py:489
  58.3 2.0 %collective-permute-start.8 = (f32[8,256]{1,0:T(8,128)S(1)}, f32[8,256]{1,0:T(8,128)S(1)}, u32[]{:S(2)}, u32[]{:S(2)}) collective-permute-start(f32[8,256]{1,0:T(8,128)S(1)} %multiply_add_fusion.1.rest_0_), channel_id=1, source_target_pairs={{0,1},{1,0},{2,3},{3,2},{4,5},{5,4},{6,7},{7,6},{8,9},{9,8},{10,11... | collective-permute-start | bytes 24584 | tf_op jit(solution)/shard_map/ppermute | solution.py:479
  60.4 1.7 %collective-permute-done.8.rest_1_ = f32[8,256]{1,0:T(8,128)S(1)} collective-permute-done((f32[8,256]{1,0:T(8,128)S(1)}, f32[8,256]{1,0:T(8,128)S(1)}, u32[]{:S(2)}, u32[]{:S(2)}) %collective-permute-start.8) | collective-permute-done | bytes 8224 | tf_op jit(solution)/shard_map/ppermute | solution.py:479
  62.0 4.6 %all-to-all-done.1.rest_2_ = f32[8,8,256]{2,1,0:T(8,128)S(1)} async-done(((f32[8,8,256]{2,1,0:T(8,128)}), f32[8,8,256]{2,1,0:T(8,128)S(1)}, u32[]{:S(2)}, u32[]{:S(2)}) %all-to-all-start.1) | async-done | bytes 65568 | tf_op jit(solution)/shard_map/all_to_all | solution.py:489
  66.6 24.0 %shard_map.61 = (f32[16,56,256]{2,1,0:T(8,128)S(1)}, f32[16,56,256]{2,1,0:T(8,128)}, f32[2,200,256]{2,1,0:T(8,128)S(1)}, f32[200,256]{1,0:T(8,128)S(1)}, f32[200...) custom-call(s32[2]{0:T(128)S(1)} %pad_add_fusion.place_ref, s32[2,24]{1,0:T(2,128)S(1)} %bitcast.22, ...), custom_call_target="tpu_custom_call" | custom-call | tf_op jit(solution)/shard_map/pallas_call | solution.py:527
  90.6 7.8 %collective-permute-start.12 = (f32[200,256]{1,0:T(8,128)S(1)}, f32[200,256]{1,0:T(8,128)S(1)}, u32[]{:S(2)}, u32[]{:S(2)}) collective-permute-start(f32[200,256]{1,0:T(8,128)S(1)} %get-tuple-element.42), channel_id=1, source_target_pairs={{0,1},{1,2},{2,3},{3,0},{4,5},{5,6},{6,7},{7,4},{8,9},{9,10},{10,1... | collective-permute-start | bytes 614408 | tf_op jit(solution)/shard_map/ppermute | solution.py:549
  98.4 5.0 %collective-permute-done.12.up_came = f32[200,256]{1,0:T(8,128)S(1)} collective-permute-done((f32[200,256]{1,0:T(8,128)S(1)}, f32[200,256]{1,0:T(8,128)S(1)}, u32[]{:S(2)}, u32[]{:S(2)}) %collective-permute-start.12) | collective-permute-done | bytes 204832 | tf_op jit(solution)/shard_map/ppermute | solution.py:549
  103.4 2.2 %collective-permute-done.13.down_came = f32[200,256]{1,0:T(8,128)S(1)} collective-permute-done((f32[200,256]{1,0:T(8,128)S(1)}, f32[200,256]{1,0:T(8,128)S(1)}, u32[]{:S(2)}, u32[]{:S(2)}) %collective-permute-start.13) | collective-permute-done | bytes 204832 | tf_op jit(solution)/shard_map/ppermute | solution.py:550
  105.6 1.2 shard_map.62
  107.1 2.9 %collective-permute-start.15 = (f32[2,200,256]{2,1,0:T(8,128)}, f32[2,200,256]{2,1,0:T(8,128)}, u32[]{:S(2)}, u32[]{:S(2)}) collective-permute-start(f32[2,200,256]{2,1,0:T(8,128)} %get-tuple-element.46), channel_id=1, source_target_pairs={{1,0},{2,1},{3,2},{0,3},{5,4},{6,5},{7,6},{4,7},{9,8},{10,9},{11,1... | collective-permute-start | bytes 1228808 | tf_op jit(solution)/shard_map/ppermute | solution.py:587
  110.8 3.2 %collective-permute-start.19 = (f32[56,256]{1,0:T(8,128)S(1)}, f32[56,256]{1,0:T(8,128)S(1)}, u32[]{:S(2)}, u32[]{:S(2)}) collective-permute-start(f32[56,256]{1,0:T(8,128)S(1)} %get-tuple-element.53), channel_id=1, source_target_pairs={{32,0},{40,8},{48,16},{56,24},{64,32},{72,40},{80,48},{88,56},{96,... | collective-permute-start | bytes 172040 | tf_op jit(solution)/shard_map/ppermute | solution.py:564
  114.0 2.2 %collective-permute-done.18.up_came = f32[56,256]{1,0:T(8,128)S(1)} collective-permute-done((f32[56,256]{1,0:T(8,128)S(1)}, f32[56,256]{1,0:T(8,128)S(1)}, u32[]{:S(2)}, u32[]{:S(2)}) %collective-permute-start.18) | collective-permute-done | bytes 57376 | tf_op jit(solution)/shard_map/ppermute | solution.py:563
  116.5 3.3 %collective-permute-start.21 = (f32[2,56,256]{2,1,0:T(8,128)S(1)}, f32[2,56,256]{2,1,0:T(8,128)S(1)}, u32[]{:S(2)}, u32[]{:S(2)}) collective-permute-start(f32[2,56,256]{2,1,0:T(8,128)S(1)} %get-tuple-element.55), channel_id=1, source_target_pairs={{32,0},{40,8},{48,16},{56,24},{64,32},{72,40},{80,48},{88,56},{96,... | collective-permute-start | bytes 344072 | tf_op jit(solution)/shard_map/ppermute | solution.py:564
  119.8 2.7 %collective-permute-done.20.up_came = f32[2,56,256]{2,1,0:T(8,128)S(1)} collective-permute-done((f32[2,56,256]{2,1,0:T(8,128)S(1)}, f32[2,56,256]{2,1,0:T(8,128)S(1)}, u32[]{:S(2)}, u32[]{:S(2)}) %collective-permute-start.20) | collective-permute-done | bytes 114720 | tf_op jit(solution)/shard_map/ppermute | solution.py:563
  122.8 3.4 %collective-permute-start.23 = (f32[2,56,256]{2,1,0:T(8,128)S(1)}, f32[2,56,256]{2,1,0:T(8,128)S(1)}, u32[]{:S(2)}, u32[]{:S(2)}) collective-permute-start(f32[2,56,256]{2,1,0:T(8,128)S(1)} %get-tuple-element.57), channel_id=1, source_target_pairs={{32,0},{40,8},{48,16},{56,24},{64,32},{72,40},{80,48},{88,56},{96,... | collective-permute-start | bytes 344072 | tf_op jit(solution)/shard_map/ppermute | solution.py:564
  126.2 1.6 %shard_map.63 = (f32[200,256]{1,0:T(8,128)S(1)}, f32[200,256]{1,0:T(8,128)S(1)}) custom-call(s32[1]{0:T(128)} %bitcast.place_ref, f32[2,200,256]{2,1,0:T(8,128)S(1)} %copy-done.5, f32[2,200,256]{2,1,0:T(8,128)} %collective-permute-done.14.up_came, f32[2,200,256]{2,1,0:T(8,128)} %collective-permute-done.15.down_came), custom_call_target="tpu_custom_call" | custom-call | tf_op jit(solution)/shard_map/pallas_call | solution.py:517
  129.1 1.2 collective-permute-start.24
  130.4 2.5 %collective-permute-start.25 = (f32[2,56,256]{2,1,0:T(8,128)S(1)}, f32[2,56,256]{2,1,0:T(8,128)S(1)}, u32[]{:S(2)}, u32[]{:S(2)}) collective-permute-start(f32[2,56,256]{2,1,0:T(8,128)S(1)} %get-tuple-element.59), channel_id=1, source_target_pairs={{32,0},{40,8},{48,16},{56,24},{64,32},{72,40},{80,48},{88,56},{96,... | collective-permute-start | bytes 344072 | tf_op jit(solution)/shard_map/ppermute | solution.py:564
  133.0 2.6 %collective-permute-done.24.up_came = f32[2,56,256]{2,1,0:T(8,128)S(1)} collective-permute-done((f32[2,56,256]{2,1,0:T(8,128)S(1)}, f32[2,56,256]{2,1,0:T(8,128)S(1)}, u32[]{:S(2)}, u32[]{:S(2)}) %collective-permute-start.24) | collective-permute-done | bytes 114720 | tf_op jit(solution)/shard_map/ppermute | solution.py:563
  137.6 3.0 %collective-permute-done.26.b_ref = f32[56,256]{1,0:T(8,128)S(1)} collective-permute-done((f32[56,256]{1,0:T(8,128)S(1)}, f32[56,256]{1,0:T(8,128)S(1)}, u32[]{:S(2)}, u32[]{:S(2)}) %collective-permute-start.26) | collective-permute-done | bytes 57376 | tf_op jit(solution)/shard_map/ppermute | solution.py:479
  (62 shorter events, 12.5 us)
Async XLA Ops:
  4.2 34.3 %copy-start.1 = (bf16[1536,256]{1,0:T(8,128)(2,1)S(1)}, bf16[1536,256]{1,0:T(8,128)(2,1)}, u32[]{:S(2)}) copy-start(bf16[1536,256]{1,0:T(8,128)(2,1)} %param.4) | copy-start | bytes 2359300
  4.2 34.3 %copy-start.3 = (bf16[1536,256]{1,0:T(8,128)(2,1)S(1)}, bf16[1536,256]{1,0:T(8,128)(2,1)}, u32[]{:S(2)}) copy-start(bf16[1536,256]{1,0:T(8,128)(2,1)} %param.5) | copy-start | bytes 2359300
  12.5 5.2 %collective-permute-start = (f32[8,256]{1,0:T(8,128)S(1)}, f32[8,256]{1,0:T(8,128)S(1)}, u32[]{:S(2)}, u32[]{:S(2)}) collective-permute-start(f32[8,256]{1,0:T(8,128)S(1)} %get-tuple-element.34), channel_id=1, source_target_pairs={{0,4},{1,5},{2,6},{3,7},{4,0},{5,1},{6,2},{7,3},{8,12},{9,13},{10,... | collective-permute-start | bytes 24584 | tf_op jit(solution)/shard_map/ppermute | solution.py:479
  13.6 7.3 %collective-permute-start.5 = (f32[8,256]{1,0:T(8,128)S(1)}, f32[8,256]{1,0:T(8,128)S(1)}, u32[]{:S(2)}, u32[]{:S(2)}) collective-permute-start(f32[8,256]{1,0:T(8,128)S(1)} %get-tuple-element.35), channel_id=1, source_target_pairs={{0,24},{8,16},{16,8},{24,0},{32,56},{40,48},{48,40},{56,32},{64,88... | collective-permute-start | bytes 24584 | tf_op jit(solution)/shard_map/ppermute | solution.py:479
  15.3 5.6 %collective-permute-start.4 = (f32[8,256]{1,0:T(8,128)S(1)}, f32[8,256]{1,0:T(8,128)S(1)}, u32[]{:S(2)}, u32[]{:S(2)}) collective-permute-start(f32[8,256]{1,0:T(8,128)S(1)} %get-tuple-element.35), channel_id=1, source_target_pairs={{0,16},{8,24},{16,0},{24,8},{32,48},{40,56},{48,32},{56,40},{64,80... | collective-permute-start | bytes 24584 | tf_op jit(solution)/shard_map/ppermute | solution.py:479
  15.3 5.6 %collective-permute-start.3 = (f32[8,256]{1,0:T(8,128)S(1)}, f32[8,256]{1,0:T(8,128)S(1)}, u32[]{:S(2)}, u32[]{:S(2)}) collective-permute-start(f32[8,256]{1,0:T(8,128)S(1)} %get-tuple-element.35), channel_id=1, source_target_pairs={{0,8},{8,0},{16,24},{24,16},{32,40},{40,32},{48,56},{56,48},{64,72... | collective-permute-start | bytes 24584 | tf_op jit(solution)/shard_map/ppermute | solution.py:479
  17.8 12.4 %collective-permute-start.1 = (f32[8,256]{1,0:T(8,128)S(1)}, f32[8,256]{1,0:T(8,128)S(1)}, u32[]{:S(2)}, u32[]{:S(2)}) collective-permute-start(f32[8,256]{1,0:T(8,128)S(1)} %multiply_add_fusion.5), channel_id=1, source_target_pairs={{0,2},{1,3},{2,0},{3,1},{4,6},{5,7},{6,4},{7,5},{8,10},{9,11},{10,... | collective-permute-start | bytes 24584 | tf_op jit(solution)/shard_map/ppermute | solution.py:479
  21.5 17.0 %all-to-all-start = ((f32[8,8,256]{2,1,0:T(8,128)}), f32[8,8,256]{2,1,0:T(8,128)S(1)}, u32[]{:S(2)}, u32[]{:S(2)}) async-start(f32[8,8,256]{2,1,0:T(8,128)} %broadcast_in_dim.4), calls=%async_computation | async-start | bytes 131072 | tf_op jit(solution)/shard_map/all_to_all | solution.py:489
  30.2 3.7 %collective-permute-start.2 = (f32[8,256]{1,0:T(8,128)S(1)}, f32[8,256]{1,0:T(8,128)S(1)}, u32[]{:S(2)}, u32[]{:S(2)}) collective-permute-start(f32[8,256]{1,0:T(8,128)S(1)} %multiply_add_fusion.4.rest_0_), channel_id=1, source_target_pairs={{0,1},{1,0},{2,3},{3,2},{4,5},{5,4},{6,7},{7,6},{8,9},{9,8},{10,11... | collective-permute-start | bytes 24584 | tf_op jit(solution)/shard_map/ppermute | solution.py:479
  46.8 5.2 %collective-permute-start.6 = (f32[8,256]{1,0:T(8,128)S(1)}, f32[8,256]{1,0:T(8,128)S(1)}, u32[]{:S(2)}, u32[]{:S(2)}) collective-permute-start(f32[8,256]{1,0:T(8,128)S(1)} %get-tuple-element.38), channel_id=1, source_target_pairs={{0,4},{1,5},{2,6},{3,7},{4,0},{5,1},{6,2},{7,3},{8,12},{9,13},{10,... | collective-permute-start | bytes 24584 | tf_op jit(solution)/shard_map/ppermute | solution.py:479
  48.2 5.2 %collective-permute-start.11 = (f32[8,256]{1,0:T(8,128)S(1)}, f32[8,256]{1,0:T(8,128)S(1)}, u32[]{:S(2)}, u32[]{:S(2)}) collective-permute-start(f32[8,256]{1,0:T(8,128)S(1)} %get-tuple-element.39), channel_id=1, source_target_pairs={{0,24},{8,16},{16,8},{24,0},{32,56},{40,48},{48,40},{56,32},{64,88... | collective-permute-start | bytes 24584 | tf_op jit(solution)/shard_map/ppermute | solution.py:479
  48.2 5.2 %collective-permute-start.10 = (f32[8,256]{1,0:T(8,128)S(1)}, f32[8,256]{1,0:T(8,128)S(1)}, u32[]{:S(2)}, u32[]{:S(2)}) collective-permute-start(f32[8,256]{1,0:T(8,128)S(1)} %get-tuple-element.39), channel_id=1, source_target_pairs={{0,16},{8,24},{16,0},{24,8},{32,48},{40,56},{48,32},{56,40},{64,80... | collective-permute-start | bytes 24584 | tf_op jit(solution)/shard_map/ppermute | solution.py:479
  48.2 5.2 %collective-permute-start.9 = (f32[8,256]{1,0:T(8,128)S(1)}, f32[8,256]{1,0:T(8,128)S(1)}, u32[]{:S(2)}, u32[]{:S(2)}) collective-permute-start(f32[8,256]{1,0:T(8,128)S(1)} %get-tuple-element.39), channel_id=1, source_target_pairs={{0,8},{8,0},{16,24},{24,16},{32,40},{40,32},{48,56},{56,48},{64,72... | collective-permute-start | bytes 24584 | tf_op jit(solution)/shard_map/ppermute | solution.py:479
  52.1 6.2 %collective-permute-start.7 = (f32[8,256]{1,0:T(8,128)S(1)}, f32[8,256]{1,0:T(8,128)S(1)}, u32[]{:S(2)}, u32[]{:S(2)}) collective-permute-start(f32[8,256]{1,0:T(8,128)S(1)} %multiply_add_fusion.2), channel_id=1, source_target_pairs={{0,2},{1,3},{2,0},{3,1},{4,6},{5,7},{6,4},{7,5},{8,10},{9,11},{10,... | collective-permute-start | bytes 24584 | tf_op jit(solution)/shard_map/ppermute | solution.py:479
  54.0 12.6 %all-to-all-start.1 = ((f32[8,8,256]{2,1,0:T(8,128)}), f32[8,8,256]{2,1,0:T(8,128)S(1)}, u32[]{:S(2)}, u32[]{:S(2)}) async-start(f32[8,8,256]{2,1,0:T(8,128)} %broadcast_in_dim.5), calls=%async_computation.1 | async-start | bytes 131072 | tf_op jit(solution)/shard_map/all_to_all | solution.py:489
  58.3 3.7 %collective-permute-start.8 = (f32[8,256]{1,0:T(8,128)S(1)}, f32[8,256]{1,0:T(8,128)S(1)}, u32[]{:S(2)}, u32[]{:S(2)}) collective-permute-start(f32[8,256]{1,0:T(8,128)S(1)} %multiply_add_fusion.1.rest_0_), channel_id=1, source_target_pairs={{0,1},{1,0},{2,3},{3,2},{4,5},{5,4},{6,7},{7,6},{8,9},{9,8},{10,11... | collective-permute-start | bytes 24584 | tf_op jit(solution)/shard_map/ppermute | solution.py:479
  90.6 16.2 %copy-start.4 = (f32[2,200,256]{2,1,0:T(8,128)}, f32[2,200,256]{2,1,0:T(8,128)S(1)}, u32[]{:S(2)}) copy-start(f32[2,200,256]{2,1,0:T(8,128)S(1)} %get-tuple-element.40.own) | copy-start | bytes 1228804
  90.6 19.5 %collective-permute-start.17 = (f32[16,56,256]{2,1,0:T(8,128)}, f32[16,56,256]{2,1,0:T(8,128)S(1)}, u32[]{:S(2)}, u32[]{:S(2)}) collective-permute-start(f32[16,56,256]{2,1,0:T(8,128)} %get-tuple-element.50), channel_id=1, source_target_pairs={{0,8},{8,0},{16,24},{24,16},{32,40},{40,32},{48,56},{56,48},{64,72... | collective-permute-start | bytes 2752520 | tf_op jit(solution)/shard_map/ppermute | solution.py:479
  90.6 12.8 %collective-permute-start.12 = (f32[200,256]{1,0:T(8,128)S(1)}, f32[200,256]{1,0:T(8,128)S(1)}, u32[]{:S(2)}, u32[]{:S(2)}) collective-permute-start(f32[200,256]{1,0:T(8,128)S(1)} %get-tuple-element.42), channel_id=1, source_target_pairs={{0,1},{1,2},{2,3},{3,0},{4,5},{5,6},{6,7},{7,4},{8,9},{9,10},{10,1... | collective-permute-start | bytes 614408 | tf_op jit(solution)/shard_map/ppermute | solution.py:549
  98.4 7.2 %collective-permute-start.13 = (f32[200,256]{1,0:T(8,128)S(1)}, f32[200,256]{1,0:T(8,128)S(1)}, u32[]{:S(2)}, u32[]{:S(2)}) collective-permute-start(f32[200,256]{1,0:T(8,128)S(1)} %get-tuple-element.44), channel_id=1, source_target_pairs={{1,0},{2,1},{3,2},{0,3},{5,4},{6,5},{7,6},{4,7},{9,8},{10,9},{11,1... | collective-permute-start | bytes 614408 | tf_op jit(solution)/shard_map/ppermute | solution.py:550
  106.8 19.4 %collective-permute-start.14 = (f32[2,200,256]{2,1,0:T(8,128)}, f32[2,200,256]{2,1,0:T(8,128)}, u32[]{:S(2)}, u32[]{:S(2)}) collective-permute-start(f32[2,200,256]{2,1,0:T(8,128)} %get-tuple-element.45), channel_id=1, source_target_pairs={{0,1},{1,2},{2,3},{3,0},{4,5},{5,6},{6,7},{7,4},{8,9},{9,10},{10,1... | collective-permute-start | bytes 1228808 | tf_op jit(solution)/shard_map/ppermute | solution.py:586
  107.1 19.1 %collective-permute-start.15 = (f32[2,200,256]{2,1,0:T(8,128)}, f32[2,200,256]{2,1,0:T(8,128)}, u32[]{:S(2)}, u32[]{:S(2)}) collective-permute-start(f32[2,200,256]{2,1,0:T(8,128)} %get-tuple-element.46), channel_id=1, source_target_pairs={{1,0},{2,1},{3,2},{0,3},{5,4},{6,5},{7,6},{4,7},{9,8},{10,9},{11,1... | collective-permute-start | bytes 1228808 | tf_op jit(solution)/shard_map/ppermute | solution.py:587
  110.5 5.7 %collective-permute-start.18 = (f32[56,256]{1,0:T(8,128)S(1)}, f32[56,256]{1,0:T(8,128)S(1)}, u32[]{:S(2)}, u32[]{:S(2)}) collective-permute-start(f32[56,256]{1,0:T(8,128)S(1)} %get-tuple-element.52), channel_id=1, source_target_pairs={{0,32},{8,40},{16,48},{24,56},{32,64},{40,72},{48,80},{56,88},{64,... | collective-permute-start | bytes 172040 | tf_op jit(solution)/shard_map/ppermute | solution.py:563
  110.8 5.4 %collective-permute-start.19 = (f32[56,256]{1,0:T(8,128)S(1)}, f32[56,256]{1,0:T(8,128)S(1)}, u32[]{:S(2)}, u32[]{:S(2)}) collective-permute-start(f32[56,256]{1,0:T(8,128)S(1)} %get-tuple-element.53), channel_id=1, source_target_pairs={{32,0},{40,8},{48,16},{56,24},{64,32},{72,40},{80,48},{88,56},{96,... | collective-permute-start | bytes 172040 | tf_op jit(solution)/shard_map/ppermute | solution.py:564
  116.4 6.1 %collective-permute-start.20 = (f32[2,56,256]{2,1,0:T(8,128)S(1)}, f32[2,56,256]{2,1,0:T(8,128)S(1)}, u32[]{:S(2)}, u32[]{:S(2)}) collective-permute-start(f32[2,56,256]{2,1,0:T(8,128)S(1)} %get-tuple-element.54), channel_id=1, source_target_pairs={{0,32},{8,40},{16,48},{24,56},{32,64},{40,72},{48,80},{56,88},{64,... | collective-permute-start | bytes 344072 | tf_op jit(solution)/shard_map/ppermute | solution.py:563
  116.5 6.0 %collective-permute-start.21 = (f32[2,56,256]{2,1,0:T(8,128)S(1)}, f32[2,56,256]{2,1,0:T(8,128)S(1)}, u32[]{:S(2)}, u32[]{:S(2)}) collective-permute-start(f32[2,56,256]{2,1,0:T(8,128)S(1)} %get-tuple-element.55), channel_id=1, source_target_pairs={{32,0},{40,8},{48,16},{56,24},{64,32},{72,40},{80,48},{88,56},{96,... | collective-permute-start | bytes 344072 | tf_op jit(solution)/shard_map/ppermute | solution.py:564
  122.7 6.2 %collective-permute-start.22 = (f32[2,56,256]{2,1,0:T(8,128)S(1)}, f32[2,56,256]{2,1,0:T(8,128)S(1)}, u32[]{:S(2)}, u32[]{:S(2)}) collective-permute-start(f32[2,56,256]{2,1,0:T(8,128)S(1)} %get-tuple-element.56), channel_id=1, source_target_pairs={{0,32},{8,40},{16,48},{24,56},{32,64},{40,72},{48,80},{56,88},{64,... | collective-permute-start | bytes 344072 | tf_op jit(solution)/shard_map/ppermute | solution.py:563
  122.8 6.1 %collective-permute-start.23 = (f32[2,56,256]{2,1,0:T(8,128)S(1)}, f32[2,56,256]{2,1,0:T(8,128)S(1)}, u32[]{:S(2)}, u32[]{:S(2)}) collective-permute-start(f32[2,56,256]{2,1,0:T(8,128)S(1)} %get-tuple-element.57), channel_id=1, source_target_pairs={{32,0},{40,8},{48,16},{56,24},{64,32},{72,40},{80,48},{88,56},{96,... | collective-permute-start | bytes 344072 | tf_op jit(solution)/shard_map/ppermute | solution.py:564
  127.8 8.8 %collective-permute-start.16 = (f32[200,256]{1,0:T(8,128)S(1)}, f32[200,256]{1,0:T(8,128)S(1)}, u32[]{:S(2)}, u32[]{:S(2)}) collective-permute-start(f32[200,256]{1,0:T(8,128)S(1)} %get-tuple-element.48), channel_id=1, source_target_pairs={{0,4},{1,5},{2,6},{3,7},{4,0},{5,1},{6,2},{7,3},{8,12},{9,13},{10,... | collective-permute-start | bytes 614408 | tf_op jit(solution)/shard_map/ppermute | solution.py:479
  129.1 6.5 %collective-permute-start.24 = (f32[2,56,256]{2,1,0:T(8,128)S(1)}, f32[2,56,256]{2,1,0:T(8,128)S(1)}, u32[]{:S(2)}, u32[]{:S(2)}) collective-permute-start(f32[2,56,256]{2,1,0:T(8,128)S(1)} %get-tuple-element.58), channel_id=1, source_target_pairs={{0,32},{8,40},{16,48},{24,56},{32,64},{40,72},{48,80},{56,88},{64,... | collective-permute-start | bytes 344072 | tf_op jit(solution)/shard_map/ppermute | solution.py:563
  130.4 5.2 %collective-permute-start.25 = (f32[2,56,256]{2,1,0:T(8,128)S(1)}, f32[2,56,256]{2,1,0:T(8,128)S(1)}, u32[]{:S(2)}, u32[]{:S(2)}) collective-permute-start(f32[2,56,256]{2,1,0:T(8,128)S(1)} %get-tuple-element.59), channel_id=1, source_target_pairs={{32,0},{40,8},{48,16},{56,24},{64,32},{72,40},{80,48},{88,56},{96,... | collective-permute-start | bytes 344072 | tf_op jit(solution)/shard_map/ppermute | solution.py:564
  136.4 4.3 %collective-permute-start.26 = (f32[56,256]{1,0:T(8,128)S(1)}, f32[56,256]{1,0:T(8,128)S(1)}, u32[]{:S(2)}, u32[]{:S(2)}) collective-permute-start(f32[56,256]{1,0:T(8,128)S(1)} %get-tuple-element.61), channel_id=1, source_target_pairs={{0,16},{8,24},{16,0},{24,8},{32,48},{40,56},{48,32},{56,40},{64,80... | collective-permute-start | bytes 172040 | tf_op jit(solution)/shard_map/ppermute | solution.py:479
  (4 other events, 12.7 us)

commit v9 on v8

--- a/solution.py
+++ b/solution.py
@@ -472,7 +472,7 @@
     pair_list = jnp.transpose(pairs[0, 0])
     kept = counts.reshape(-1)
     smem = pl.BlockSpec(memory_space=pltpu.SMEM)
-    large = pltpu.CompilerParams(vmem_limit_bytes=36 * 1024 * 1024)
+    large = pltpu.CompilerParams(vmem_limit_bytes=26 * 1024 * 1024)
     little = pltpu.CompilerParams(vmem_limit_bytes=8 * 1024 * 1024)
 
     def swap(value, axis, size, bit):
@@ -562,6 +562,10 @@
     for away in range(n_z // 2 - 1, -1, -1):
         z_up = lax.ppermute(z_up, "src", z_ups)
         z_down = lax.ppermute(z_down, "src", z_downs)
+        if away == n_z // 2 - 1:
+            up_came, down_came, z_up, z_down = lax.optimization_barrier(
+                (up_came, down_came, z_up, z_down)
+            )
         if away:
             z_up, z_down = call(
                 functools.partial(ring_kernel, b_rows, away),

time: 142 us -> 139 us (0.979)
  starting transfers between devices: 51.9 us -> 65.6 us
  waiting for transfers between devices: 36.6 us -> 26.4 us
  Pallas kernels: 47 us -> 38.5 us
  local copies, waits for them, and re-layouts: 4.23 us -> 6.47 us
    ppermute x15, starting transfers between devices: 13.9 us -> 32 us  [swap(): return lax.ppermute(value, axis, [(k, k ^ bit) for k in range(size)])]
    pallas_call x1, Pallas kernels: 24 us -> 19.5 us  [per_device(): pl.pallas_call(functools.partial(maps_kernel, 2, scale, blocks), out_shap...]
    ppermute x15, waiting for transfers between devices: 11.8 us -> 8.09 us  [swap(): return lax.ppermute(value, axis, [(k, k ^ bit) for k in range(size)])]
    ppermute x1, waiting for transfers between devices: 5 us -> 1.57 us  [per_device(): up_came = lax.ppermute(up_first, 'tgt', ups)]
    ppermute x4, waiting for transfers between devices: 8.38 us -> 5.46 us  [per_device(): z_up = lax.ppermute(z_up, 'src', z_ups)]
    ppermute x1, starting transfers between devices: 7.78 us -> 5.06 us  [per_device(): up_came = lax.ppermute(up_first, 'tgt', ups)]
    unnamed x14 -> x22, local copies, waits for them, and re-layouts: 2.95 us -> 5.19 us
  transfers between devices with their start and end apart: 29 -> 29, of which waited for: 13 -> 11; matrix products, arithmetic and copies ran while one was open for 1% -> 1% of each run, Pallas kernels for 4% -> 3%
where the time goes in v9:
time: 139 us
  starting transfers between devices  65.6 us (47%)
  Pallas kernels  38.5 us (28%)
  waiting for transfers between devices  26.4 us (19%)
  local copies, waits for them, and re-layouts  6.47 us (5%)
  between operations  1.45 us (1%)
    ppermute x15, starting transfers between devices, swap(): return lax.ppermute(value, axis, [(k, k ^ bit) for k in range(size)])  32 us
    pallas_call x1, Pallas kernels, per_device(): pl.pallas_call(functools.partial(maps_kernel, 2, scale, blocks), out_shap...  19.5 us
    ppermute x4, starting transfers between devices, per_device(): z_down = lax.ppermute(z_down, 'src', z_downs)  11.9 us
    all_to_all x2, starting transfers between devices, exchange(): lax.all_to_all(copies, 'src', 0, 0, axis_index_groups=along_z, tiled=True)  11.8 us
    all_to_all x2, waiting for transfers between devices, exchange(): lax.all_to_all(copies, 'src', 0, 0, axis_index_groups=along_z, tiled=True)  9.13 us
    ppermute x15, waiting for transfers between devices, swap(): return lax.ppermute(value, axis, [(k, k ^ bit) for k in range(size)])  8.09 us
    pallas_call x1, Pallas kernels, per_device(): pl.pallas_call(functools.partial(first_kernel, scale, blocks), out_shape=...  6.97 us
    pallas_call x1, Pallas kernels, per_device(): pl.pallas_call(functools.partial(second_kernel, 2, scale, blocks), out_sh...  6.91 us
  transfers between devices with their start and end apart: 29, of which 11 were waited for; matrix products, arithmetic and copies ran while one was open for 1% of the time, Pallas kernels for 3%

profile of v9, /device:TPU:8, one launch (start us, length us, event | category | flops | bytes accessed | tf_op | source)
XLA Modules:
  0.0 138.7 jit_solution(3034553031610520181)
XLA Ops:
  2.0 1.1 copy-done
  3.1 1.1 copy-done.2
  4.2 7.0 %shard_map.59 = (f32[8,256]{1,0:T(8,128)S(1)}, f32[8,256]{1,0:T(8,128)S(1)}, f32[8,256]{1,0:T(8,128)S(1)}, f32[8,256]{1,0:T(8,128)S(1)}) custom-call(s32[2,24]{1,0:T(2,128)S(1)} %bitcast.20, s32[1]{0:T(128)} %bitcast.11.count_ref, bf16[6,256,256]{2,1,0:T(8,128)(2,1)S(1)} %bitcast.14, bf16[6,256,256]{2,1,0:T(8,128)(2,1)S(1)} %bitcast.17), custom_call_target="tpu_custom_call" | custom-call | tf_op jit(solution)/shard_map/pallas_call | solution.py:492
  11.2 4.7 %collective-permute-start = (f32[8,256]{1,0:T(8,128)S(1)}, f32[8,256]{1,0:T(8,128)S(1)}, u32[]{:S(2)}, u32[]{:S(2)}) collective-permute-start(f32[8,256]{1,0:T(8,128)S(1)} %get-tuple-element.38), channel_id=1, source_target_pairs={{0,4},{1,5},{2,6},{3,7},{4,0},{5,1},{6,2},{7,3},{8,12},{9,13},{10,... | collective-permute-start | bytes 24584 | tf_op jit(solution)/shard_map/ppermute | solution.py:479
  15.9 1.5 %collective-permute-start.4 = (f32[8,256]{1,0:T(8,128)S(1)}, f32[8,256]{1,0:T(8,128)S(1)}, u32[]{:S(2)}, u32[]{:S(2)}) collective-permute-start(f32[8,256]{1,0:T(8,128)S(1)} %get-tuple-element.39), channel_id=1, source_target_pairs={{0,16},{8,24},{16,0},{24,8},{32,48},{40,56},{48,32},{56,40},{64,80... | collective-permute-start | bytes 24584 | tf_op jit(solution)/shard_map/ppermute | solution.py:479
  17.8 3.3 %collective-permute-start.1 = (f32[8,256]{1,0:T(8,128)S(1)}, f32[8,256]{1,0:T(8,128)S(1)}, u32[]{:S(2)}, u32[]{:S(2)}) collective-permute-start(f32[8,256]{1,0:T(8,128)S(1)} %multiply_add_fusion.5), channel_id=1, source_target_pairs={{0,2},{1,3},{2,0},{3,1},{4,6},{5,7},{6,4},{7,5},{8,10},{9,11},{10,... | collective-permute-start | bytes 24584 | tf_op jit(solution)/shard_map/ppermute | solution.py:479
  21.8 8.5 %all-to-all-start = ((f32[8,8,256]{2,1,0:T(8,128)}), f32[8,8,256]{2,1,0:T(8,128)S(1)}, u32[]{:S(2)}, u32[]{:S(2)}) async-start(f32[8,8,256]{2,1,0:T(8,128)} %broadcast_in_dim.4), calls=%async_computation | async-start | bytes 131072 | tf_op jit(solution)/shard_map/all_to_all | solution.py:489
  30.3 1.3 collective-permute-start.2
  31.6 2.4 %collective-permute-done.2.rest_1_ = f32[8,256]{1,0:T(8,128)S(1)} collective-permute-done((f32[8,256]{1,0:T(8,128)S(1)}, f32[8,256]{1,0:T(8,128)S(1)}, u32[]{:S(2)}, u32[]{:S(2)}) %collective-permute-start.2) | collective-permute-done | bytes 8224 | tf_op jit(solution)/shard_map/ppermute | solution.py:479
  34.0 4.6 %all-to-all-done.rest_2_ = f32[8,8,256]{2,1,0:T(8,128)S(1)} async-done(((f32[8,8,256]{2,1,0:T(8,128)}), f32[8,8,256]{2,1,0:T(8,128)S(1)}, u32[]{:S(2)}, u32[]{:S(2)}) %all-to-all-start) | async-done | bytes 65568 | tf_op jit(solution)/shard_map/all_to_all | solution.py:489
  38.6 6.9 %shard_map.60 = (f32[8,256]{1,0:T(8,128)S(1)}, f32[8,256]{1,0:T(8,128)S(1)}, f32[8,256]{1,0:T(8,128)S(1)}, f32[8,256]{1,0:T(8,128)S(1)}) custom-call(s32[2,24]{1,0:T(2,128)S(1)} %bitcast.21, s32[1]{0:T(128)} %bitcast.12.count_ref, bf16[6,256,256]{2,1,0:T(8,128)(2,1)S(1)} %bitcast.15, bf16[6,256,256]{2,1,0:T(8,128)(2,1)S(1)} %bitcast.18, ...), custom_call_target="tpu_custom_call" | custom-call | tf_op jit(solution)/shard_map/pallas_call | solution.py:501
  45.5 5.7 %collective-permute-start.6 = (f32[8,256]{1,0:T(8,128)S(1)}, f32[8,256]{1,0:T(8,128)S(1)}, u32[]{:S(2)}, u32[]{:S(2)}) collective-permute-start(f32[8,256]{1,0:T(8,128)S(1)} %get-tuple-element.42), channel_id=1, source_target_pairs={{0,4},{1,5},{2,6},{3,7},{4,0},{5,1},{6,2},{7,3},{8,12},{9,13},{10,... | collective-permute-start | bytes 24584 | tf_op jit(solution)/shard_map/ppermute | solution.py:479
  55.6 3.4 %all-to-all-start.1 = ((f32[8,8,256]{2,1,0:T(8,128)}), f32[8,8,256]{2,1,0:T(8,128)S(1)}, u32[]{:S(2)}, u32[]{:S(2)}) async-start(f32[8,8,256]{2,1,0:T(8,128)} %broadcast_in_dim.5), calls=%async_computation.1 | async-start | bytes 131072 | tf_op jit(solution)/shard_map/all_to_all | solution.py:489
  59.0 1.5 %collective-permute-start.8 = (f32[8,256]{1,0:T(8,128)S(1)}, f32[8,256]{1,0:T(8,128)S(1)}, u32[]{:S(2)}, u32[]{:S(2)}) collective-permute-start(f32[8,256]{1,0:T(8,128)S(1)} %multiply_add_fusion.1.rest_0_), channel_id=1, source_target_pairs={{0,1},{1,0},{2,3},{3,2},{4,5},{5,4},{6,7},{7,6},{8,9},{9,8},{10,11... | collective-permute-start | bytes 24584 | tf_op jit(solution)/shard_map/ppermute | solution.py:479
  60.6 2.2 %collective-permute-done.8.rest_1_ = f32[8,256]{1,0:T(8,128)S(1)} collective-permute-done((f32[8,256]{1,0:T(8,128)S(1)}, f32[8,256]{1,0:T(8,128)S(1)}, u32[]{:S(2)}, u32[]{:S(2)}) %collective-permute-start.8) | collective-permute-done | bytes 8224 | tf_op jit(solution)/shard_map/ppermute | solution.py:479
  62.8 4.5 %all-to-all-done.1.rest_2_ = f32[8,8,256]{2,1,0:T(8,128)S(1)} async-done(((f32[8,8,256]{2,1,0:T(8,128)}), f32[8,8,256]{2,1,0:T(8,128)S(1)}, u32[]{:S(2)}, u32[]{:S(2)}) %all-to-all-start.1) | async-done | bytes 65568 | tf_op jit(solution)/shard_map/all_to_all | solution.py:489
  67.3 19.5 %shard_map.61 = (f32[16,56,256]{2,1,0:T(8,128)S(1)}, f32[16,56,256]{2,1,0:T(8,128)}, f32[2,200,256]{2,1,0:T(8,128)S(1)}, f32[200,256]{1,0:T(8,128)}, f32[200,256...) custom-call(s32[2]{0:T(128)S(1)} %pad_add_fusion.place_ref, s32[2,24]{1,0:T(2,128)S(1)} %bitcast.22, ...), custom_call_target="tpu_custom_call" | custom-call | tf_op jit(solution)/shard_map/pallas_call | solution.py:527
  89.1 5.5 %collective-permute-start.14 = (f32[16,56,256]{2,1,0:T(8,128)}, f32[16,56,256]{2,1,0:T(8,128)S(1)}, u32[]{:S(2)}, u32[]{:S(2)}) collective-permute-start(f32[16,56,256]{2,1,0:T(8,128)} %get-tuple-element.49), channel_id=1, source_target_pairs={{0,8},{8,0},{16,24},{24,16},{32,40},{40,32},{48,56},{56,48},{64,72... | collective-permute-start | bytes 2752520 | tf_op jit(solution)/shard_map/ppermute | solution.py:479
  94.6 5.1 %collective-permute-start.12 = (f32[200,256]{1,0:T(8,128)}, f32[200,256]{1,0:T(8,128)S(1)}, u32[]{:S(2)}, u32[]{:S(2)}) collective-permute-start(f32[200,256]{1,0:T(8,128)} %get-tuple-element.46), channel_id=1, source_target_pairs={{0,1},{1,2},{2,3},{3,0},{4,5},{5,6},{6,7},{7,4},{8,9},{9,10},{10,1... | collective-permute-start | bytes 614408 | tf_op jit(solution)/shard_map/ppermute | solution.py:549
  100.6 2.8 %collective-permute-start.16 = (f32[56,256]{1,0:T(8,128)S(1)}, f32[56,256]{1,0:T(8,128)S(1)}, u32[]{:S(2)}, u32[]{:S(2)}) collective-permute-start(f32[56,256]{1,0:T(8,128)S(1)} %get-tuple-element.51), channel_id=1, source_target_pairs={{32,0},{40,8},{48,16},{56,24},{64,32},{72,40},{80,48},{88,56},{96,... | collective-permute-start | bytes 172040 | tf_op jit(solution)/shard_map/ppermute | solution.py:564
  103.4 1.6 %collective-permute-done.12.up_came = f32[200,256]{1,0:T(8,128)S(1)} collective-permute-done((f32[200,256]{1,0:T(8,128)}, f32[200,256]{1,0:T(8,128)S(1)}, u32[]{:S(2)}, u32[]{:S(2)}) %collective-permute-start.12) | collective-permute-done | bytes 204832 | tf_op jit(solution)/shard_map/ppermute | solution.py:549
  104.9 2.1 %collective-permute-done.13.down_came = f32[200,256]{1,0:T(8,128)S(1)} collective-permute-done((f32[200,256]{1,0:T(8,128)}, f32[200,256]{1,0:T(8,128)S(1)}, u32[]{:S(2)}, u32[]{:S(2)}) %collective-permute-start.13) | collective-permute-done | bytes 204832 | tf_op jit(solution)/shard_map/ppermute | solution.py:550
  107.4 1.4 %collective-permute-start.17 = (f32[2,200,256]{2,1,0:T(8,128)S(1)}, f32[2,200,256]{2,1,0:T(8,128)S(1)}, u32[]{:S(2)}, u32[]{:S(2)}) collective-permute-start(f32[2,200,256]{2,1,0:T(8,128)S(1)} %get-tuple-element.55), channel_id=1, source_target_pairs={{0,1},{1,2},{2,3},{3,0},{4,5},{5,6},{6,7},{7,4},{8,9},{9,10},{10,1... | collective-permute-start | bytes 1228808 | tf_op jit(solution)/shard_map/ppermute | solution.py:590
  108.9 2.1 %collective-permute-start.18 = (f32[2,200,256]{2,1,0:T(8,128)S(1)}, f32[2,200,256]{2,1,0:T(8,128)S(1)}, u32[]{:S(2)}, u32[]{:S(2)}) collective-permute-start(f32[2,200,256]{2,1,0:T(8,128)S(1)} %get-tuple-element.56), channel_id=1, source_target_pairs={{1,0},{2,1},{3,2},{0,3},{5,4},{6,5},{7,6},{4,7},{9,8},{10,9},{11,1... | collective-permute-start | bytes 1228808 | tf_op jit(solution)/shard_map/ppermute | solution.py:591
  111.9 2.6 %collective-permute-start.21 = (f32[2,56,256]{2,1,0:T(8,128)S(1)}, f32[2,56,256]{2,1,0:T(8,128)S(1)}, u32[]{:S(2)}, u32[]{:S(2)}) collective-permute-start(f32[2,56,256]{2,1,0:T(8,128)S(1)} %get-tuple-element.63), channel_id=1, source_target_pairs={{32,0},{40,8},{48,16},{56,24},{64,32},{72,40},{80,48},{88,56},{96,... | collective-permute-start | bytes 344072 | tf_op jit(solution)/shard_map/ppermute | solution.py:564
  114.5 2.8 %collective-permute-done.20.up_came = f32[2,56,256]{2,1,0:T(8,128)S(1)} collective-permute-done((f32[2,56,256]{2,1,0:T(8,128)S(1)}, f32[2,56,256]{2,1,0:T(8,128)S(1)}, u32[]{:S(2)}, u32[]{:S(2)}) %collective-permute-start.20) | collective-permute-done | bytes 114720 | tf_op jit(solution)/shard_map/ppermute | solution.py:563
  118.1 3.2 %collective-permute-start.23 = (f32[2,56,256]{2,1,0:T(8,128)S(1)}, f32[2,56,256]{2,1,0:T(8,128)S(1)}, u32[]{:S(2)}, u32[]{:S(2)}) collective-permute-start(f32[2,56,256]{2,1,0:T(8,128)S(1)} %get-tuple-element.65), channel_id=1, source_target_pairs={{32,0},{40,8},{48,16},{56,24},{64,32},{72,40},{80,48},{88,56},{96,... | collective-permute-start | bytes 344072 | tf_op jit(solution)/shard_map/ppermute | solution.py:564
  121.8 2.8 %collective-permute-start.19 = (f32[200,256]{1,0:T(8,128)S(1)}, f32[200,256]{1,0:T(8,128)S(1)}, u32[]{:S(2)}, u32[]{:S(2)}) collective-permute-start(f32[200,256]{1,0:T(8,128)S(1)} %get-tuple-element.58), channel_id=1, source_target_pairs={{0,4},{1,5},{2,6},{3,7},{4,0},{5,1},{6,2},{7,3},{8,12},{9,13},{10,... | collective-permute-start | bytes 614408 | tf_op jit(solution)/shard_map/ppermute | solution.py:479
  124.9 3.2 %collective-permute-start.25 = (f32[2,56,256]{2,1,0:T(8,128)S(1)}, f32[2,56,256]{2,1,0:T(8,128)S(1)}, u32[]{:S(2)}, u32[]{:S(2)}) collective-permute-start(f32[2,56,256]{2,1,0:T(8,128)S(1)} %get-tuple-element.67), channel_id=1, source_target_pairs={{32,0},{40,8},{48,16},{56,24},{64,32},{72,40},{80,48},{88,56},{96,... | collective-permute-start | bytes 344072 | tf_op jit(solution)/shard_map/ppermute | solution.py:564
  128.2 2.7 %collective-permute-done.24.up_came = f32[2,56,256]{2,1,0:T(8,128)S(1)} collective-permute-done((f32[2,56,256]{2,1,0:T(8,128)S(1)}, f32[2,56,256]{2,1,0:T(8,128)S(1)}, u32[]{:S(2)}, u32[]{:S(2)}) %collective-permute-start.24) | collective-permute-done | bytes 114720 | tf_op jit(solution)/shard_map/ppermute | solution.py:563
  131.7 3.0 %collective-permute-start.26 = (f32[56,256]{1,0:T(8,128)S(1)}, f32[56,256]{1,0:T(8,128)S(1)}, u32[]{:S(2)}, u32[]{:S(2)}) collective-permute-start(f32[56,256]{1,0:T(8,128)S(1)} %get-tuple-element.69), channel_id=1, source_target_pairs={{0,16},{8,24},{16,0},{24,8},{32,48},{40,56},{48,32},{56,40},{64,80... | collective-permute-start | bytes 172040 | tf_op jit(solution)/shard_map/ppermute | solution.py:479
  134.7 2.2 %collective-permute-done.26.b_ref = f32[56,256]{1,0:T(8,128)S(1)} collective-permute-done((f32[56,256]{1,0:T(8,128)S(1)}, f32[56,256]{1,0:T(8,128)S(1)}, u32[]{:S(2)}, u32[]{:S(2)}) %collective-permute-start.26) | collective-permute-done | bytes 57376 | tf_op jit(solution)/shard_map/ppermute | solution.py:479
  (70 shorter events, 14.9 us)
Async XLA Ops:
  4.2 34.4 %copy-start.1 = (bf16[1536,256]{1,0:T(8,128)(2,1)S(1)}, bf16[1536,256]{1,0:T(8,128)(2,1)}, u32[]{:S(2)}) copy-start(bf16[1536,256]{1,0:T(8,128)(2,1)} %param.4) | copy-start | bytes 2359300
  4.2 34.4 %copy-start.3 = (bf16[1536,256]{1,0:T(8,128)(2,1)S(1)}, bf16[1536,256]{1,0:T(8,128)(2,1)}, u32[]{:S(2)}) copy-start(bf16[1536,256]{1,0:T(8,128)(2,1)} %param.5) | copy-start | bytes 2359300
  11.2 6.6 %collective-permute-start = (f32[8,256]{1,0:T(8,128)S(1)}, f32[8,256]{1,0:T(8,128)S(1)}, u32[]{:S(2)}, u32[]{:S(2)}) collective-permute-start(f32[8,256]{1,0:T(8,128)S(1)} %get-tuple-element.38), channel_id=1, source_target_pairs={{0,4},{1,5},{2,6},{3,7},{4,0},{5,1},{6,2},{7,3},{8,12},{9,13},{10,... | collective-permute-start | bytes 24584 | tf_op jit(solution)/shard_map/ppermute | solution.py:479
  15.9 5.2 %collective-permute-start.5 = (f32[8,256]{1,0:T(8,128)S(1)}, f32[8,256]{1,0:T(8,128)S(1)}, u32[]{:S(2)}, u32[]{:S(2)}) collective-permute-start(f32[8,256]{1,0:T(8,128)S(1)} %get-tuple-element.39), channel_id=1, source_target_pairs={{0,24},{8,16},{16,8},{24,0},{32,56},{40,48},{48,40},{56,32},{64,88... | collective-permute-start | bytes 24584 | tf_op jit(solution)/shard_map/ppermute | solution.py:479
  15.9 5.2 %collective-permute-start.4 = (f32[8,256]{1,0:T(8,128)S(1)}, f32[8,256]{1,0:T(8,128)S(1)}, u32[]{:S(2)}, u32[]{:S(2)}) collective-permute-start(f32[8,256]{1,0:T(8,128)S(1)} %get-tuple-element.39), channel_id=1, source_target_pairs={{0,16},{8,24},{16,0},{24,8},{32,48},{40,56},{48,32},{56,40},{64,80... | collective-permute-start | bytes 24584 | tf_op jit(solution)/shard_map/ppermute | solution.py:479
  17.5 3.6 %collective-permute-start.3 = (f32[8,256]{1,0:T(8,128)S(1)}, f32[8,256]{1,0:T(8,128)S(1)}, u32[]{:S(2)}, u32[]{:S(2)}) collective-permute-start(f32[8,256]{1,0:T(8,128)S(1)} %get-tuple-element.39), channel_id=1, source_target_pairs={{0,8},{8,0},{16,24},{24,16},{32,40},{40,32},{48,56},{56,48},{64,72... | collective-permute-start | bytes 24584 | tf_op jit(solution)/shard_map/ppermute | solution.py:479
  17.8 12.4 %collective-permute-start.1 = (f32[8,256]{1,0:T(8,128)S(1)}, f32[8,256]{1,0:T(8,128)S(1)}, u32[]{:S(2)}, u32[]{:S(2)}) collective-permute-start(f32[8,256]{1,0:T(8,128)S(1)} %multiply_add_fusion.5), channel_id=1, source_target_pairs={{0,2},{1,3},{2,0},{3,1},{4,6},{5,7},{6,4},{7,5},{8,10},{9,11},{10,... | collective-permute-start | bytes 24584 | tf_op jit(solution)/shard_map/ppermute | solution.py:479
  21.8 16.8 %all-to-all-start = ((f32[8,8,256]{2,1,0:T(8,128)}), f32[8,8,256]{2,1,0:T(8,128)S(1)}, u32[]{:S(2)}, u32[]{:S(2)}) async-start(f32[8,8,256]{2,1,0:T(8,128)} %broadcast_in_dim.4), calls=%async_computation | async-start | bytes 131072 | tf_op jit(solution)/shard_map/all_to_all | solution.py:489
  30.3 3.7 %collective-permute-start.2 = (f32[8,256]{1,0:T(8,128)S(1)}, f32[8,256]{1,0:T(8,128)S(1)}, u32[]{:S(2)}, u32[]{:S(2)}) collective-permute-start(f32[8,256]{1,0:T(8,128)S(1)} %multiply_add_fusion.4.rest_0_), channel_id=1, source_target_pairs={{0,1},{1,0},{2,3},{3,2},{4,5},{5,4},{6,7},{7,6},{8,9},{9,8},{10,11... | collective-permute-start | bytes 24584 | tf_op jit(solution)/shard_map/ppermute | solution.py:479
  45.5 7.6 %collective-permute-start.6 = (f32[8,256]{1,0:T(8,128)S(1)}, f32[8,256]{1,0:T(8,128)S(1)}, u32[]{:S(2)}, u32[]{:S(2)}) collective-permute-start(f32[8,256]{1,0:T(8,128)S(1)} %get-tuple-element.42), channel_id=1, source_target_pairs={{0,4},{1,5},{2,6},{3,7},{4,0},{5,1},{6,2},{7,3},{8,12},{9,13},{10,... | collective-permute-start | bytes 24584 | tf_op jit(solution)/shard_map/ppermute | solution.py:479
  51.3 3.1 %collective-permute-start.11 = (f32[8,256]{1,0:T(8,128)S(1)}, f32[8,256]{1,0:T(8,128)S(1)}, u32[]{:S(2)}, u32[]{:S(2)}) collective-permute-start(f32[8,256]{1,0:T(8,128)S(1)} %get-tuple-element.43), channel_id=1, source_target_pairs={{0,24},{8,16},{16,8},{24,0},{32,56},{40,48},{48,40},{56,32},{64,88... | collective-permute-start | bytes 24584 | tf_op jit(solution)/shard_map/ppermute | solution.py:479
  51.3 3.7 %collective-permute-start.10 = (f32[8,256]{1,0:T(8,128)S(1)}, f32[8,256]{1,0:T(8,128)S(1)}, u32[]{:S(2)}, u32[]{:S(2)}) collective-permute-start(f32[8,256]{1,0:T(8,128)S(1)} %get-tuple-element.43), channel_id=1, source_target_pairs={{0,16},{8,24},{16,0},{24,8},{32,48},{40,56},{48,32},{56,40},{64,80... | collective-permute-start | bytes 24584 | tf_op jit(solution)/shard_map/ppermute | solution.py:479
  52.4 2.6 %collective-permute-start.9 = (f32[8,256]{1,0:T(8,128)S(1)}, f32[8,256]{1,0:T(8,128)S(1)}, u32[]{:S(2)}, u32[]{:S(2)}) collective-permute-start(f32[8,256]{1,0:T(8,128)S(1)} %get-tuple-element.43), channel_id=1, source_target_pairs={{0,8},{8,0},{16,24},{24,16},{32,40},{40,32},{48,56},{56,48},{64,72... | collective-permute-start | bytes 24584 | tf_op jit(solution)/shard_map/ppermute | solution.py:479
  53.2 5.8 %collective-permute-start.7 = (f32[8,256]{1,0:T(8,128)S(1)}, f32[8,256]{1,0:T(8,128)S(1)}, u32[]{:S(2)}, u32[]{:S(2)}) collective-permute-start(f32[8,256]{1,0:T(8,128)S(1)} %multiply_add_fusion.2), channel_id=1, source_target_pairs={{0,2},{1,3},{2,0},{3,1},{4,6},{5,7},{6,4},{7,5},{8,10},{9,11},{10,... | collective-permute-start | bytes 24584 | tf_op jit(solution)/shard_map/ppermute | solution.py:479
  55.6 11.7 %all-to-all-start.1 = ((f32[8,8,256]{2,1,0:T(8,128)}), f32[8,8,256]{2,1,0:T(8,128)S(1)}, u32[]{:S(2)}, u32[]{:S(2)}) async-start(f32[8,8,256]{2,1,0:T(8,128)} %broadcast_in_dim.5), calls=%async_computation.1 | async-start | bytes 131072 | tf_op jit(solution)/shard_map/all_to_all | solution.py:489
  59.0 3.7 %collective-permute-start.8 = (f32[8,256]{1,0:T(8,128)S(1)}, f32[8,256]{1,0:T(8,128)S(1)}, u32[]{:S(2)}, u32[]{:S(2)}) collective-permute-start(f32[8,256]{1,0:T(8,128)S(1)} %multiply_add_fusion.1.rest_0_), channel_id=1, source_target_pairs={{0,1},{1,0},{2,3},{3,2},{4,5},{5,4},{6,7},{7,6},{8,9},{9,8},{10,11... | collective-permute-start | bytes 24584 | tf_op jit(solution)/shard_map/ppermute | solution.py:479
  89.1 10.5 %collective-permute-start.14 = (f32[16,56,256]{2,1,0:T(8,128)}, f32[16,56,256]{2,1,0:T(8,128)S(1)}, u32[]{:S(2)}, u32[]{:S(2)}) collective-permute-start(f32[16,56,256]{2,1,0:T(8,128)} %get-tuple-element.49), channel_id=1, source_target_pairs={{0,8},{8,0},{16,24},{24,16},{32,40},{40,32},{48,56},{56,48},{64,72... | collective-permute-start | bytes 2752520 | tf_op jit(solution)/shard_map/ppermute | solution.py:479
  94.6 10.4 %collective-permute-start.12 = (f32[200,256]{1,0:T(8,128)}, f32[200,256]{1,0:T(8,128)S(1)}, u32[]{:S(2)}, u32[]{:S(2)}) collective-permute-start(f32[200,256]{1,0:T(8,128)} %get-tuple-element.46), channel_id=1, source_target_pairs={{0,1},{1,2},{2,3},{3,0},{4,5},{5,6},{6,7},{7,4},{8,9},{9,10},{10,1... | collective-permute-start | bytes 614408 | tf_op jit(solution)/shard_map/ppermute | solution.py:549
  99.6 7.4 %collective-permute-start.13 = (f32[200,256]{1,0:T(8,128)}, f32[200,256]{1,0:T(8,128)S(1)}, u32[]{:S(2)}, u32[]{:S(2)}) collective-permute-start(f32[200,256]{1,0:T(8,128)} %get-tuple-element.47), channel_id=1, source_target_pairs={{1,0},{2,1},{3,2},{0,3},{5,4},{6,5},{7,6},{4,7},{9,8},{10,9},{11,1... | collective-permute-start | bytes 614408 | tf_op jit(solution)/shard_map/ppermute | solution.py:550
  100.0 7.0 %collective-permute-start.15 = (f32[56,256]{1,0:T(8,128)S(1)}, f32[56,256]{1,0:T(8,128)S(1)}, u32[]{:S(2)}, u32[]{:S(2)}) collective-permute-start(f32[56,256]{1,0:T(8,128)S(1)} %get-tuple-element.50), channel_id=1, source_target_pairs={{0,32},{8,40},{16,48},{24,56},{32,64},{40,72},{48,80},{56,88},{64,... | collective-permute-start | bytes 172040 | tf_op jit(solution)/shard_map/ppermute | solution.py:563
  100.6 6.5 %collective-permute-start.16 = (f32[56,256]{1,0:T(8,128)S(1)}, f32[56,256]{1,0:T(8,128)S(1)}, u32[]{:S(2)}, u32[]{:S(2)}) collective-permute-start(f32[56,256]{1,0:T(8,128)S(1)} %get-tuple-element.51), channel_id=1, source_target_pairs={{32,0},{40,8},{48,16},{56,24},{64,32},{72,40},{80,48},{88,56},{96,... | collective-permute-start | bytes 172040 | tf_op jit(solution)/shard_map/ppermute | solution.py:564
  107.4 13.9 %collective-permute-start.17 = (f32[2,200,256]{2,1,0:T(8,128)S(1)}, f32[2,200,256]{2,1,0:T(8,128)S(1)}, u32[]{:S(2)}, u32[]{:S(2)}) collective-permute-start(f32[2,200,256]{2,1,0:T(8,128)S(1)} %get-tuple-element.55), channel_id=1, source_target_pairs={{0,1},{1,2},{2,3},{3,0},{4,5},{5,6},{6,7},{7,4},{8,9},{9,10},{10,1... | collective-permute-start | bytes 1228808 | tf_op jit(solution)/shard_map/ppermute | solution.py:590
  108.9 12.5 %collective-permute-start.18 = (f32[2,200,256]{2,1,0:T(8,128)S(1)}, f32[2,200,256]{2,1,0:T(8,128)S(1)}, u32[]{:S(2)}, u32[]{:S(2)}) collective-permute-start(f32[2,200,256]{2,1,0:T(8,128)S(1)} %get-tuple-element.56), channel_id=1, source_target_pairs={{1,0},{2,1},{3,2},{0,3},{5,4},{6,5},{7,6},{4,7},{9,8},{10,9},{11,1... | collective-permute-start | bytes 1228808 | tf_op jit(solution)/shard_map/ppermute | solution.py:591
  111.2 6.1 %collective-permute-start.20 = (f32[2,56,256]{2,1,0:T(8,128)S(1)}, f32[2,56,256]{2,1,0:T(8,128)S(1)}, u32[]{:S(2)}, u32[]{:S(2)}) collective-permute-start(f32[2,56,256]{2,1,0:T(8,128)S(1)} %get-tuple-element.62), channel_id=1, source_target_pairs={{0,32},{8,40},{16,48},{24,56},{32,64},{40,72},{48,80},{56,88},{64,... | collective-permute-start | bytes 344072 | tf_op jit(solution)/shard_map/ppermute | solution.py:563
  111.9 9.5 %copy-start.5 = (f32[2,200,256]{2,1,0:T(8,128)S(1)}, f32[2,200,256]{2,1,0:T(8,128)}, u32[]{:S(2)}) copy-start(f32[2,200,256]{2,1,0:T(8,128)} %copy-done.4) | copy-start | bytes 1228804
  111.9 5.4 %collective-permute-start.21 = (f32[2,56,256]{2,1,0:T(8,128)S(1)}, f32[2,56,256]{2,1,0:T(8,128)S(1)}, u32[]{:S(2)}, u32[]{:S(2)}) collective-permute-start(f32[2,56,256]{2,1,0:T(8,128)S(1)} %get-tuple-element.63), channel_id=1, source_target_pairs={{32,0},{40,8},{48,16},{56,24},{64,32},{72,40},{80,48},{88,56},{96,... | collective-permute-start | bytes 344072 | tf_op jit(solution)/shard_map/ppermute | solution.py:564
  118.1 6.5 %collective-permute-start.22 = (f32[2,56,256]{2,1,0:T(8,128)}, f32[2,56,256]{2,1,0:T(8,128)S(1)}, u32[]{:S(2)}, u32[]{:S(2)}) collective-permute-start(f32[2,56,256]{2,1,0:T(8,128)} %get-tuple-element.64), channel_id=1, source_target_pairs={{0,32},{8,40},{16,48},{24,56},{32,64},{40,72},{48,80},{56,88},{64,... | collective-permute-start | bytes 344072 | tf_op jit(solution)/shard_map/ppermute | solution.py:563
  118.1 6.5 %collective-permute-start.23 = (f32[2,56,256]{2,1,0:T(8,128)S(1)}, f32[2,56,256]{2,1,0:T(8,128)S(1)}, u32[]{:S(2)}, u32[]{:S(2)}) collective-permute-start(f32[2,56,256]{2,1,0:T(8,128)S(1)} %get-tuple-element.65), channel_id=1, source_target_pairs={{32,0},{40,8},{48,16},{56,24},{64,32},{72,40},{80,48},{88,56},{96,... | collective-permute-start | bytes 344072 | tf_op jit(solution)/shard_map/ppermute | solution.py:564
  121.8 15.9 %collective-permute-start.19 = (f32[200,256]{1,0:T(8,128)S(1)}, f32[200,256]{1,0:T(8,128)S(1)}, u32[]{:S(2)}, u32[]{:S(2)}) collective-permute-start(f32[200,256]{1,0:T(8,128)S(1)} %get-tuple-element.58), channel_id=1, source_target_pairs={{0,4},{1,5},{2,6},{3,7},{4,0},{5,1},{6,2},{7,3},{8,12},{9,13},{10,... | collective-permute-start | bytes 614408 | tf_op jit(solution)/shard_map/ppermute | solution.py:479
  124.8 6.1 %collective-permute-start.24 = (f32[2,56,256]{2,1,0:T(8,128)S(1)}, f32[2,56,256]{2,1,0:T(8,128)S(1)}, u32[]{:S(2)}, u32[]{:S(2)}) collective-permute-start(f32[2,56,256]{2,1,0:T(8,128)S(1)} %get-tuple-element.66), channel_id=1, source_target_pairs={{0,32},{8,40},{16,48},{24,56},{32,64},{40,72},{48,80},{56,88},{64,... | collective-permute-start | bytes 344072 | tf_op jit(solution)/shard_map/ppermute | solution.py:563
  124.9 6.0 %collective-permute-start.25 = (f32[2,56,256]{2,1,0:T(8,128)S(1)}, f32[2,56,256]{2,1,0:T(8,128)S(1)}, u32[]{:S(2)}, u32[]{:S(2)}) collective-permute-start(f32[2,56,256]{2,1,0:T(8,128)S(1)} %get-tuple-element.67), channel_id=1, source_target_pairs={{32,0},{40,8},{48,16},{56,24},{64,32},{72,40},{80,48},{88,56},{96,... | collective-permute-start | bytes 344072 | tf_op jit(solution)/shard_map/ppermute | solution.py:564
  131.7 5.2 %collective-permute-start.26 = (f32[56,256]{1,0:T(8,128)S(1)}, f32[56,256]{1,0:T(8,128)S(1)}, u32[]{:S(2)}, u32[]{:S(2)}) collective-permute-start(f32[56,256]{1,0:T(8,128)S(1)} %get-tuple-element.69), channel_id=1, source_target_pairs={{0,16},{8,24},{16,0},{24,8},{32,48},{40,56},{48,32},{56,40},{64,80... | collective-permute-start | bytes 172040 | tf_op jit(solution)/shard_map/ppermute | solution.py:479
  (8 other events, 20.0 us)

commit v10 on v8

--- a/solution.py
+++ b/solution.py
@@ -562,6 +562,8 @@
     for away in range(n_z // 2 - 1, -1, -1):
         z_up = lax.ppermute(z_up, "src", z_ups)
         z_down = lax.ppermute(z_down, "src", z_downs)
+        if away == n_z // 2 - 1:
+            up_came, down_came, _, _ = lax.optimization_barrier((up_came, down_came, z_up, z_down))
         if away:
             z_up, z_down = call(
                 functools.partial(ring_kernel, b_rows, away),

time: 142 us -> 138 us (0.972)
  starting transfers between devices: 51.9 us -> 69.7 us
  Pallas kernels: 47 us -> 32.1 us
  waiting for transfers between devices: 36.6 us -> 27.1 us
  local copies, waits for them, and re-layouts: 4.23 us -> 6.47 us
    ppermute x15, starting transfers between devices: 13.9 us -> 35.7 us  [swap(): return lax.ppermute(value, axis, [(k, k ^ bit) for k in range(size)])]
    pallas_call x1, Pallas kernels: 24 us -> 15.5 us  [per_device(): pl.pallas_call(functools.partial(maps_kernel, 2, scale, blocks), out_shap...]
    ppermute x1, starting transfers between devices: 7.78 us -> 0.28 us  [per_device(): up_came = lax.ppermute(up_first, 'tgt', ups)]
    ppermute x15, waiting for transfers between devices: 11.8 us -> 8.04 us  [swap(): return lax.ppermute(value, axis, [(k, k ^ bit) for k in range(size)])]
    ppermute x1, waiting for transfers between devices: 5 us -> 1.43 us  [per_device(): up_came = lax.ppermute(up_first, 'tgt', ups)]
    ppermute x1, starting transfers between devices: 0.01 us -> 2.96 us  [per_device(): down_came = lax.ppermute(down_first, 'tgt', downs)]
    pallas_call x1, Pallas kernels: 8.25 us -> 5.73 us  [per_device(): pl.pallas_call(functools.partial(second_kernel, 2, scale, blocks), out_sh...]
    pallas_call x1, Pallas kernels: 8.31 us -> 5.8 us  [per_device(): pl.pallas_call(functools.partial(first_kernel, scale, blocks), out_shape=...]
  transfers between devices with their start and end apart: 29 -> 29, of which waited for: 13 -> 11; matrix products, arithmetic and copies ran while one was open for 1% -> 1% of each run, Pallas kernels for 4% -> 3%
where the time goes in v10:
time: 138 us; the launch traced here: 137 us
  starting transfers between devices  69.7 us (51%)
  Pallas kernels  32.1 us (23%)
  waiting for transfers between devices  27.1 us (20%)
  local copies, waits for them, and re-layouts  6.47 us (5%)
  between operations  1.46 us (1%)
    ppermute x15, starting transfers between devices, swap(): return lax.ppermute(value, axis, [(k, k ^ bit) for k in range(size)])  35.7 us
    pallas_call x1, Pallas kernels, per_device(): pl.pallas_call(functools.partial(maps_kernel, 2, scale, blocks), out_shap...  15.5 us
    all_to_all x2, starting transfers between devices, exchange(): lax.all_to_all(copies, 'src', 0, 0, axis_index_groups=along_z, tiled=True)  13.9 us
    ppermute x4, starting transfers between devices, per_device(): z_down = lax.ppermute(z_down, 'src', z_downs)  13.1 us
    all_to_all x2, waiting for transfers between devices, exchange(): lax.all_to_all(copies, 'src', 0, 0, axis_index_groups=along_z, tiled=True)  9.09 us
    ppermute x4, waiting for transfers between devices, per_device(): z_up = lax.ppermute(z_up, 'src', z_ups)  8.49 us
    ppermute x15, waiting for transfers between devices, swap(): return lax.ppermute(value, axis, [(k, k ^ bit) for k in range(size)])  8.04 us
    pallas_call x1, Pallas kernels, per_device(): pl.pallas_call(functools.partial(first_kernel, scale, blocks), out_shape=...  5.8 us
  transfers between devices with their start and end apart: 29, of which 11 were waited for; matrix products, arithmetic and copies ran while one was open for 1% of the time, Pallas kernels for 3%

profile of v10, /device:TPU:8, one launch (start us, length us, event | category | flops | bytes accessed | tf_op | source)
XLA Modules:
  0.0 137.1 jit_solution(13550944973765991232)
XLA Ops:
  2.0 1.1 copy-done
  3.1 1.1 copy-done.2
  4.2 5.8 %shard_map.59 = (f32[8,256]{1,0:T(8,128)S(1)}, f32[8,256]{1,0:T(8,128)S(1)}, f32[8,256]{1,0:T(8,128)S(1)}, f32[8,256]{1,0:T(8,128)S(1)}) custom-call(s32[2,24]{1,0:T(2,128)S(1)} %bitcast.20, s32[1]{0:T(128)} %bitcast.11.count_ref, bf16[6,256,256]{2,1,0:T(8,128)(2,1)S(1)} %bitcast.14, bf16[6,256,256]{2,1,0:T(8,128)(2,1)S(1)} %bitcast.17), custom_call_target="tpu_custom_call" | custom-call | tf_op jit(solution)/shard_map/pallas_call | solution.py:492
  10.0 4.3 %collective-permute-start = (f32[8,256]{1,0:T(8,128)S(1)}, f32[8,256]{1,0:T(8,128)S(1)}, u32[]{:S(2)}, u32[]{:S(2)}) collective-permute-start(f32[8,256]{1,0:T(8,128)S(1)} %get-tuple-element.36), channel_id=1, source_target_pairs={{0,4},{1,5},{2,6},{3,7},{4,0},{5,1},{6,2},{7,3},{8,12},{9,13},{10,... | collective-permute-start | bytes 24584 | tf_op jit(solution)/shard_map/ppermute | solution.py:479
  14.3 3.0 %collective-permute-start.4 = (f32[8,256]{1,0:T(8,128)S(1)}, f32[8,256]{1,0:T(8,128)S(1)}, u32[]{:S(2)}, u32[]{:S(2)}) collective-permute-start(f32[8,256]{1,0:T(8,128)S(1)} %get-tuple-element.37), channel_id=1, source_target_pairs={{0,16},{8,24},{16,0},{24,8},{32,48},{40,56},{48,32},{56,40},{64,80... | collective-permute-start | bytes 24584 | tf_op jit(solution)/shard_map/ppermute | solution.py:479
  17.3 2.4 %collective-permute-start.1 = (f32[8,256]{1,0:T(8,128)S(1)}, f32[8,256]{1,0:T(8,128)S(1)}, u32[]{:S(2)}, u32[]{:S(2)}) collective-permute-start(f32[8,256]{1,0:T(8,128)S(1)} %multiply_add_fusion.5), channel_id=1, source_target_pairs={{0,2},{1,3},{2,0},{3,1},{4,6},{5,7},{6,4},{7,5},{8,10},{9,11},{10,... | collective-permute-start | bytes 24584 | tf_op jit(solution)/shard_map/ppermute | solution.py:479
  20.4 9.7 %all-to-all-start = ((f32[8,8,256]{2,1,0:T(8,128)}), f32[8,8,256]{2,1,0:T(8,128)S(1)}, u32[]{:S(2)}, u32[]{:S(2)}) async-start(f32[8,8,256]{2,1,0:T(8,128)} %broadcast_in_dim.4), calls=%async_computation | async-start | bytes 131072 | tf_op jit(solution)/shard_map/all_to_all | solution.py:489
  30.1 1.6 %collective-permute-start.2 = (f32[8,256]{1,0:T(8,128)S(1)}, f32[8,256]{1,0:T(8,128)S(1)}, u32[]{:S(2)}, u32[]{:S(2)}) collective-permute-start(f32[8,256]{1,0:T(8,128)S(1)} %multiply_add_fusion.4.rest_0_), channel_id=1, source_target_pairs={{0,1},{1,0},{2,3},{3,2},{4,5},{5,4},{6,7},{7,6},{8,9},{9,8},{10,11... | collective-permute-start | bytes 24584 | tf_op jit(solution)/shard_map/ppermute | solution.py:479
  31.7 2.2 %collective-permute-done.2.rest_1_ = f32[8,256]{1,0:T(8,128)S(1)} collective-permute-done((f32[8,256]{1,0:T(8,128)S(1)}, f32[8,256]{1,0:T(8,128)S(1)}, u32[]{:S(2)}, u32[]{:S(2)}) %collective-permute-start.2) | collective-permute-done | bytes 8224 | tf_op jit(solution)/shard_map/ppermute | solution.py:479
  33.8 4.6 %all-to-all-done.rest_2_ = f32[8,8,256]{2,1,0:T(8,128)S(1)} async-done(((f32[8,8,256]{2,1,0:T(8,128)}), f32[8,8,256]{2,1,0:T(8,128)S(1)}, u32[]{:S(2)}, u32[]{:S(2)}) %all-to-all-start) | async-done | bytes 65568 | tf_op jit(solution)/shard_map/all_to_all | solution.py:489
  38.4 5.7 %shard_map.60 = (f32[8,256]{1,0:T(8,128)S(1)}, f32[8,256]{1,0:T(8,128)S(1)}, f32[8,256]{1,0:T(8,128)S(1)}, f32[8,256]{1,0:T(8,128)S(1)}) custom-call(s32[2,24]{1,0:T(2,128)S(1)} %bitcast.21, s32[1]{0:T(128)} %bitcast.12.count_ref, bf16[6,256,256]{2,1,0:T(8,128)(2,1)S(1)} %bitcast.15, bf16[6,256,256]{2,1,0:T(8,128)(2,1)S(1)} %bitcast.18, ...), custom_call_target="tpu_custom_call" | custom-call | tf_op jit(solution)/shard_map/pallas_call | solution.py:501
  44.2 4.0 %collective-permute-start.6 = (f32[8,256]{1,0:T(8,128)S(1)}, f32[8,256]{1,0:T(8,128)S(1)}, u32[]{:S(2)}, u32[]{:S(2)}) collective-permute-start(f32[8,256]{1,0:T(8,128)S(1)} %get-tuple-element.40), channel_id=1, source_target_pairs={{0,4},{1,5},{2,6},{3,7},{4,0},{5,1},{6,2},{7,3},{8,12},{9,13},{10,... | collective-permute-start | bytes 24584 | tf_op jit(solution)/shard_map/ppermute | solution.py:479
  48.2 2.9 %collective-permute-start.10 = (f32[8,256]{1,0:T(8,128)S(1)}, f32[8,256]{1,0:T(8,128)S(1)}, u32[]{:S(2)}, u32[]{:S(2)}) collective-permute-start(f32[8,256]{1,0:T(8,128)S(1)} %get-tuple-element.41), channel_id=1, source_target_pairs={{0,16},{8,24},{16,0},{24,8},{32,48},{40,56},{48,32},{56,40},{64,80... | collective-permute-start | bytes 24584 | tf_op jit(solution)/shard_map/ppermute | solution.py:479
  51.5 1.3 collective-permute-done.10
  53.5 4.2 %all-to-all-start.1 = ((f32[8,8,256]{2,1,0:T(8,128)}), f32[8,8,256]{2,1,0:T(8,128)S(1)}, u32[]{:S(2)}, u32[]{:S(2)}) async-start(f32[8,8,256]{2,1,0:T(8,128)} %broadcast_in_dim.5), calls=%async_computation.1 | async-start | bytes 131072 | tf_op jit(solution)/shard_map/all_to_all | solution.py:489
  57.7 2.4 %collective-permute-start.8 = (f32[8,256]{1,0:T(8,128)S(1)}, f32[8,256]{1,0:T(8,128)S(1)}, u32[]{:S(2)}, u32[]{:S(2)}) collective-permute-start(f32[8,256]{1,0:T(8,128)S(1)} %multiply_add_fusion.1.rest_0_), channel_id=1, source_target_pairs={{0,1},{1,0},{2,3},{3,2},{4,5},{5,4},{6,7},{7,6},{8,9},{9,8},{10,11... | collective-permute-start | bytes 24584 | tf_op jit(solution)/shard_map/ppermute | solution.py:479
  60.2 1.6 %collective-permute-done.8.rest_1_ = f32[8,256]{1,0:T(8,128)S(1)} collective-permute-done((f32[8,256]{1,0:T(8,128)S(1)}, f32[8,256]{1,0:T(8,128)S(1)}, u32[]{:S(2)}, u32[]{:S(2)}) %collective-permute-start.8) | collective-permute-done | bytes 8224 | tf_op jit(solution)/shard_map/ppermute | solution.py:479
  61.8 4.5 %all-to-all-done.1.rest_2_ = f32[8,8,256]{2,1,0:T(8,128)S(1)} async-done(((f32[8,8,256]{2,1,0:T(8,128)}), f32[8,8,256]{2,1,0:T(8,128)S(1)}, u32[]{:S(2)}, u32[]{:S(2)}) %all-to-all-start.1) | async-done | bytes 65568 | tf_op jit(solution)/shard_map/all_to_all | solution.py:489
  66.3 15.5 %shard_map.61 = (f32[16,56,256]{2,1,0:T(8,128)S(1)}, f32[16,56,256]{2,1,0:T(8,128)}, f32[2,200,256]{2,1,0:T(8,128)S(1)}, f32[200,256]{1,0:T(8,128)}, f32[200,256...) custom-call(s32[2]{0:T(128)S(1)} %pad_add_fusion.place_ref, s32[2,24]{1,0:T(2,128)S(1)} %bitcast.22, ...), custom_call_target="tpu_custom_call" | custom-call | tf_op jit(solution)/shard_map/pallas_call | solution.py:527
  84.0 13.4 %collective-permute-start.14 = (f32[16,56,256]{2,1,0:T(8,128)}, f32[16,56,256]{2,1,0:T(8,128)S(1)}, u32[]{:S(2)}, u32[]{:S(2)}) collective-permute-start(f32[16,56,256]{2,1,0:T(8,128)} %get-tuple-element.47), channel_id=1, source_target_pairs={{0,8},{8,0},{16,24},{24,16},{32,40},{40,32},{48,56},{56,48},{64,72... | collective-permute-start | bytes 2752520 | tf_op jit(solution)/shard_map/ppermute | solution.py:479
  97.7 3.0 %collective-permute-start.13 = (f32[200,256]{1,0:T(8,128)}, f32[200,256]{1,0:T(8,128)S(1)}, u32[]{:S(2)}, u32[]{:S(2)}) collective-permute-start(f32[200,256]{1,0:T(8,128)} %get-tuple-element.45), channel_id=1, source_target_pairs={{1,0},{2,1},{3,2},{0,3},{5,4},{6,5},{7,6},{4,7},{9,8},{10,9},{11,1... | collective-permute-start | bytes 614408 | tf_op jit(solution)/shard_map/ppermute | solution.py:550
  101.1 3.2 %collective-permute-start.16 = (f32[56,256]{1,0:T(8,128)S(1)}, f32[56,256]{1,0:T(8,128)S(1)}, u32[]{:S(2)}, u32[]{:S(2)}) collective-permute-start(f32[56,256]{1,0:T(8,128)S(1)} %get-tuple-element.49), channel_id=1, source_target_pairs={{32,0},{40,8},{48,16},{56,24},{64,32},{72,40},{80,48},{88,56},{96,... | collective-permute-start | bytes 172040 | tf_op jit(solution)/shard_map/ppermute | solution.py:564
  104.4 1.4 %collective-permute-done.12.up_came = f32[200,256]{1,0:T(8,128)S(1)} collective-permute-done((f32[200,256]{1,0:T(8,128)}, f32[200,256]{1,0:T(8,128)S(1)}, u32[]{:S(2)}, u32[]{:S(2)}) %collective-permute-start.12) | collective-permute-done | bytes 204832 | tf_op jit(solution)/shard_map/ppermute | solution.py:549
  107.2 3.2 %collective-permute-start.18 = (f32[2,200,256]{2,1,0:T(8,128)S(1)}, f32[2,200,256]{2,1,0:T(8,128)S(1)}, u32[]{:S(2)}, u32[]{:S(2)}) collective-permute-start(f32[2,200,256]{2,1,0:T(8,128)S(1)} %get-tuple-element.54), channel_id=1, source_target_pairs={{1,0},{2,1},{3,2},{0,3},{5,4},{6,5},{7,6},{4,7},{9,8},{10,9},{11,1... | collective-permute-start | bytes 1228808 | tf_op jit(solution)/shard_map/ppermute | solution.py:589
  110.7 3.3 %collective-permute-start.21 = (f32[2,56,256]{2,1,0:T(8,128)S(1)}, f32[2,56,256]{2,1,0:T(8,128)S(1)}, u32[]{:S(2)}, u32[]{:S(2)}) collective-permute-start(f32[2,56,256]{2,1,0:T(8,128)S(1)} %get-tuple-element.59), channel_id=1, source_target_pairs={{32,0},{40,8},{48,16},{56,24},{64,32},{72,40},{80,48},{88,56},{96,... | collective-permute-start | bytes 344072 | tf_op jit(solution)/shard_map/ppermute | solution.py:564
  114.1 2.7 %collective-permute-done.20.up_came = f32[2,56,256]{2,1,0:T(8,128)S(1)} collective-permute-done((f32[2,56,256]{2,1,0:T(8,128)S(1)}, f32[2,56,256]{2,1,0:T(8,128)S(1)}, u32[]{:S(2)}, u32[]{:S(2)}) %collective-permute-start.20) | collective-permute-done | bytes 114720 | tf_op jit(solution)/shard_map/ppermute | solution.py:563
  117.6 3.3 %collective-permute-start.23 = (f32[2,56,256]{2,1,0:T(8,128)S(1)}, f32[2,56,256]{2,1,0:T(8,128)S(1)}, u32[]{:S(2)}, u32[]{:S(2)}) collective-permute-start(f32[2,56,256]{2,1,0:T(8,128)S(1)} %get-tuple-element.61), channel_id=1, source_target_pairs={{32,0},{40,8},{48,16},{56,24},{64,32},{72,40},{80,48},{88,56},{96,... | collective-permute-start | bytes 344072 | tf_op jit(solution)/shard_map/ppermute | solution.py:564
  121.5 2.4 %collective-permute-done.22.up_came = f32[2,56,256]{2,1,0:T(8,128)S(1)} collective-permute-done((f32[2,56,256]{2,1,0:T(8,128)}, f32[2,56,256]{2,1,0:T(8,128)S(1)}, u32[]{:S(2)}, u32[]{:S(2)}) %collective-permute-start.22) | collective-permute-done | bytes 114720 | tf_op jit(solution)/shard_map/ppermute | solution.py:563
  124.2 3.2 %collective-permute-start.25 = (f32[2,56,256]{2,1,0:T(8,128)S(1)}, f32[2,56,256]{2,1,0:T(8,128)S(1)}, u32[]{:S(2)}, u32[]{:S(2)}) collective-permute-start(f32[2,56,256]{2,1,0:T(8,128)S(1)} %get-tuple-element.63), channel_id=1, source_target_pairs={{32,0},{40,8},{48,16},{56,24},{64,32},{72,40},{80,48},{88,56},{96,... | collective-permute-start | bytes 344072 | tf_op jit(solution)/shard_map/ppermute | solution.py:564
  127.5 2.7 %collective-permute-done.24.up_came = f32[2,56,256]{2,1,0:T(8,128)S(1)} collective-permute-done((f32[2,56,256]{2,1,0:T(8,128)S(1)}, f32[2,56,256]{2,1,0:T(8,128)S(1)}, u32[]{:S(2)}, u32[]{:S(2)}) %collective-permute-start.24) | collective-permute-done | bytes 114720 | tf_op jit(solution)/shard_map/ppermute | solution.py:563
  131.0 1.3 collective-permute-start.26
  132.3 3.0 %collective-permute-done.26.b_ref = f32[56,256]{1,0:T(8,128)S(1)} collective-permute-done((f32[56,256]{1,0:T(8,128)S(1)}, f32[56,256]{1,0:T(8,128)S(1)}, u32[]{:S(2)}, u32[]{:S(2)}) %collective-permute-start.26) | collective-permute-done | bytes 57376 | tf_op jit(solution)/shard_map/ppermute | solution.py:479
  (70 shorter events, 11.7 us)
Async XLA Ops:
  4.2 34.2 %copy-start.1 = (bf16[1536,256]{1,0:T(8,128)(2,1)S(1)}, bf16[1536,256]{1,0:T(8,128)(2,1)}, u32[]{:S(2)}) copy-start(bf16[1536,256]{1,0:T(8,128)(2,1)} %param.4) | copy-start | bytes 2359300
  4.2 34.2 %copy-start.3 = (bf16[1536,256]{1,0:T(8,128)(2,1)S(1)}, bf16[1536,256]{1,0:T(8,128)(2,1)}, u32[]{:S(2)}) copy-start(bf16[1536,256]{1,0:T(8,128)(2,1)} %param.5) | copy-start | bytes 2359300
  10.0 7.3 %collective-permute-start = (f32[8,256]{1,0:T(8,128)S(1)}, f32[8,256]{1,0:T(8,128)S(1)}, u32[]{:S(2)}, u32[]{:S(2)}) collective-permute-start(f32[8,256]{1,0:T(8,128)S(1)} %get-tuple-element.36), channel_id=1, source_target_pairs={{0,4},{1,5},{2,6},{3,7},{4,0},{5,1},{6,2},{7,3},{8,12},{9,13},{10,... | collective-permute-start | bytes 24584 | tf_op jit(solution)/shard_map/ppermute | solution.py:479
  14.3 5.4 %collective-permute-start.5 = (f32[8,256]{1,0:T(8,128)S(1)}, f32[8,256]{1,0:T(8,128)S(1)}, u32[]{:S(2)}, u32[]{:S(2)}) collective-permute-start(f32[8,256]{1,0:T(8,128)S(1)} %get-tuple-element.37), channel_id=1, source_target_pairs={{0,24},{8,16},{16,8},{24,0},{32,56},{40,48},{48,40},{56,32},{64,88... | collective-permute-start | bytes 24584 | tf_op jit(solution)/shard_map/ppermute | solution.py:479
  14.3 5.4 %collective-permute-start.4 = (f32[8,256]{1,0:T(8,128)S(1)}, f32[8,256]{1,0:T(8,128)S(1)}, u32[]{:S(2)}, u32[]{:S(2)}) collective-permute-start(f32[8,256]{1,0:T(8,128)S(1)} %get-tuple-element.37), channel_id=1, source_target_pairs={{0,16},{8,24},{16,0},{24,8},{32,48},{40,56},{48,32},{56,40},{64,80... | collective-permute-start | bytes 24584 | tf_op jit(solution)/shard_map/ppermute | solution.py:479
  17.3 2.4 %collective-permute-start.3 = (f32[8,256]{1,0:T(8,128)S(1)}, f32[8,256]{1,0:T(8,128)S(1)}, u32[]{:S(2)}, u32[]{:S(2)}) collective-permute-start(f32[8,256]{1,0:T(8,128)S(1)} %get-tuple-element.37), channel_id=1, source_target_pairs={{0,8},{8,0},{16,24},{24,16},{32,40},{40,32},{48,56},{56,48},{64,72... | collective-permute-start | bytes 24584 | tf_op jit(solution)/shard_map/ppermute | solution.py:479
  17.3 12.7 %collective-permute-start.1 = (f32[8,256]{1,0:T(8,128)S(1)}, f32[8,256]{1,0:T(8,128)S(1)}, u32[]{:S(2)}, u32[]{:S(2)}) collective-permute-start(f32[8,256]{1,0:T(8,128)S(1)} %multiply_add_fusion.5), channel_id=1, source_target_pairs={{0,2},{1,3},{2,0},{3,1},{4,6},{5,7},{6,4},{7,5},{8,10},{9,11},{10,... | collective-permute-start | bytes 24584 | tf_op jit(solution)/shard_map/ppermute | solution.py:479
  20.4 18.1 %all-to-all-start = ((f32[8,8,256]{2,1,0:T(8,128)}), f32[8,8,256]{2,1,0:T(8,128)S(1)}, u32[]{:S(2)}, u32[]{:S(2)}) async-start(f32[8,8,256]{2,1,0:T(8,128)} %broadcast_in_dim.4), calls=%async_computation | async-start | bytes 131072 | tf_op jit(solution)/shard_map/all_to_all | solution.py:489
  30.1 3.7 %collective-permute-start.2 = (f32[8,256]{1,0:T(8,128)S(1)}, f32[8,256]{1,0:T(8,128)S(1)}, u32[]{:S(2)}, u32[]{:S(2)}) collective-permute-start(f32[8,256]{1,0:T(8,128)S(1)} %multiply_add_fusion.4.rest_0_), channel_id=1, source_target_pairs={{0,1},{1,0},{2,3},{3,2},{4,5},{5,4},{6,7},{7,6},{8,9},{9,8},{10,11... | collective-permute-start | bytes 24584 | tf_op jit(solution)/shard_map/ppermute | solution.py:479
  44.2 7.0 %collective-permute-start.6 = (f32[8,256]{1,0:T(8,128)S(1)}, f32[8,256]{1,0:T(8,128)S(1)}, u32[]{:S(2)}, u32[]{:S(2)}) collective-permute-start(f32[8,256]{1,0:T(8,128)S(1)} %get-tuple-element.40), channel_id=1, source_target_pairs={{0,4},{1,5},{2,6},{3,7},{4,0},{5,1},{6,2},{7,3},{8,12},{9,13},{10,... | collective-permute-start | bytes 24584 | tf_op jit(solution)/shard_map/ppermute | solution.py:479
  48.2 3.3 %collective-permute-start.11 = (f32[8,256]{1,0:T(8,128)S(1)}, f32[8,256]{1,0:T(8,128)S(1)}, u32[]{:S(2)}, u32[]{:S(2)}) collective-permute-start(f32[8,256]{1,0:T(8,128)S(1)} %get-tuple-element.41), channel_id=1, source_target_pairs={{0,24},{8,16},{16,8},{24,0},{32,56},{40,48},{48,40},{56,32},{64,88... | collective-permute-start | bytes 24584 | tf_op jit(solution)/shard_map/ppermute | solution.py:479
  48.2 4.6 %collective-permute-start.10 = (f32[8,256]{1,0:T(8,128)S(1)}, f32[8,256]{1,0:T(8,128)S(1)}, u32[]{:S(2)}, u32[]{:S(2)}) collective-permute-start(f32[8,256]{1,0:T(8,128)S(1)} %get-tuple-element.41), channel_id=1, source_target_pairs={{0,16},{8,24},{16,0},{24,8},{32,48},{40,56},{48,32},{56,40},{64,80... | collective-permute-start | bytes 24584 | tf_op jit(solution)/shard_map/ppermute | solution.py:479
  51.0 1.8 %collective-permute-start.9 = (f32[8,256]{1,0:T(8,128)S(1)}, f32[8,256]{1,0:T(8,128)S(1)}, u32[]{:S(2)}, u32[]{:S(2)}) collective-permute-start(f32[8,256]{1,0:T(8,128)S(1)} %get-tuple-element.41), channel_id=1, source_target_pairs={{0,8},{8,0},{16,24},{24,16},{32,40},{40,32},{48,56},{56,48},{64,72... | collective-permute-start | bytes 24584 | tf_op jit(solution)/shard_map/ppermute | solution.py:479
  51.2 6.6 %collective-permute-start.7 = (f32[8,256]{1,0:T(8,128)S(1)}, f32[8,256]{1,0:T(8,128)S(1)}, u32[]{:S(2)}, u32[]{:S(2)}) collective-permute-start(f32[8,256]{1,0:T(8,128)S(1)} %multiply_add_fusion.2), channel_id=1, source_target_pairs={{0,2},{1,3},{2,0},{3,1},{4,6},{5,7},{6,4},{7,5},{8,10},{9,11},{10,... | collective-permute-start | bytes 24584 | tf_op jit(solution)/shard_map/ppermute | solution.py:479
  53.5 12.8 %all-to-all-start.1 = ((f32[8,8,256]{2,1,0:T(8,128)}), f32[8,8,256]{2,1,0:T(8,128)S(1)}, u32[]{:S(2)}, u32[]{:S(2)}) async-start(f32[8,8,256]{2,1,0:T(8,128)} %broadcast_in_dim.5), calls=%async_computation.1 | async-start | bytes 131072 | tf_op jit(solution)/shard_map/all_to_all | solution.py:489
  57.7 4.0 %collective-permute-start.8 = (f32[8,256]{1,0:T(8,128)S(1)}, f32[8,256]{1,0:T(8,128)S(1)}, u32[]{:S(2)}, u32[]{:S(2)}) collective-permute-start(f32[8,256]{1,0:T(8,128)S(1)} %multiply_add_fusion.1.rest_0_), channel_id=1, source_target_pairs={{0,1},{1,0},{2,3},{3,2},{4,5},{5,4},{6,7},{7,6},{8,9},{9,8},{10,11... | collective-permute-start | bytes 24584 | tf_op jit(solution)/shard_map/ppermute | solution.py:479
  84.0 16.7 %collective-permute-start.14 = (f32[16,56,256]{2,1,0:T(8,128)}, f32[16,56,256]{2,1,0:T(8,128)S(1)}, u32[]{:S(2)}, u32[]{:S(2)}) collective-permute-start(f32[16,56,256]{2,1,0:T(8,128)} %get-tuple-element.47), channel_id=1, source_target_pairs={{0,8},{8,0},{16,24},{24,16},{32,40},{40,32},{48,56},{56,48},{64,72... | collective-permute-start | bytes 2752520 | tf_op jit(solution)/shard_map/ppermute | solution.py:479
  97.4 8.4 %collective-permute-start.12 = (f32[200,256]{1,0:T(8,128)}, f32[200,256]{1,0:T(8,128)S(1)}, u32[]{:S(2)}, u32[]{:S(2)}) collective-permute-start(f32[200,256]{1,0:T(8,128)} %get-tuple-element.44), channel_id=1, source_target_pairs={{0,1},{1,2},{2,3},{3,0},{4,5},{5,6},{6,7},{7,4},{8,9},{9,10},{10,1... | collective-permute-start | bytes 614408 | tf_op jit(solution)/shard_map/ppermute | solution.py:549
  97.7 8.1 %collective-permute-start.13 = (f32[200,256]{1,0:T(8,128)}, f32[200,256]{1,0:T(8,128)S(1)}, u32[]{:S(2)}, u32[]{:S(2)}) collective-permute-start(f32[200,256]{1,0:T(8,128)} %get-tuple-element.45), channel_id=1, source_target_pairs={{1,0},{2,1},{3,2},{0,3},{5,4},{6,5},{7,6},{4,7},{9,8},{10,9},{11,1... | collective-permute-start | bytes 614408 | tf_op jit(solution)/shard_map/ppermute | solution.py:550
  101.0 5.5 %collective-permute-start.15 = (f32[56,256]{1,0:T(8,128)S(1)}, f32[56,256]{1,0:T(8,128)S(1)}, u32[]{:S(2)}, u32[]{:S(2)}) collective-permute-start(f32[56,256]{1,0:T(8,128)S(1)} %get-tuple-element.48), channel_id=1, source_target_pairs={{0,32},{8,40},{16,48},{24,56},{32,64},{40,72},{48,80},{56,88},{64,... | collective-permute-start | bytes 172040 | tf_op jit(solution)/shard_map/ppermute | solution.py:563
  101.1 5.4 %collective-permute-start.16 = (f32[56,256]{1,0:T(8,128)S(1)}, f32[56,256]{1,0:T(8,128)S(1)}, u32[]{:S(2)}, u32[]{:S(2)}) collective-permute-start(f32[56,256]{1,0:T(8,128)S(1)} %get-tuple-element.49), channel_id=1, source_target_pairs={{32,0},{40,8},{48,16},{56,24},{64,32},{72,40},{80,48},{88,56},{96,... | collective-permute-start | bytes 172040 | tf_op jit(solution)/shard_map/ppermute | solution.py:564
  106.9 14.0 %collective-permute-start.17 = (f32[2,200,256]{2,1,0:T(8,128)S(1)}, f32[2,200,256]{2,1,0:T(8,128)S(1)}, u32[]{:S(2)}, u32[]{:S(2)}) collective-permute-start(f32[2,200,256]{2,1,0:T(8,128)S(1)} %get-tuple-element.53), channel_id=1, source_target_pairs={{0,1},{1,2},{2,3},{3,0},{4,5},{5,6},{6,7},{7,4},{8,9},{9,10},{10,1... | collective-permute-start | bytes 1228808 | tf_op jit(solution)/shard_map/ppermute | solution.py:588
  107.2 13.7 %collective-permute-start.18 = (f32[2,200,256]{2,1,0:T(8,128)S(1)}, f32[2,200,256]{2,1,0:T(8,128)S(1)}, u32[]{:S(2)}, u32[]{:S(2)}) collective-permute-start(f32[2,200,256]{2,1,0:T(8,128)S(1)} %get-tuple-element.54), channel_id=1, source_target_pairs={{1,0},{2,1},{3,2},{0,3},{5,4},{6,5},{7,6},{4,7},{9,8},{10,9},{11,1... | collective-permute-start | bytes 1228808 | tf_op jit(solution)/shard_map/ppermute | solution.py:589
  110.6 6.1 %collective-permute-start.20 = (f32[2,56,256]{2,1,0:T(8,128)S(1)}, f32[2,56,256]{2,1,0:T(8,128)S(1)}, u32[]{:S(2)}, u32[]{:S(2)}) collective-permute-start(f32[2,56,256]{2,1,0:T(8,128)S(1)} %get-tuple-element.58), channel_id=1, source_target_pairs={{0,32},{8,40},{16,48},{24,56},{32,64},{40,72},{48,80},{56,88},{64,... | collective-permute-start | bytes 344072 | tf_op jit(solution)/shard_map/ppermute | solution.py:563
  110.7 10.2 %copy-start.5 = (f32[2,200,256]{2,1,0:T(8,128)S(1)}, f32[2,200,256]{2,1,0:T(8,128)}, u32[]{:S(2)}) copy-start(f32[2,200,256]{2,1,0:T(8,128)} %copy-done.4) | copy-start | bytes 1228804
  110.7 6.0 %collective-permute-start.21 = (f32[2,56,256]{2,1,0:T(8,128)S(1)}, f32[2,56,256]{2,1,0:T(8,128)S(1)}, u32[]{:S(2)}, u32[]{:S(2)}) collective-permute-start(f32[2,56,256]{2,1,0:T(8,128)S(1)} %get-tuple-element.59), channel_id=1, source_target_pairs={{32,0},{40,8},{48,16},{56,24},{64,32},{72,40},{80,48},{88,56},{96,... | collective-permute-start | bytes 344072 | tf_op jit(solution)/shard_map/ppermute | solution.py:564
  117.6 6.3 %collective-permute-start.22 = (f32[2,56,256]{2,1,0:T(8,128)}, f32[2,56,256]{2,1,0:T(8,128)S(1)}, u32[]{:S(2)}, u32[]{:S(2)}) collective-permute-start(f32[2,56,256]{2,1,0:T(8,128)} %get-tuple-element.60), channel_id=1, source_target_pairs={{0,32},{8,40},{16,48},{24,56},{32,64},{40,72},{48,80},{56,88},{64,... | collective-permute-start | bytes 344072 | tf_op jit(solution)/shard_map/ppermute | solution.py:563
  117.6 6.3 %collective-permute-start.23 = (f32[2,56,256]{2,1,0:T(8,128)S(1)}, f32[2,56,256]{2,1,0:T(8,128)S(1)}, u32[]{:S(2)}, u32[]{:S(2)}) collective-permute-start(f32[2,56,256]{2,1,0:T(8,128)S(1)} %get-tuple-element.61), channel_id=1, source_target_pairs={{32,0},{40,8},{48,16},{56,24},{64,32},{72,40},{80,48},{88,56},{96,... | collective-permute-start | bytes 344072 | tf_op jit(solution)/shard_map/ppermute | solution.py:564
  121.4 14.7 %collective-permute-start.19 = (f32[200,256]{1,0:T(8,128)S(1)}, f32[200,256]{1,0:T(8,128)S(1)}, u32[]{:S(2)}, u32[]{:S(2)}) collective-permute-start(f32[200,256]{1,0:T(8,128)S(1)} %get-tuple-element.56), channel_id=1, source_target_pairs={{0,4},{1,5},{2,6},{3,7},{4,0},{5,1},{6,2},{7,3},{8,12},{9,13},{10,... | collective-permute-start | bytes 614408 | tf_op jit(solution)/shard_map/ppermute | solution.py:479
  124.1 6.1 %collective-permute-start.24 = (f32[2,56,256]{2,1,0:T(8,128)S(1)}, f32[2,56,256]{2,1,0:T(8,128)S(1)}, u32[]{:S(2)}, u32[]{:S(2)}) collective-permute-start(f32[2,56,256]{2,1,0:T(8,128)S(1)} %get-tuple-element.62), channel_id=1, source_target_pairs={{0,32},{8,40},{16,48},{24,56},{32,64},{40,72},{48,80},{56,88},{64,... | collective-permute-start | bytes 344072 | tf_op jit(solution)/shard_map/ppermute | solution.py:563
  124.2 6.0 %collective-permute-start.25 = (f32[2,56,256]{2,1,0:T(8,128)S(1)}, f32[2,56,256]{2,1,0:T(8,128)S(1)}, u32[]{:S(2)}, u32[]{:S(2)}) collective-permute-start(f32[2,56,256]{2,1,0:T(8,128)S(1)} %get-tuple-element.63), channel_id=1, source_target_pairs={{32,0},{40,8},{48,16},{56,24},{64,32},{72,40},{80,48},{88,56},{96,... | collective-permute-start | bytes 344072 | tf_op jit(solution)/shard_map/ppermute | solution.py:564
  131.0 4.3 %collective-permute-start.26 = (f32[56,256]{1,0:T(8,128)S(1)}, f32[56,256]{1,0:T(8,128)S(1)}, u32[]{:S(2)}, u32[]{:S(2)}) collective-permute-start(f32[56,256]{1,0:T(8,128)S(1)} %get-tuple-element.65), channel_id=1, source_target_pairs={{0,16},{8,24},{16,0},{24,8},{32,48},{40,56},{48,32},{56,40},{64,80... | collective-permute-start | bytes 172040 | tf_op jit(solution)/shard_map/ppermute | solution.py:479
  (8 other events, 17.0 us)
